TPU v7x, 32 devices: a whole 2x2x4 slice. The times are simulated.
32 devices in a mesh: dp: 4 (over y, x), expert: 8 (over z, core).
Axes of the slice: x: 2, y: 2, z: 4, core: 2. Of those that a mesh axis runs over, the one named last changes fastest.
Arguments:
- tokens: bfloat16 [4096, 2048], P(('dp', 'expert')), may hold values from -6 to 6
- cotangent: bfloat16 [4096, 2048], P(('dp', 'expert')), may hold values from -6 to 6
- gate_probs: float32 [4096, 2], P(('dp', 'expert')), may hold values from 0.05 to 1
- expert_ids: int32 [4096, 2], P(('dp', 'expert')), may hold values from 0 to 7, all different within a row; in each aligned block of 128 rows (0 to 127, 128 to 255, ...) at most 40 rows name the same one
- gate_up: bfloat16 [8, 2048, 1536], P('expert'), may hold values from -0.125 to 0.125
- down: bfloat16 [8, 768, 2048], P('expert'), may hold values from -0.21875 to 0.21875
Outputs:
- grad_probs: float32 [4096, 2], P(('dp', 'expert'))
- grad_gate_up: bfloat16 [8, 2048, 1536], P('expert', 'dp')
- grad_down: bfloat16 [8, 768, 2048], P('expert', None, 'dp')
Inputs may be any that keep to these rules, and one draw needn't show every extreme that they name: `expert_ids`: each token names 2 different experts. Among the 128 rows of one device no expert is named more than 40 times, and in every draw some expert is named exactly 40 times by the rows of some device.
All inputs are finite; a program needn't handle non-finite values.
Results may differ from a plain program's by a relative error of at most 0.025.
Values may be sent and summed in bfloat16 or wider, within the bound.
No kernel may reach another device: no remote copies, remote signals or barrier semaphores. Data moves between devices by JAX's collectives and lax.ppermute only.
A program may use at most 128 MiB of HBM per device.

v0:
```python
import functools

import jax
import jax.numpy as jnp
from jax import lax
from jax.experimental import pallas as pl
from jax.experimental.pallas import tpu as pltpu
from jax.sharding import PartitionSpec as P

EXPERTS = 8
CAP = 40
PAIR = 2 * CAP
TILE = 256
MIB = 1024 * 1024
BF16 = jnp.bfloat16
F32 = jnp.float32


def dispatch_kernel(ids_ref, probs_ref, x_ref, dy_ref, *outs):
    row_refs, slot_ref = outs[:-1], outs[-1]
    me = lax.axis_index("expert")
    tok = x_ref.shape[0]
    width = x_ref.shape[1]
    numbers = lax.broadcasted_iota(jnp.int32, (EXPERTS, tok), 0)
    first = jnp.bitwise_xor(ids_ref[0:1, :], me) == numbers
    second = jnp.bitwise_xor(ids_ref[1:2, :], me) == numbers
    either = jnp.where(first | second, 1.0, 0.0)
    prob = jnp.where(first, probs_ref[0:1, :], 0.0) + jnp.where(second, probs_ref[1:2, :], 0.0)
    before = jnp.where(
        lax.broadcasted_iota(jnp.int32, (tok, tok), 0)
        < lax.broadcasted_iota(jnp.int32, (tok, tok), 1),
        1.0,
        0.0,
    )
    position = jnp.dot(either.astype(BF16), before.astype(BF16), preferred_element_type=F32)
    slot = position.astype(jnp.int32) + numbers * CAP
    slot_ref[0:1, :] = jnp.sum(jnp.where(first, slot, 0), axis=0, keepdims=True)
    slot_ref[1:2, :] = jnp.sum(jnp.where(second, slot, 0), axis=0, keepdims=True)
    target = jnp.where(either > 0.5, position, -1.0)
    places = lax.broadcasted_iota(jnp.int32, (CAP, tok), 0).astype(F32)
    picks = [
        jnp.where(places == target[e : e + 1, :], 1.0, 0.0) for e in range(EXPERTS)
    ]
    row_prob = jnp.concatenate(
        [jnp.sum(picks[e] * prob[e : e + 1, :], axis=1, keepdims=True) for e in range(EXPERTS)],
        axis=0,
    )
    pick = jnp.concatenate(picks, axis=0).astype(BF16)
    step = 512
    for at in range(0, width, step):
        rows_x = jnp.dot(pick, x_ref[:, at : at + step], preferred_element_type=F32)
        rows_dy = jnp.dot(pick, dy_ref[:, at : at + step], preferred_element_type=F32)
        scaled = row_prob * rows_dy
        for pair, ref in enumerate(row_refs):
            part = slice(pair * PAIR, (pair + 1) * PAIR)
            ref[:, at : at + step] = rows_x[part].astype(BF16)
            ref[:, width + at : width + at + step] = scaled[part].astype(BF16)


def dispatch_rows(ids, probs, tokens, cotangent):
    tok, width = tokens.shape
    return pl.pallas_call(
        dispatch_kernel,
        out_shape=[jax.ShapeDtypeStruct((PAIR, 2 * width), BF16)] * (EXPERTS // 2)
        + [jax.ShapeDtypeStruct((2, tok), jnp.int32)],
        compiler_params=pltpu.CompilerParams(vmem_limit_bytes=16 * MIB),
        cost_estimate=pl.CostEstimate(
            flops=4 * EXPERTS * CAP * tok * width, bytes_accessed=4_000_000, transcendentals=0
        ),
        name="dispatch_rows",
    )(ids, probs, tokens, cotangent)


def split_rows(top, half):
    blocks = 3 * half // TILE
    low = PAIR - top
    return blocks, low, (blocks + 4) * top, (blocks + 4) * low


def expert_kernel(top, a_ref, b_ref, gate_ref, up_ref, down_ref, *rest):
    own_ref, to_x, to_y, inner_ref, x_rows, s_rows, s_turned, total = rest
    width = gate_ref.shape[0]
    steps = pl.num_programs(0)
    half = TILE * 3
    quarter = width // 4
    blocks, low, from_x, from_y = split_rows(top, half)
    step = pl.program_id(0)
    group = lax.axis_index("dp")

    @pl.when(step == 0)
    def _():
        for rows, start in ((x_rows, 0), (s_rows, width)):
            rows[...] = jnp.concatenate(
                [
                    a_ref[:CAP, start : start + width].astype(F32),
                    b_ref[:, start : start + width].astype(F32),
                ],
                axis=0,
            ).astype(BF16)
        for q in range(4):
            rows = (x_rows, s_rows)[q // 2]

            def cut(mask):
                at = jnp.bitwise_xor(group, mask) * quarter + q % 2 * TILE
                return rows[:, pl.ds(pl.multiple_of(at, TILE), TILE)]

            at = blocks + q
            own_ref[at * PAIR : (at + 1) * PAIR] = cut(0)
            far = cut(3)
            to_x[at * top : (at + 1) * top] = far[:top]
            to_y[at * low : (at + 1) * low] = far[top:]
            start = from_x + blocks * low + q * PAIR
            to_x[start : start + PAIR] = cut(1)
            start = from_y + blocks * top + q * PAIR
            to_y[start : start + PAIR] = cut(2)
        s_turned[...] = s_rows[...].T
        total[...] = jnp.zeros_like(total)

    x = x_rows[...]
    gate = jnp.dot(x, gate_ref[...], preferred_element_type=F32)
    up = jnp.dot(x, up_ref[...], preferred_element_type=F32)
    grad_hidden = jnp.dot(down_ref[...], s_turned[...], preferred_element_type=F32).T
    sigmoid = 1.0 / (1.0 + jnp.exp(-gate))
    activated = gate * sigmoid
    hidden = (activated * up).astype(BF16)
    grad_gate = (grad_hidden * up * sigmoid * (1.0 + gate * (1.0 - sigmoid))).astype(BF16)
    grad_up = (grad_hidden * activated).astype(BF16)
    total[...] += jnp.sum(hidden.astype(F32) * grad_hidden, axis=1, keepdims=True)
    for part, values in enumerate((grad_gate, grad_up, hidden)):
        block = part * steps + step

        def rows_at(start, count):
            return pl.ds(pl.multiple_of(start + block * count, 16), count)

        own_ref[rows_at(0, PAIR)] = values
        to_x[rows_at(0, top)] = values[:top]
        to_x[rows_at(from_x, low)] = values[top:]
        to_y[rows_at(0, low)] = values[top:]
        to_y[rows_at(from_y, top)] = values[:top]

    @pl.when(step == steps - 1)
    def _():
        inner_ref[...] = jnp.broadcast_to(total[...], (PAIR, 128)).T[0:1]


def expert_rows(rows_a, rows_b, weight_gu, weight_down, top):
    width, both = weight_gu.shape
    half = both // 2
    steps = half // TILE
    blocks, low, from_x, from_y = split_rows(top, half)
    shapes = [
        ((blocks + 4) * PAIR, TILE),
        (from_x + blocks * low + 4 * PAIR, TILE),
        (from_y + blocks * top + 4 * PAIR, TILE),
    ]

    def whole(shape):
        return pl.BlockSpec(shape, lambda h: (0, 0))

    return pl.pallas_call(
        functools.partial(expert_kernel, top),
        grid=(steps,),
        in_specs=[
            whole(rows_a.shape),
            whole(rows_b.shape),
            pl.BlockSpec((width, TILE), lambda h: (0, h)),
            pl.BlockSpec((width, TILE), lambda h: (0, h + steps)),
            pl.BlockSpec((TILE, width), lambda h: (h, 0)),
        ],
        out_specs=[whole(shape) for shape in shapes] + [whole((1, PAIR))],
        out_shape=[jax.ShapeDtypeStruct(shape, BF16) for shape in shapes]
        + [jax.ShapeDtypeStruct((1, PAIR), F32)],
        scratch_shapes=[
            pltpu.VMEM((PAIR, width), BF16),
            pltpu.VMEM((PAIR, width), BF16),
            pltpu.VMEM((width, PAIR), BF16),
            pltpu.VMEM((PAIR, 1), F32),
        ],
        compiler_params=pltpu.CompilerParams(vmem_limit_bytes=20 * MIB),
        cost_estimate=pl.CostEstimate(flops=1_000_000, bytes_accessed=1_000_000, transcendentals=0),
        name="expert_rows",
    )(rows_a, rows_b, weight_gu, weight_gu, weight_down)


def gradient_kernel(tops, half, adding, *refs):
    groups, refs = [refs[5 * n : 5 * n + 5] for n in range(len(tops))], refs[5 * len(tops) :]
    if adding:
        (acc_gu, acc_down), refs = refs[:2], refs[2:]
    out_gu, out_down, turned, s_rows = refs
    both = 2 * half // TILE

    def factor(block):
        parts = []
        for top, (own, got_x, got_y, far_top, far_low) in zip(tops, groups):
            _, low, from_x, from_y = split_rows(top, half)
            parts += [
                own[block * PAIR : (block + 1) * PAIR],
                got_x[block * top : (block + 1) * top],
                got_x[from_x + block * low : from_x + (block + 1) * low],
                got_y[from_y + block * top : from_y + (block + 1) * top],
                got_y[block * low : (block + 1) * low],
                far_top[block * top : (block + 1) * top],
                far_low[block * low : (block + 1) * low],
            ]
        return jnp.concatenate(parts, axis=0)

    def piece(q):
        parts = []
        for top, (own, got_x, got_y, far_top, far_low) in zip(tops, groups):
            blocks, low, from_x, from_y = split_rows(top, half)
            block = blocks + q
            at_x = from_x + blocks * low + q * PAIR
            at_y = from_y + blocks * top + q * PAIR
            parts += [
                own[block * PAIR : (block + 1) * PAIR],
                got_x[at_x : at_x + PAIR],
                got_y[at_y : at_y + PAIR],
                far_top[block * top : (block + 1) * top],
                far_low[block * low : (block + 1) * low],
            ]
        return jnp.concatenate(parts, axis=0)

    for q in range(2):
        turned[q * TILE : (q + 1) * TILE, :] = piece(q).T
        s_rows[:, q * TILE : (q + 1) * TILE] = piece(2 + q)
    for block in range(both):
        at = slice(block * TILE, (block + 1) * TILE)
        grad = jnp.dot(turned[...], factor(block), preferred_element_type=F32)
        if adding:
            grad = grad + acc_gu[:, at]
        out_gu[:, at] = grad.astype(out_gu.dtype)
    for block in range(half // TILE):
        at = slice(block * TILE, (block + 1) * TILE)
        grad = jnp.dot(factor(both + block).T, s_rows[...], preferred_element_type=F32)
        if adding:
            grad = grad + acc_down[at, :]
        out_down[at, :] = grad.astype(out_down.dtype)


def gradients(tops, pieces, half, quarter, sums=(), final=False):
    kept = BF16 if final else F32
    rows = 4 * PAIR * len(tops)
    vmem = pl.BlockSpec(memory_space=pltpu.VMEM)
    return pl.pallas_call(
        functools.partial(gradient_kernel, tops, half, len(sums)),
        in_specs=[vmem] * (len(pieces) + len(sums)),
        out_specs=[vmem] * 2,
        out_shape=[
            jax.ShapeDtypeStruct((quarter, 2 * half), kept),
            jax.ShapeDtypeStruct((half, quarter), kept),
        ],
        scratch_shapes=[pltpu.VMEM((quarter, rows), BF16), pltpu.VMEM((rows, quarter), BF16)],
        compiler_params=pltpu.CompilerParams(vmem_limit_bytes=24 * MIB),
        cost_estimate=pl.CostEstimate(flops=1_000_000, bytes_accessed=1_000_000, transcendentals=0),
        name="gradients",
    )(*pieces, *sums)


def exchange(values, axis, mask):
    size = lax.axis_size(axis)
    return lax.ppermute(values, axis, [(n, n ^ mask) for n in range(size)])


def swap(values):
    return lax.all_to_all(values, "expert", split_axis=0, concat_axis=0, tiled=True)


def after(values, *others):
    return lax.optimization_barrier((values,) + others)[0]


def plane_body(tokens, cotangent, gate_probs, expert_ids, gate_up, down):
    me = lax.axis_index("expert")
    half = gate_up.shape[2] // 2
    quarter = tokens.shape[1] // 4
    ids, probs = expert_ids.T, gate_probs.T
    *local, slots = dispatch_rows(ids, probs, tokens, cotangent)
    tops = (48, 32, 48, 32)
    inner, pieces = [], []

    def other_core(rows):
        return exchange(rows[CAP:], "expert", 1)

    def compute(rows, other, *others):
        top = tops[len(inner)]
        other = after(other, *others)
        own, to_x, to_y, found = expert_rows(rows, other, gate_up[0], down[0], top)
        inner.append(found)
        _, _, from_x, from_y = split_rows(top, half)
        got_x, got_y = exchange(to_x, "dp", 1), exchange(to_y, "dp", 2)
        forward = (got_x[:from_x], got_y[:from_y])
        far_top, far_low = exchange(forward[0], "dp", 2), exchange(forward[1], "dp", 1)
        pieces.append([own, got_x, got_y, far_top, far_low])

    rows_1 = exchange(local[1], "expert", 2)
    other = other_core(local[0])
    rows_2 = exchange(local[2], "expert", 4)
    compute(local[0], other)
    rows_1 = after(rows_1, inner[0])
    compute(rows_1, other_core(rows_1))
    rows_2 = after(rows_2, inner[1])
    rows_3 = exchange(after(local[3], rows_2), "expert", 6)
    compute(rows_2, other_core(rows_2), *pieces[0])
    rows_3 = after(rows_3, inner[2])
    compute(rows_3, other_core(rows_3), *pieces[1])
    early = after(tuple(pieces[0] + pieces[1]), inner[3])
    sums = gradients(tops[:2], early, half, quarter)
    sums = gradients(tops[2:3], pieces[2], half, quarter, sums)
    grad_gu, grad_down = gradients(tops[3:], pieces[3], half, quarter, sums, True)
    numbers = jnp.arange(EXPERTS, dtype=jnp.int32)
    mine = (numbers[:, None] == jnp.bitwise_xor(numbers, me)[None, :])[:, :, None]
    rows_inner = after(jnp.concatenate(inner, axis=1), *pieces[2]).reshape(EXPERTS, CAP)
    sent = jnp.sum(jnp.where(mine, rows_inner[None], 0.0), axis=1)
    returned = jnp.sum(jnp.where(mine, swap(sent)[None], 0.0), axis=1).reshape(-1)
    chosen = slots[:, None, :] == jnp.arange(EXPERTS * CAP, dtype=jnp.int32)[None, :, None]
    grad_probs = jnp.sum(jnp.where(chosen, returned[None, :, None], 0.0), axis=1) / probs
    return (grad_probs.T, grad_gu[None], grad_down[None])


def widen(values, slices, expert_count):
    tail = values.shape[1:]
    spread = values.reshape((EXPERTS, 1, CAP) + tail)
    spread = jnp.broadcast_to(spread, (EXPERTS, slices, CAP) + tail)
    return spread.reshape((expert_count, CAP) + tail)


def sliced_body(tokens, cotangent, gate_probs, expert_ids, gate_up, down):
    expert_count = lax.axis_size("expert")
    slices = expert_count // EXPERTS
    tok_count, width = tokens.shape
    choose_count = expert_ids.shape[1]
    half = gate_up.shape[2] // 2
    slot_rows = EXPERTS * CAP
    flat_ids = expert_ids.reshape(-1)
    choose = (flat_ids[:, None] == jnp.arange(EXPERTS, dtype=jnp.int32)[None, :]).astype(jnp.int32)
    earlier = jnp.cumsum(choose, axis=0) - choose
    slot_of = flat_ids * CAP + jnp.sum(earlier * choose, axis=1)
    picked = jnp.arange(slot_rows, dtype=jnp.int32)[:, None] == slot_of[None, :]
    picked_tok = jnp.any(picked.reshape(slot_rows, tok_count, choose_count), axis=2).astype(BF16)
    slot_prob = jnp.sum(jnp.where(picked, gate_probs.reshape(-1)[None, :], 0.0), axis=1)
    local_x = jnp.dot(picked_tok, tokens, preferred_element_type=F32).astype(BF16)
    local_dy = jnp.dot(picked_tok, cotangent, preferred_element_type=F32)
    local_scaled = (slot_prob[:, None] * local_dy).astype(BF16)
    rows_x = swap(widen(local_x, slices, expert_count)).reshape(-1, width)
    rows_s = swap(widen(local_scaled, slices, expert_count)).reshape(-1, width)
    both = jnp.dot(rows_x, gate_up[0], preferred_element_type=F32)
    gate, up = both[:, :half], both[:, half:]
    sigmoid = jax.nn.sigmoid(gate)
    activated = gate * sigmoid
    hidden = (activated * up).astype(BF16)
    grad_hidden = lax.dot_general(
        rows_s, down[0], (((1,), (1,)), ((), ())), preferred_element_type=F32
    )
    inner = jnp.sum(hidden.astype(F32) * grad_hidden, axis=1)
    grad_gate = (grad_hidden * up * sigmoid * (1.0 + gate * (1.0 - sigmoid))).astype(BF16)
    grad_up = (grad_hidden * activated).astype(BF16)
    grad_both = jnp.concatenate([grad_gate, grad_up], axis=1)
    over_rows = (((0,), (0,)), ((), ()))
    grad_gu = lax.dot_general(rows_x, grad_both, over_rows, preferred_element_type=F32)
    grad_down = lax.dot_general(hidden, rows_s, over_rows, preferred_element_type=F32)
    returned = swap(inner.reshape(expert_count, CAP))
    per_slot = jnp.sum(returned.reshape(EXPERTS, slices, CAP), axis=1).reshape(slot_rows)
    grad_probs = jnp.sum(jnp.where(picked, per_slot[:, None], 0.0), axis=0)
    grad_probs = grad_probs.reshape(tok_count, choose_count) / gate_probs
    reduced_gu = lax.psum_scatter(grad_gu.astype(BF16), "dp", scatter_dimension=0, tiled=True)
    reduced_down = lax.psum_scatter(grad_down.astype(BF16), "dp", scatter_dimension=1, tiled=True)
    return (grad_probs, reduced_gu[None], reduced_down[None])


def solution(mesh):
    whole_experts = mesh.shape["expert"] == EXPERTS and mesh.shape["dp"] == 4
    return jax.shard_map(
        plane_body if whole_experts else sliced_body,
        mesh=mesh,
        in_specs=(
            P(("dp", "expert"), None),
            P(("dp", "expert"), None),
            P(("dp", "expert"), None),
            P(("dp", "expert"), None),
            P("expert", None, None),
            P("expert", None, None),
        ),
        out_specs=(P(("dp", "expert"), None), P("expert", "dp", None), P("expert", None, "dp")),
        check_vma=False,
    )
```

profile of v0, /device:TPU:0, one launch (start us, length us, event | category | flops | bytes accessed | tf_op | source)
XLA Modules:
  0.0 163.6 jit_solution(9900257095766156772)
XLA Ops:
  1.3 1.0 copy-done.33
  2.4 1.0 copy-done.34
  4.1 1.0 dispatch_rows.1
  5.0 3.1 %collective-permute-start.1 = (bf16[80,4096]{1,0:T(8,128)(2,1)S(1)}, bf16[80,4096]{1,0:T(8,128)(2,1)S(1)}, u32[]{:S(2)}, u32[]{:S(2)}) collective-permute-start(bf16[80,4096]{1,0:T(8,128)(2,1)S(1)} %get-tuple-element.50), channel_id=1, source_target_pairs={{0,2},{1,3},{2,0},{3,1},{4,6},{5,7},{6,4},{7,5},{8,10},{9,11},{10,... | collective-permute-start | bytes 1966088 | tf_op jit(solution)/shard_map/ppermute | solution.py:261
  8.2 2.6 %collective-permute-start.3 = (bf16[80,4096]{1,0:T(8,128)(2,1)S(1)}, bf16[80,4096]{1,0:T(8,128)(2,1)S(1)}, u32[]{:S(2)}, u32[]{:S(2)}) collective-permute-start(bf16[80,4096]{1,0:T(8,128)(2,1)S(1)} %get-tuple-element.53), channel_id=1, source_target_pairs={{0,4},{1,5},{2,6},{3,7},{4,0},{5,1},{6,2},{7,3},{8,12},{9,13},{10,... | collective-permute-start | bytes 1966088 | tf_op jit(solution)/shard_map/ppermute | solution.py:261
  10.9 2.8 %copy-done = bf16[1,2048,1536]{2,1,0:T(8,128)(2,1)S(1)} copy-done((bf16[1,2048,1536]{2,1,0:T(8,128)(2,1)S(1)}, bf16[1,2048,1536]{2,1,0:T(8,128)(2,1)}, u32[]{:S(2)}) %copy-start) | copy-done | bytes 6291480
  13.7 1.9 %copy-done.3 = bf16[1,768,2048]{2,1,0:T(8,128)(2,1)S(1)} copy-done((bf16[1,768,2048]{2,1,0:T(8,128)(2,1)S(1)}, bf16[1,768,2048]{2,1,0:T(8,128)(2,1)}, u32[]{:S(2)}) %copy-start.3) | copy-done | bytes 3145752
  15.6 3.6 %expert_rows.4 = (bf16[1040,256]{1,0:T(8,128)(2,1)S(1)}, bf16[1232,256]{1,0:T(8,128)(2,1)S(1)}, bf16[1168,256]{1,0:T(8,128)(2,1)S(1)}, f32[1,80]{1,0:T(1,128)S(1)}) custom-call(bf16[80,4096]{1,0:T(8,128)(2,1)S(1)} %get-tuple-element.48.a_ref, bf16[40,4096]{1,0:T(8,128)(2,1)S(1)} %collective-permute-done.b_ref, bf16[2048,1536]{1,0:T(8,128)(2,1)S(1)} %bitcast.12, ...), custom_call_target="tpu_custom_call" | custom-call | flops 1000000 | bytes 1000000 | tf_op jit(solution)/shard_map/expert_rows/pallas_call | solution.py:160
  19.2 1.5 collective-permute-start.6
  20.8 1.5 collective-permute-start.5
  22.3 13.5 %collective-permute-done.1.a_ref = bf16[80,4096]{1,0:T(8,128)(2,1)S(1)} collective-permute-done((bf16[80,4096]{1,0:T(8,128)(2,1)S(1)}, bf16[80,4096]{1,0:T(8,128)(2,1)S(1)}, u32[]{:S(2)}, u32[]{:S(2)}) %collective-permute-start.1) | collective-permute-done | bytes 655392 | tf_op jit(solution)/shard_map/ppermute | solution.py:261
  35.9 0.8 copy-done.13
  36.7 1.7 %collective-permute-start.8 = (bf16[416,256]{1,0:T(8,128)(2,1)S(1)}, bf16[416,256]{1,0:T(8,128)(2,1)S(1)}, u32[]{:S(2)}, u32[]{:S(2)}) collective-permute-start(bf16[416,256]{1,0:T(8,128)(2,1)S(1)} %slice.49), channel_id=1, source_target_pairs={{0,8},{8,0},{16,24},{24,16},{1,9},{9,1},{17,25},{25,17},{2,10},{10... | collective-permute-start | bytes 638984 | tf_op jit(solution)/shard_map/ppermute | solution.py:261
  38.4 3.7 %expert_rows.5 = (bf16[1040,256]{1,0:T(8,128)(2,1)S(1)}, bf16[1168,256]{1,0:T(8,128)(2,1)S(1)}, bf16[1232,256]{1,0:T(8,128)(2,1)S(1)}, f32[1,80]{1,0:T(1,128)S(1)}) custom-call(bf16[80,4096]{1,0:T(8,128)(2,1)S(1)} %collective-permute-done.1.a_ref, bf16[40,4096]{1,0:T(8,128)(2,1)S(1)} %collective-permute-done.2.b_ref, bf16[2048,1536]{1,0:T(8,128)(2,1)S(1)} %bitcast.14, ...), custom_call_target="tpu_custom_call" | custom-call | flops 1000000 | bytes 1000000 | tf_op jit(solution)/shard_map/expert_rows/pallas_call | solution.py:160
  42.0 2.5 %collective-permute-start.9 = (bf16[80,4096]{1,0:T(8,128)(2,1)S(1)}, bf16[80,4096]{1,0:T(8,128)(2,1)S(1)}, u32[]{:S(2)}, u32[]{:S(2)}) collective-permute-start(bf16[80,4096]{1,0:T(8,128)(2,1)S(1)} %get-tuple-element.61), channel_id=1, source_target_pairs={{0,6},{1,7},{2,4},{3,5},{4,2},{5,3},{6,0},{7,1},{8,14},{9,15},{10,... | collective-permute-start | bytes 1966088 | tf_op jit(solution)/shard_map/ppermute | solution.py:261
  44.5 1.5 collective-permute-start.12
  46.8 0.7 copy-done.27
  47.5 0.7 collective-permute-start.11
  48.2 19.2 %collective-permute-done.7.refs_3_ = bf16[624,256]{1,0:T(8,128)(2,1)S(1)} collective-permute-done((bf16[624,256]{1,0:T(8,128)(2,1)S(1)}, bf16[624,256]{1,0:T(8,128)(2,1)S(1)}, u32[]{:S(2)}, u32[]{:S(2)}) %collective-permute-start.7) | collective-permute-done | bytes 319520 | tf_op jit(solution)/shard_map/ppermute | solution.py:261
  67.4 0.7 copy-done.25
  68.2 4.7 %expert_rows.6 = (bf16[1040,256]{1,0:T(8,128)(2,1)S(1)}, bf16[1232,256]{1,0:T(8,128)(2,1)}, bf16[1168,256]{1,0:T(8,128)(2,1)}, f32[1,80]{1,0:T(1,128)S(1)}) custom-call(bf16[80,4096]{1,0:T(8,128)(2,1)S(1)} %collective-permute-done.3.a_ref, bf16[40,4096]{1,0:T(8,128)(2,1)S(1)} %collective-permute-done.4.b_ref, bf16[2048,1536]{1,0:T(8,128)(2,1)S(1)} %bitcast.16, ...), custom_call_target="tpu_custom_call" | custom-call | flops 1000000 | bytes 1000000 | tf_op jit(solution)/shard_map/expert_rows/pallas_call | solution.py:160
  73.5 1.5 collective-permute-start.16
  75.0 0.7 slice.41
  75.8 0.8 copy-done.7
  76.6 0.8 slice.51
  77.4 0.8 copy-done.11
  78.3 1.4 collective-permute-start.14
  79.6 0.7 slice.50
  80.3 0.8 copy-done.15
  81.7 10.8 %collective-permute-done.13.refs_8_ = bf16[416,256]{1,0:T(8,128)(2,1)} collective-permute-done((bf16[416,256]{1,0:T(8,128)(2,1)}, bf16[416,256]{1,0:T(8,128)(2,1)}, u32[]{:S(2)}, u32[]{:S(2)}) %collective-permute-start.13) | collective-permute-done | bytes 213024 | tf_op jit(solution)/shard_map/ppermute | solution.py:261
  92.5 2.7 %collective-permute-done.14.refs_9_ = bf16[624,256]{1,0:T(8,128)(2,1)} collective-permute-done((bf16[624,256]{1,0:T(8,128)(2,1)}, bf16[624,256]{1,0:T(8,128)(2,1)}, u32[]{:S(2)}, u32[]{:S(2)}) %collective-permute-start.14) | collective-permute-done | bytes 319520 | tf_op jit(solution)/shard_map/ppermute | solution.py:261
  95.2 2.8 %copy-done.2 = bf16[1,2048,1536]{2,1,0:T(8,128)(2,1)S(1)} copy-done((bf16[1,2048,1536]{2,1,0:T(8,128)(2,1)S(1)}, bf16[1,2048,1536]{2,1,0:T(8,128)(2,1)}, u32[]{:S(2)}) %copy-start.2) | copy-done | bytes 6291480
  98.0 1.1 copy-done.8
  99.1 4.7 %expert_rows.7 = (bf16[1040,256]{1,0:T(8,128)(2,1)S(1)}, bf16[1168,256]{1,0:T(8,128)(2,1)}, bf16[1232,256]{1,0:T(8,128)(2,1)}, f32[1,80]{1,0:T(1,128)S(1)}) custom-call(bf16[80,4096]{1,0:T(8,128)(2,1)S(1)} %copy-done.8, bf16[40,4096]{1,0:T(8,128)(2,1)S(1)} %collective-permute-done.10.b_ref, bf16[2048,1536]{1,0:T(8,128)(2,1)S(1)} %bitcast.18, ...), custom_call_target="tpu_custom_call" | custom-call | flops 1000000 | bytes 1000000 | tf_op jit(solution)/shard_map/expert_rows/pallas_call | solution.py:160
  103.7 0.8 copy-done.23
  104.6 1.5 collective-permute-start.20
  106.1 0.9 slice.53
  107.7 1.0 slice.52
  109.3 1.5 collective-permute-start.19
  110.8 4.5 %collective-permute-done.18.refs_4_ = bf16[416,256]{1,0:T(8,128)(2,1)S(1)} collective-permute-done((bf16[416,256]{1,0:T(8,128)(2,1)S(1)}, bf16[416,256]{1,0:T(8,128)(2,1)S(1)}, u32[]{:S(2)}, u32[]{:S(2)}) %collective-permute-start.18) | collective-permute-done | bytes 213024 | tf_op jit(solution)/shard_map/ppermute | solution.py:261
  115.3 0.7 copy-done.29
  116.0 9.9 %collective-permute-done.17.refs_3_ = bf16[624,256]{1,0:T(8,128)(2,1)S(1)} collective-permute-done((bf16[624,256]{1,0:T(8,128)(2,1)S(1)}, bf16[624,256]{1,0:T(8,128)(2,1)S(1)}, u32[]{:S(2)}, u32[]{:S(2)}) %collective-permute-start.17) | collective-permute-done | bytes 319520 | tf_op jit(solution)/shard_map/ppermute | solution.py:261
  126.0 0.7 select_reduce_fusion.2
  126.7 3.3 %all-to-all-start = ((f32[8,1,40]{2,1,0:T(1,128)}), f32[8,1,40]{2,1,0:T(1,128)S(1)}, u32[]{:S(2)}, u32[]{:S(2)}) async-start(f32[8,1,40]{2,1,0:T(1,128)} %bitcast.5), calls=%async_computation | async-start | bytes 8192 | tf_op jit(solution)/shard_map/all_to_all | solution.py:265
  130.0 1.1 copy-done.10
  131.0 1.1 copy-done.12
  132.1 1.1 copy-done.14
  133.2 1.1 copy-done.16
  134.3 1.0 copy-done.18
  135.3 1.0 copy-done.20
  136.3 1.0 copy-done.26
  137.3 0.9 copy-done.28
  138.2 3.2 %gradients.3 = (f32[512,1536]{1,0:T(8,128)S(1)}, f32[768,512]{1,0:T(8,128)S(1)}) custom-call(bf16[1040,256]{1,0:T(8,128)(2,1)S(1)} %copy-done.18, bf16[1232,256]{1,0:T(8,128)(2,1)S(1)} %copy-done.10, bf16[1168,256]{1,0:T(8,128)(2,1)S(1)} %copy-done.14, bf16[624,256]{1,0:T(8,128)(2,1)S(1)} %copy-done.26, bf16[416,256]{1,0:T(8,128)(2,1)S(1)} %copy-done.28, ...), custom_call_target="tpu_custom_call" | custom-call | flops 1000000 | bytes 1000000 | tf_op jit(solution)/shard_map/gradients/pallas_call | solution.py:244
  141.4 1.0 copy-done.22
  142.5 2.7 %gradients.4 = (f32[512,1536]{1,0:T(8,128)S(1)}, f32[768,512]{1,0:T(8,128)S(1)}) custom-call(bf16[1040,256]{1,0:T(8,128)(2,1)S(1)} %copy-done.22, bf16[1232,256]{1,0:T(8,128)(2,1)} %collective-permute-done.15.refs_1_, bf16[1168,256]{1,0:T(8,128)(2,1)} %collective-permute-done.16.refs_2_, bf16[624,256]{1,0:T(8,128)(2,1)S(1)} %collective-permute-done.17.refs_3_, ...), custom_call_target="tpu_custom_call" | custom-call | flops 1000000 | bytes 1000000 | tf_op jit(solution)/shard_map/gradients/pallas_call | solution.py:244
  145.2 1.1 copy-done.5
  146.5 1.0 slice.55
  148.2 0.9 slice.54
  149.2 1.6 collective-permute-start.21
  151.3 5.2 %collective-permute-done.21.refs_3_ = bf16[416,256]{1,0:T(8,128)(2,1)S(1)} collective-permute-done((bf16[416,256]{1,0:T(8,128)(2,1)S(1)}, bf16[416,256]{1,0:T(8,128)(2,1)S(1)}, u32[]{:S(2)}, u32[]{:S(2)}) %collective-permute-start.21) | collective-permute-done | bytes 213024 | tf_op jit(solution)/shard_map/ppermute | solution.py:261
  156.5 0.9 collective-permute-done.22.refs_4_
  157.4 1.4 copy-done.6
  158.8 1.0 copy-done.24
  159.9 3.7 %gradients.5 = (bf16[512,1536]{1,0:T(8,128)(2,1)}, bf16[768,512]{1,0:T(8,128)(2,1)}) custom-call(bf16[1040,256]{1,0:T(8,128)(2,1)S(1)} %copy-done.24, bf16[1168,256]{1,0:T(8,128)(2,1)} %collective-permute-done.19.refs_1_, bf16[1232,256]{1,0:T(8,128)(2,1)} %collective-permute-done.20.refs_2_, bf16[416,256]{1,0:T(8,128)(2,1)S(1)} %collective-permute-done.21.refs_3_, ...), custom_call_target="tpu_custom_call" | custom-call | flops 1000000 | bytes 1000000 | tf_op jit(solution)/shard_map/gradients/pallas_call | solution.py:244
  (86 shorter events, 6.4 us)
Async XLA Ops:
  0.6 0.7 copy-start.31
  1.3 1.0 copy-start.33
  2.4 1.0 copy-start.34
  3.4 0.7 copy-start.35
  5.0 30.7 %collective-permute-start.1 = (bf16[80,4096]{1,0:T(8,128)(2,1)S(1)}, bf16[80,4096]{1,0:T(8,128)(2,1)S(1)}, u32[]{:S(2)}, u32[]{:S(2)}) collective-permute-start(bf16[80,4096]{1,0:T(8,128)(2,1)S(1)} %get-tuple-element.50), channel_id=1, source_target_pairs={{0,2},{1,3},{2,0},{3,1},{4,6},{5,7},{6,4},{7,5},{8,10},{9,11},{10,... | collective-permute-start | bytes 1966088 | tf_op jit(solution)/shard_map/ppermute | solution.py:261
  8.2 2.7 %collective-permute-start = (bf16[40,4096]{1,0:T(8,128)(2,1)S(1)}, bf16[40,4096]{1,0:T(8,128)(2,1)S(1)}, u32[]{:S(2)}, u32[]{:S(2)}) collective-permute-start(bf16[40,4096]{1,0:T(8,128)(2,1)S(1)} %slice.36), channel_id=1, source_target_pairs={{0,1},{1,0},{2,3},{3,2},{4,5},{5,4},{6,7},{7,6},{8,9},{9,8},{10,11... | collective-permute-start | bytes 983048 | tf_op jit(solution)/shard_map/ppermute | solution.py:261
  8.2 33.8 %collective-permute-start.3 = (bf16[80,4096]{1,0:T(8,128)(2,1)S(1)}, bf16[80,4096]{1,0:T(8,128)(2,1)S(1)}, u32[]{:S(2)}, u32[]{:S(2)}) collective-permute-start(bf16[80,4096]{1,0:T(8,128)(2,1)S(1)} %get-tuple-element.53), channel_id=1, source_target_pairs={{0,4},{1,5},{2,6},{3,7},{4,0},{5,1},{6,2},{7,3},{8,12},{9,13},{10,... | collective-permute-start | bytes 1966088 | tf_op jit(solution)/shard_map/ppermute | solution.py:261
  10.9 2.8 %copy-start = (bf16[1,2048,1536]{2,1,0:T(8,128)(2,1)S(1)}, bf16[1,2048,1536]{2,1,0:T(8,128)(2,1)}, u32[]{:S(2)}) copy-start(bf16[1,2048,1536]{2,1,0:T(8,128)(2,1)} %param.10) | copy-start | bytes 18874372
  13.7 1.9 %copy-start.3 = (bf16[1,768,2048]{2,1,0:T(8,128)(2,1)S(1)}, bf16[1,768,2048]{2,1,0:T(8,128)(2,1)}, u32[]{:S(2)}) copy-start(bf16[1,768,2048]{2,1,0:T(8,128)(2,1)} %param.11) | copy-start | bytes 9437188
  15.6 22.8 %copy-start.1 = (bf16[1,2048,1536]{2,1,0:T(8,128)(2,1)S(1)}, bf16[1,2048,1536]{2,1,0:T(8,128)(2,1)}, u32[]{:S(2)}) copy-start(bf16[1,2048,1536]{2,1,0:T(8,128)(2,1)} %param.10) | copy-start | bytes 18874372
  15.6 22.8 %copy-start.4 = (bf16[1,768,2048]{2,1,0:T(8,128)(2,1)S(1)}, bf16[1,768,2048]{2,1,0:T(8,128)(2,1)}, u32[]{:S(2)}) copy-start(bf16[1,768,2048]{2,1,0:T(8,128)(2,1)} %param.11) | copy-start | bytes 9437188
  19.2 16.7 %copy-start.17 = (bf16[1040,256]{1,0:T(8,128)(2,1)}, bf16[1040,256]{1,0:T(8,128)(2,1)S(1)}, u32[]{:S(2)}) copy-start(bf16[1040,256]{1,0:T(8,128)(2,1)S(1)} %get-tuple-element.75.refs_0_) | copy-start | bytes 1597444
  19.2 16.6 %collective-permute-start.6 = (bf16[1168,256]{1,0:T(8,128)(2,1)S(1)}, bf16[1168,256]{1,0:T(8,128)(2,1)S(1)}, u32[]{:S(2)}, u32[]{:S(2)}) collective-permute-start(bf16[1168,256]{1,0:T(8,128)(2,1)S(1)} %get-tuple-element.57), channel_id=1, source_target_pairs={{0,16},{8,24},{16,0},{24,8},{1,17},{9,25},{17,1},{25,9},{2,18},{10... | collective-permute-start | bytes 1794056 | tf_op jit(solution)/shard_map/ppermute | solution.py:261
  20.8 25.4 %collective-permute-start.5 = (bf16[1232,256]{1,0:T(8,128)(2,1)S(1)}, bf16[1232,256]{1,0:T(8,128)(2,1)S(1)}, u32[]{:S(2)}, u32[]{:S(2)}) collective-permute-start(bf16[1232,256]{1,0:T(8,128)(2,1)S(1)} %get-tuple-element.56), channel_id=1, source_target_pairs={{0,8},{8,0},{16,24},{24,16},{1,9},{9,1},{17,25},{25,17},{2,10},{10... | collective-permute-start | bytes 1892360 | tf_op jit(solution)/shard_map/ppermute | solution.py:261
  35.8 2.6 %collective-permute-start.2 = (bf16[40,4096]{1,0:T(8,128)(2,1)S(1)}, bf16[40,4096]{1,0:T(8,128)(2,1)S(1)}, u32[]{:S(2)}, u32[]{:S(2)}) collective-permute-start(bf16[40,4096]{1,0:T(8,128)(2,1)S(1)} %slice.37), channel_id=1, source_target_pairs={{0,1},{1,0},{2,3},{3,2},{4,5},{5,4},{6,7},{7,6},{8,9},{9,8},{10,11... | collective-permute-start | bytes 983048 | tf_op jit(solution)/shard_map/ppermute | solution.py:261
  35.9 0.8 copy-start.13
  36.7 10.1 %collective-permute-start.8 = (bf16[416,256]{1,0:T(8,128)(2,1)S(1)}, bf16[416,256]{1,0:T(8,128)(2,1)S(1)}, u32[]{:S(2)}, u32[]{:S(2)}) collective-permute-start(bf16[416,256]{1,0:T(8,128)(2,1)S(1)} %slice.49), channel_id=1, source_target_pairs={{0,8},{8,0},{16,24},{24,16},{1,9},{9,1},{17,25},{25,17},{2,10},{10... | collective-permute-start | bytes 638984 | tf_op jit(solution)/shard_map/ppermute | solution.py:261
  42.0 4.8 %copy-start.19 = (bf16[1040,256]{1,0:T(8,128)(2,1)}, bf16[1040,256]{1,0:T(8,128)(2,1)S(1)}, u32[]{:S(2)}) copy-start(bf16[1040,256]{1,0:T(8,128)(2,1)S(1)} %get-tuple-element.80.refs_5_) | copy-start | bytes 1597444
  42.0 33.0 %collective-permute-start.9 = (bf16[80,4096]{1,0:T(8,128)(2,1)S(1)}, bf16[80,4096]{1,0:T(8,128)(2,1)S(1)}, u32[]{:S(2)}, u32[]{:S(2)}) collective-permute-start(bf16[80,4096]{1,0:T(8,128)(2,1)S(1)} %get-tuple-element.61), channel_id=1, source_target_pairs={{0,6},{1,7},{2,4},{3,5},{4,2},{5,3},{6,0},{7,1},{8,14},{9,15},{10,... | collective-permute-start | bytes 1966088 | tf_op jit(solution)/shard_map/ppermute | solution.py:261
  44.5 32.1 %collective-permute-start.12 = (bf16[1232,256]{1,0:T(8,128)(2,1)S(1)}, bf16[1232,256]{1,0:T(8,128)(2,1)S(1)}, u32[]{:S(2)}, u32[]{:S(2)}) collective-permute-start(bf16[1232,256]{1,0:T(8,128)(2,1)S(1)} %get-tuple-element.65), channel_id=1, source_target_pairs={{0,16},{8,24},{16,0},{24,8},{1,17},{9,25},{17,1},{25,9},{2,18},{10... | collective-permute-start | bytes 1892360 | tf_op jit(solution)/shard_map/ppermute | solution.py:261
  46.1 22.1 %collective-permute-start.4 = (bf16[40,4096]{1,0:T(8,128)(2,1)S(1)}, bf16[40,4096]{1,0:T(8,128)(2,1)S(1)}, u32[]{:S(2)}, u32[]{:S(2)}) collective-permute-start(bf16[40,4096]{1,0:T(8,128)(2,1)S(1)} %slice.38), channel_id=1, source_target_pairs={{0,1},{1,0},{2,3},{3,2},{4,5},{5,4},{6,7},{7,6},{8,9},{9,8},{10,11... | collective-permute-start | bytes 983048 | tf_op jit(solution)/shard_map/ppermute | solution.py:261
  46.2 26.7 %copy-start.9 = (bf16[1232,256]{1,0:T(8,128)(2,1)}, bf16[1232,256]{1,0:T(8,128)(2,1)S(1)}, u32[]{:S(2)}) copy-start(bf16[1232,256]{1,0:T(8,128)(2,1)S(1)} %collective-permute-done.5.refs_1_) | copy-start | bytes 1892356
  46.2 21.2 %collective-permute-start.7 = (bf16[624,256]{1,0:T(8,128)(2,1)S(1)}, bf16[624,256]{1,0:T(8,128)(2,1)S(1)}, u32[]{:S(2)}, u32[]{:S(2)}) collective-permute-start(bf16[624,256]{1,0:T(8,128)(2,1)S(1)} %slice.48), channel_id=1, source_target_pairs={{0,16},{8,24},{16,0},{24,8},{1,17},{9,25},{17,1},{25,9},{2,18},{10... | collective-permute-start | bytes 958472 | tf_op jit(solution)/shard_map/ppermute | solution.py:261
  46.8 0.7 copy-start.27
  47.5 32.2 %collective-permute-start.11 = (bf16[1168,256]{1,0:T(8,128)(2,1)S(1)}, bf16[1168,256]{1,0:T(8,128)(2,1)S(1)}, u32[]{:S(2)}, u32[]{:S(2)}) collective-permute-start(bf16[1168,256]{1,0:T(8,128)(2,1)S(1)} %get-tuple-element.64), channel_id=1, source_target_pairs={{0,8},{8,0},{16,24},{24,16},{1,9},{9,1},{17,25},{25,17},{2,10},{10... | collective-permute-start | bytes 1794056 | tf_op jit(solution)/shard_map/ppermute | solution.py:261
  67.4 0.7 copy-start.25
  72.9 7.5 %copy-start.21 = (bf16[1040,256]{1,0:T(8,128)(2,1)}, bf16[1040,256]{1,0:T(8,128)(2,1)S(1)}, u32[]{:S(2)}) copy-start(bf16[1040,256]{1,0:T(8,128)(2,1)S(1)} %get-tuple-element.68.refs_0_) | copy-start | bytes 1597444
  72.9 34.8 %collective-permute-start.15 = (bf16[1232,256]{1,0:T(8,128)(2,1)}, bf16[1232,256]{1,0:T(8,128)(2,1)}, u32[]{:S(2)}, u32[]{:S(2)}) collective-permute-start(bf16[1232,256]{1,0:T(8,128)(2,1)} %get-tuple-element.69), channel_id=1, source_target_pairs={{0,8},{8,0},{16,24},{24,16},{1,9},{9,1},{17,25},{25,17},{2,10},{10... | collective-permute-start | bytes 1892360 | tf_op jit(solution)/shard_map/ppermute | solution.py:261
  73.5 32.6 %collective-permute-start.16 = (bf16[1168,256]{1,0:T(8,128)(2,1)}, bf16[1168,256]{1,0:T(8,128)(2,1)}, u32[]{:S(2)}, u32[]{:S(2)}) collective-permute-start(bf16[1168,256]{1,0:T(8,128)(2,1)} %get-tuple-element.70), channel_id=1, source_target_pairs={{0,16},{8,24},{16,0},{24,8},{1,17},{9,25},{17,1},{25,9},{2,18},{10... | collective-permute-start | bytes 1794056 | tf_op jit(solution)/shard_map/ppermute | solution.py:261
  75.8 0.8 copy-start.7
  76.6 18.6 %collective-permute-start.10 = (bf16[40,4096]{1,0:T(8,128)(2,1)}, bf16[40,4096]{1,0:T(8,128)(2,1)S(1)}, u32[]{:S(2)}, u32[]{:S(2)}) collective-permute-start(bf16[40,4096]{1,0:T(8,128)(2,1)} %slice.41), channel_id=1, source_target_pairs={{0,1},{1,0},{2,3},{3,2},{4,5},{5,4},{6,7},{7,6},{8,9},{9,8},{10,11... | collective-permute-start | bytes 983048 | tf_op jit(solution)/shard_map/ppermute | solution.py:261
  77.4 0.8 copy-start.11
  78.3 16.9 %collective-permute-start.14 = (bf16[624,256]{1,0:T(8,128)(2,1)}, bf16[624,256]{1,0:T(8,128)(2,1)}, u32[]{:S(2)}, u32[]{:S(2)}) collective-permute-start(bf16[624,256]{1,0:T(8,128)(2,1)} %slice.51), channel_id=1, source_target_pairs={{0,8},{8,0},{16,24},{24,16},{1,9},{9,1},{17,25},{25,17},{2,10},{10... | collective-permute-start | bytes 958472 | tf_op jit(solution)/shard_map/ppermute | solution.py:261
  80.3 0.8 copy-start.15
  81.2 11.3 %collective-permute-start.13 = (bf16[416,256]{1,0:T(8,128)(2,1)}, bf16[416,256]{1,0:T(8,128)(2,1)}, u32[]{:S(2)}, u32[]{:S(2)}) collective-permute-start(bf16[416,256]{1,0:T(8,128)(2,1)} %slice.50), channel_id=1, source_target_pairs={{0,16},{8,24},{16,0},{24,8},{1,17},{9,25},{17,1},{25,9},{2,18},{10... | collective-permute-start | bytes 638984 | tf_op jit(solution)/shard_map/ppermute | solution.py:261
  95.2 2.8 %copy-start.2 = (bf16[1,2048,1536]{2,1,0:T(8,128)(2,1)S(1)}, bf16[1,2048,1536]{2,1,0:T(8,128)(2,1)}, u32[]{:S(2)}) copy-start(bf16[1,2048,1536]{2,1,0:T(8,128)(2,1)} %param.10) | copy-start | bytes 18874372
  98.0 1.1 copy-start.8
  103.7 0.8 copy-start.23
  104.6 41.9 %collective-permute-start.20 = (bf16[1232,256]{1,0:T(8,128)(2,1)}, bf16[1232,256]{1,0:T(8,128)(2,1)}, u32[]{:S(2)}, u32[]{:S(2)}) collective-permute-start(bf16[1232,256]{1,0:T(8,128)(2,1)} %get-tuple-element.74), channel_id=1, source_target_pairs={{0,16},{8,24},{16,0},{24,8},{1,17},{9,25},{17,1},{25,9},{2,18},{10... | collective-permute-start | bytes 1892360 | tf_op jit(solution)/shard_map/ppermute | solution.py:261
  107.1 8.3 %collective-permute-start.18 = (bf16[416,256]{1,0:T(8,128)(2,1)S(1)}, bf16[416,256]{1,0:T(8,128)(2,1)S(1)}, u32[]{:S(2)}, u32[]{:S(2)}) collective-permute-start(bf16[416,256]{1,0:T(8,128)(2,1)S(1)} %slice.53), channel_id=1, source_target_pairs={{0,8},{8,0},{16,24},{24,16},{1,9},{9,1},{17,25},{25,17},{2,10},{10... | collective-permute-start | bytes 638984 | tf_op jit(solution)/shard_map/ppermute | solution.py:261
  108.7 17.2 %collective-permute-start.17 = (bf16[624,256]{1,0:T(8,128)(2,1)S(1)}, bf16[624,256]{1,0:T(8,128)(2,1)S(1)}, u32[]{:S(2)}, u32[]{:S(2)}) collective-permute-start(bf16[624,256]{1,0:T(8,128)(2,1)S(1)} %slice.52), channel_id=1, source_target_pairs={{0,16},{8,24},{16,0},{24,8},{1,17},{9,25},{17,1},{25,9},{2,18},{10... | collective-permute-start | bytes 958472 | tf_op jit(solution)/shard_map/ppermute | solution.py:261
  109.3 38.9 %collective-permute-start.19 = (bf16[1168,256]{1,0:T(8,128)(2,1)}, bf16[1168,256]{1,0:T(8,128)(2,1)}, u32[]{:S(2)}, u32[]{:S(2)}) collective-permute-start(bf16[1168,256]{1,0:T(8,128)(2,1)} %get-tuple-element.73), channel_id=1, source_target_pairs={{0,8},{8,0},{16,24},{24,16},{1,9},{9,1},{17,25},{25,17},{2,10},{10... | collective-permute-start | bytes 1794056 | tf_op jit(solution)/shard_map/ppermute | solution.py:261
  115.3 0.7 copy-start.29
  126.7 19.6 %all-to-all-start = ((f32[8,1,40]{2,1,0:T(1,128)}), f32[8,1,40]{2,1,0:T(1,128)S(1)}, u32[]{:S(2)}, u32[]{:S(2)}) async-start(f32[8,1,40]{2,1,0:T(1,128)} %bitcast.5), calls=%async_computation | async-start | bytes 8192 | tf_op jit(solution)/shard_map/all_to_all | solution.py:265
  130.0 1.1 copy-start.10
  131.0 1.1 copy-start.12
  132.1 1.1 copy-start.14
  133.2 1.1 copy-start.16
  134.3 1.0 copy-start.18
  135.3 1.0 copy-start.20
  136.3 1.0 copy-start.26
  137.3 0.9 copy-start.28
  138.2 3.2 %copy-start.30 = (bf16[416,256]{1,0:T(8,128)(2,1)S(1)}, bf16[416,256]{1,0:T(8,128)(2,1)}, u32[]{:S(2)}) copy-start(bf16[416,256]{1,0:T(8,128)(2,1)} %copy-done.29) | copy-start | bytes 638980
  141.4 1.0 copy-start.22
  142.5 8.3 %copy-start.32 = (f32[128,2]{0,1:T(2,128)S(1)}, f32[128,2]{0,1:T(2,128)}, u32[]{:S(2)}) copy-start(f32[128,2]{0,1:T(2,128)} %param.8) | copy-start | bytes 3076
  145.2 1.1 copy-start.5
  147.5 9.9 %collective-permute-start.22 = (bf16[624,256]{1,0:T(8,128)(2,1)S(1)}, bf16[624,256]{1,0:T(8,128)(2,1)S(1)}, u32[]{:S(2)}, u32[]{:S(2)}) collective-permute-start(bf16[624,256]{1,0:T(8,128)(2,1)S(1)} %slice.55), channel_id=1, source_target_pairs={{0,8},{8,0},{16,24},{24,16},{1,9},{9,1},{17,25},{25,17},{2,10},{10... | collective-permute-start | bytes 958472 | tf_op jit(solution)/shard_map/ppermute | solution.py:261
  149.2 7.4 %collective-permute-start.21 = (bf16[416,256]{1,0:T(8,128)(2,1)S(1)}, bf16[416,256]{1,0:T(8,128)(2,1)S(1)}, u32[]{:S(2)}, u32[]{:S(2)}) collective-permute-start(bf16[416,256]{1,0:T(8,128)(2,1)S(1)} %slice.54), channel_id=1, source_target_pairs={{0,16},{8,24},{16,0},{24,8},{1,17},{9,25},{17,1},{25,9},{2,18},{10... | collective-permute-start | bytes 638984 | tf_op jit(solution)/shard_map/ppermute | solution.py:261
  157.4 1.4 copy-start.6
  158.8 1.0 copy-start.24
where the time goes:
time: 165 us; the launch traced here: 164 us
  waiting for transfers between devices  66.8 us (40%)
  local copies, waits for them, and re-layouts  37.6 us (23%)
  starting transfers between devices  29.6 us (18%)
  Pallas kernels  27.2 us (16%)
    ppermute x23, waiting for transfers between devices, exchange(): return lax.ppermute(values, axis, [(n, n ^ mask) for n in range(size)])  66.8 us
    unnamed x72, local copies, waits for them, and re-layouts  31.2 us
    ppermute x23, starting transfers between devices, exchange(): return lax.ppermute(values, axis, [(n, n ^ mask) for n in range(size)])  26.3 us
    pallas_call x4, Pallas kernels, expert_rows(): pl.pallas_call(functools.partial(expert_kernel, top), grid=(steps,), in_s...  16.7 us
    pallas_call x3, Pallas kernels, gradients(): pl.pallas_call(functools.partial(gradient_kernel, tops, half, len(sums)),...  9.55 us
    slice x8, local copies, waits for them, and re-layouts, compute(): forward = (got_x[:from_x], got_y[:from_y])  5.42 us
  transfers between devices with their start and end apart: 24, of which 8 were waited for; matrix products, arithmetic and copies ran while one was open for 5% of the time, Pallas kernels for 14%

commit v1 on v0

--- a/solution.py
+++ b/solution.py
@@ -176,7 +176,7 @@
             pltpu.VMEM((width, PAIR), BF16),
             pltpu.VMEM((PAIR, 1), F32),
         ],
-        compiler_params=pltpu.CompilerParams(vmem_limit_bytes=20 * MIB),
+        compiler_params=pltpu.CompilerParams(vmem_limit_bytes=14 * MIB),
         cost_estimate=pl.CostEstimate(flops=1_000_000, bytes_accessed=1_000_000, transcendentals=0),
         name="expert_rows",
     )(rows_a, rows_b, weight_gu, weight_gu, weight_down)
@@ -250,7 +250,7 @@
             jax.ShapeDtypeStruct((half, quarter), kept),
         ],
         scratch_shapes=[pltpu.VMEM((quarter, rows), BF16), pltpu.VMEM((rows, quarter), BF16)],
-        compiler_params=pltpu.CompilerParams(vmem_limit_bytes=24 * MIB),
+        compiler_params=pltpu.CompilerParams(vmem_limit_bytes=14 * MIB),
         cost_estimate=pl.CostEstimate(flops=1_000_000, bytes_accessed=1_000_000, transcendentals=0),
         name="gradients",
     )(*pieces, *sums)
@@ -276,40 +276,43 @@
     ids, probs = expert_ids.T, gate_probs.T
     *local, slots = dispatch_rows(ids, probs, tokens, cotangent)
     tops = (48, 32, 48, 32)
-    inner, pieces = [], []
+    inner, pieces, forwards = [], [], []
 
     def other_core(rows):
         return exchange(rows[CAP:], "expert", 1)
 
-    def compute(rows, other, *others):
+    def compute(rows):
         top = tops[len(inner)]
-        other = after(other, *others)
-        own, to_x, to_y, found = expert_rows(rows, other, gate_up[0], down[0], top)
+        own, to_x, to_y, found = expert_rows(rows, other_core(rows), gate_up[0], down[0], top)
         inner.append(found)
         _, _, from_x, from_y = split_rows(top, half)
         got_x, got_y = exchange(to_x, "dp", 1), exchange(to_y, "dp", 2)
         forward = (got_x[:from_x], got_y[:from_y])
         far_top, far_low = exchange(forward[0], "dp", 2), exchange(forward[1], "dp", 1)
+        forwards.append(forward)
         pieces.append([own, got_x, got_y, far_top, far_low])
 
+    def add(chunk, sums=()):
+        return gradients(
+            tops[chunk : chunk + 1], pieces[chunk], half, quarter, sums, chunk == len(tops) - 1
+        )
+
+    rows_2 = exchange(local[2], "expert", 4)
     rows_1 = exchange(local[1], "expert", 2)
-    other = other_core(local[0])
-    rows_2 = exchange(local[2], "expert", 4)
-    compute(local[0], other)
-    rows_1 = after(rows_1, inner[0])
-    compute(rows_1, other_core(rows_1))
-    rows_2 = after(rows_2, inner[1])
+    compute(local[0])
+    rows_2 = after(rows_2, *forwards[0])
     rows_3 = exchange(after(local[3], rows_2), "expert", 6)
-    compute(rows_2, other_core(rows_2), *pieces[0])
-    rows_3 = after(rows_3, inner[2])
-    compute(rows_3, other_core(rows_3), *pieces[1])
-    early = after(tuple(pieces[0] + pieces[1]), inner[3])
-    sums = gradients(tops[:2], early, half, quarter)
-    sums = gradients(tops[2:3], pieces[2], half, quarter, sums)
-    grad_gu, grad_down = gradients(tops[3:], pieces[3], half, quarter, sums, True)
+    compute(rows_2)
+    compute(after(rows_1, inner[1]))
+    sums = add(0)
+    compute(after(rows_3, inner[2], *forwards[1], *sums))
+    sums = add(1, sums)
+    sums = add(2, sums)
+    grad_gu, grad_down = add(3, sums)
     numbers = jnp.arange(EXPERTS, dtype=jnp.int32)
     mine = (numbers[:, None] == jnp.bitwise_xor(numbers, me)[None, :])[:, :, None]
-    rows_inner = after(jnp.concatenate(inner, axis=1), *pieces[2]).reshape(EXPERTS, CAP)
+    in_order = [inner[0], inner[2], inner[1], inner[3]]
+    rows_inner = after(jnp.concatenate(in_order, axis=1), *forwards[2]).reshape(EXPERTS, CAP)
     sent = jnp.sum(jnp.where(mine, rows_inner[None], 0.0), axis=1)
     returned = jnp.sum(jnp.where(mine, swap(sent)[None], 0.0), axis=1).reshape(-1)
     chosen = slots[:, None, :] == jnp.arange(EXPERTS * CAP, dtype=jnp.int32)[None, :, None]

time: 165 us -> 153 us (0.927)
  waiting for transfers between devices: 66.8 us -> 59.1 us
  local copies, waits for them, and re-layouts: 37.6 us -> 34 us
    ppermute x23, waiting for transfers between devices: 66.8 us -> 59.1 us  [exchange(): return lax.ppermute(values, axis, [(n, n ^ mask) for n in range(size)])]
    unnamed x72 -> x60, local copies, waits for them, and re-layouts: 31.2 us -> 26.1 us
    pallas_call x3 -> x4, Pallas kernels: 9.55 us -> 9.44 us  [gradients(): pl.pallas_call(functools.partial(gradient_kernel, tops, half, len(sums)),...]
  transfers between devices with their start and end apart: 24 -> 24, of which waited for: 8 -> 8; matrix products, arithmetic and copies ran while one was open for 5% -> 6% of each run, Pallas kernels for 14% -> 15%
where the time goes in v1:
time: 153 us; the launch traced here: 152 us
  waiting for transfers between devices  59.1 us (39%)
  local copies, waits for them, and re-layouts  34 us (22%)
  starting transfers between devices  29.4 us (19%)
  Pallas kernels  27.1 us (18%)
  other arithmetic  1.57 us (1%)
    ppermute x23, waiting for transfers between devices, exchange(): return lax.ppermute(values, axis, [(n, n ^ mask) for n in range(size)])  59.1 us
    unnamed x60, local copies, waits for them, and re-layouts  26.1 us
    ppermute x23, starting transfers between devices, exchange(): return lax.ppermute(values, axis, [(n, n ^ mask) for n in range(size)])  26 us
    pallas_call x4, Pallas kernels, expert_rows(): pl.pallas_call(functools.partial(expert_kernel, top), grid=(steps,), in_s...  16.7 us
    pallas_call x4, Pallas kernels, gradients(): pl.pallas_call(functools.partial(gradient_kernel, tops, half, len(sums)),...  9.44 us
    slice x8, local copies, waits for them, and re-layouts, compute(): forward = (got_x[:from_x], got_y[:from_y])  6.91 us
    all_to_all x1, starting transfers between devices, swap(): lax.all_to_all(values, 'expert', split_axis=0, concat_axis=0, tiled=True)  3.47 us
  transfers between devices with their start and end apart: 24, of which 8 were waited for; matrix products, arithmetic and copies ran while one was open for 6% of the time, Pallas kernels for 15%

profile of v1, /device:TPU:0, one launch (start us, length us, event | category | flops | bytes accessed | tf_op | source)
XLA Modules:
  0.0 152.0 jit_solution(15081619932724730423)
XLA Ops:
  0.6 0.7 copy-done.25
  1.3 1.0 copy-done.27
  2.4 1.0 copy-done.28
  3.4 0.7 copy-done.29
  4.1 1.0 dispatch_rows.1
  5.1 0.5 collective-permute-start
  5.6 3.7 %collective-permute-start.2 = (bf16[80,4096]{1,0:T(8,128)(2,1)S(1)}, bf16[80,4096]{1,0:T(8,128)(2,1)S(1)}, u32[]{:S(2)}, u32[]{:S(2)}) collective-permute-start(bf16[80,4096]{1,0:T(8,128)(2,1)S(1)} %get-tuple-element.41), channel_id=1, source_target_pairs={{0,4},{1,5},{2,6},{3,7},{4,0},{5,1},{6,2},{7,3},{8,12},{9,13},{10,... | collective-permute-start | bytes 1966088 | tf_op jit(solution)/shard_map/ppermute | solution.py:261
  9.3 2.8 %copy-done = bf16[1,2048,1536]{2,1,0:T(8,128)(2,1)S(1)} copy-done((bf16[1,2048,1536]{2,1,0:T(8,128)(2,1)S(1)}, bf16[1,2048,1536]{2,1,0:T(8,128)(2,1)}, u32[]{:S(2)}) %copy-start) | copy-done | bytes 6291480
  12.0 1.9 %copy-done.3 = bf16[1,768,2048]{2,1,0:T(8,128)(2,1)S(1)} copy-done((bf16[1,768,2048]{2,1,0:T(8,128)(2,1)S(1)}, bf16[1,768,2048]{2,1,0:T(8,128)(2,1)}, u32[]{:S(2)}) %copy-start.3) | copy-done | bytes 3145752
  13.9 3.6 %expert_rows.4 = (bf16[1040,256]{1,0:T(8,128)(2,1)S(1)}, bf16[1232,256]{1,0:T(8,128)(2,1)S(1)}, bf16[1168,256]{1,0:T(8,128)(2,1)S(1)}, f32[1,80]{1,0:T(1,128)S(1)}) custom-call(bf16[80,4096]{1,0:T(8,128)(2,1)S(1)} %get-tuple-element.38.a_ref, bf16[40,4096]{1,0:T(8,128)(2,1)S(1)} %collective-permute-done.b_ref, bf16[2048,1536]{1,0:T(8,128)(2,1)S(1)} %bitcast.12, ...), custom_call_target="tpu_custom_call" | custom-call | flops 1000000 | bytes 1000000 | tf_op jit(solution)/shard_map/expert_rows/pallas_call | solution.py:160
  17.6 1.5 collective-permute-start.3
  19.1 1.5 collective-permute-start.4
  20.6 1.6 %collective-permute-start.1 = (bf16[80,4096]{1,0:T(8,128)(2,1)S(1)}, bf16[80,4096]{1,0:T(8,128)(2,1)S(1)}, u32[]{:S(2)}, u32[]{:S(2)}) collective-permute-start(bf16[80,4096]{1,0:T(8,128)(2,1)S(1)} %get-tuple-element.40), channel_id=1, source_target_pairs={{0,2},{1,3},{2,0},{3,1},{4,6},{5,7},{6,4},{7,5},{8,10},{9,11},{10,... | collective-permute-start | bytes 1966088 | tf_op jit(solution)/shard_map/ppermute | solution.py:261
  22.2 12.2 %collective-permute-done.4.refs_2_ = bf16[1168,256]{1,0:T(8,128)(2,1)S(1)} collective-permute-done((bf16[1168,256]{1,0:T(8,128)(2,1)S(1)}, bf16[1168,256]{1,0:T(8,128)(2,1)S(1)}, u32[]{:S(2)}, u32[]{:S(2)}) %collective-permute-start.4) | collective-permute-done | bytes 598048 | tf_op jit(solution)/shard_map/ppermute | solution.py:261
  34.4 4.3 %collective-permute-done.2.a_ref = bf16[80,4096]{1,0:T(8,128)(2,1)S(1)} collective-permute-done((bf16[80,4096]{1,0:T(8,128)(2,1)S(1)}, bf16[80,4096]{1,0:T(8,128)(2,1)S(1)}, u32[]{:S(2)}, u32[]{:S(2)}) %collective-permute-start.2) | collective-permute-done | bytes 655392 | tf_op jit(solution)/shard_map/ppermute | solution.py:261
  38.8 3.6 %collective-permute-start.7 = (bf16[80,4096]{1,0:T(8,128)(2,1)S(1)}, bf16[80,4096]{1,0:T(8,128)(2,1)S(1)}, u32[]{:S(2)}, u32[]{:S(2)}) collective-permute-start(bf16[80,4096]{1,0:T(8,128)(2,1)S(1)} %get-tuple-element.49), channel_id=1, source_target_pairs={{0,6},{1,7},{2,4},{3,5},{4,2},{5,3},{6,0},{7,1},{8,14},{9,15},{10,... | collective-permute-start | bytes 1966088 | tf_op jit(solution)/shard_map/ppermute | solution.py:261
  42.5 3.7 %expert_rows.5 = (bf16[1040,256]{1,0:T(8,128)(2,1)S(1)}, bf16[1168,256]{1,0:T(8,128)(2,1)S(1)}, bf16[1232,256]{1,0:T(8,128)(2,1)S(1)}, f32[1,80]{1,0:T(1,128)S(1)}) custom-call(bf16[80,4096]{1,0:T(8,128)(2,1)S(1)} %collective-permute-done.2.a_ref, bf16[40,4096]{1,0:T(8,128)(2,1)S(1)} %collective-permute-done.5.b_ref, bf16[2048,1536]{1,0:T(8,128)(2,1)S(1)} %bitcast.14, ...), custom_call_target="tpu_custom_call" | custom-call | flops 1000000 | bytes 1000000 | tf_op jit(solution)/shard_map/expert_rows/pallas_call | solution.py:160
  46.1 1.6 %collective-permute-start.9 = (bf16[1232,256]{1,0:T(8,128)(2,1)S(1)}, bf16[1232,256]{1,0:T(8,128)(2,1)S(1)}, u32[]{:S(2)}, u32[]{:S(2)}) collective-permute-start(bf16[1232,256]{1,0:T(8,128)(2,1)S(1)} %get-tuple-element.51), channel_id=1, source_target_pairs={{0,16},{8,24},{16,0},{24,8},{1,17},{9,25},{17,1},{25,9},{2,18},{10... | collective-permute-start | bytes 1892360 | tf_op jit(solution)/shard_map/ppermute | solution.py:261
  47.7 1.5 collective-permute-start.8
  49.2 0.5 collective-permute-start.11
  49.7 14.0 %collective-permute-done.1.a_ref = bf16[80,4096]{1,0:T(8,128)(2,1)S(1)} collective-permute-done((bf16[80,4096]{1,0:T(8,128)(2,1)S(1)}, bf16[80,4096]{1,0:T(8,128)(2,1)S(1)}, u32[]{:S(2)}, u32[]{:S(2)}) %collective-permute-start.1) | collective-permute-done | bytes 655392 | tf_op jit(solution)/shard_map/ppermute | solution.py:261
  63.9 3.7 %collective-permute-done.11.refs_4_ = bf16[416,256]{1,0:T(8,128)(2,1)S(1)} collective-permute-done((bf16[416,256]{1,0:T(8,128)(2,1)S(1)}, bf16[416,256]{1,0:T(8,128)(2,1)S(1)}, u32[]{:S(2)}, u32[]{:S(2)}) %collective-permute-start.11) | collective-permute-done | bytes 213024 | tf_op jit(solution)/shard_map/ppermute | solution.py:261
  68.0 8.0 %collective-permute-done.10.refs_3_ = bf16[624,256]{1,0:T(8,128)(2,1)S(1)} collective-permute-done((bf16[624,256]{1,0:T(8,128)(2,1)S(1)}, bf16[624,256]{1,0:T(8,128)(2,1)S(1)}, u32[]{:S(2)}, u32[]{:S(2)}) %collective-permute-start.10) | collective-permute-done | bytes 319520 | tf_op jit(solution)/shard_map/ppermute | solution.py:261
  76.0 1.4 gradients.4
  77.5 4.7 %expert_rows.6 = (bf16[1040,256]{1,0:T(8,128)(2,1)S(1)}, bf16[1232,256]{1,0:T(8,128)(2,1)}, bf16[1168,256]{1,0:T(8,128)(2,1)}, f32[1,80]{1,0:T(1,128)S(1)}) custom-call(bf16[80,4096]{1,0:T(8,128)(2,1)S(1)} %collective-permute-done.1.a_ref, bf16[40,4096]{1,0:T(8,128)(2,1)S(1)} %collective-permute-done.6.b_ref, bf16[2048,1536]{1,0:T(8,128)(2,1)S(1)} %bitcast.16, ...), custom_call_target="tpu_custom_call" | custom-call | flops 1000000 | bytes 1000000 | tf_op jit(solution)/shard_map/expert_rows/pallas_call | solution.py:160
  82.2 0.8 copy-done.17
  83.0 0.8 slice.50
  83.8 0.8 slice.51
  84.6 0.8 slice.43
  85.3 0.8 copy-done.11
  86.2 1.5 collective-permute-start.13
  88.2 2.8 %copy-done.2 = bf16[1,2048,1536]{2,1,0:T(8,128)(2,1)S(1)} copy-done((bf16[1,2048,1536]{2,1,0:T(8,128)(2,1)S(1)}, bf16[1,2048,1536]{2,1,0:T(8,128)(2,1)}, u32[]{:S(2)}) %copy-start.2) | copy-done | bytes 6291480
  90.9 1.1 copy-done.12
  92.0 4.7 %expert_rows.7 = (bf16[1040,256]{1,0:T(8,128)(2,1)S(1)}, bf16[1168,256]{1,0:T(8,128)(2,1)}, bf16[1232,256]{1,0:T(8,128)(2,1)}, f32[1,80]{1,0:T(1,128)S(1)}) custom-call(bf16[80,4096]{1,0:T(8,128)(2,1)S(1)} %copy-done.12, bf16[40,4096]{1,0:T(8,128)(2,1)S(1)} %collective-permute-done.12.b_ref, bf16[2048,1536]{1,0:T(8,128)(2,1)S(1)} %bitcast.18, ...), custom_call_target="tpu_custom_call" | custom-call | flops 1000000 | bytes 1000000 | tf_op jit(solution)/shard_map/expert_rows/pallas_call | solution.py:160
  96.7 0.8 copy-done.21
  97.5 1.5 collective-permute-start.16
  99.0 0.5 collective-permute-start.22
  99.6 1.5 collective-permute-start.15
  101.1 3.2 %collective-permute-done.14.refs_2_ = bf16[1168,256]{1,0:T(8,128)(2,1)} collective-permute-done((bf16[1168,256]{1,0:T(8,128)(2,1)}, bf16[1168,256]{1,0:T(8,128)(2,1)}, u32[]{:S(2)}, u32[]{:S(2)}) %collective-permute-start.14) | collective-permute-done | bytes 598048 | tf_op jit(solution)/shard_map/ppermute | solution.py:261
  104.8 1.6 %slice.53 = bf16[416,256]{1,0:T(8,128)(2,1)} slice(bf16[1168,256]{1,0:T(8,128)(2,1)} %collective-permute-done.14.refs_2_), slice={[0:416], [0:256]} | slice | bytes 425984 | tf_op jit(solution)/shard_map/slice | solution.py:290
  106.4 1.7 %slice.52 = bf16[624,256]{1,0:T(8,128)(2,1)} slice(bf16[1232,256]{1,0:T(8,128)(2,1)} %collective-permute-done.13.refs_1_), slice={[0:624], [0:256]} | slice | bytes 638976 | tf_op jit(solution)/shard_map/slice | solution.py:290
  108.4 0.7 select_reduce_fusion.2
  109.0 3.5 %all-to-all-start = ((f32[8,1,40]{2,1,0:T(1,128)}), f32[8,1,40]{2,1,0:T(1,128)S(1)}, u32[]{:S(2)}, u32[]{:S(2)}) async-start(f32[8,1,40]{2,1,0:T(1,128)} %bitcast.5), calls=%async_computation | async-start | bytes 8192 | tf_op jit(solution)/shard_map/all_to_all | solution.py:265
  112.5 0.6 collective-permute-start.20
  113.1 8.5 %collective-permute-done.21.refs_3_ = bf16[416,256]{1,0:T(8,128)(2,1)S(1)} collective-permute-done((bf16[416,256]{1,0:T(8,128)(2,1)}, bf16[416,256]{1,0:T(8,128)(2,1)S(1)}, u32[]{:S(2)}, u32[]{:S(2)}) %collective-permute-start.21) | collective-permute-done | bytes 213024 | tf_op jit(solution)/shard_map/ppermute | solution.py:261
  121.6 0.7 copy-done.23
  122.3 1.9 %copy-done.6 = f32[512,1536]{1,0:T(8,128)S(1)} copy-done((f32[512,1536]{1,0:T(8,128)S(1)}, f32[512,1536]{1,0:T(8,128)}, u32[]{:S(2)}) %copy-start.6) | copy-done | bytes 3145752
  124.2 1.4 copy-done.8
  125.6 1.1 copy-done.14
  126.6 1.1 copy-done.16
  127.7 1.0 copy-done.20
  128.8 0.9 copy-done.24
  129.7 1.5 gradients.5
  131.2 1.1 copy-done.9
  133.0 1.0 slice.55
  134.0 0.6 collective-permute-start.18
  134.7 0.9 slice.54
  135.7 1.6 %collective-permute-start.17 = (bf16[416,256]{1,0:T(8,128)(2,1)S(1)}, bf16[416,256]{1,0:T(8,128)(2,1)S(1)}, u32[]{:S(2)}, u32[]{:S(2)}) collective-permute-start(bf16[416,256]{1,0:T(8,128)(2,1)S(1)} %slice.54), channel_id=1, source_target_pairs={{0,16},{8,24},{16,0},{24,8},{1,17},{9,25},{17,1},{25,9},{2,18},{10... | collective-permute-start | bytes 638984 | tf_op jit(solution)/shard_map/ppermute | solution.py:261
  137.3 0.6 bitcast_divide_fusion
  137.9 5.1 %collective-permute-done.19.refs_3_ = bf16[624,256]{1,0:T(8,128)(2,1)S(1)} collective-permute-done((bf16[624,256]{1,0:T(8,128)(2,1)}, bf16[624,256]{1,0:T(8,128)(2,1)S(1)}, u32[]{:S(2)}, u32[]{:S(2)}) %collective-permute-start.19) | collective-permute-done | bytes 319520 | tf_op jit(solution)/shard_map/ppermute | solution.py:261
  143.0 1.4 copy-done.10
  144.4 1.0 copy-done.18
  145.5 2.8 %gradients.6 = (f32[512,1536]{1,0:T(8,128)S(1)}, f32[768,512]{1,0:T(8,128)S(1)}) custom-call(bf16[1040,256]{1,0:T(8,128)(2,1)S(1)} %copy-done.18, bf16[1232,256]{1,0:T(8,128)(2,1)} %collective-permute-done.13.refs_1_, bf16[1168,256]{1,0:T(8,128)(2,1)} %collective-permute-done.14.refs_2_, bf16[624,256]{1,0:T(8,128)(2,1)S(1)} %collective-permute-done.19.refs_3_, ...), custom_call_target="tpu_custom_call" | custom-call | flops 1000000 | bytes 1000000 | tf_op jit(solution)/shard_map/gradients/pallas_call | solution.py:244
  148.3 3.7 %gradients.7 = (bf16[512,1536]{1,0:T(8,128)(2,1)}, bf16[768,512]{1,0:T(8,128)(2,1)}) custom-call(bf16[1040,256]{1,0:T(8,128)(2,1)S(1)} %copy-done.22, bf16[1168,256]{1,0:T(8,128)(2,1)} %collective-permute-done.15.refs_1_, bf16[1232,256]{1,0:T(8,128)(2,1)} %collective-permute-done.16.refs_2_, bf16[416,256]{1,0:T(8,128)(2,1)S(1)} %collective-permute-done.17.refs_3_, ...), custom_call_target="tpu_custom_call" | custom-call | flops 1000000 | bytes 1000000 | tf_op jit(solution)/shard_map/gradients/pallas_call | solution.py:244
  (75 shorter events, 2.9 us)
Async XLA Ops:
  0.6 0.7 copy-start.25
  1.3 1.0 copy-start.27
  2.4 1.0 copy-start.28
  3.4 0.7 copy-start.29
  5.1 4.2 %collective-permute-start = (bf16[40,4096]{1,0:T(8,128)(2,1)S(1)}, bf16[40,4096]{1,0:T(8,128)(2,1)S(1)}, u32[]{:S(2)}, u32[]{:S(2)}) collective-permute-start(bf16[40,4096]{1,0:T(8,128)(2,1)S(1)} %slice.36), channel_id=1, source_target_pairs={{0,1},{1,0},{2,3},{3,2},{4,5},{5,4},{6,7},{7,6},{8,9},{9,8},{10,11... | collective-permute-start | bytes 983048 | tf_op jit(solution)/shard_map/ppermute | solution.py:261
  5.6 33.1 %collective-permute-start.2 = (bf16[80,4096]{1,0:T(8,128)(2,1)S(1)}, bf16[80,4096]{1,0:T(8,128)(2,1)S(1)}, u32[]{:S(2)}, u32[]{:S(2)}) collective-permute-start(bf16[80,4096]{1,0:T(8,128)(2,1)S(1)} %get-tuple-element.41), channel_id=1, source_target_pairs={{0,4},{1,5},{2,6},{3,7},{4,0},{5,1},{6,2},{7,3},{8,12},{9,13},{10,... | collective-permute-start | bytes 1966088 | tf_op jit(solution)/shard_map/ppermute | solution.py:261
  9.3 2.8 %copy-start = (bf16[1,2048,1536]{2,1,0:T(8,128)(2,1)S(1)}, bf16[1,2048,1536]{2,1,0:T(8,128)(2,1)}, u32[]{:S(2)}) copy-start(bf16[1,2048,1536]{2,1,0:T(8,128)(2,1)} %param.10) | copy-start | bytes 18874372
  12.0 1.9 %copy-start.3 = (bf16[1,768,2048]{2,1,0:T(8,128)(2,1)S(1)}, bf16[1,768,2048]{2,1,0:T(8,128)(2,1)}, u32[]{:S(2)}) copy-start(bf16[1,768,2048]{2,1,0:T(8,128)(2,1)} %param.11) | copy-start | bytes 9437188
  13.9 28.5 %copy-start.1 = (bf16[1,2048,1536]{2,1,0:T(8,128)(2,1)S(1)}, bf16[1,2048,1536]{2,1,0:T(8,128)(2,1)}, u32[]{:S(2)}) copy-start(bf16[1,2048,1536]{2,1,0:T(8,128)(2,1)} %param.10) | copy-start | bytes 18874372
  13.9 28.5 %copy-start.4 = (bf16[1,768,2048]{2,1,0:T(8,128)(2,1)S(1)}, bf16[1,768,2048]{2,1,0:T(8,128)(2,1)}, u32[]{:S(2)}) copy-start(bf16[1,768,2048]{2,1,0:T(8,128)(2,1)} %param.11) | copy-start | bytes 9437188
  17.6 16.8 %collective-permute-start.3 = (bf16[1232,256]{1,0:T(8,128)(2,1)S(1)}, bf16[1232,256]{1,0:T(8,128)(2,1)S(1)}, u32[]{:S(2)}, u32[]{:S(2)}) collective-permute-start(bf16[1232,256]{1,0:T(8,128)(2,1)S(1)} %get-tuple-element.42), channel_id=1, source_target_pairs={{0,8},{8,0},{16,24},{24,16},{1,9},{9,1},{17,25},{25,17},{2,10},{10... | collective-permute-start | bytes 1892360 | tf_op jit(solution)/shard_map/ppermute | solution.py:261
  19.1 15.3 %collective-permute-start.4 = (bf16[1168,256]{1,0:T(8,128)(2,1)S(1)}, bf16[1168,256]{1,0:T(8,128)(2,1)S(1)}, u32[]{:S(2)}, u32[]{:S(2)}) collective-permute-start(bf16[1168,256]{1,0:T(8,128)(2,1)S(1)} %get-tuple-element.43), channel_id=1, source_target_pairs={{0,16},{8,24},{16,0},{24,8},{1,17},{9,25},{17,1},{25,9},{2,18},{10... | collective-permute-start | bytes 1794056 | tf_op jit(solution)/shard_map/ppermute | solution.py:261
  20.6 43.2 %collective-permute-start.1 = (bf16[80,4096]{1,0:T(8,128)(2,1)S(1)}, bf16[80,4096]{1,0:T(8,128)(2,1)S(1)}, u32[]{:S(2)}, u32[]{:S(2)}) collective-permute-start(bf16[80,4096]{1,0:T(8,128)(2,1)S(1)} %get-tuple-element.40), channel_id=1, source_target_pairs={{0,2},{1,3},{2,0},{3,1},{4,6},{5,7},{6,4},{7,5},{8,10},{9,11},{10,... | collective-permute-start | bytes 1966088 | tf_op jit(solution)/shard_map/ppermute | solution.py:261
  38.8 3.7 %collective-permute-start.5 = (bf16[40,4096]{1,0:T(8,128)(2,1)S(1)}, bf16[40,4096]{1,0:T(8,128)(2,1)S(1)}, u32[]{:S(2)}, u32[]{:S(2)}) collective-permute-start(bf16[40,4096]{1,0:T(8,128)(2,1)S(1)} %slice.39), channel_id=1, source_target_pairs={{0,1},{1,0},{2,3},{3,2},{4,5},{5,4},{6,7},{7,6},{8,9},{9,8},{10,11... | collective-permute-start | bytes 983048 | tf_op jit(solution)/shard_map/ppermute | solution.py:261
  38.8 45.7 %collective-permute-start.7 = (bf16[80,4096]{1,0:T(8,128)(2,1)S(1)}, bf16[80,4096]{1,0:T(8,128)(2,1)S(1)}, u32[]{:S(2)}, u32[]{:S(2)}) collective-permute-start(bf16[80,4096]{1,0:T(8,128)(2,1)S(1)} %get-tuple-element.49), channel_id=1, source_target_pairs={{0,6},{1,7},{2,4},{3,5},{4,2},{5,3},{6,0},{7,1},{8,14},{9,15},{10,... | collective-permute-start | bytes 1966088 | tf_op jit(solution)/shard_map/ppermute | solution.py:261
  46.1 36.1 %copy-start.19 = (bf16[1040,256]{1,0:T(8,128)(2,1)}, bf16[1040,256]{1,0:T(8,128)(2,1)S(1)}, u32[]{:S(2)}) copy-start(bf16[1040,256]{1,0:T(8,128)(2,1)S(1)} %get-tuple-element.64.refs_0_) | copy-start | bytes 1597444
  46.1 37.6 %collective-permute-start.9 = (bf16[1232,256]{1,0:T(8,128)(2,1)S(1)}, bf16[1232,256]{1,0:T(8,128)(2,1)S(1)}, u32[]{:S(2)}, u32[]{:S(2)}) collective-permute-start(bf16[1232,256]{1,0:T(8,128)(2,1)S(1)} %get-tuple-element.51), channel_id=1, source_target_pairs={{0,16},{8,24},{16,0},{24,8},{1,17},{9,25},{17,1},{25,9},{2,18},{10... | collective-permute-start | bytes 1892360 | tf_op jit(solution)/shard_map/ppermute | solution.py:261
  47.7 35.3 %collective-permute-start.8 = (bf16[1168,256]{1,0:T(8,128)(2,1)S(1)}, bf16[1168,256]{1,0:T(8,128)(2,1)S(1)}, u32[]{:S(2)}, u32[]{:S(2)}) collective-permute-start(bf16[1168,256]{1,0:T(8,128)(2,1)S(1)} %get-tuple-element.50), channel_id=1, source_target_pairs={{0,8},{8,0},{16,24},{24,16},{1,9},{9,1},{17,25},{25,17},{2,10},{10... | collective-permute-start | bytes 1794056 | tf_op jit(solution)/shard_map/ppermute | solution.py:261
  49.2 18.4 %collective-permute-start.11 = (bf16[416,256]{1,0:T(8,128)(2,1)S(1)}, bf16[416,256]{1,0:T(8,128)(2,1)S(1)}, u32[]{:S(2)}, u32[]{:S(2)}) collective-permute-start(bf16[416,256]{1,0:T(8,128)(2,1)S(1)} %slice.49), channel_id=1, source_target_pairs={{0,8},{8,0},{16,24},{24,16},{1,9},{9,1},{17,25},{25,17},{2,10},{10... | collective-permute-start | bytes 638984 | tf_op jit(solution)/shard_map/ppermute | solution.py:261
  63.8 13.7 %collective-permute-start.6 = (bf16[40,4096]{1,0:T(8,128)(2,1)S(1)}, bf16[40,4096]{1,0:T(8,128)(2,1)S(1)}, u32[]{:S(2)}, u32[]{:S(2)}) collective-permute-start(bf16[40,4096]{1,0:T(8,128)(2,1)S(1)} %slice.40), channel_id=1, source_target_pairs={{0,1},{1,0},{2,3},{3,2},{4,5},{5,4},{6,7},{7,6},{8,9},{9,8},{10,11... | collective-permute-start | bytes 983048 | tf_op jit(solution)/shard_map/ppermute | solution.py:261
  67.5 8.5 %collective-permute-start.10 = (bf16[624,256]{1,0:T(8,128)(2,1)S(1)}, bf16[624,256]{1,0:T(8,128)(2,1)S(1)}, u32[]{:S(2)}, u32[]{:S(2)}) collective-permute-start(bf16[624,256]{1,0:T(8,128)(2,1)S(1)} %slice.48), channel_id=1, source_target_pairs={{0,16},{8,24},{16,0},{24,8},{1,17},{9,25},{17,1},{25,9},{2,18},{10... | collective-permute-start | bytes 958472 | tf_op jit(solution)/shard_map/ppermute | solution.py:261
  77.4 4.7 %copy-start.5 = (f32[512,1536]{1,0:T(8,128)}, f32[512,1536]{1,0:T(8,128)S(1)}, u32[]{:S(2)}) copy-start(f32[512,1536]{1,0:T(8,128)S(1)} %get-tuple-element.53.refs_5_) | copy-start | bytes 9437188
  77.5 4.7 %copy-start.7 = (f32[768,512]{1,0:T(8,128)}, f32[768,512]{1,0:T(8,128)S(1)}, u32[]{:S(2)}) copy-start(f32[768,512]{1,0:T(8,128)S(1)} %get-tuple-element.54.refs_6_) | copy-start | bytes 4718596
  82.2 0.8 copy-start.17
  83.0 3.2 %copy-start.15 = (bf16[1168,256]{1,0:T(8,128)(2,1)}, bf16[1168,256]{1,0:T(8,128)(2,1)S(1)}, u32[]{:S(2)}) copy-start(bf16[1168,256]{1,0:T(8,128)(2,1)S(1)} %collective-permute-done.8.refs_1_) | copy-start | bytes 1794052
  83.7 1.6 %copy-start.13 = (bf16[1232,256]{1,0:T(8,128)(2,1)}, bf16[1232,256]{1,0:T(8,128)(2,1)S(1)}, u32[]{:S(2)}) copy-start(bf16[1232,256]{1,0:T(8,128)(2,1)S(1)} %collective-permute-done.9.refs_2_) | copy-start | bytes 1892356
  85.3 0.8 copy-start.11
  86.2 2.0 %collective-permute-start.12 = (bf16[40,4096]{1,0:T(8,128)(2,1)}, bf16[40,4096]{1,0:T(8,128)(2,1)S(1)}, u32[]{:S(2)}, u32[]{:S(2)}) collective-permute-start(bf16[40,4096]{1,0:T(8,128)(2,1)} %slice.43), channel_id=1, source_target_pairs={{0,1},{1,0},{2,3},{3,2},{4,5},{5,4},{6,7},{7,6},{8,9},{9,8},{10,11... | collective-permute-start | bytes 983048 | tf_op jit(solution)/shard_map/ppermute | solution.py:261
  86.2 20.3 %collective-permute-start.13 = (bf16[1232,256]{1,0:T(8,128)(2,1)}, bf16[1232,256]{1,0:T(8,128)(2,1)}, u32[]{:S(2)}, u32[]{:S(2)}) collective-permute-start(bf16[1232,256]{1,0:T(8,128)(2,1)} %get-tuple-element.57), channel_id=1, source_target_pairs={{0,8},{8,0},{16,24},{24,16},{1,9},{9,1},{17,25},{25,17},{2,10},{10... | collective-permute-start | bytes 1892360 | tf_op jit(solution)/shard_map/ppermute | solution.py:261
  87.6 16.7 %collective-permute-start.14 = (bf16[1168,256]{1,0:T(8,128)(2,1)}, bf16[1168,256]{1,0:T(8,128)(2,1)}, u32[]{:S(2)}, u32[]{:S(2)}) collective-permute-start(bf16[1168,256]{1,0:T(8,128)(2,1)} %get-tuple-element.58), channel_id=1, source_target_pairs={{0,16},{8,24},{16,0},{24,8},{1,17},{9,25},{17,1},{25,9},{2,18},{10... | collective-permute-start | bytes 1794056 | tf_op jit(solution)/shard_map/ppermute | solution.py:261
  88.2 2.8 %copy-start.2 = (bf16[1,2048,1536]{2,1,0:T(8,128)(2,1)S(1)}, bf16[1,2048,1536]{2,1,0:T(8,128)(2,1)}, u32[]{:S(2)}) copy-start(bf16[1,2048,1536]{2,1,0:T(8,128)(2,1)} %param.10) | copy-start | bytes 18874372
  90.9 1.1 copy-start.12
  96.7 0.8 copy-start.21
  97.5 35.5 %collective-permute-start.16 = (bf16[1232,256]{1,0:T(8,128)(2,1)}, bf16[1232,256]{1,0:T(8,128)(2,1)}, u32[]{:S(2)}, u32[]{:S(2)}) collective-permute-start(bf16[1232,256]{1,0:T(8,128)(2,1)} %get-tuple-element.62), channel_id=1, source_target_pairs={{0,16},{8,24},{16,0},{24,8},{1,17},{9,25},{17,1},{25,9},{2,18},{10... | collective-permute-start | bytes 1892360 | tf_op jit(solution)/shard_map/ppermute | solution.py:261
  99.0 23.2 %collective-permute-start.22 = (bf16[624,256]{1,0:T(8,128)(2,1)}, bf16[624,256]{1,0:T(8,128)(2,1)S(1)}, u32[]{:S(2)}, u32[]{:S(2)}) collective-permute-start(bf16[624,256]{1,0:T(8,128)(2,1)} %slice.51), channel_id=1, source_target_pairs={{0,8},{8,0},{16,24},{24,16},{1,9},{9,1},{17,25},{25,17},{2,10},{10... | collective-permute-start | bytes 958472 | tf_op jit(solution)/shard_map/ppermute | solution.py:261
  99.6 35.1 %collective-permute-start.15 = (bf16[1168,256]{1,0:T(8,128)(2,1)}, bf16[1168,256]{1,0:T(8,128)(2,1)}, u32[]{:S(2)}, u32[]{:S(2)}) collective-permute-start(bf16[1168,256]{1,0:T(8,128)(2,1)} %get-tuple-element.61), channel_id=1, source_target_pairs={{0,8},{8,0},{16,24},{24,16},{1,9},{9,1},{17,25},{25,17},{2,10},{10... | collective-permute-start | bytes 1794056 | tf_op jit(solution)/shard_map/ppermute | solution.py:261
  104.3 17.3 %collective-permute-start.21 = (bf16[416,256]{1,0:T(8,128)(2,1)}, bf16[416,256]{1,0:T(8,128)(2,1)S(1)}, u32[]{:S(2)}, u32[]{:S(2)}) collective-permute-start(bf16[416,256]{1,0:T(8,128)(2,1)} %slice.50), channel_id=1, source_target_pairs={{0,16},{8,24},{16,0},{24,8},{1,17},{9,25},{17,1},{25,9},{2,18},{10... | collective-permute-start | bytes 638984 | tf_op jit(solution)/shard_map/ppermute | solution.py:261
  109.0 23.8 %all-to-all-start = ((f32[8,1,40]{2,1,0:T(1,128)}), f32[8,1,40]{2,1,0:T(1,128)S(1)}, u32[]{:S(2)}, u32[]{:S(2)}) async-start(f32[8,1,40]{2,1,0:T(1,128)} %bitcast.5), calls=%async_computation | async-start | bytes 8192 | tf_op jit(solution)/shard_map/all_to_all | solution.py:265
  112.5 25.3 %collective-permute-start.20 = (bf16[416,256]{1,0:T(8,128)(2,1)}, bf16[416,256]{1,0:T(8,128)(2,1)}, u32[]{:S(2)}, u32[]{:S(2)}) collective-permute-start(bf16[416,256]{1,0:T(8,128)(2,1)} %slice.53), channel_id=1, source_target_pairs={{0,8},{8,0},{16,24},{24,16},{1,9},{9,1},{17,25},{25,17},{2,10},{10... | collective-permute-start | bytes 638984 | tf_op jit(solution)/shard_map/ppermute | solution.py:261
  121.6 0.7 copy-start.23
  122.3 1.9 %copy-start.6 = (f32[512,1536]{1,0:T(8,128)S(1)}, f32[512,1536]{1,0:T(8,128)}, u32[]{:S(2)}) copy-start(f32[512,1536]{1,0:T(8,128)} %copy-done.5) | copy-start | bytes 9437188
  124.2 1.4 copy-start.8
  125.6 1.1 copy-start.14
  126.6 1.1 copy-start.16
  127.7 1.0 copy-start.20
  128.8 0.9 copy-start.24
  129.7 7.6 %copy-start.26 = (f32[128,2]{0,1:T(2,128)S(1)}, f32[128,2]{0,1:T(2,128)}, u32[]{:S(2)}) copy-start(f32[128,2]{0,1:T(2,128)} %param.8) | copy-start | bytes 3076
  131.2 1.1 copy-start.9
  132.3 10.7 %collective-permute-start.19 = (bf16[624,256]{1,0:T(8,128)(2,1)}, bf16[624,256]{1,0:T(8,128)(2,1)S(1)}, u32[]{:S(2)}, u32[]{:S(2)}) collective-permute-start(bf16[624,256]{1,0:T(8,128)(2,1)} %slice.52), channel_id=1, source_target_pairs={{0,16},{8,24},{16,0},{24,8},{1,17},{9,25},{17,1},{25,9},{2,18},{10... | collective-permute-start | bytes 958472 | tf_op jit(solution)/shard_map/ppermute | solution.py:261
  134.0 14.3 %collective-permute-start.18 = (bf16[624,256]{1,0:T(8,128)(2,1)S(1)}, bf16[624,256]{1,0:T(8,128)(2,1)S(1)}, u32[]{:S(2)}, u32[]{:S(2)}) collective-permute-start(bf16[624,256]{1,0:T(8,128)(2,1)S(1)} %slice.55), channel_id=1, source_target_pairs={{0,8},{8,0},{16,24},{24,16},{1,9},{9,1},{17,25},{25,17},{2,10},{10... | collective-permute-start | bytes 958472 | tf_op jit(solution)/shard_map/ppermute | solution.py:261
  135.7 12.6 %collective-permute-start.17 = (bf16[416,256]{1,0:T(8,128)(2,1)S(1)}, bf16[416,256]{1,0:T(8,128)(2,1)S(1)}, u32[]{:S(2)}, u32[]{:S(2)}) collective-permute-start(bf16[416,256]{1,0:T(8,128)(2,1)S(1)} %slice.54), channel_id=1, source_target_pairs={{0,16},{8,24},{16,0},{24,8},{1,17},{9,25},{17,1},{25,9},{2,18},{10... | collective-permute-start | bytes 638984 | tf_op jit(solution)/shard_map/ppermute | solution.py:261
  143.0 1.4 copy-start.10
  144.4 1.0 copy-start.18
  145.5 2.8 %copy-start.22 = (bf16[1040,256]{1,0:T(8,128)(2,1)S(1)}, bf16[1040,256]{1,0:T(8,128)(2,1)}, u32[]{:S(2)}) copy-start(bf16[1040,256]{1,0:T(8,128)(2,1)} %copy-done.21) | copy-start | bytes 1597444

commit v2 on v1

--- a/solution.py
+++ b/solution.py
@@ -71,19 +71,25 @@
     )(ids, probs, tokens, cotangent)
 
 
-def split_rows(top, half):
+def split_rows(count, top, half):
     blocks = 3 * half // TILE
-    low = PAIR - top
+    low = count - top
     return blocks, low, (blocks + 4) * top, (blocks + 4) * low
 
 
-def expert_kernel(top, a_ref, b_ref, gate_ref, up_ref, down_ref, *rest):
+def expert_kernel(pairs, top, *refs):
+    row_refs, (gate_ref, up_ref, down_ref), rest = (
+        refs[: 2 * pairs],
+        refs[2 * pairs : 2 * pairs + 3],
+        refs[2 * pairs + 3 :],
+    )
     own_ref, to_x, to_y, inner_ref, x_rows, s_rows, s_turned, total = rest
+    count = pairs * PAIR
     width = gate_ref.shape[0]
     steps = pl.num_programs(0)
     half = TILE * 3
     quarter = width // 4
-    blocks, low, from_x, from_y = split_rows(top, half)
+    blocks, low, from_x, from_y = split_rows(count, top, half)
     step = pl.program_id(0)
     group = lax.axis_index("dp")
 
@@ -91,10 +97,7 @@
     def _():
         for rows, start in ((x_rows, 0), (s_rows, width)):
             rows[...] = jnp.concatenate(
-                [
-                    a_ref[:CAP, start : start + width].astype(F32),
-                    b_ref[:, start : start + width].astype(F32),
-                ],
+                [ref[:CAP, start : start + width].astype(F32) for ref in row_refs],
                 axis=0,
             ).astype(BF16)
         for q in range(4):
@@ -105,14 +108,14 @@
                 return rows[:, pl.ds(pl.multiple_of(at, TILE), TILE)]
 
             at = blocks + q
-            own_ref[at * PAIR : (at + 1) * PAIR] = cut(0)
+            own_ref[at * count : (at + 1) * count] = cut(0)
             far = cut(3)
             to_x[at * top : (at + 1) * top] = far[:top]
             to_y[at * low : (at + 1) * low] = far[top:]
-            start = from_x + blocks * low + q * PAIR
-            to_x[start : start + PAIR] = cut(1)
-            start = from_y + blocks * top + q * PAIR
-            to_y[start : start + PAIR] = cut(2)
+            start = from_x + blocks * low + q * count
+            to_x[start : start + count] = cut(1)
+            start = from_y + blocks * top + q * count
+            to_y[start : start + count] = cut(2)
         s_turned[...] = s_rows[...].T
         total[...] = jnp.zeros_like(total)
 
@@ -132,7 +135,7 @@
         def rows_at(start, count):
             return pl.ds(pl.multiple_of(start + block * count, 16), count)
 
-        own_ref[rows_at(0, PAIR)] = values
+        own_ref[rows_at(0, count)] = values
         to_x[rows_at(0, top)] = values[:top]
         to_x[rows_at(from_x, low)] = values[top:]
         to_y[rows_at(0, low)] = values[top:]
@@ -140,85 +143,85 @@
 
     @pl.when(step == steps - 1)
     def _():
-        inner_ref[...] = jnp.broadcast_to(total[...], (PAIR, 128)).T[0:1]
-
-
-def expert_rows(rows_a, rows_b, weight_gu, weight_down, top):
+        inner_ref[...] = jnp.broadcast_to(total[...], (count, 128)).T[0:1]
+
+
+def expert_rows(rows, weight_gu, weight_down, top):
+    count = len(rows) // 2 * PAIR
     width, both = weight_gu.shape
     half = both // 2
     steps = half // TILE
-    blocks, low, from_x, from_y = split_rows(top, half)
+    blocks, low, from_x, from_y = split_rows(count, top, half)
     shapes = [
-        ((blocks + 4) * PAIR, TILE),
-        (from_x + blocks * low + 4 * PAIR, TILE),
-        (from_y + blocks * top + 4 * PAIR, TILE),
+        ((blocks + 4) * count, TILE),
+        (from_x + blocks * low + 4 * count, TILE),
+        (from_y + blocks * top + 4 * count, TILE),
     ]
 
     def whole(shape):
         return pl.BlockSpec(shape, lambda h: (0, 0))
 
     return pl.pallas_call(
-        functools.partial(expert_kernel, top),
+        functools.partial(expert_kernel, len(rows) // 2, top),
         grid=(steps,),
         in_specs=[
-            whole(rows_a.shape),
-            whole(rows_b.shape),
+            *[whole(part.shape) for part in rows],
             pl.BlockSpec((width, TILE), lambda h: (0, h)),
             pl.BlockSpec((width, TILE), lambda h: (0, h + steps)),
             pl.BlockSpec((TILE, width), lambda h: (h, 0)),
         ],
-        out_specs=[whole(shape) for shape in shapes] + [whole((1, PAIR))],
+        out_specs=[whole(shape) for shape in shapes] + [whole((1, count))],
         out_shape=[jax.ShapeDtypeStruct(shape, BF16) for shape in shapes]
-        + [jax.ShapeDtypeStruct((1, PAIR), F32)],
+        + [jax.ShapeDtypeStruct((1, count), F32)],
         scratch_shapes=[
-            pltpu.VMEM((PAIR, width), BF16),
-            pltpu.VMEM((PAIR, width), BF16),
-            pltpu.VMEM((width, PAIR), BF16),
-            pltpu.VMEM((PAIR, 1), F32),
+            pltpu.VMEM((count, width), BF16),
+            pltpu.VMEM((count, width), BF16),
+            pltpu.VMEM((width, count), BF16),
+            pltpu.VMEM((count, 1), F32),
         ],
-        compiler_params=pltpu.CompilerParams(vmem_limit_bytes=14 * MIB),
-        cost_estimate=pl.CostEstimate(flops=1_000_000, bytes_accessed=1_000_000, transcendentals=0),
+        compiler_params=pltpu.CompilerParams(vmem_limit_bytes=20 * MIB),
+        cost_estimate=pl.CostEstimate(flops=1_000, bytes_accessed=1_000, transcendentals=0),
         name="expert_rows",
-    )(rows_a, rows_b, weight_gu, weight_gu, weight_down)
-
-
-def gradient_kernel(tops, half, adding, *refs):
-    groups, refs = [refs[5 * n : 5 * n + 5] for n in range(len(tops))], refs[5 * len(tops) :]
+    )(*rows, weight_gu, weight_gu, weight_down)
+
+
+def gradient_kernel(top, half, adding, *refs):
+    (own, got_x, got_y, far_top, far_low), refs = refs[:5], refs[5:]
+    count = own.shape[0] // (3 * half // TILE + 4)
+    blocks, low, from_x, from_y = split_rows(count, top, half)
     if adding:
         (acc_gu, acc_down), refs = refs[:2], refs[2:]
     out_gu, out_down, turned, s_rows = refs
     both = 2 * half // TILE
 
     def factor(block):
-        parts = []
-        for top, (own, got_x, got_y, far_top, far_low) in zip(tops, groups):
-            _, low, from_x, from_y = split_rows(top, half)
-            parts += [
-                own[block * PAIR : (block + 1) * PAIR],
+        return jnp.concatenate(
+            [
+                own[block * count : (block + 1) * count],
                 got_x[block * top : (block + 1) * top],
                 got_x[from_x + block * low : from_x + (block + 1) * low],
                 got_y[from_y + block * top : from_y + (block + 1) * top],
                 got_y[block * low : (block + 1) * low],
                 far_top[block * top : (block + 1) * top],
                 far_low[block * low : (block + 1) * low],
-            ]
-        return jnp.concatenate(parts, axis=0)
+            ],
+            axis=0,
+        )
 
     def piece(q):
-        parts = []
-        for top, (own, got_x, got_y, far_top, far_low) in zip(tops, groups):
-            blocks, low, from_x, from_y = split_rows(top, half)
-            block = blocks + q
-            at_x = from_x + blocks * low + q * PAIR
-            at_y = from_y + blocks * top + q * PAIR
-            parts += [
-                own[block * PAIR : (block + 1) * PAIR],
-                got_x[at_x : at_x + PAIR],
-                got_y[at_y : at_y + PAIR],
+        block = blocks + q
+        at_x = from_x + blocks * low + q * count
+        at_y = from_y + blocks * top + q * count
+        return jnp.concatenate(
+            [
+                own[block * count : (block + 1) * count],
+                got_x[at_x : at_x + count],
+                got_y[at_y : at_y + count],
                 far_top[block * top : (block + 1) * top],
                 far_low[block * low : (block + 1) * low],
-            ]
-        return jnp.concatenate(parts, axis=0)
+            ],
+            axis=0,
+        )
 
     for q in range(2):
         turned[q * TILE : (q + 1) * TILE, :] = piece(q).T
@@ -237,21 +240,22 @@
         out_down[at, :] = grad.astype(out_down.dtype)
 
 
-def gradients(tops, pieces, half, quarter, sums=(), final=False):
+def gradients(top, pieces, half, quarter, sums=(), final=False):
     kept = BF16 if final else F32
-    rows = 4 * PAIR * len(tops)
+    rows = 4 * pieces[0].shape[0] // (3 * half // TILE + 4)
     vmem = pl.BlockSpec(memory_space=pltpu.VMEM)
     return pl.pallas_call(
-        functools.partial(gradient_kernel, tops, half, len(sums)),
+        functools.partial(gradient_kernel, top, half, len(sums)),
         in_specs=[vmem] * (len(pieces) + len(sums)),
         out_specs=[vmem] * 2,
         out_shape=[
             jax.ShapeDtypeStruct((quarter, 2 * half), kept),
             jax.ShapeDtypeStruct((half, quarter), kept),
         ],
+        input_output_aliases={} if final or not sums else {len(pieces): 0, len(pieces) + 1: 1},
         scratch_shapes=[pltpu.VMEM((quarter, rows), BF16), pltpu.VMEM((rows, quarter), BF16)],
         compiler_params=pltpu.CompilerParams(vmem_limit_bytes=14 * MIB),
-        cost_estimate=pl.CostEstimate(flops=1_000_000, bytes_accessed=1_000_000, transcendentals=0),
+        cost_estimate=pl.CostEstimate(flops=1_000, bytes_accessed=1_000, transcendentals=0),
         name="gradients",
     )(*pieces, *sums)
 
@@ -275,17 +279,17 @@
     quarter = tokens.shape[1] // 4
     ids, probs = expert_ids.T, gate_probs.T
     *local, slots = dispatch_rows(ids, probs, tokens, cotangent)
-    tops = (48, 32, 48, 32)
+    tops = (48, PAIR, 32)
     inner, pieces, forwards = [], [], []
 
     def other_core(rows):
         return exchange(rows[CAP:], "expert", 1)
 
-    def compute(rows):
+    def compute(*rows):
         top = tops[len(inner)]
-        own, to_x, to_y, found = expert_rows(rows, other_core(rows), gate_up[0], down[0], top)
+        own, to_x, to_y, found = expert_rows(rows, gate_up[0], down[0], top)
         inner.append(found)
-        _, _, from_x, from_y = split_rows(top, half)
+        _, _, from_x, from_y = split_rows(len(rows) // 2 * PAIR, top, half)
         got_x, got_y = exchange(to_x, "dp", 1), exchange(to_y, "dp", 2)
         forward = (got_x[:from_x], got_y[:from_y])
         far_top, far_low = exchange(forward[0], "dp", 2), exchange(forward[1], "dp", 1)
@@ -293,26 +297,24 @@
         pieces.append([own, got_x, got_y, far_top, far_low])
 
     def add(chunk, sums=()):
-        return gradients(
-            tops[chunk : chunk + 1], pieces[chunk], half, quarter, sums, chunk == len(tops) - 1
-        )
-
+        return gradients(tops[chunk], pieces[chunk], half, quarter, sums, chunk == len(tops) - 1)
+
+    rows_1 = exchange(local[1], "expert", 2)
     rows_2 = exchange(local[2], "expert", 4)
-    rows_1 = exchange(local[1], "expert", 2)
-    compute(local[0])
+    compute(local[0], other_core(local[0]))
+    rows_1 = after(rows_1, inner[0])
+    other_1 = other_core(rows_1)
+    rows_3 = exchange(after(local[3], rows_2), "expert", 6)
     rows_2 = after(rows_2, *forwards[0])
-    rows_3 = exchange(after(local[3], rows_2), "expert", 6)
-    compute(rows_2)
-    compute(after(rows_1, inner[1]))
+    compute(rows_1, other_1, rows_2, other_core(rows_2))
     sums = add(0)
-    compute(after(rows_3, inner[2], *forwards[1], *sums))
+    rows_3 = after(rows_3, inner[1], *sums)
+    compute(rows_3, after(other_core(rows_3), *forwards[1]))
     sums = add(1, sums)
-    sums = add(2, sums)
-    grad_gu, grad_down = add(3, sums)
+    grad_gu, grad_down = add(2, sums)
     numbers = jnp.arange(EXPERTS, dtype=jnp.int32)
     mine = (numbers[:, None] == jnp.bitwise_xor(numbers, me)[None, :])[:, :, None]
-    in_order = [inner[0], inner[2], inner[1], inner[3]]
-    rows_inner = after(jnp.concatenate(in_order, axis=1), *forwards[2]).reshape(EXPERTS, CAP)
+    rows_inner = after(jnp.concatenate(inner, axis=1), *forwards[2]).reshape(EXPERTS, CAP)
     sent = jnp.sum(jnp.where(mine, rows_inner[None], 0.0), axis=1)
     returned = jnp.sum(jnp.where(mine, swap(sent)[None], 0.0), axis=1).reshape(-1)
     chosen = slots[:, None, :] == jnp.arange(EXPERTS * CAP, dtype=jnp.int32)[None, :, None]

time: 153 us -> 148 us (0.967)
  waiting for transfers between devices: 59.1 us -> 74.1 us
  local copies, waits for them, and re-layouts: 34 us -> 24.3 us
  Pallas kernels: 27.1 us -> 21.8 us
  starting transfers between devices: 29.4 us -> 24.8 us
    ppermute x23 -> x19, waiting for transfers between devices: 59.1 us -> 74.1 us  [exchange(): return lax.ppermute(values, axis, [(n, n ^ mask) for n in range(size)])]
    unnamed x60 -> x42, local copies, waits for them, and re-layouts: 26.1 us -> 18.8 us
    pallas_call x8 -> x6, Pallas kernels: 26.1 us -> 20.8 us  [the longest x3 12.3 us: expert_rows(): pl.pallas_call(functools.partial(expert_kernel, len(rows) // 2, top), gri...]
    ppermute x23 -> x19, starting transfers between devices: 26 us -> 21.1 us  [exchange(): return lax.ppermute(values, axis, [(n, n ^ mask) for n in range(size)])]
    slice x8 -> x6, local copies, waits for them, and re-layouts: 6.91 us -> 5.32 us  [compute(): forward = (got_x[:from_x], got_y[:from_y])]
  transfers between devices with their start and end apart: 24 -> 20, of which waited for: 8 -> 10; matrix products, arithmetic and copies ran while one was open for 6% -> 5% of each run, Pallas kernels for 15% -> 6%
where the time goes in v2:
time: 148 us; the launch traced here: 147 us
  waiting for transfers between devices  74.1 us (50%)
  starting transfers between devices  24.8 us (17%)
  local copies, waits for them, and re-layouts  24.3 us (16%)
  Pallas kernels  21.8 us (15%)
  other arithmetic  1.57 us (1%)
    ppermute x19, waiting for transfers between devices, exchange(): return lax.ppermute(values, axis, [(n, n ^ mask) for n in range(size)])  74.1 us
    ppermute x19, starting transfers between devices, exchange(): return lax.ppermute(values, axis, [(n, n ^ mask) for n in range(size)])  21.1 us
    unnamed x42, local copies, waits for them, and re-layouts  18.8 us
    pallas_call x3, Pallas kernels, expert_rows(): pl.pallas_call(functools.partial(expert_kernel, len(rows) // 2, top), gri...  12.3 us
    pallas_call x3, Pallas kernels, gradients(): pl.pallas_call(functools.partial(gradient_kernel, top, half, len(sums)),...  8.56 us
    slice x6, local copies, waits for them, and re-layouts, compute(): forward = (got_x[:from_x], got_y[:from_y])  5.32 us
    all_to_all x1, starting transfers between devices, swap(): lax.all_to_all(values, 'expert', split_axis=0, concat_axis=0, tiled=True)  3.74 us
  transfers between devices with their start and end apart: 20, of which 10 were waited for; matrix products, arithmetic and copies ran while one was open for 5% of the time, Pallas kernels for 6%

profile of v2, /device:TPU:0, one launch (start us, length us, event | category | flops | bytes accessed | tf_op | source)
XLA Modules:
  0.0 147.5 jit_solution(16867689545642701251)
XLA Ops:
  0.6 0.7 copy-done.16
  1.3 1.0 copy-done.18
  2.4 1.0 copy-done.19
  3.4 0.7 copy-done.20
  4.1 1.0 dispatch_rows.1
  5.1 0.5 collective-permute-start
  5.6 2.7 %collective-permute-start.1 = (bf16[80,4096]{1,0:T(8,128)(2,1)S(1)}, bf16[80,4096]{1,0:T(8,128)(2,1)S(1)}, u32[]{:S(2)}, u32[]{:S(2)}) collective-permute-start(bf16[80,4096]{1,0:T(8,128)(2,1)S(1)} %get-tuple-element.35), channel_id=1, source_target_pairs={{0,2},{1,3},{2,0},{3,1},{4,6},{5,7},{6,4},{7,5},{8,10},{9,11},{10,... | collective-permute-start | bytes 1966088 | tf_op jit(solution)/shard_map/ppermute | solution.py:265
  8.2 2.6 %collective-permute-start.3 = (bf16[80,4096]{1,0:T(8,128)(2,1)S(1)}, bf16[80,4096]{1,0:T(8,128)(2,1)S(1)}, u32[]{:S(2)}, u32[]{:S(2)}) collective-permute-start(bf16[80,4096]{1,0:T(8,128)(2,1)S(1)} %get-tuple-element.37), channel_id=1, source_target_pairs={{0,4},{1,5},{2,6},{3,7},{4,0},{5,1},{6,2},{7,3},{8,12},{9,13},{10,... | collective-permute-start | bytes 1966088 | tf_op jit(solution)/shard_map/ppermute | solution.py:265
  10.8 2.8 %copy-done = bf16[1,2048,1536]{2,1,0:T(8,128)(2,1)S(1)} copy-done((bf16[1,2048,1536]{2,1,0:T(8,128)(2,1)S(1)}, bf16[1,2048,1536]{2,1,0:T(8,128)(2,1)}, u32[]{:S(2)}) %copy-start) | copy-done | bytes 6291480
  13.6 1.9 %copy-done.2 = bf16[1,768,2048]{2,1,0:T(8,128)(2,1)S(1)} copy-done((bf16[1,768,2048]{2,1,0:T(8,128)(2,1)S(1)}, bf16[1,768,2048]{2,1,0:T(8,128)(2,1)}, u32[]{:S(2)}) %copy-start.2) | copy-done | bytes 3145752
  15.5 3.6 %expert_rows.3 = (bf16[1040,256]{1,0:T(8,128)(2,1)S(1)}, bf16[1232,256]{1,0:T(8,128)(2,1)S(1)}, bf16[1168,256]{1,0:T(8,128)(2,1)S(1)}, f32[1,80]{1,0:T(1,128)S(1)}) custom-call(bf16[80,4096]{1,0:T(8,128)(2,1)S(1)} %get-tuple-element.33.refs_0_, bf16[40,4096]{1,0:T(8,128)(2,1)S(1)} %collective-permute-done.refs_1_, bf16[2048,1536]{1,0:T(8,128)(2,1)S(1)} %bitcast.12, ...), custom_call_target="tpu_custom_call" | custom-call | flops 1000 | bytes 1000 | tf_op jit(solution)/shard_map/expert_rows/pallas_call | solution.py:164
  19.1 1.5 %collective-permute-start.4 = (bf16[1232,256]{1,0:T(8,128)(2,1)S(1)}, bf16[1232,256]{1,0:T(8,128)(2,1)S(1)}, u32[]{:S(2)}, u32[]{:S(2)}) collective-permute-start(bf16[1232,256]{1,0:T(8,128)(2,1)S(1)} %get-tuple-element.38), channel_id=1, source_target_pairs={{0,8},{8,0},{16,24},{24,16},{1,9},{9,1},{17,25},{25,17},{2,10},{10... | collective-permute-start | bytes 1892360 | tf_op jit(solution)/shard_map/ppermute | solution.py:265
  20.7 1.5 %collective-permute-start.5 = (bf16[1168,256]{1,0:T(8,128)(2,1)S(1)}, bf16[1168,256]{1,0:T(8,128)(2,1)S(1)}, u32[]{:S(2)}, u32[]{:S(2)}) collective-permute-start(bf16[1168,256]{1,0:T(8,128)(2,1)S(1)} %get-tuple-element.39), channel_id=1, source_target_pairs={{0,16},{8,24},{16,0},{24,8},{1,17},{9,25},{17,1},{25,9},{2,18},{10... | collective-permute-start | bytes 1794056 | tf_op jit(solution)/shard_map/ppermute | solution.py:265
  22.2 15.3 %collective-permute-done.1.refs_0_ = bf16[80,4096]{1,0:T(8,128)(2,1)S(1)} collective-permute-done((bf16[80,4096]{1,0:T(8,128)(2,1)S(1)}, bf16[80,4096]{1,0:T(8,128)(2,1)S(1)}, u32[]{:S(2)}, u32[]{:S(2)}) %collective-permute-start.1) | collective-permute-done | bytes 655392 | tf_op jit(solution)/shard_map/ppermute | solution.py:265
  37.5 0.1 collective-permute-start.2
  37.7 2.4 %collective-permute-done.3.refs_2_ = bf16[80,4096]{1,0:T(8,128)(2,1)S(1)} collective-permute-done((bf16[80,4096]{1,0:T(8,128)(2,1)S(1)}, bf16[80,4096]{1,0:T(8,128)(2,1)S(1)}, u32[]{:S(2)}, u32[]{:S(2)}) %collective-permute-start.3) | collective-permute-done | bytes 655392 | tf_op jit(solution)/shard_map/ppermute | solution.py:265
  40.1 0.1 collective-permute-start.6
  40.2 1.6 %collective-permute-done.6.refs_3_ = bf16[40,4096]{1,0:T(8,128)(2,1)S(1)} collective-permute-done((bf16[40,4096]{1,0:T(8,128)(2,1)S(1)}, bf16[40,4096]{1,0:T(8,128)(2,1)S(1)}, u32[]{:S(2)}, u32[]{:S(2)}) %collective-permute-start.6) | collective-permute-done | bytes 327712 | tf_op jit(solution)/shard_map/ppermute | solution.py:265
  41.8 3.9 %expert_rows.4 = (bf16[2080,256]{1,0:T(8,128)(2,1)S(1)}, bf16[2400,256]{1,0:T(8,128)(2,1)S(1)}, bf16[2400,256]{1,0:T(8,128)(2,1)S(1)}, f32[1,160]{1,0:T(1,128)S(1)}) custom-call(bf16[80,4096]{1,0:T(8,128)(2,1)S(1)} %collective-permute-done.1.refs_0_, bf16[40,4096]{1,0:T(8,128)(2,1)S(1)} %collective-permute-done.2.refs_1_, ...), custom_call_target="tpu_custom_call" | custom-call | flops 1000 | bytes 1000 | tf_op jit(solution)/shard_map/expert_rows/pallas_call | solution.py:164
  45.7 1.0 copy-done.12
  46.7 1.5 %collective-permute-start.11 = (bf16[2400,256]{1,0:T(8,128)(2,1)S(1)}, bf16[2400,256]{1,0:T(8,128)(2,1)S(1)}, u32[]{:S(2)}, u32[]{:S(2)}) collective-permute-start(bf16[2400,256]{1,0:T(8,128)(2,1)S(1)} %get-tuple-element.48), channel_id=1, source_target_pairs={{0,8},{8,0},{16,24},{24,16},{1,9},{9,1},{17,25},{25,17},{2,10},{10... | collective-permute-start | bytes 3686408 | tf_op jit(solution)/shard_map/ppermute | solution.py:265
  48.2 1.5 %collective-permute-start.12 = (bf16[2400,256]{1,0:T(8,128)(2,1)S(1)}, bf16[2400,256]{1,0:T(8,128)(2,1)S(1)}, u32[]{:S(2)}, u32[]{:S(2)}) collective-permute-start(bf16[2400,256]{1,0:T(8,128)(2,1)S(1)} %get-tuple-element.49), channel_id=1, source_target_pairs={{0,16},{8,24},{16,0},{24,8},{1,17},{9,25},{17,1},{25,9},{2,18},{10... | collective-permute-start | bytes 3686408 | tf_op jit(solution)/shard_map/ppermute | solution.py:265
  49.8 2.5 %collective-permute-start.7 = (bf16[80,4096]{1,0:T(8,128)(2,1)S(1)}, bf16[80,4096]{1,0:T(8,128)(2,1)S(1)}, u32[]{:S(2)}, u32[]{:S(2)}) collective-permute-start(bf16[80,4096]{1,0:T(8,128)(2,1)S(1)} %get-tuple-element.43), channel_id=1, source_target_pairs={{0,6},{1,7},{2,4},{3,5},{4,2},{5,3},{6,0},{7,1},{8,14},{9,15},{10,... | collective-permute-start | bytes 1966088 | tf_op jit(solution)/shard_map/ppermute | solution.py:265
  52.2 0.5 collective-permute-start.8
  52.7 0.5 collective-permute-start.9
  53.3 27.1 %collective-permute-done.9.refs_4_ = bf16[416,256]{1,0:T(8,128)(2,1)S(1)} collective-permute-done((bf16[416,256]{1,0:T(8,128)(2,1)S(1)}, bf16[416,256]{1,0:T(8,128)(2,1)S(1)}, u32[]{:S(2)}, u32[]{:S(2)}) %collective-permute-start.9) | collective-permute-done | bytes 213024 | tf_op jit(solution)/shard_map/ppermute | solution.py:265
  80.4 3.5 %collective-permute-done.8.refs_3_ = bf16[624,256]{1,0:T(8,128)(2,1)S(1)} collective-permute-done((bf16[624,256]{1,0:T(8,128)(2,1)S(1)}, bf16[624,256]{1,0:T(8,128)(2,1)S(1)}, u32[]{:S(2)}, u32[]{:S(2)}) %collective-permute-start.8) | collective-permute-done | bytes 319520 | tf_op jit(solution)/shard_map/ppermute | solution.py:265
  83.9 1.4 gradients.3
  85.3 0.0 copy-start.4
  85.3 0.1 collective-permute-start.10
  85.4 1.0 slice.42
  86.5 0.9 slice.43
  87.4 4.7 %expert_rows.5 = (bf16[1040,256]{1,0:T(8,128)(2,1)S(1)}, bf16[1168,256]{1,0:T(8,128)(2,1)}, bf16[1232,256]{1,0:T(8,128)(2,1)}, f32[1,80]{1,0:T(1,128)S(1)}) custom-call(bf16[80,4096]{1,0:T(8,128)(2,1)S(1)} %collective-permute-done.7.refs_0_, bf16[40,4096]{1,0:T(8,128)(2,1)S(1)} %collective-permute-done.10.refs_1_, bf16[2048,1536]{1,0:T(8,128)(2,1)S(1)} %bitcast.16, ...), custom_call_target="tpu_custom_call" | custom-call | flops 1000 | bytes 1000 | tf_op jit(solution)/shard_map/expert_rows/pallas_call | solution.py:164
  92.1 0.8 copy-done.14
  92.9 1.5 %collective-permute-start.14 = (bf16[1232,256]{1,0:T(8,128)(2,1)}, bf16[1232,256]{1,0:T(8,128)(2,1)}, u32[]{:S(2)}, u32[]{:S(2)}) collective-permute-start(bf16[1232,256]{1,0:T(8,128)(2,1)} %get-tuple-element.53), channel_id=1, source_target_pairs={{0,16},{8,24},{16,0},{24,8},{1,17},{9,25},{17,1},{25,9},{2,18},{10... | collective-permute-start | bytes 1892360 | tf_op jit(solution)/shard_map/ppermute | solution.py:265
  94.5 0.5 collective-permute-start.13
  95.0 0.5 collective-permute-start.17
  95.5 1.5 %collective-permute-start.18 = (bf16[1040,256]{1,0:T(8,128)(2,1)}, bf16[1040,256]{1,0:T(8,128)(2,1)}, u32[]{:S(2)}, u32[]{:S(2)}) collective-permute-start(bf16[1040,256]{1,0:T(8,128)(2,1)} %slice.43), channel_id=1, source_target_pairs={{0,8},{8,0},{16,24},{24,16},{1,9},{9,1},{17,25},{25,17},{2,10},{10... | collective-permute-start | bytes 1597448 | tf_op jit(solution)/shard_map/ppermute | solution.py:265
  97.0 0.1 pad_maximum_fusion
  97.1 14.1 %collective-permute-done.13.refs_1_ = bf16[1168,256]{1,0:T(8,128)(2,1)} collective-permute-done((bf16[1168,256]{1,0:T(8,128)(2,1)}, bf16[1168,256]{1,0:T(8,128)(2,1)}, u32[]{:S(2)}, u32[]{:S(2)}) %collective-permute-start.13) | collective-permute-done | bytes 598048 | tf_op jit(solution)/shard_map/ppermute | solution.py:265
  111.1 1.6 %slice.44 = bf16[416,256]{1,0:T(8,128)(2,1)} slice(bf16[1168,256]{1,0:T(8,128)(2,1)} %collective-permute-done.13.refs_1_), slice={[0:416], [0:256]} | slice | bytes 425984 | tf_op jit(solution)/shard_map/slice | solution.py:294
  112.8 1.7 %slice.45 = bf16[624,256]{1,0:T(8,128)(2,1)} slice(bf16[1232,256]{1,0:T(8,128)(2,1)} %collective-permute-done.14.refs_2_), slice={[0:624], [0:256]} | slice | bytes 638976 | tf_op jit(solution)/shard_map/slice | solution.py:294
  114.5 0.1 broadcast_in_dim.60
  114.6 0.7 select_reduce_fusion.2
  115.3 3.7 %all-to-all-start = ((f32[8,1,40]{2,1,0:T(1,128)}), f32[8,1,40]{2,1,0:T(1,128)S(1)}, u32[]{:S(2)}, u32[]{:S(2)}) async-start(f32[8,1,40]{2,1,0:T(1,128)} %bitcast.5), calls=%async_computation | async-start | bytes 8192 | tf_op jit(solution)/shard_map/all_to_all | solution.py:269
  119.0 2.1 %collective-permute-done.17.refs_3_ = bf16[1040,256]{1,0:T(8,128)(2,1)} collective-permute-done((bf16[1040,256]{1,0:T(8,128)(2,1)}, bf16[1040,256]{1,0:T(8,128)(2,1)}, u32[]{:S(2)}, u32[]{:S(2)}) %collective-permute-start.17) | collective-permute-done | bytes 532512 | tf_op jit(solution)/shard_map/ppermute | solution.py:265
  121.1 0.6 collective-permute-done.18.refs_4_
  121.7 1.4 copy-done.5
  123.1 1.3 copy-done.9
  124.3 1.3 copy-done.11
  125.6 1.2 copy-done.13
  126.9 3.4 %gradients.4 = (f32[512,1536]{1,0:T(8,128)S(1)}, f32[768,512]{1,0:T(8,128)S(1)}) custom-call(bf16[2080,256]{1,0:T(8,128)(2,1)S(1)} %copy-done.13, bf16[2400,256]{1,0:T(8,128)(2,1)S(1)} %copy-done.9, bf16[2400,256]{1,0:T(8,128)(2,1)S(1)} %copy-done.11, ...), custom_call_target="tpu_custom_call", output_to_operand_aliasing={{0}: (5, {}), {1}: (6, {})} | custom-call | flops 1000 | bytes 1000 | tf_op jit(solution)/shard_map/gradients/pallas_call | solution.py:247
  130.3 1.1 copy-done.6
  131.4 1.0 collective-permute-start.15
  132.4 0.5 collective-permute-start.16
  132.9 0.1 select_reduce_fusion.1
  133.0 0.1 broadcast_in_dim.65
  133.1 0.1 select_reduce_fusion
  133.2 0.6 bitcast_divide_fusion
  133.8 4.3 %collective-permute-done.15.refs_3_ = bf16[416,256]{1,0:T(8,128)(2,1)} collective-permute-done((bf16[416,256]{1,0:T(8,128)(2,1)}, bf16[416,256]{1,0:T(8,128)(2,1)}, u32[]{:S(2)}, u32[]{:S(2)}) %collective-permute-start.15) | collective-permute-done | bytes 213024 | tf_op jit(solution)/shard_map/ppermute | solution.py:265
  138.1 3.2 %collective-permute-done.16.refs_4_ = bf16[624,256]{1,0:T(8,128)(2,1)S(1)} collective-permute-done((bf16[624,256]{1,0:T(8,128)(2,1)}, bf16[624,256]{1,0:T(8,128)(2,1)S(1)}, u32[]{:S(2)}, u32[]{:S(2)}) %collective-permute-start.16) | collective-permute-done | bytes 319520 | tf_op jit(solution)/shard_map/ppermute | solution.py:265
  141.3 1.4 copy-done.7
  142.7 1.0 copy-done.15
  143.7 3.7 %gradients.5 = (bf16[512,1536]{1,0:T(8,128)(2,1)}, bf16[768,512]{1,0:T(8,128)(2,1)}) custom-call(bf16[1040,256]{1,0:T(8,128)(2,1)S(1)} %copy-done.15, bf16[1168,256]{1,0:T(8,128)(2,1)} %collective-permute-done.13.refs_1_, bf16[1232,256]{1,0:T(8,128)(2,1)} %collective-permute-done.14.refs_2_, bf16[416,256]{1,0:T(8,128)(2,1)} %collective-permute-done.15.refs_3_, ...), custom_call_target="tpu_custom_call" | custom-call | flops 1000 | bytes 1000 | tf_op jit(solution)/shard_map/gradients/pallas_call | solution.py:247
  (45 shorter events, 0.2 us)
Async XLA Ops:
  0.6 0.7 copy-start.16
  1.3 1.0 copy-start.18
  2.4 1.0 copy-start.19
  3.4 0.7 copy-start.20
  5.1 5.8 %collective-permute-start = (bf16[40,4096]{1,0:T(8,128)(2,1)S(1)}, bf16[40,4096]{1,0:T(8,128)(2,1)S(1)}, u32[]{:S(2)}, u32[]{:S(2)}) collective-permute-start(bf16[40,4096]{1,0:T(8,128)(2,1)S(1)} %slice.30), channel_id=1, source_target_pairs={{0,1},{1,0},{2,3},{3,2},{4,5},{5,4},{6,7},{7,6},{8,9},{9,8},{10,11... | collective-permute-start | bytes 983048 | tf_op jit(solution)/shard_map/ppermute | solution.py:265
  5.6 31.9 %collective-permute-start.1 = (bf16[80,4096]{1,0:T(8,128)(2,1)S(1)}, bf16[80,4096]{1,0:T(8,128)(2,1)S(1)}, u32[]{:S(2)}, u32[]{:S(2)}) collective-permute-start(bf16[80,4096]{1,0:T(8,128)(2,1)S(1)} %get-tuple-element.35), channel_id=1, source_target_pairs={{0,2},{1,3},{2,0},{3,1},{4,6},{5,7},{6,4},{7,5},{8,10},{9,11},{10,... | collective-permute-start | bytes 1966088 | tf_op jit(solution)/shard_map/ppermute | solution.py:265
  8.2 31.8 %collective-permute-start.3 = (bf16[80,4096]{1,0:T(8,128)(2,1)S(1)}, bf16[80,4096]{1,0:T(8,128)(2,1)S(1)}, u32[]{:S(2)}, u32[]{:S(2)}) collective-permute-start(bf16[80,4096]{1,0:T(8,128)(2,1)S(1)} %get-tuple-element.37), channel_id=1, source_target_pairs={{0,4},{1,5},{2,6},{3,7},{4,0},{5,1},{6,2},{7,3},{8,12},{9,13},{10,... | collective-permute-start | bytes 1966088 | tf_op jit(solution)/shard_map/ppermute | solution.py:265
  10.8 2.8 %copy-start = (bf16[1,2048,1536]{2,1,0:T(8,128)(2,1)S(1)}, bf16[1,2048,1536]{2,1,0:T(8,128)(2,1)}, u32[]{:S(2)}) copy-start(bf16[1,2048,1536]{2,1,0:T(8,128)(2,1)} %param.10) | copy-start | bytes 18874372
  13.6 1.9 %copy-start.2 = (bf16[1,768,2048]{2,1,0:T(8,128)(2,1)S(1)}, bf16[1,768,2048]{2,1,0:T(8,128)(2,1)}, u32[]{:S(2)}) copy-start(bf16[1,768,2048]{2,1,0:T(8,128)(2,1)} %param.11) | copy-start | bytes 9437188
  15.5 26.2 %copy-start.1 = (bf16[1,2048,1536]{2,1,0:T(8,128)(2,1)S(1)}, bf16[1,2048,1536]{2,1,0:T(8,128)(2,1)}, u32[]{:S(2)}) copy-start(bf16[1,2048,1536]{2,1,0:T(8,128)(2,1)} %param.10) | copy-start | bytes 18874372
  15.5 26.2 %copy-start.3 = (bf16[1,768,2048]{2,1,0:T(8,128)(2,1)S(1)}, bf16[1,768,2048]{2,1,0:T(8,128)(2,1)}, u32[]{:S(2)}) copy-start(bf16[1,768,2048]{2,1,0:T(8,128)(2,1)} %param.11) | copy-start | bytes 9437188
  19.1 18.5 %collective-permute-start.4 = (bf16[1232,256]{1,0:T(8,128)(2,1)S(1)}, bf16[1232,256]{1,0:T(8,128)(2,1)S(1)}, u32[]{:S(2)}, u32[]{:S(2)}) collective-permute-start(bf16[1232,256]{1,0:T(8,128)(2,1)S(1)} %get-tuple-element.38), channel_id=1, source_target_pairs={{0,8},{8,0},{16,24},{24,16},{1,9},{9,1},{17,25},{25,17},{2,10},{10... | collective-permute-start | bytes 1892360 | tf_op jit(solution)/shard_map/ppermute | solution.py:265
  20.7 16.9 %collective-permute-start.5 = (bf16[1168,256]{1,0:T(8,128)(2,1)S(1)}, bf16[1168,256]{1,0:T(8,128)(2,1)S(1)}, u32[]{:S(2)}, u32[]{:S(2)}) collective-permute-start(bf16[1168,256]{1,0:T(8,128)(2,1)S(1)} %get-tuple-element.39), channel_id=1, source_target_pairs={{0,16},{8,24},{16,0},{24,8},{1,17},{9,25},{17,1},{25,9},{2,18},{10... | collective-permute-start | bytes 1794056 | tf_op jit(solution)/shard_map/ppermute | solution.py:265
  37.5 2.6 %collective-permute-start.2 = (bf16[40,4096]{1,0:T(8,128)(2,1)S(1)}, bf16[40,4096]{1,0:T(8,128)(2,1)S(1)}, u32[]{:S(2)}, u32[]{:S(2)}) collective-permute-start(bf16[40,4096]{1,0:T(8,128)(2,1)S(1)} %slice.31), channel_id=1, source_target_pairs={{0,1},{1,0},{2,3},{3,2},{4,5},{5,4},{6,7},{7,6},{8,9},{9,8},{10,11... | collective-permute-start | bytes 983048 | tf_op jit(solution)/shard_map/ppermute | solution.py:265
  40.1 1.7 %collective-permute-start.6 = (bf16[40,4096]{1,0:T(8,128)(2,1)S(1)}, bf16[40,4096]{1,0:T(8,128)(2,1)S(1)}, u32[]{:S(2)}, u32[]{:S(2)}) collective-permute-start(bf16[40,4096]{1,0:T(8,128)(2,1)S(1)} %slice.34), channel_id=1, source_target_pairs={{0,1},{1,0},{2,3},{3,2},{4,5},{5,4},{6,7},{7,6},{8,9},{9,8},{10,11... | collective-permute-start | bytes 983048 | tf_op jit(solution)/shard_map/ppermute | solution.py:265
  45.7 1.0 copy-start.12
  46.7 38.7 %collective-permute-start.11 = (bf16[2400,256]{1,0:T(8,128)(2,1)S(1)}, bf16[2400,256]{1,0:T(8,128)(2,1)S(1)}, u32[]{:S(2)}, u32[]{:S(2)}) collective-permute-start(bf16[2400,256]{1,0:T(8,128)(2,1)S(1)} %get-tuple-element.48), channel_id=1, source_target_pairs={{0,8},{8,0},{16,24},{24,16},{1,9},{9,1},{17,25},{25,17},{2,10},{10... | collective-permute-start | bytes 3686408 | tf_op jit(solution)/shard_map/ppermute | solution.py:265
  48.2 38.3 %collective-permute-start.12 = (bf16[2400,256]{1,0:T(8,128)(2,1)S(1)}, bf16[2400,256]{1,0:T(8,128)(2,1)S(1)}, u32[]{:S(2)}, u32[]{:S(2)}) collective-permute-start(bf16[2400,256]{1,0:T(8,128)(2,1)S(1)} %get-tuple-element.49), channel_id=1, source_target_pairs={{0,16},{8,24},{16,0},{24,8},{1,17},{9,25},{17,1},{25,9},{2,18},{10... | collective-permute-start | bytes 3686408 | tf_op jit(solution)/shard_map/ppermute | solution.py:265
  49.8 35.6 %collective-permute-start.7 = (bf16[80,4096]{1,0:T(8,128)(2,1)S(1)}, bf16[80,4096]{1,0:T(8,128)(2,1)S(1)}, u32[]{:S(2)}, u32[]{:S(2)}) collective-permute-start(bf16[80,4096]{1,0:T(8,128)(2,1)S(1)} %get-tuple-element.43), channel_id=1, source_target_pairs={{0,6},{1,7},{2,4},{3,5},{4,2},{5,3},{6,0},{7,1},{8,14},{9,15},{10,... | collective-permute-start | bytes 1966088 | tf_op jit(solution)/shard_map/ppermute | solution.py:265
  52.2 31.6 %collective-permute-start.8 = (bf16[624,256]{1,0:T(8,128)(2,1)S(1)}, bf16[624,256]{1,0:T(8,128)(2,1)S(1)}, u32[]{:S(2)}, u32[]{:S(2)}) collective-permute-start(bf16[624,256]{1,0:T(8,128)(2,1)S(1)} %slice.40), channel_id=1, source_target_pairs={{0,16},{8,24},{16,0},{24,8},{1,17},{9,25},{17,1},{25,9},{2,18},{10... | collective-permute-start | bytes 958472 | tf_op jit(solution)/shard_map/ppermute | solution.py:265
  52.7 27.6 %collective-permute-start.9 = (bf16[416,256]{1,0:T(8,128)(2,1)S(1)}, bf16[416,256]{1,0:T(8,128)(2,1)S(1)}, u32[]{:S(2)}, u32[]{:S(2)}) collective-permute-start(bf16[416,256]{1,0:T(8,128)(2,1)S(1)} %slice.41), channel_id=1, source_target_pairs={{0,8},{8,0},{16,24},{24,16},{1,9},{9,1},{17,25},{25,17},{2,10},{10... | collective-permute-start | bytes 638984 | tf_op jit(solution)/shard_map/ppermute | solution.py:265
  85.3 6.8 %copy-start.4 = (f32[768,512]{1,0:T(8,128)}, f32[768,512]{1,0:T(8,128)S(1)}, u32[]{:S(2)}) copy-start(f32[768,512]{1,0:T(8,128)S(1)} %get-tuple-element.46.refs_6_) | copy-start | bytes 4718596
  85.3 2.0 %collective-permute-start.10 = (bf16[40,4096]{1,0:T(8,128)(2,1)S(1)}, bf16[40,4096]{1,0:T(8,128)(2,1)S(1)}, u32[]{:S(2)}, u32[]{:S(2)}) collective-permute-start(bf16[40,4096]{1,0:T(8,128)(2,1)S(1)} %slice.35), channel_id=1, source_target_pairs={{0,1},{1,0},{2,3},{3,2},{4,5},{5,4},{6,7},{7,6},{8,9},{9,8},{10,11... | collective-permute-start | bytes 983048 | tf_op jit(solution)/shard_map/ppermute | solution.py:265
  85.4 6.7 %copy-start.8 = (bf16[2400,256]{1,0:T(8,128)(2,1)}, bf16[2400,256]{1,0:T(8,128)(2,1)S(1)}, u32[]{:S(2)}) copy-start(bf16[2400,256]{1,0:T(8,128)(2,1)S(1)} %collective-permute-done.11.refs_1_) | copy-start | bytes 3686404
  86.5 5.6 %copy-start.10 = (bf16[2400,256]{1,0:T(8,128)(2,1)}, bf16[2400,256]{1,0:T(8,128)(2,1)S(1)}, u32[]{:S(2)}) copy-start(bf16[2400,256]{1,0:T(8,128)(2,1)S(1)} %collective-permute-done.12.refs_2_) | copy-start | bytes 3686404
  92.1 0.8 copy-start.14
  92.9 19.8 %collective-permute-start.14 = (bf16[1232,256]{1,0:T(8,128)(2,1)}, bf16[1232,256]{1,0:T(8,128)(2,1)}, u32[]{:S(2)}, u32[]{:S(2)}) collective-permute-start(bf16[1232,256]{1,0:T(8,128)(2,1)} %get-tuple-element.53), channel_id=1, source_target_pairs={{0,16},{8,24},{16,0},{24,8},{1,17},{9,25},{17,1},{25,9},{2,18},{10... | collective-permute-start | bytes 1892360 | tf_op jit(solution)/shard_map/ppermute | solution.py:265
  94.5 16.7 %collective-permute-start.13 = (bf16[1168,256]{1,0:T(8,128)(2,1)}, bf16[1168,256]{1,0:T(8,128)(2,1)}, u32[]{:S(2)}, u32[]{:S(2)}) collective-permute-start(bf16[1168,256]{1,0:T(8,128)(2,1)} %get-tuple-element.52), channel_id=1, source_target_pairs={{0,8},{8,0},{16,24},{24,16},{1,9},{9,1},{17,25},{25,17},{2,10},{10... | collective-permute-start | bytes 1794056 | tf_op jit(solution)/shard_map/ppermute | solution.py:265
  95.0 26.1 %collective-permute-start.17 = (bf16[1040,256]{1,0:T(8,128)(2,1)}, bf16[1040,256]{1,0:T(8,128)(2,1)}, u32[]{:S(2)}, u32[]{:S(2)}) collective-permute-start(bf16[1040,256]{1,0:T(8,128)(2,1)} %slice.42), channel_id=1, source_target_pairs={{0,16},{8,24},{16,0},{24,8},{1,17},{9,25},{17,1},{25,9},{2,18},{10... | collective-permute-start | bytes 1597448 | tf_op jit(solution)/shard_map/ppermute | solution.py:265
  95.5 26.2 %collective-permute-start.18 = (bf16[1040,256]{1,0:T(8,128)(2,1)}, bf16[1040,256]{1,0:T(8,128)(2,1)}, u32[]{:S(2)}, u32[]{:S(2)}) collective-permute-start(bf16[1040,256]{1,0:T(8,128)(2,1)} %slice.43), channel_id=1, source_target_pairs={{0,8},{8,0},{16,24},{24,16},{1,9},{9,1},{17,25},{25,17},{2,10},{10... | collective-permute-start | bytes 1597448 | tf_op jit(solution)/shard_map/ppermute | solution.py:265
  115.3 17.7 %all-to-all-start = ((f32[8,1,40]{2,1,0:T(1,128)}), f32[8,1,40]{2,1,0:T(1,128)S(1)}, u32[]{:S(2)}, u32[]{:S(2)}) async-start(f32[8,1,40]{2,1,0:T(1,128)} %bitcast.5), calls=%async_computation | async-start | bytes 8192 | tf_op jit(solution)/shard_map/all_to_all | solution.py:269
  121.6 1.4 copy-start.5
  123.1 1.3 copy-start.9
  124.3 1.3 copy-start.11
  125.6 1.2 copy-start.13
  126.9 6.4 %copy-start.17 = (f32[128,2]{0,1:T(2,128)S(1)}, f32[128,2]{0,1:T(2,128)}, u32[]{:S(2)}) copy-start(f32[128,2]{0,1:T(2,128)} %param.8) | copy-start | bytes 3076
  130.3 1.1 copy-start.6
  131.4 6.7 %collective-permute-start.15 = (bf16[416,256]{1,0:T(8,128)(2,1)}, bf16[416,256]{1,0:T(8,128)(2,1)}, u32[]{:S(2)}, u32[]{:S(2)}) collective-permute-start(bf16[416,256]{1,0:T(8,128)(2,1)} %slice.44), channel_id=1, source_target_pairs={{0,16},{8,24},{16,0},{24,8},{1,17},{9,25},{17,1},{25,9},{2,18},{10... | collective-permute-start | bytes 638984 | tf_op jit(solution)/shard_map/ppermute | solution.py:265
  132.4 8.9 %collective-permute-start.16 = (bf16[624,256]{1,0:T(8,128)(2,1)}, bf16[624,256]{1,0:T(8,128)(2,1)S(1)}, u32[]{:S(2)}, u32[]{:S(2)}) collective-permute-start(bf16[624,256]{1,0:T(8,128)(2,1)} %slice.45), channel_id=1, source_target_pairs={{0,8},{8,0},{16,24},{24,16},{1,9},{9,1},{17,25},{25,17},{2,10},{10... | collective-permute-start | bytes 958472 | tf_op jit(solution)/shard_map/ppermute | solution.py:265
  141.3 1.4 copy-start.7
  142.7 1.0 copy-start.15

commit v3 on v2

--- a/solution.py
+++ b/solution.py
@@ -74,154 +74,163 @@
 def split_rows(count, top, half):
     blocks = 3 * half // TILE
     low = count - top
-    return blocks, low, (blocks + 4) * top, (blocks + 4) * low
-
-
-def expert_kernel(pairs, top, *refs):
-    row_refs, (gate_ref, up_ref, down_ref), rest = (
-        refs[: 2 * pairs],
-        refs[2 * pairs : 2 * pairs + 3],
-        refs[2 * pairs + 3 :],
-    )
-    own_ref, to_x, to_y, inner_ref, x_rows, s_rows, s_turned, total = rest
+    from_x, from_y = (blocks + 4) * top, (blocks + 4) * low
+    sizes = (from_x + blocks * low + 4 * count, from_y + blocks * top + 4 * count)
+    return blocks, low, from_x, from_y, sizes
+
+
+def expert_kernel(pairs, top, relays, *refs):
+    row_refs, refs = refs[: 2 * pairs], refs[2 * pairs :]
+    (gu_hbm, down_hbm), refs = refs[:2], refs[2:]
+    relay_refs, refs = refs[: len(relays)], refs[len(relays) :]
+    own_ref, to_x, to_y, inner_ref, gu_tiles, down_tiles, x_rows, s_turned, sems = refs
     count = pairs * PAIR
-    width = gate_ref.shape[0]
-    steps = pl.num_programs(0)
-    half = TILE * 3
+    width, both = gu_hbm.shape
+    half = both // 2
     quarter = width // 4
-    blocks, low, from_x, from_y = split_rows(count, top, half)
-    step = pl.program_id(0)
+    steps = half // TILE
+    blocks, low, from_x, from_y, sizes = split_rows(count, top, half)
     group = lax.axis_index("dp")
-
-    @pl.when(step == 0)
-    def _():
-        for rows, start in ((x_rows, 0), (s_rows, width)):
-            rows[...] = jnp.concatenate(
-                [ref[:CAP, start : start + width].astype(F32) for ref in row_refs],
-                axis=0,
-            ).astype(BF16)
-        for q in range(4):
-            rows = (x_rows, s_rows)[q // 2]
-
-            def cut(mask):
-                at = jnp.bitwise_xor(group, mask) * quarter + q % 2 * TILE
-                return rows[:, pl.ds(pl.multiple_of(at, TILE), TILE)]
-
-            at = blocks + q
-            own_ref[at * count : (at + 1) * count] = cut(0)
-            far = cut(3)
-            to_x[at * top : (at + 1) * top] = far[:top]
-            to_y[at * low : (at + 1) * low] = far[top:]
-            start = from_x + blocks * low + q * count
-            to_x[start : start + count] = cut(1)
-            start = from_y + blocks * top + q * count
-            to_y[start : start + count] = cut(2)
-        s_turned[...] = s_rows[...].T
-        total[...] = jnp.zeros_like(total)
-
-    x = x_rows[...]
-    gate = jnp.dot(x, gate_ref[...], preferred_element_type=F32)
-    up = jnp.dot(x, up_ref[...], preferred_element_type=F32)
-    grad_hidden = jnp.dot(down_ref[...], s_turned[...], preferred_element_type=F32).T
-    sigmoid = 1.0 / (1.0 + jnp.exp(-gate))
-    activated = gate * sigmoid
-    hidden = (activated * up).astype(BF16)
-    grad_gate = (grad_hidden * up * sigmoid * (1.0 + gate * (1.0 - sigmoid))).astype(BF16)
-    grad_up = (grad_hidden * activated).astype(BF16)
-    total[...] += jnp.sum(hidden.astype(F32) * grad_hidden, axis=1, keepdims=True)
-    for part, values in enumerate((grad_gate, grad_up, hidden)):
-        block = part * steps + step
-
-        def rows_at(start, count):
-            return pl.ds(pl.multiple_of(start + block * count, 16), count)
-
-        own_ref[rows_at(0, count)] = values
-        to_x[rows_at(0, top)] = values[:top]
-        to_x[rows_at(from_x, low)] = values[top:]
-        to_y[rows_at(0, low)] = values[top:]
-        to_y[rows_at(from_y, top)] = values[:top]
-
-    @pl.when(step == steps - 1)
-    def _():
-        inner_ref[...] = jnp.broadcast_to(total[...], (count, 128)).T[0:1]
-
-
-def expert_rows(rows, weight_gu, weight_down, top):
-    count = len(rows) // 2 * PAIR
+    copies = []
+    for step in range(steps):
+        for n, at in enumerate((step * TILE, half + step * TILE)):
+            copies.append(
+                pltpu.make_async_copy(
+                    gu_hbm.at[:, at : at + TILE], gu_tiles.at[2 * step + n], sems.at[3 * step + n]
+                )
+            )
+        copies.append(
+            pltpu.make_async_copy(
+                down_hbm.at[step * TILE : (step + 1) * TILE, :],
+                down_tiles.at[step],
+                sems.at[3 * step + 2],
+            )
+        )
+    for copy in copies:
+        copy.start()
+    for ref, relay, rows, at in zip((to_x, to_y), relay_refs, relays, sizes):
+        ref[at : at + rows] = relay[:rows]
+
+    for n, start in enumerate((0, width)):
+        x_rows[n] = jnp.concatenate(
+            [ref[:CAP, start : start + width].astype(F32) for ref in row_refs], axis=0
+        ).astype(BF16)
+    s_turned[...] = x_rows[1].T
+    for q in range(4):
+
+        def cut(mask):
+            at = jnp.bitwise_xor(group, mask) * quarter + q % 2 * TILE
+            return x_rows[q // 2, :, pl.ds(pl.multiple_of(at, TILE), TILE)]
+
+        at = blocks + q
+        own_ref[at * count : (at + 1) * count] = cut(0)
+        far = cut(3)
+        to_x[at * top : (at + 1) * top] = far[:top]
+        to_y[at * low : (at + 1) * low] = far[top:]
+        start = from_x + blocks * low + q * count
+        to_x[start : start + count] = cut(1)
+        start = from_y + blocks * top + q * count
+        to_y[start : start + count] = cut(2)
+
+    total = jnp.zeros((count, 1), F32)
+    for step in range(steps):
+        for copy in copies[3 * step : 3 * step + 3]:
+            copy.wait()
+        x = x_rows[0]
+        gate = jnp.dot(x, gu_tiles[2 * step], preferred_element_type=F32)
+        up = jnp.dot(x, gu_tiles[2 * step + 1], preferred_element_type=F32)
+        grad_hidden = jnp.dot(down_tiles[step], s_turned[...], preferred_element_type=F32).T
+        sigmoid = 1.0 / (1.0 + jnp.exp(-gate))
+        activated = gate * sigmoid
+        hidden = (activated * up).astype(BF16)
+        grad_gate = (grad_hidden * up * sigmoid * (1.0 + gate * (1.0 - sigmoid))).astype(BF16)
+        grad_up = (grad_hidden * activated).astype(BF16)
+        total += jnp.sum(hidden.astype(F32) * grad_hidden, axis=1, keepdims=True)
+        for part, values in enumerate((grad_gate, grad_up, hidden)):
+            block = part * steps + step
+            own_ref[block * count : (block + 1) * count] = values
+            to_x[block * top : (block + 1) * top] = values[:top]
+            to_x[from_x + block * low : from_x + (block + 1) * low] = values[top:]
+            to_y[block * low : (block + 1) * low] = values[top:]
+            to_y[from_y + block * top : from_y + (block + 1) * top] = values[:top]
+    inner_ref[...] = jnp.broadcast_to(total, (count, 128)).T[0:1]
+
+
+def expert_rows(rows, weight_gu, weight_down, top, relay=(), relays=(), room=26):
+    pairs = len(rows) // 2
+    count = pairs * PAIR
     width, both = weight_gu.shape
     half = both // 2
     steps = half // TILE
-    blocks, low, from_x, from_y = split_rows(count, top, half)
-    shapes = [
-        ((blocks + 4) * count, TILE),
-        (from_x + blocks * low + 4 * count, TILE),
-        (from_y + blocks * top + 4 * count, TILE),
+    blocks, _, _, _, sizes = split_rows(count, top, half)
+    sizes = [(blocks + 4) * count] + [
+        size + extra for size, extra in zip(sizes, relays or (0, 0))
     ]
-
-    def whole(shape):
-        return pl.BlockSpec(shape, lambda h: (0, 0))
-
+    vmem = pl.BlockSpec(memory_space=pltpu.VMEM)
+    hbm = pl.BlockSpec(memory_space=pl.ANY)
     return pl.pallas_call(
-        functools.partial(expert_kernel, len(rows) // 2, top),
-        grid=(steps,),
-        in_specs=[
-            *[whole(part.shape) for part in rows],
-            pl.BlockSpec((width, TILE), lambda h: (0, h)),
-            pl.BlockSpec((width, TILE), lambda h: (0, h + steps)),
-            pl.BlockSpec((TILE, width), lambda h: (h, 0)),
-        ],
-        out_specs=[whole(shape) for shape in shapes] + [whole((1, count))],
-        out_shape=[jax.ShapeDtypeStruct(shape, BF16) for shape in shapes]
+        functools.partial(expert_kernel, pairs, top, tuple(relays)),
+        in_specs=[vmem] * len(rows) + [hbm] * 2 + [vmem] * len(relay),
+        out_specs=[vmem] * 4,
+        out_shape=[jax.ShapeDtypeStruct((size, TILE), BF16) for size in sizes]
         + [jax.ShapeDtypeStruct((1, count), F32)],
         scratch_shapes=[
-            pltpu.VMEM((count, width), BF16),
-            pltpu.VMEM((count, width), BF16),
+            pltpu.VMEM((2 * steps, width, TILE), BF16),
+            pltpu.VMEM((steps, TILE, width), BF16),
+            pltpu.VMEM((2, count, width), BF16),
             pltpu.VMEM((width, count), BF16),
-            pltpu.VMEM((count, 1), F32),
+            pltpu.SemaphoreType.DMA((3 * steps,)),
         ],
-        compiler_params=pltpu.CompilerParams(vmem_limit_bytes=20 * MIB),
+        compiler_params=pltpu.CompilerParams(vmem_limit_bytes=room * MIB),
         cost_estimate=pl.CostEstimate(flops=1_000, bytes_accessed=1_000, transcendentals=0),
         name="expert_rows",
-    )(*rows, weight_gu, weight_gu, weight_down)
-
-
-def gradient_kernel(top, half, adding, *refs):
-    (own, got_x, got_y, far_top, far_low), refs = refs[:5], refs[5:]
-    count = own.shape[0] // (3 * half // TILE + 4)
-    blocks, low, from_x, from_y = split_rows(count, top, half)
+    )(*rows, weight_gu, weight_down, *relay)
+
+
+def gradient_kernel(chunks, half, adding, *refs):
+    groups, refs = (
+        [refs[5 * n : 5 * n + 5] for n in range(len(chunks))],
+        refs[5 * len(chunks) :],
+    )
     if adding:
         (acc_gu, acc_down), refs = refs[:2], refs[2:]
     out_gu, out_down, turned, s_rows = refs
     both = 2 * half // TILE
 
+    def far_parts(block, top, low, at_top, at_low, far_top, far_low):
+        return [
+            far_top[at_top + block * top : at_top + (block + 1) * top],
+            far_low[at_low + block * low : at_low + (block + 1) * low],
+        ]
+
     def factor(block):
-        return jnp.concatenate(
-            [
+        parts = []
+        for (count, top, at_top, at_low), group in zip(chunks, groups):
+            own, got_x, got_y, *far = group
+            _, low, from_x, from_y, _ = split_rows(count, top, half)
+            parts += [
                 own[block * count : (block + 1) * count],
                 got_x[block * top : (block + 1) * top],
                 got_x[from_x + block * low : from_x + (block + 1) * low],
                 got_y[from_y + block * top : from_y + (block + 1) * top],
                 got_y[block * low : (block + 1) * low],
-                far_top[block * top : (block + 1) * top],
-                far_low[block * low : (block + 1) * low],
-            ],
-            axis=0,
-        )
+            ] + far_parts(block, top, low, at_top, at_low, *far)
+        return jnp.concatenate(parts, axis=0)
 
     def piece(q):
-        block = blocks + q
-        at_x = from_x + blocks * low + q * count
-        at_y = from_y + blocks * top + q * count
-        return jnp.concatenate(
-            [
+        parts = []
+        for (count, top, at_top, at_low), group in zip(chunks, groups):
+            own, got_x, got_y, *far = group
+            blocks, low, from_x, from_y, _ = split_rows(count, top, half)
+            block = blocks + q
+            at_x = from_x + blocks * low + q * count
+            at_y = from_y + blocks * top + q * count
+            parts += [
                 own[block * count : (block + 1) * count],
                 got_x[at_x : at_x + count],
                 got_y[at_y : at_y + count],
-                far_top[block * top : (block + 1) * top],
-                far_low[block * low : (block + 1) * low],
-            ],
-            axis=0,
-        )
+            ] + far_parts(block, top, low, at_top, at_low, *far)
+        return jnp.concatenate(parts, axis=0)
 
     for q in range(2):
         turned[q * TILE : (q + 1) * TILE, :] = piece(q).T
@@ -240,21 +249,20 @@
         out_down[at, :] = grad.astype(out_down.dtype)
 
 
-def gradients(top, pieces, half, quarter, sums=(), final=False):
+def gradients(chunks, pieces, half, quarter, sums=(), final=False):
     kept = BF16 if final else F32
-    rows = 4 * pieces[0].shape[0] // (3 * half // TILE + 4)
+    rows = 4 * sum(chunk[0] for chunk in chunks)
     vmem = pl.BlockSpec(memory_space=pltpu.VMEM)
     return pl.pallas_call(
-        functools.partial(gradient_kernel, top, half, len(sums)),
+        functools.partial(gradient_kernel, chunks, half, len(sums)),
         in_specs=[vmem] * (len(pieces) + len(sums)),
         out_specs=[vmem] * 2,
         out_shape=[
             jax.ShapeDtypeStruct((quarter, 2 * half), kept),
             jax.ShapeDtypeStruct((half, quarter), kept),
         ],
-        input_output_aliases={} if final or not sums else {len(pieces): 0, len(pieces) + 1: 1},
         scratch_shapes=[pltpu.VMEM((quarter, rows), BF16), pltpu.VMEM((rows, quarter), BF16)],
-        compiler_params=pltpu.CompilerParams(vmem_limit_bytes=14 * MIB),
+        compiler_params=pltpu.CompilerParams(vmem_limit_bytes=20 * MIB),
         cost_estimate=pl.CostEstimate(flops=1_000, bytes_accessed=1_000, transcendentals=0),
         name="gradients",
     )(*pieces, *sums)
@@ -279,44 +287,62 @@
     quarter = tokens.shape[1] // 4
     ids, probs = expert_ids.T, gate_probs.T
     *local, slots = dispatch_rows(ids, probs, tokens, cotangent)
-    tops = (48, PAIR, 32)
-    inner, pieces, forwards = [], [], []
+    weights = (gate_up[0], down[0])
+    _, _, cut_x0, cut_y0, _ = split_rows(PAIR, 48, half)
+    _, _, cut_x1, cut_y1, sizes = split_rows(2 * PAIR, PAIR, half)
+    _, _, cut_x2, cut_y2, _ = split_rows(PAIR, 32, half)
 
     def other_core(rows):
         return exchange(rows[CAP:], "expert", 1)
 
-    def compute(*rows):
-        top = tops[len(inner)]
-        own, to_x, to_y, found = expert_rows(rows, gate_up[0], down[0], top)
-        inner.append(found)
-        _, _, from_x, from_y = split_rows(len(rows) // 2 * PAIR, top, half)
-        got_x, got_y = exchange(to_x, "dp", 1), exchange(to_y, "dp", 2)
-        forward = (got_x[:from_x], got_y[:from_y])
-        far_top, far_low = exchange(forward[0], "dp", 2), exchange(forward[1], "dp", 1)
-        forwards.append(forward)
-        pieces.append([own, got_x, got_y, far_top, far_low])
-
-    def add(chunk, sums=()):
-        return gradients(tops[chunk], pieces[chunk], half, quarter, sums, chunk == len(tops) - 1)
+    def to_plane(to_x, to_y):
+        return exchange(to_x, "dp", 1), exchange(to_y, "dp", 2)
 
     rows_1 = exchange(local[1], "expert", 2)
     rows_2 = exchange(local[2], "expert", 4)
-    compute(local[0], other_core(local[0]))
-    rows_1 = after(rows_1, inner[0])
-    other_1 = other_core(rows_1)
+    own_0, to_x, to_y, inner_0 = expert_rows(
+        (local[0], other_core(local[0])), *weights, 48, room=58
+    )
+    got_x0, got_y0 = to_plane(to_x, to_y)
+    rows_1 = after(rows_1, inner_0)
     rows_3 = exchange(after(local[3], rows_2), "expert", 6)
-    rows_2 = after(rows_2, *forwards[0])
-    compute(rows_1, other_1, rows_2, other_core(rows_2))
-    sums = add(0)
-    rows_3 = after(rows_3, inner[1], *sums)
-    compute(rows_3, after(other_core(rows_3), *forwards[1]))
-    sums = add(1, sums)
-    grad_gu, grad_down = add(2, sums)
+    rows_2 = after(rows_2, inner_0)
+    own_1, to_x, to_y, inner_1 = expert_rows(
+        (rows_1, other_core(rows_1), rows_2, other_core(rows_2)),
+        *weights,
+        PAIR,
+        (got_y0, got_x0),
+        (cut_y0, cut_x0),
+    )
+    got_x1, got_y1 = to_plane(to_x, to_y)
+    rows_3 = after(rows_3, inner_1)
+    own_2, to_x, to_y, inner_2 = expert_rows((rows_3, other_core(rows_3)), *weights, 32)
+    got_x2, got_y2 = to_plane(to_x, to_y)
+    got_x1, got_y1 = after((got_x1, got_y1), inner_2)
+    turn_1 = (got_y1[:cut_y1], got_x1[:cut_x1])
+    low_1, top_1 = to_plane(*turn_1)
+    sums = gradients(
+        ((PAIR, 48, sizes[1], sizes[0]),),
+        (own_0, got_x0, got_y0, got_y1, got_x1),
+        half,
+        quarter,
+    )
     numbers = jnp.arange(EXPERTS, dtype=jnp.int32)
     mine = (numbers[:, None] == jnp.bitwise_xor(numbers, me)[None, :])[:, :, None]
-    rows_inner = after(jnp.concatenate(inner, axis=1), *forwards[2]).reshape(EXPERTS, CAP)
-    sent = jnp.sum(jnp.where(mine, rows_inner[None], 0.0), axis=1)
-    returned = jnp.sum(jnp.where(mine, swap(sent)[None], 0.0), axis=1).reshape(-1)
+    inner = jnp.concatenate([inner_0, inner_1, inner_2], axis=1)
+    rows_inner = after(inner, *turn_1).reshape(EXPERTS, CAP)
+    returned = swap(jnp.sum(jnp.where(mine, rows_inner[None], 0.0), axis=1))
+    got_x2, got_y2 = after((got_x2, got_y2), returned, *sums)
+    low_2, top_2 = to_plane(got_y2[:cut_y2], got_x2[:cut_x2])
+    grad_gu, grad_down = gradients(
+        ((2 * PAIR, PAIR, 0, 0), (PAIR, 32, 0, 0)),
+        (own_1, got_x1, got_y1, top_1, low_1, own_2, got_x2, got_y2, top_2, low_2),
+        half,
+        quarter,
+        sums,
+        True,
+    )
+    returned = jnp.sum(jnp.where(mine, returned[None], 0.0), axis=1).reshape(-1)
     chosen = slots[:, None, :] == jnp.arange(EXPERTS * CAP, dtype=jnp.int32)[None, :, None]
     grad_probs = jnp.sum(jnp.where(chosen, returned[None, :, None], 0.0), axis=1) / probs
     return (grad_probs.T, grad_gu[None], grad_down[None])

time: 148 us -> 135 us (0.912)
  the two profiles are of different devices: /device:TPU:0 before, /device:TPU:12 now
where the time goes in v3:
time: 135 us; the launch traced here: 134 us
  waiting for transfers between devices  61 us (45%)
  Pallas kernels  27.2 us (20%)
  local copies, waits for them, and re-layouts  25.5 us (19%)
  starting transfers between devices  18.1 us (13%)
  other arithmetic  1.58 us (1%)
    ppermute x17, waiting for transfers between devices, exchange(): return lax.ppermute(values, axis, [(n, n ^ mask) for n in range(size)])  61 us
    unnamed x48, local copies, waits for them, and re-layouts  20.3 us
    pallas_call x3, Pallas kernels, expert_rows(): pl.pallas_call(functools.partial(expert_kernel, pairs, top, tuple(relays)...  18.4 us
    ppermute x17, starting transfers between devices, exchange(): return lax.ppermute(values, axis, [(n, n ^ mask) for n in range(size)])  14.6 us
    pallas_call x2, Pallas kernels, gradients(): pl.pallas_call(functools.partial(gradient_kernel, chunks, half, len(sums)...  6.76 us
    all_to_all x1, starting transfers between devices, swap(): lax.all_to_all(values, 'expert', split_axis=0, concat_axis=0, tiled=True)  3.46 us
    slice x2, local copies, waits for them, and re-layouts, plane_body(): low_2, top_2 = to_plane(got_y2[:cut_y2], got_x2[:cut_x2])  3.34 us
  transfers between devices with their start and end apart: 18, of which 10 were waited for; matrix products, arithmetic and copies ran while one was open for 5% of the time, Pallas kernels for 11%

profile of v3, /device:TPU:12, one launch (start us, length us, event | category | flops | bytes accessed | tf_op | source)
XLA Modules:
  0.0 134.2 jit_solution(7902412837822810455)
XLA Ops:
  0.6 0.0 copy-start.17
  0.6 0.7 copy-done.17
  1.3 1.0 copy-done.19
  2.4 1.0 copy-done.20
  3.4 0.7 copy-done.21
  4.1 2.0 %dispatch_rows.1 = (bf16[80,4096]{1,0:T(8,128)(2,1)S(1)}, bf16[80,4096]{1,0:T(8,128)(2,1)S(1)}, bf16[80,4096]{1,0:T(8,128)(2,1)}, bf16[80,4096]{1,0:T(8,128)(2,1)}, s32[2,128]{1,0:T(2,128)S(1)}) custom-call(s32[2,128]{1,0:T(2,128)S(1)} %bitcast.19, f32[2,128]{1,0:T(2,128)S(1)} %bitcast.18, bf16[128,2048]{1,0:T(8,128)(2,1)S(1)} %copy-done.19, ...), custom_call_target="tpu_custom_call" | custom-call | flops 335544320 | bytes 4000000 | tf_op jit(solution)/shard_map/dispatch_rows/pallas_call | solution.py:62
  6.1 2.6 %collective-permute-start.3 = (bf16[80,4096]{1,0:T(8,128)(2,1)}, bf16[80,4096]{1,0:T(8,128)(2,1)S(1)}, u32[]{:S(2)}, u32[]{:S(2)}) collective-permute-start(bf16[80,4096]{1,0:T(8,128)(2,1)} %get-tuple-element.38), channel_id=1, source_target_pairs={{0,4},{1,5},{2,6},{3,7},{4,0},{5,1},{6,2},{7,3},{8,12},{9,13},{10,... | collective-permute-start | bytes 1966088 | tf_op jit(solution)/shard_map/ppermute | solution.py:273
  8.6 0.4 collective-permute-start.1
  9.1 0.1 collective-permute-start
  9.2 1.6 %collective-permute-done.refs_1_ = bf16[40,4096]{1,0:T(8,128)(2,1)S(1)} collective-permute-done((bf16[40,4096]{1,0:T(8,128)(2,1)S(1)}, bf16[40,4096]{1,0:T(8,128)(2,1)S(1)}, u32[]{:S(2)}, u32[]{:S(2)}) %collective-permute-start) | collective-permute-done | bytes 327712 | tf_op jit(solution)/shard_map/ppermute | solution.py:273
  10.8 0.7 copy-done.22
  11.6 8.0 %expert_rows.3 = (bf16[1040,256]{1,0:T(8,128)(2,1)}, bf16[1232,256]{1,0:T(8,128)(2,1)}, bf16[1168,256]{1,0:T(8,128)(2,1)}, f32[1,80]{1,0:T(1,128)}) custom-call(bf16[80,4096]{1,0:T(8,128)(2,1)} %copy-done.11, bf16[40,4096]{1,0:T(8,128)(2,1)} %copy-done.22, bf16[2048,1536]{1,0:T(8,128)(2,1)} %bitcast.12, bf16[768,2048]{1,0:T(8,128)(2,1)} %bitcast.15), custom_call_target="tpu_custom_call" | custom-call | flops 1000 | bytes 1000 | tf_op jit(solution)/shard_map/expert_rows/pallas_call | solution.py:171
  19.6 1.6 %collective-permute-start.6 = (bf16[1232,256]{1,0:T(8,128)(2,1)}, bf16[1232,256]{1,0:T(8,128)(2,1)S(1)}, u32[]{:S(2)}, u32[]{:S(2)}) collective-permute-start(bf16[1232,256]{1,0:T(8,128)(2,1)} %get-tuple-element.41), channel_id=1, source_target_pairs={{0,8},{8,0},{16,24},{24,16},{1,9},{9,1},{17,25},{25,17},{2,10},{10... | collective-permute-start | bytes 1892360 | tf_op jit(solution)/shard_map/ppermute | solution.py:273
  21.1 0.5 collective-permute-start.5
  21.7 15.2 %collective-permute-done.3.refs_2_ = bf16[80,4096]{1,0:T(8,128)(2,1)S(1)} collective-permute-done((bf16[80,4096]{1,0:T(8,128)(2,1)}, bf16[80,4096]{1,0:T(8,128)(2,1)S(1)}, u32[]{:S(2)}, u32[]{:S(2)}) %collective-permute-start.3) | collective-permute-done | bytes 655392 | tf_op jit(solution)/shard_map/ppermute | solution.py:273
  36.9 1.0 collective-permute-done.1.refs_0_
  37.9 0.1 collective-permute-start.4
  38.0 0.5 collective-permute-start.2
  38.5 1.1 collective-permute-done.4.refs_3_
  39.6 0.5 collective-permute-done.2.refs_1_
  40.1 2.8 %copy-done = bf16[1,2048,1536]{2,1,0:T(8,128)(2,1)S(1)} copy-done((bf16[1,2048,1536]{2,1,0:T(8,128)(2,1)S(1)}, bf16[1,2048,1536]{2,1,0:T(8,128)(2,1)}, u32[]{:S(2)}) %copy-start) | copy-done | bytes 6291480
  42.9 5.7 %expert_rows.4 = (bf16[2080,256]{1,0:T(8,128)(2,1)S(1)}, bf16[2816,256]{1,0:T(8,128)(2,1)}, bf16[3024,256]{1,0:T(8,128)(2,1)}, f32[1,160]{1,0:T(1,128)S(1)}) custom-call(bf16[80,4096]{1,0:T(8,128)(2,1)S(1)} %collective-permute-done.1.refs_0_, bf16[40,4096]{1,0:T(8,128)(2,1)S(1)} %collective-permute-done.2.refs_1_, ...), custom_call_target="tpu_custom_call" | custom-call | flops 1000 | bytes 1000 | tf_op jit(solution)/shard_map/expert_rows/pallas_call | solution.py:171
  48.6 1.0 copy-done.12
  49.6 0.5 collective-permute-start.10
  50.1 0.4 collective-permute-start.7
  50.5 1.5 %collective-permute-start.9 = (bf16[2816,256]{1,0:T(8,128)(2,1)}, bf16[2816,256]{1,0:T(8,128)(2,1)S(1)}, u32[]{:S(2)}, u32[]{:S(2)}) collective-permute-start(bf16[2816,256]{1,0:T(8,128)(2,1)} %get-tuple-element.47), channel_id=1, source_target_pairs={{0,8},{8,0},{16,24},{24,16},{1,9},{9,1},{17,25},{25,17},{2,10},{10... | collective-permute-start | bytes 4325384 | tf_op jit(solution)/shard_map/ppermute | solution.py:273
  52.0 28.8 %collective-permute-done.7.refs_0_ = bf16[80,4096]{1,0:T(8,128)(2,1)S(1)} collective-permute-done((bf16[80,4096]{1,0:T(8,128)(2,1)}, bf16[80,4096]{1,0:T(8,128)(2,1)S(1)}, u32[]{:S(2)}, u32[]{:S(2)}) %collective-permute-start.7) | collective-permute-done | bytes 655392 | tf_op jit(solution)/shard_map/ppermute | solution.py:273
  80.8 0.0 copy-start.23
  80.9 0.1 collective-permute-start.8
  80.9 1.6 %collective-permute-done.8.refs_1_ = bf16[40,4096]{1,0:T(8,128)(2,1)S(1)} collective-permute-done((bf16[40,4096]{1,0:T(8,128)(2,1)S(1)}, bf16[40,4096]{1,0:T(8,128)(2,1)S(1)}, u32[]{:S(2)}, u32[]{:S(2)}) %collective-permute-start.8) | collective-permute-done | bytes 327712 | tf_op jit(solution)/shard_map/ppermute | solution.py:273
  82.6 4.7 %expert_rows.5 = (bf16[1040,256]{1,0:T(8,128)(2,1)S(1)}, bf16[1168,256]{1,0:T(8,128)(2,1)}, bf16[1232,256]{1,0:T(8,128)(2,1)}, f32[1,80]{1,0:T(1,128)S(1)}) custom-call(bf16[80,4096]{1,0:T(8,128)(2,1)S(1)} %collective-permute-done.7.refs_0_, bf16[40,4096]{1,0:T(8,128)(2,1)S(1)} %collective-permute-done.8.refs_1_, bf16[2048,1536]{1,0:T(8,128)(2,1)S(1)} %bitcast.14, ...), custom_call_target="tpu_custom_call" | custom-call | flops 1000 | bytes 1000 | tf_op jit(solution)/shard_map/expert_rows/pallas_call | solution.py:171
  87.3 0.8 copy-done.15
  88.1 1.5 %collective-permute-start.14 = (bf16[1232,256]{1,0:T(8,128)(2,1)}, bf16[1232,256]{1,0:T(8,128)(2,1)}, u32[]{:S(2)}, u32[]{:S(2)}) collective-permute-start(bf16[1232,256]{1,0:T(8,128)(2,1)} %get-tuple-element.55), channel_id=1, source_target_pairs={{0,16},{8,24},{16,0},{24,8},{1,17},{9,25},{17,1},{25,9},{2,18},{10... | collective-permute-start | bytes 1892360 | tf_op jit(solution)/shard_map/ppermute | solution.py:273
  89.6 1.5 %collective-permute-start.13 = (bf16[1168,256]{1,0:T(8,128)(2,1)}, bf16[1168,256]{1,0:T(8,128)(2,1)}, u32[]{:S(2)}, u32[]{:S(2)}) collective-permute-start(bf16[1168,256]{1,0:T(8,128)(2,1)} %get-tuple-element.54), channel_id=1, source_target_pairs={{0,8},{8,0},{16,24},{24,16},{1,9},{9,1},{17,25},{25,17},{2,10},{10... | collective-permute-start | bytes 1794056 | tf_op jit(solution)/shard_map/ppermute | solution.py:273
  91.1 0.1 pad_maximum_fusion
  91.2 0.8 slice.28
  92.0 0.8 slice.29
  92.8 0.5 collective-permute-start.11
  93.3 0.5 collective-permute-start.12
  93.9 0.1 broadcast_in_dim.60
  94.0 0.7 select_reduce_fusion.2
  94.7 3.5 %all-to-all-start = ((f32[8,1,40]{2,1,0:T(1,128)}), f32[8,1,40]{2,1,0:T(1,128)S(1)}, u32[]{:S(2)}, u32[]{:S(2)}) async-start(f32[8,1,40]{2,1,0:T(1,128)} %bitcast.5), calls=%async_computation | async-start | bytes 8192 | tf_op jit(solution)/shard_map/all_to_all | solution.py:277
  98.1 1.1 copy-done.6
  99.2 1.1 copy-done.8
  100.3 1.0 copy-done.14
  101.3 1.4 %gradients.2 = (f32[512,1536]{1,0:T(8,128)S(1)}, f32[768,512]{1,0:T(8,128)S(1)}) custom-call(bf16[1040,256]{1,0:T(8,128)(2,1)S(1)} %copy-done.14, bf16[1232,256]{1,0:T(8,128)(2,1)S(1)} %copy-done.6, bf16[1168,256]{1,0:T(8,128)(2,1)S(1)} %copy-done.8, bf16[3024,256]{1,0:T(8,128)(2,1)S(1)} %collective-permute-done.10.refs_3_.refs_2_, ...), custom_call_target="tpu_custom_call" | custom-call | flops 1000 | bytes 1000 | tf_op jit(solution)/shard_map/gradients/pallas_call | solution.py:256
  102.8 1.6 %copy-done.3 = f32[512,1536]{1,0:T(8,128)} copy-done((f32[512,1536]{1,0:T(8,128)}, f32[512,1536]{1,0:T(8,128)S(1)}, u32[]{:S(2)}) %copy-start.3) | copy-done | bytes 3145752
  104.4 1.1 copy-done.9
  105.6 0.7 collective-permute-done.13.refs_6_
  106.3 1.6 %slice.30 = bf16[416,256]{1,0:T(8,128)(2,1)} slice(bf16[1168,256]{1,0:T(8,128)(2,1)} %collective-permute-done.13.refs_6_), slice={[0:416], [0:256]} | slice | bytes 425984 | tf_op jit(solution)/shard_map/slice | solution.py:336
  107.9 0.8 collective-permute-start.15
  108.7 1.7 %slice.31 = bf16[624,256]{1,0:T(8,128)(2,1)} slice(bf16[1232,256]{1,0:T(8,128)(2,1)} %collective-permute-done.14.refs_7_), slice={[0:624], [0:256]} | slice | bytes 638976 | tf_op jit(solution)/shard_map/slice | solution.py:336
  110.4 1.5 %collective-permute-start.16 = (bf16[624,256]{1,0:T(8,128)(2,1)}, bf16[624,256]{1,0:T(8,128)(2,1)S(1)}, u32[]{:S(2)}, u32[]{:S(2)}) collective-permute-start(bf16[624,256]{1,0:T(8,128)(2,1)} %slice.31), channel_id=1, source_target_pairs={{0,8},{8,0},{16,24},{24,16},{1,9},{9,1},{17,25},{25,17},{2,10},{10... | collective-permute-start | bytes 958472 | tf_op jit(solution)/shard_map/ppermute | solution.py:273
  111.9 0.1 select_reduce_fusion.1
  112.0 0.1 broadcast_in_dim.65
  112.1 0.1 select_reduce_fusion
  112.2 0.6 bitcast_divide_fusion
  112.8 7.8 %collective-permute-done.15.refs_8_ = bf16[416,256]{1,0:T(8,128)(2,1)} collective-permute-done((bf16[416,256]{1,0:T(8,128)(2,1)}, bf16[416,256]{1,0:T(8,128)(2,1)}, u32[]{:S(2)}, u32[]{:S(2)}) %collective-permute-start.15) | collective-permute-done | bytes 213024 | tf_op jit(solution)/shard_map/ppermute | solution.py:273
  120.6 2.7 %collective-permute-done.16.refs_9_ = bf16[624,256]{1,0:T(8,128)(2,1)S(1)} collective-permute-done((bf16[624,256]{1,0:T(8,128)(2,1)}, bf16[624,256]{1,0:T(8,128)(2,1)S(1)}, u32[]{:S(2)}, u32[]{:S(2)}) %collective-permute-start.16) | collective-permute-done | bytes 319520 | tf_op jit(solution)/shard_map/ppermute | solution.py:273
  123.3 1.9 %copy-done.4 = f32[512,1536]{1,0:T(8,128)S(1)} copy-done((f32[512,1536]{1,0:T(8,128)S(1)}, f32[512,1536]{1,0:T(8,128)}, u32[]{:S(2)}) %copy-start.4) | copy-done | bytes 3145752
  125.2 1.4 %copy-done.10 = f32[768,512]{1,0:T(8,128)S(1)} copy-done((f32[768,512]{1,0:T(8,128)S(1)}, f32[768,512]{1,0:T(8,128)}, u32[]{:S(2)}) %copy-start.10) | copy-done | bytes 1572888
  126.6 1.2 copy-done.13
  127.9 1.0 copy-done.16
  128.9 5.3 %gradients.3 = (bf16[512,1536]{1,0:T(8,128)(2,1)}, bf16[768,512]{1,0:T(8,128)(2,1)}) custom-call(bf16[2080,256]{1,0:T(8,128)(2,1)S(1)} %copy-done.13, bf16[2816,256]{1,0:T(8,128)(2,1)S(1)} %collective-permute-done.9.refs_4_.refs_1_, bf16[3024,256]{1,0:T(8,128)(2,1)S(1)} %collective-permute-done.10.refs_3_.refs_2_, ...), custom_call_target="tpu_custom_call" | custom-call | flops 1000 | bytes 1000 | tf_op jit(solution)/shard_map/gradients/pallas_call | solution.py:256
  (44 shorter events, 0.2 us)
Async XLA Ops:
  0.6 0.7 copy-start.17
  1.3 1.0 copy-start.19
  2.4 1.0 copy-start.20
  3.4 0.7 copy-start.21
  6.1 4.8 %copy-start.11 = (bf16[80,4096]{1,0:T(8,128)(2,1)}, bf16[80,4096]{1,0:T(8,128)(2,1)S(1)}, u32[]{:S(2)}) copy-start(bf16[80,4096]{1,0:T(8,128)(2,1)S(1)} %get-tuple-element.34.refs_0_) | copy-start | bytes 1966084
  6.1 30.8 %collective-permute-start.3 = (bf16[80,4096]{1,0:T(8,128)(2,1)}, bf16[80,4096]{1,0:T(8,128)(2,1)S(1)}, u32[]{:S(2)}, u32[]{:S(2)}) collective-permute-start(bf16[80,4096]{1,0:T(8,128)(2,1)} %get-tuple-element.38), channel_id=1, source_target_pairs={{0,4},{1,5},{2,6},{3,7},{4,0},{5,1},{6,2},{7,3},{8,12},{9,13},{10,... | collective-permute-start | bytes 1966088 | tf_op jit(solution)/shard_map/ppermute | solution.py:273
  8.6 29.2 %collective-permute-start.1 = (bf16[80,4096]{1,0:T(8,128)(2,1)S(1)}, bf16[80,4096]{1,0:T(8,128)(2,1)S(1)}, u32[]{:S(2)}, u32[]{:S(2)}) collective-permute-start(bf16[80,4096]{1,0:T(8,128)(2,1)S(1)} %get-tuple-element.36), channel_id=1, source_target_pairs={{0,2},{1,3},{2,0},{3,1},{4,6},{5,7},{6,4},{7,5},{8,10},{9,11},{10,... | collective-permute-start | bytes 1966088 | tf_op jit(solution)/shard_map/ppermute | solution.py:273
  9.1 1.7 %collective-permute-start = (bf16[40,4096]{1,0:T(8,128)(2,1)S(1)}, bf16[40,4096]{1,0:T(8,128)(2,1)S(1)}, u32[]{:S(2)}, u32[]{:S(2)}) collective-permute-start(bf16[40,4096]{1,0:T(8,128)(2,1)S(1)} %slice.24), channel_id=1, source_target_pairs={{0,1},{1,0},{2,3},{3,2},{4,5},{5,4},{6,7},{7,6},{8,9},{9,8},{10,11... | collective-permute-start | bytes 983048 | tf_op jit(solution)/shard_map/ppermute | solution.py:273
  10.8 0.7 copy-start.22
  11.6 28.5 %copy-start.2 = (bf16[1,768,2048]{2,1,0:T(8,128)(2,1)S(1)}, bf16[1,768,2048]{2,1,0:T(8,128)(2,1)}, u32[]{:S(2)}) copy-start(bf16[1,768,2048]{2,1,0:T(8,128)(2,1)} %param.11) | copy-start | bytes 9437188
  19.6 18.9 %collective-permute-start.6 = (bf16[1232,256]{1,0:T(8,128)(2,1)}, bf16[1232,256]{1,0:T(8,128)(2,1)S(1)}, u32[]{:S(2)}, u32[]{:S(2)}) collective-permute-start(bf16[1232,256]{1,0:T(8,128)(2,1)} %get-tuple-element.41), channel_id=1, source_target_pairs={{0,8},{8,0},{16,24},{24,16},{1,9},{9,1},{17,25},{25,17},{2,10},{10... | collective-permute-start | bytes 1892360 | tf_op jit(solution)/shard_map/ppermute | solution.py:273
  21.1 17.3 %collective-permute-start.5 = (bf16[1168,256]{1,0:T(8,128)(2,1)}, bf16[1168,256]{1,0:T(8,128)(2,1)S(1)}, u32[]{:S(2)}, u32[]{:S(2)}) collective-permute-start(bf16[1168,256]{1,0:T(8,128)(2,1)} %get-tuple-element.40), channel_id=1, source_target_pairs={{0,16},{8,24},{16,0},{24,8},{1,17},{9,25},{17,1},{25,9},{2,18},{10... | collective-permute-start | bytes 1794056 | tf_op jit(solution)/shard_map/ppermute | solution.py:273
  37.9 1.7 %collective-permute-start.4 = (bf16[40,4096]{1,0:T(8,128)(2,1)S(1)}, bf16[40,4096]{1,0:T(8,128)(2,1)S(1)}, u32[]{:S(2)}, u32[]{:S(2)}) collective-permute-start(bf16[40,4096]{1,0:T(8,128)(2,1)S(1)} %slice.26), channel_id=1, source_target_pairs={{0,1},{1,0},{2,3},{3,2},{4,5},{5,4},{6,7},{7,6},{8,9},{9,8},{10,11... | collective-permute-start | bytes 983048 | tf_op jit(solution)/shard_map/ppermute | solution.py:273
  38.0 2.1 %collective-permute-start.2 = (bf16[40,4096]{1,0:T(8,128)(2,1)S(1)}, bf16[40,4096]{1,0:T(8,128)(2,1)S(1)}, u32[]{:S(2)}, u32[]{:S(2)}) collective-permute-start(bf16[40,4096]{1,0:T(8,128)(2,1)S(1)} %slice.25), channel_id=1, source_target_pairs={{0,1},{1,0},{2,3},{3,2},{4,5},{5,4},{6,7},{7,6},{8,9},{9,8},{10,11... | collective-permute-start | bytes 983048 | tf_op jit(solution)/shard_map/ppermute | solution.py:273
  38.5 10.1 %copy-start.7 = (bf16[1168,256]{1,0:T(8,128)(2,1)}, bf16[1168,256]{1,0:T(8,128)(2,1)S(1)}, u32[]{:S(2)}) copy-start(bf16[1168,256]{1,0:T(8,128)(2,1)S(1)} %collective-permute-done.5.refs_6_.refs_2_) | copy-start | bytes 1794052
  38.5 10.1 %copy-start.5 = (bf16[1232,256]{1,0:T(8,128)(2,1)}, bf16[1232,256]{1,0:T(8,128)(2,1)S(1)}, u32[]{:S(2)}) copy-start(bf16[1232,256]{1,0:T(8,128)(2,1)S(1)} %collective-permute-done.6.refs_7_.refs_1_) | copy-start | bytes 1892356
  40.1 2.8 %copy-start = (bf16[1,2048,1536]{2,1,0:T(8,128)(2,1)S(1)}, bf16[1,2048,1536]{2,1,0:T(8,128)(2,1)}, u32[]{:S(2)}) copy-start(bf16[1,2048,1536]{2,1,0:T(8,128)(2,1)} %param.10) | copy-start | bytes 18874372
  42.9 39.7 %copy-start.1 = (bf16[1,2048,1536]{2,1,0:T(8,128)(2,1)S(1)}, bf16[1,2048,1536]{2,1,0:T(8,128)(2,1)}, u32[]{:S(2)}) copy-start(bf16[1,2048,1536]{2,1,0:T(8,128)(2,1)} %param.10) | copy-start | bytes 18874372
  48.6 1.0 copy-start.12
  49.6 41.6 %collective-permute-start.10 = (bf16[3024,256]{1,0:T(8,128)(2,1)}, bf16[3024,256]{1,0:T(8,128)(2,1)S(1)}, u32[]{:S(2)}, u32[]{:S(2)}) collective-permute-start(bf16[3024,256]{1,0:T(8,128)(2,1)} %get-tuple-element.48), channel_id=1, source_target_pairs={{0,16},{8,24},{16,0},{24,8},{1,17},{9,25},{17,1},{25,9},{2,18},{10... | collective-permute-start | bytes 4644872 | tf_op jit(solution)/shard_map/ppermute | solution.py:273
  50.1 30.8 %collective-permute-start.7 = (bf16[80,4096]{1,0:T(8,128)(2,1)}, bf16[80,4096]{1,0:T(8,128)(2,1)S(1)}, u32[]{:S(2)}, u32[]{:S(2)}) collective-permute-start(bf16[80,4096]{1,0:T(8,128)(2,1)} %get-tuple-element.44), channel_id=1, source_target_pairs={{0,6},{1,7},{2,4},{3,5},{4,2},{5,3},{6,0},{7,1},{8,14},{9,15},{10,... | collective-permute-start | bytes 1966088 | tf_op jit(solution)/shard_map/ppermute | solution.py:273
  50.5 40.7 %collective-permute-start.9 = (bf16[2816,256]{1,0:T(8,128)(2,1)}, bf16[2816,256]{1,0:T(8,128)(2,1)S(1)}, u32[]{:S(2)}, u32[]{:S(2)}) collective-permute-start(bf16[2816,256]{1,0:T(8,128)(2,1)} %get-tuple-element.47), channel_id=1, source_target_pairs={{0,8},{8,0},{16,24},{24,16},{1,9},{9,1},{17,25},{25,17},{2,10},{10... | collective-permute-start | bytes 4325384 | tf_op jit(solution)/shard_map/ppermute | solution.py:273
  80.8 10.2 %copy-start.23 = (f32[1,80]{1,0:T(1,128)S(1)}, f32[1,80]{1,0:T(1,128)}, u32[]{:S(2)}) copy-start(f32[1,80]{1,0:T(1,128)} %get-tuple-element.35) | copy-start | bytes 964
  80.9 1.7 %collective-permute-start.8 = (bf16[40,4096]{1,0:T(8,128)(2,1)S(1)}, bf16[40,4096]{1,0:T(8,128)(2,1)S(1)}, u32[]{:S(2)}, u32[]{:S(2)}) collective-permute-start(bf16[40,4096]{1,0:T(8,128)(2,1)S(1)} %slice.27), channel_id=1, source_target_pairs={{0,1},{1,0},{2,3},{3,2},{4,5},{5,4},{6,7},{7,6},{8,9},{9,8},{10,11... | collective-permute-start | bytes 983048 | tf_op jit(solution)/shard_map/ppermute | solution.py:273
  87.3 0.8 copy-start.15
  88.1 18.2 %collective-permute-start.14 = (bf16[1232,256]{1,0:T(8,128)(2,1)}, bf16[1232,256]{1,0:T(8,128)(2,1)}, u32[]{:S(2)}, u32[]{:S(2)}) collective-permute-start(bf16[1232,256]{1,0:T(8,128)(2,1)} %get-tuple-element.55), channel_id=1, source_target_pairs={{0,16},{8,24},{16,0},{24,8},{1,17},{9,25},{17,1},{25,9},{2,18},{10... | collective-permute-start | bytes 1892360 | tf_op jit(solution)/shard_map/ppermute | solution.py:273
  89.6 16.7 %collective-permute-start.13 = (bf16[1168,256]{1,0:T(8,128)(2,1)}, bf16[1168,256]{1,0:T(8,128)(2,1)}, u32[]{:S(2)}, u32[]{:S(2)}) collective-permute-start(bf16[1168,256]{1,0:T(8,128)(2,1)} %get-tuple-element.54), channel_id=1, source_target_pairs={{0,8},{8,0},{16,24},{24,16},{1,9},{9,1},{17,25},{25,17},{2,10},{10... | collective-permute-start | bytes 1794056 | tf_op jit(solution)/shard_map/ppermute | solution.py:273
  92.8 30.5 %collective-permute-start.11 = (bf16[1040,256]{1,0:T(8,128)(2,1)}, bf16[1040,256]{1,0:T(8,128)(2,1)}, u32[]{:S(2)}, u32[]{:S(2)}) collective-permute-start(bf16[1040,256]{1,0:T(8,128)(2,1)} %slice.29), channel_id=1, source_target_pairs={{0,16},{8,24},{16,0},{24,8},{1,17},{9,25},{17,1},{25,9},{2,18},{10... | collective-permute-start | bytes 1597448 | tf_op jit(solution)/shard_map/ppermute | solution.py:273
  93.3 30.0 %collective-permute-start.12 = (bf16[1040,256]{1,0:T(8,128)(2,1)}, bf16[1040,256]{1,0:T(8,128)(2,1)}, u32[]{:S(2)}, u32[]{:S(2)}) collective-permute-start(bf16[1040,256]{1,0:T(8,128)(2,1)} %slice.28), channel_id=1, source_target_pairs={{0,8},{8,0},{16,24},{24,16},{1,9},{9,1},{17,25},{25,17},{2,10},{10... | collective-permute-start | bytes 1597448 | tf_op jit(solution)/shard_map/ppermute | solution.py:273
  94.7 17.3 %all-to-all-start = ((f32[8,1,40]{2,1,0:T(1,128)}), f32[8,1,40]{2,1,0:T(1,128)S(1)}, u32[]{:S(2)}, u32[]{:S(2)}) async-start(f32[8,1,40]{2,1,0:T(1,128)} %bitcast.5), calls=%async_computation | async-start | bytes 8192 | tf_op jit(solution)/shard_map/all_to_all | solution.py:277
  98.1 1.1 copy-start.6
  99.2 1.1 copy-start.8
  100.3 1.0 copy-start.14
  101.3 10.9 %copy-start.18 = (f32[128,2]{0,1:T(2,128)S(1)}, f32[128,2]{0,1:T(2,128)}, u32[]{:S(2)}) copy-start(f32[128,2]{0,1:T(2,128)} %param.8) | copy-start | bytes 3076
  102.8 1.6 %copy-start.3 = (f32[512,1536]{1,0:T(8,128)}, f32[512,1536]{1,0:T(8,128)S(1)}, u32[]{:S(2)}) copy-start(f32[512,1536]{1,0:T(8,128)S(1)} %get-tuple-element.57.refs_10_) | copy-start | bytes 9437188
  104.4 1.1 copy-start.9
  107.9 12.7 %collective-permute-start.15 = (bf16[416,256]{1,0:T(8,128)(2,1)}, bf16[416,256]{1,0:T(8,128)(2,1)}, u32[]{:S(2)}, u32[]{:S(2)}) collective-permute-start(bf16[416,256]{1,0:T(8,128)(2,1)} %slice.30), channel_id=1, source_target_pairs={{0,16},{8,24},{16,0},{24,8},{1,17},{9,25},{17,1},{25,9},{2,18},{10... | collective-permute-start | bytes 638984 | tf_op jit(solution)/shard_map/ppermute | solution.py:273
  110.4 12.9 %collective-permute-start.16 = (bf16[624,256]{1,0:T(8,128)(2,1)}, bf16[624,256]{1,0:T(8,128)(2,1)S(1)}, u32[]{:S(2)}, u32[]{:S(2)}) collective-permute-start(bf16[624,256]{1,0:T(8,128)(2,1)} %slice.31), channel_id=1, source_target_pairs={{0,8},{8,0},{16,24},{24,16},{1,9},{9,1},{17,25},{25,17},{2,10},{10... | collective-permute-start | bytes 958472 | tf_op jit(solution)/shard_map/ppermute | solution.py:273
  123.3 1.9 %copy-start.4 = (f32[512,1536]{1,0:T(8,128)S(1)}, f32[512,1536]{1,0:T(8,128)}, u32[]{:S(2)}) copy-start(f32[512,1536]{1,0:T(8,128)} %copy-done.3) | copy-start | bytes 9437188
  125.2 1.4 %copy-start.10 = (f32[768,512]{1,0:T(8,128)S(1)}, f32[768,512]{1,0:T(8,128)}, u32[]{:S(2)}) copy-start(f32[768,512]{1,0:T(8,128)} %copy-done.9) | copy-start | bytes 4718596
  126.6 1.2 copy-start.13
  127.9 1.0 copy-start.16

commit v4 on v2

--- a/solution.py
+++ b/solution.py
@@ -10,6 +10,7 @@
 EXPERTS = 8
 CAP = 40
 PAIR = 2 * CAP
+LANES = 128
 TILE = 256
 MIB = 1024 * 1024
 BF16 = jnp.bfloat16
@@ -74,27 +75,32 @@
 def split_rows(count, top, half):
     blocks = 3 * half // TILE
     low = count - top
-    return blocks, low, (blocks + 4) * top, (blocks + 4) * low
-
-
-def expert_kernel(pairs, top, *refs):
+    from_x, from_y = (blocks + 4) * top, (blocks + 4) * low
+    sizes = (from_x + blocks * low + 4 * count, from_y + blocks * top + 4 * count)
+    return blocks, low, from_x, from_y, sizes
+
+
+def expert_kernel(pairs, top, relays, *refs):
     row_refs, (gate_ref, up_ref, down_ref), rest = (
         refs[: 2 * pairs],
         refs[2 * pairs : 2 * pairs + 3],
         refs[2 * pairs + 3 :],
     )
-    own_ref, to_x, to_y, inner_ref, x_rows, s_rows, s_turned, total = rest
+    relay_refs, rest = rest[: len(relays)], rest[len(relays) :]
+    own_ref, to_x, to_y, *inner_refs, x_rows, s_rows, s_turned, total = rest
     count = pairs * PAIR
     width = gate_ref.shape[0]
     steps = pl.num_programs(0)
     half = TILE * 3
     quarter = width // 4
-    blocks, low, from_x, from_y = split_rows(count, top, half)
+    blocks, low, from_x, from_y, sizes = split_rows(count, top, half)
     step = pl.program_id(0)
     group = lax.axis_index("dp")
 
     @pl.when(step == 0)
     def _():
+        for ref, relay, size, at in zip((to_x, to_y), relay_refs, relays, sizes):
+            ref[at : at + size] = relay[:size]
         for rows, start in ((x_rows, 0), (s_rows, width)):
             rows[...] = jnp.concatenate(
                 [ref[:CAP, start : start + width].astype(F32) for ref in row_refs],
@@ -143,36 +149,39 @@
 
     @pl.when(step == steps - 1)
     def _():
-        inner_ref[...] = jnp.broadcast_to(total[...], (count, 128)).T[0:1]
-
-
-def expert_rows(rows, weight_gu, weight_down, top):
-    count = len(rows) // 2 * PAIR
+        for pair, ref in enumerate(inner_refs):
+            part = total[pair * PAIR : (pair + 1) * PAIR]
+            ref[...] = jnp.broadcast_to(part, ref.shape)
+
+
+def expert_rows(rows, weight_gu, weight_down, top, relay=(), relays=()):
+    pairs = len(rows) // 2
+    count = pairs * PAIR
     width, both = weight_gu.shape
     half = both // 2
     steps = half // TILE
-    blocks, low, from_x, from_y = split_rows(count, top, half)
-    shapes = [
-        ((blocks + 4) * count, TILE),
-        (from_x + blocks * low + 4 * count, TILE),
-        (from_y + blocks * top + 4 * count, TILE),
+    blocks, _, _, _, sizes = split_rows(count, top, half)
+    sizes = [(blocks + 4) * count] + [
+        size + extra for size, extra in zip(sizes, relays or (0, 0))
     ]
+    shapes = [(size, TILE) for size in sizes]
 
     def whole(shape):
         return pl.BlockSpec(shape, lambda h: (0, 0))
 
     return pl.pallas_call(
-        functools.partial(expert_kernel, len(rows) // 2, top),
+        functools.partial(expert_kernel, pairs, top, tuple(relays)),
         grid=(steps,),
         in_specs=[
             *[whole(part.shape) for part in rows],
             pl.BlockSpec((width, TILE), lambda h: (0, h)),
             pl.BlockSpec((width, TILE), lambda h: (0, h + steps)),
             pl.BlockSpec((TILE, width), lambda h: (h, 0)),
+            *[whole(part.shape) for part in relay],
         ],
-        out_specs=[whole(shape) for shape in shapes] + [whole((1, count))],
+        out_specs=[whole(shape) for shape in shapes] + [whole((PAIR, LANES))] * pairs,
         out_shape=[jax.ShapeDtypeStruct(shape, BF16) for shape in shapes]
-        + [jax.ShapeDtypeStruct((1, count), F32)],
+        + [jax.ShapeDtypeStruct((PAIR, LANES), F32)] * pairs,
         scratch_shapes=[
             pltpu.VMEM((count, width), BF16),
             pltpu.VMEM((count, width), BF16),
@@ -182,46 +191,53 @@
         compiler_params=pltpu.CompilerParams(vmem_limit_bytes=20 * MIB),
         cost_estimate=pl.CostEstimate(flops=1_000, bytes_accessed=1_000, transcendentals=0),
         name="expert_rows",
-    )(*rows, weight_gu, weight_gu, weight_down)
-
-
-def gradient_kernel(top, half, adding, *refs):
-    (own, got_x, got_y, far_top, far_low), refs = refs[:5], refs[5:]
-    count = own.shape[0] // (3 * half // TILE + 4)
-    blocks, low, from_x, from_y = split_rows(count, top, half)
+    )(*rows, weight_gu, weight_gu, weight_down, *relay)
+
+
+def gradient_kernel(chunks, half, adding, *refs):
+    groups, refs = (
+        [refs[5 * n : 5 * n + 5] for n in range(len(chunks))],
+        refs[5 * len(chunks) :],
+    )
     if adding:
         (acc_gu, acc_down), refs = refs[:2], refs[2:]
     out_gu, out_down, turned, s_rows = refs
     both = 2 * half // TILE
 
+    def far_parts(block, top, low, at_top, at_low, far_top, far_low):
+        return [
+            far_top[at_top + block * top : at_top + (block + 1) * top],
+            far_low[at_low + block * low : at_low + (block + 1) * low],
+        ]
+
     def factor(block):
-        return jnp.concatenate(
-            [
+        parts = []
+        for (count, top, at_top, at_low), group in zip(chunks, groups):
+            own, got_x, got_y, *far = group
+            _, low, from_x, from_y, _ = split_rows(count, top, half)
+            parts += [
                 own[block * count : (block + 1) * count],
                 got_x[block * top : (block + 1) * top],
                 got_x[from_x + block * low : from_x + (block + 1) * low],
                 got_y[from_y + block * top : from_y + (block + 1) * top],
                 got_y[block * low : (block + 1) * low],
-                far_top[block * top : (block + 1) * top],
-                far_low[block * low : (block + 1) * low],
-            ],
-            axis=0,
-        )
+            ] + far_parts(block, top, low, at_top, at_low, *far)
+        return jnp.concatenate(parts, axis=0)
 
     def piece(q):
-        block = blocks + q
-        at_x = from_x + blocks * low + q * count
-        at_y = from_y + blocks * top + q * count
-        return jnp.concatenate(
-            [
+        parts = []
+        for (count, top, at_top, at_low), group in zip(chunks, groups):
+            own, got_x, got_y, *far = group
+            blocks, low, from_x, from_y, _ = split_rows(count, top, half)
+            block = blocks + q
+            at_x = from_x + blocks * low + q * count
+            at_y = from_y + blocks * top + q * count
+            parts += [
                 own[block * count : (block + 1) * count],
                 got_x[at_x : at_x + count],
                 got_y[at_y : at_y + count],
-                far_top[block * top : (block + 1) * top],
-                far_low[block * low : (block + 1) * low],
-            ],
-            axis=0,
-        )
+            ] + far_parts(block, top, low, at_top, at_low, *far)
+        return jnp.concatenate(parts, axis=0)
 
     for q in range(2):
         turned[q * TILE : (q + 1) * TILE, :] = piece(q).T
@@ -240,26 +256,53 @@
         out_down[at, :] = grad.astype(out_down.dtype)
 
 
-def gradients(top, pieces, half, quarter, sums=(), final=False):
+def gradients(chunks, pieces, half, quarter, sums=(), final=False):
     kept = BF16 if final else F32
-    rows = 4 * pieces[0].shape[0] // (3 * half // TILE + 4)
+    rows = 4 * sum(chunk[0] for chunk in chunks)
     vmem = pl.BlockSpec(memory_space=pltpu.VMEM)
     return pl.pallas_call(
-        functools.partial(gradient_kernel, top, half, len(sums)),
+        functools.partial(gradient_kernel, chunks, half, len(sums)),
         in_specs=[vmem] * (len(pieces) + len(sums)),
         out_specs=[vmem] * 2,
         out_shape=[
             jax.ShapeDtypeStruct((quarter, 2 * half), kept),
             jax.ShapeDtypeStruct((half, quarter), kept),
         ],
-        input_output_aliases={} if final or not sums else {len(pieces): 0, len(pieces) + 1: 1},
         scratch_shapes=[pltpu.VMEM((quarter, rows), BF16), pltpu.VMEM((rows, quarter), BF16)],
-        compiler_params=pltpu.CompilerParams(vmem_limit_bytes=14 * MIB),
+        compiler_params=pltpu.CompilerParams(vmem_limit_bytes=20 * MIB),
         cost_estimate=pl.CostEstimate(flops=1_000, bytes_accessed=1_000, transcendentals=0),
         name="gradients",
     )(*pieces, *sums)
 
 
+def prob_kernel(own_0, own_1, own_2, own_3, other_ref, slot_ref, prob_ref, out_ref):
+    owns = (own_0, own_1, own_2, own_3)
+    tok = slot_ref.shape[1]
+    places = lax.broadcasted_iota(jnp.int32, (CAP, tok), 0)
+    for choice in range(2):
+        slot = slot_ref[choice : choice + 1, :]
+        grad = jnp.zeros((CAP, tok), F32)
+        for e in range(EXPERTS):
+            chunk = e // 2
+            if e % 2 == 0:
+                values = owns[chunk][:CAP, :]
+            else:
+                values = other_ref[chunk * CAP : (chunk + 1) * CAP, :]
+            grad += jnp.where(places + e * CAP == slot, values, 0.0)
+        grad = jnp.sum(grad, axis=0, keepdims=True)
+        out_ref[choice : choice + 1, :] = grad / prob_ref[choice : choice + 1, :]
+
+
+def prob_gradients(owns, other, slots, probs):
+    return pl.pallas_call(
+        prob_kernel,
+        out_shape=jax.ShapeDtypeStruct(probs.shape, F32),
+        compiler_params=pltpu.CompilerParams(vmem_limit_bytes=4 * MIB),
+        cost_estimate=pl.CostEstimate(flops=1_000, bytes_accessed=1_000, transcendentals=0),
+        name="prob_gradients",
+    )(*owns, other, slots, probs)
+
+
 def exchange(values, axis, mask):
     size = lax.axis_size(axis)
     return lax.ppermute(values, axis, [(n, n ^ mask) for n in range(size)])
@@ -274,51 +317,66 @@
 
 
 def plane_body(tokens, cotangent, gate_probs, expert_ids, gate_up, down):
-    me = lax.axis_index("expert")
     half = gate_up.shape[2] // 2
     quarter = tokens.shape[1] // 4
     ids, probs = expert_ids.T, gate_probs.T
     *local, slots = dispatch_rows(ids, probs, tokens, cotangent)
-    tops = (48, PAIR, 32)
-    inner, pieces, forwards = [], [], []
+    weights = (gate_up[0], down[0])
+    _, _, cut_x0, cut_y0, _ = split_rows(PAIR, 48, half)
+    _, _, cut_x1, cut_y1, sizes = split_rows(2 * PAIR, PAIR, half)
+    _, _, cut_x2, cut_y2, _ = split_rows(PAIR, 32, half)
 
     def other_core(rows):
         return exchange(rows[CAP:], "expert", 1)
 
-    def compute(*rows):
-        top = tops[len(inner)]
-        own, to_x, to_y, found = expert_rows(rows, gate_up[0], down[0], top)
-        inner.append(found)
-        _, _, from_x, from_y = split_rows(len(rows) // 2 * PAIR, top, half)
-        got_x, got_y = exchange(to_x, "dp", 1), exchange(to_y, "dp", 2)
-        forward = (got_x[:from_x], got_y[:from_y])
-        far_top, far_low = exchange(forward[0], "dp", 2), exchange(forward[1], "dp", 1)
-        forwards.append(forward)
-        pieces.append([own, got_x, got_y, far_top, far_low])
-
-    def add(chunk, sums=()):
-        return gradients(tops[chunk], pieces[chunk], half, quarter, sums, chunk == len(tops) - 1)
+    def to_plane(to_x, to_y):
+        return exchange(to_x, "dp", 1), exchange(to_y, "dp", 2)
 
     rows_1 = exchange(local[1], "expert", 2)
     rows_2 = exchange(local[2], "expert", 4)
-    compute(local[0], other_core(local[0]))
-    rows_1 = after(rows_1, inner[0])
-    other_1 = other_core(rows_1)
+    own_0, to_x, to_y, inner_0 = expert_rows((local[0], other_core(local[0])), *weights, 48)
+    got_x0, got_y0 = to_plane(to_x, to_y)
+    rows_1 = after(rows_1, inner_0)
     rows_3 = exchange(after(local[3], rows_2), "expert", 6)
-    rows_2 = after(rows_2, *forwards[0])
-    compute(rows_1, other_1, rows_2, other_core(rows_2))
-    sums = add(0)
-    rows_3 = after(rows_3, inner[1], *sums)
-    compute(rows_3, after(other_core(rows_3), *forwards[1]))
-    sums = add(1, sums)
-    grad_gu, grad_down = add(2, sums)
-    numbers = jnp.arange(EXPERTS, dtype=jnp.int32)
-    mine = (numbers[:, None] == jnp.bitwise_xor(numbers, me)[None, :])[:, :, None]
-    rows_inner = after(jnp.concatenate(inner, axis=1), *forwards[2]).reshape(EXPERTS, CAP)
-    sent = jnp.sum(jnp.where(mine, rows_inner[None], 0.0), axis=1)
-    returned = jnp.sum(jnp.where(mine, swap(sent)[None], 0.0), axis=1).reshape(-1)
-    chosen = slots[:, None, :] == jnp.arange(EXPERTS * CAP, dtype=jnp.int32)[None, :, None]
-    grad_probs = jnp.sum(jnp.where(chosen, returned[None, :, None], 0.0), axis=1) / probs
+    rows_2 = after(rows_2, inner_0)
+    own_1, to_x, to_y, inner_1, inner_2 = expert_rows(
+        (rows_1, other_core(rows_1), rows_2, other_core(rows_2)),
+        *weights,
+        PAIR,
+        (got_y0, got_x0),
+        (cut_y0, cut_x0),
+    )
+    got_x1, got_y1 = to_plane(to_x, to_y)
+    rows_3 = after(rows_3, inner_1)
+    own_2, to_x, to_y, inner_3 = expert_rows((rows_3, other_core(rows_3)), *weights, 32)
+    got_x2, got_y2 = to_plane(to_x, to_y)
+    returned = [inner_0] + [
+        exchange(part, "expert", 2 * n + 2)
+        for n, part in enumerate((inner_1, inner_2, inner_3))
+    ]
+    other = exchange(
+        jnp.concatenate([part[CAP:] for part in returned], axis=0), "expert", 1
+    )
+    got_x1, got_y1 = after((got_x1, got_y1), inner_3, other)
+    turn_1 = (got_y1[:cut_y1], got_x1[:cut_x1])
+    low_1, top_1 = to_plane(*turn_1)
+    sums = gradients(
+        ((PAIR, 48, sizes[1], sizes[0]),),
+        (own_0, got_x0, got_y0, got_y1, got_x1),
+        half,
+        quarter,
+    )
+    grad_probs = prob_gradients(returned, other, slots, probs)
+    got_x2, got_y2 = after((got_x2, got_y2), *sums)
+    low_2, top_2 = to_plane(got_y2[:cut_y2], got_x2[:cut_x2])
+    grad_gu, grad_down = gradients(
+        ((2 * PAIR, PAIR, 0, 0), (PAIR, 32, 0, 0)),
+        (own_1, got_x1, got_y1, top_1, low_1, own_2, got_x2, got_y2, top_2, low_2),
+        half,
+        quarter,
+        sums,
+        True,
+    )
     return (grad_probs.T, grad_gu[None], grad_down[None])
 
 

time: 148 us -> 125 us (0.84)
  waiting for transfers between devices: 74.1 us -> 58.1 us
  local copies, waits for them, and re-layouts: 24.3 us -> 8.33 us
  starting transfers between devices: 24.8 us -> 39.6 us
  Pallas kernels: 21.8 us -> 17.8 us
  other arithmetic: 1.57 us -> 0.01 us
    ppermute x19 -> x21, starting transfers between devices: 21.1 us -> 39.6 us  [exchange(): return lax.ppermute(values, axis, [(n, n ^ mask) for n in range(size)])]
    ppermute x19 -> x21, waiting for transfers between devices: 74.1 us -> 58.1 us  [exchange(): return lax.ppermute(values, axis, [(n, n ^ mask) for n in range(size)])]
    unnamed x42 -> x18, local copies, waits for them, and re-layouts: 18.8 us -> 8.12 us
    slice x6 -> x8, local copies, waits for them, and re-layouts: 5.32 us -> 0.12 us  [the longest x2 0.07 us: plane_body(): turn_1 = (got_y1[:cut_y1], got_x1[:cut_x1])]
    pallas_call x6, Pallas kernels: 20.8 us -> 16.8 us  [the longest x3 11.2 us: expert_rows(): pl.pallas_call(functools.partial(expert_kernel, pairs, top, tuple(relays)...]
    all_to_all x1 -> x0, starting transfers between devices: 3.74 us -> none  [swap(): lax.all_to_all(values, 'expert', split_axis=0, concat_axis=0, tiled=True)]
  transfers between devices with their start and end apart: 20 -> 21, of which waited for: 10 -> 13; matrix products, arithmetic and copies ran while one was open for 5% -> 0% of each run, Pallas kernels for 6% -> 7%
where the time goes in v4:
time: 125 us
  waiting for transfers between devices  58.1 us (46%)
  starting transfers between devices  39.6 us (32%)
  Pallas kernels  17.8 us (14%)
  local copies, waits for them, and re-layouts  8.33 us (7%)
    ppermute x21, waiting for transfers between devices, exchange(): return lax.ppermute(values, axis, [(n, n ^ mask) for n in range(size)])  58.1 us
    ppermute x21, starting transfers between devices, exchange(): return lax.ppermute(values, axis, [(n, n ^ mask) for n in range(size)])  39.6 us
    pallas_call x3, Pallas kernels, expert_rows(): pl.pallas_call(functools.partial(expert_kernel, pairs, top, tuple(relays)...  11.2 us
    unnamed x18, local copies, waits for them, and re-layouts  8.12 us
    pallas_call x2, Pallas kernels, gradients(): pl.pallas_call(functools.partial(gradient_kernel, chunks, half, len(sums)...  5.07 us
  transfers between devices with their start and end apart: 21, of which 13 were waited for; matrix products, arithmetic and copies ran while one was open for 0% of the time, Pallas kernels for 7%

profile of v4, /device:TPU:0, one launch (start us, length us, event | category | flops | bytes accessed | tf_op | source)
XLA Modules:
  0.0 124.6 jit_solution(1892368324793212727)
XLA Ops:
  0.6 0.0 copy-start.4
  0.6 0.7 copy-done.4
  1.3 0.0 copy-start.6
  1.3 1.0 copy-done.6
  2.4 0.0 copy-start.7
  2.4 1.0 copy-done.7
  3.4 0.0 copy-start.8
  3.4 0.7 copy-done.8
  4.1 1.0 dispatch_rows.1
  5.0 4.1 %collective-permute-start.3 = (bf16[80,4096]{1,0:T(8,128)(2,1)S(1)}, bf16[80,4096]{1,0:T(8,128)(2,1)S(1)}, u32[]{:S(2)}, u32[]{:S(2)}) collective-permute-start(bf16[80,4096]{1,0:T(8,128)(2,1)S(1)} %get-tuple-element.37), channel_id=1, source_target_pairs={{0,4},{1,5},{2,6},{3,7},{4,0},{5,1},{6,2},{7,3},{8,12},{9,13},{10,... | collective-permute-start | bytes 1966088 | tf_op jit(solution)/shard_map/ppermute | solution.py:308
  9.1 1.6 %collective-permute-start.1 = (bf16[80,4096]{1,0:T(8,128)(2,1)S(1)}, bf16[80,4096]{1,0:T(8,128)(2,1)S(1)}, u32[]{:S(2)}, u32[]{:S(2)}) collective-permute-start(bf16[80,4096]{1,0:T(8,128)(2,1)S(1)} %get-tuple-element.35), channel_id=1, source_target_pairs={{0,2},{1,3},{2,0},{3,1},{4,6},{5,7},{6,4},{7,5},{8,10},{9,11},{10,... | collective-permute-start | bytes 1966088 | tf_op jit(solution)/shard_map/ppermute | solution.py:308
  10.7 0.1 collective-permute-start
  10.8 1.6 %collective-permute-done.refs_1_ = bf16[40,4096]{1,0:T(8,128)(2,1)S(1)} collective-permute-done((bf16[40,4096]{1,0:T(8,128)(2,1)S(1)}, bf16[40,4096]{1,0:T(8,128)(2,1)S(1)}, u32[]{:S(2)}, u32[]{:S(2)}) %collective-permute-start) | collective-permute-done | bytes 327712 | tf_op jit(solution)/shard_map/ppermute | solution.py:308
  12.4 0.0 copy-start
  12.4 2.8 %copy-done = bf16[1,2048,1536]{2,1,0:T(8,128)(2,1)S(1)} copy-done((bf16[1,2048,1536]{2,1,0:T(8,128)(2,1)S(1)}, bf16[1,2048,1536]{2,1,0:T(8,128)(2,1)}, u32[]{:S(2)}) %copy-start) | copy-done | bytes 6291480
  15.2 0.0 copy-start.2
  15.2 1.9 %copy-done.2 = bf16[1,768,2048]{2,1,0:T(8,128)(2,1)S(1)} copy-done((bf16[1,768,2048]{2,1,0:T(8,128)(2,1)S(1)}, bf16[1,768,2048]{2,1,0:T(8,128)(2,1)}, u32[]{:S(2)}) %copy-start.2) | copy-done | bytes 3145752
  17.1 3.6 %expert_rows.3 = (bf16[1040,256]{1,0:T(8,128)(2,1)S(1)}, bf16[1232,256]{1,0:T(8,128)(2,1)S(1)}, bf16[1168,256]{1,0:T(8,128)(2,1)S(1)}, f32[80,128]{1,0:T(8,128)S(1)}) custom-call(bf16[80,4096]{1,0:T(8,128)(2,1)S(1)} %get-tuple-element.33.refs_0_, bf16[40,4096]{1,0:T(8,128)(2,1)S(1)} %collective-permute-done.refs_1_, bf16[2048,1536]{1,0:T(8,128)(2,1)S(1)} %bitcast.7, ...), custom_call_target="tpu_custom_call" | custom-call | flops 1000 | bytes 1000 | tf_op jit(solution)/shard_map/expert_rows/pallas_call | solution.py:172
  20.7 1.6 %collective-permute-start.6 = (bf16[1232,256]{1,0:T(8,128)(2,1)S(1)}, bf16[1232,256]{1,0:T(8,128)(2,1)S(1)}, u32[]{:S(2)}, u32[]{:S(2)}) collective-permute-start(bf16[1232,256]{1,0:T(8,128)(2,1)S(1)} %get-tuple-element.40), channel_id=1, source_target_pairs={{0,8},{8,0},{16,24},{24,16},{1,9},{9,1},{17,25},{25,17},{2,10},{10... | collective-permute-start | bytes 1892360 | tf_op jit(solution)/shard_map/ppermute | solution.py:308
  22.3 1.5 %collective-permute-start.5 = (bf16[1168,256]{1,0:T(8,128)(2,1)S(1)}, bf16[1168,256]{1,0:T(8,128)(2,1)S(1)}, u32[]{:S(2)}, u32[]{:S(2)}) collective-permute-start(bf16[1168,256]{1,0:T(8,128)(2,1)S(1)} %get-tuple-element.39), channel_id=1, source_target_pairs={{0,16},{8,24},{16,0},{24,8},{1,17},{9,25},{17,1},{25,9},{2,18},{10... | collective-permute-start | bytes 1794056 | tf_op jit(solution)/shard_map/ppermute | solution.py:308
  23.8 14.2 %collective-permute-done.3.refs_2_ = bf16[80,4096]{1,0:T(8,128)(2,1)S(1)} collective-permute-done((bf16[80,4096]{1,0:T(8,128)(2,1)S(1)}, bf16[80,4096]{1,0:T(8,128)(2,1)S(1)}, u32[]{:S(2)}, u32[]{:S(2)}) %collective-permute-start.3) | collective-permute-done | bytes 655392 | tf_op jit(solution)/shard_map/ppermute | solution.py:308
  38.0 0.2 collective-permute-done.1.refs_0_
  38.3 0.1 collective-permute-start.4
  38.4 0.5 collective-permute-start.2
  38.8 0.0 collective-permute-done.5.refs_7_.refs_2_
  38.9 0.0 collective-permute-done.6.refs_8_.refs_1_
  38.9 1.1 collective-permute-done.4.refs_3_
  40.0 0.5 collective-permute-done.2.refs_1_
  40.4 0.0 copy-done.1
  40.4 0.0 copy-done.3
  40.4 4.0 %expert_rows.4 = (bf16[2080,256]{1,0:T(8,128)(2,1)S(1)}, bf16[2816,256]{1,0:T(8,128)(2,1)S(1)}, bf16[3024,256]{1,0:T(8,128)(2,1)S(1)}, f32[80,128]{1,0:T(8,128)S(1)}, f32[80,128]{1,0:T(8,128)S(1)}) custom-call(bf16[80,4096]{1,0:T(8,128)(2,1)S(1)} %collective-permute-done.1.refs_0_, bf16[40,4096]{1,0:T(8,128)(2,1)S(1)} %collective-permute-done.2.refs_1_, ...), custom_call_target="tpu_custom_call" | custom-call | flops 1000 | bytes 1000 | tf_op jit(solution)/shard_map/expert_rows/pallas_call | solution.py:172
  44.4 1.6 %collective-permute-start.14 = (bf16[3024,256]{1,0:T(8,128)(2,1)S(1)}, bf16[3024,256]{1,0:T(8,128)(2,1)S(1)}, u32[]{:S(2)}, u32[]{:S(2)}) collective-permute-start(bf16[3024,256]{1,0:T(8,128)(2,1)S(1)} %get-tuple-element.50), channel_id=1, source_target_pairs={{0,16},{8,24},{16,0},{24,8},{1,17},{9,25},{17,1},{25,9},{2,18},{10... | collective-permute-start | bytes 4644872 | tf_op jit(solution)/shard_map/ppermute | solution.py:308
  46.1 1.5 %collective-permute-start.13 = (bf16[2816,256]{1,0:T(8,128)(2,1)S(1)}, bf16[2816,256]{1,0:T(8,128)(2,1)S(1)}, u32[]{:S(2)}, u32[]{:S(2)}) collective-permute-start(bf16[2816,256]{1,0:T(8,128)(2,1)S(1)} %get-tuple-element.49), channel_id=1, source_target_pairs={{0,8},{8,0},{16,24},{24,16},{1,9},{9,1},{17,25},{25,17},{2,10},{10... | collective-permute-start | bytes 4325384 | tf_op jit(solution)/shard_map/ppermute | solution.py:308
  47.6 3.2 %collective-permute-start.9 = (bf16[80,4096]{1,0:T(8,128)(2,1)S(1)}, bf16[80,4096]{1,0:T(8,128)(2,1)S(1)}, u32[]{:S(2)}, u32[]{:S(2)}) collective-permute-start(bf16[80,4096]{1,0:T(8,128)(2,1)S(1)} %get-tuple-element.44), channel_id=1, source_target_pairs={{0,6},{1,7},{2,4},{3,5},{4,2},{5,3},{6,0},{7,1},{8,14},{9,15},{10,... | collective-permute-start | bytes 1966088 | tf_op jit(solution)/shard_map/ppermute | solution.py:308
  50.8 14.9 %collective-permute-done.9.refs_0_ = bf16[80,4096]{1,0:T(8,128)(2,1)S(1)} collective-permute-done((bf16[80,4096]{1,0:T(8,128)(2,1)S(1)}, bf16[80,4096]{1,0:T(8,128)(2,1)S(1)}, u32[]{:S(2)}, u32[]{:S(2)}) %collective-permute-start.9) | collective-permute-done | bytes 655392 | tf_op jit(solution)/shard_map/ppermute | solution.py:308
  65.7 0.1 collective-permute-start.10
  65.8 1.6 %collective-permute-done.10.refs_1_ = bf16[40,4096]{1,0:T(8,128)(2,1)S(1)} collective-permute-done((bf16[40,4096]{1,0:T(8,128)(2,1)S(1)}, bf16[40,4096]{1,0:T(8,128)(2,1)S(1)}, u32[]{:S(2)}, u32[]{:S(2)}) %collective-permute-start.10) | collective-permute-done | bytes 327712 | tf_op jit(solution)/shard_map/ppermute | solution.py:308
  67.4 3.6 %expert_rows.5 = (bf16[1040,256]{1,0:T(8,128)(2,1)S(1)}, bf16[1168,256]{1,0:T(8,128)(2,1)S(1)}, bf16[1232,256]{1,0:T(8,128)(2,1)S(1)}, f32[80,128]{1,0:T(8,128)S(1)}) custom-call(bf16[80,4096]{1,0:T(8,128)(2,1)S(1)} %collective-permute-done.9.refs_0_, bf16[40,4096]{1,0:T(8,128)(2,1)S(1)} %collective-permute-done.10.refs_1_, bf16[2048,1536]{1,0:T(8,128)(2,1)S(1)} %bitcast.11, ...), custom_call_target="tpu_custom_call" | custom-call | flops 1000 | bytes 1000 | tf_op jit(solution)/shard_map/expert_rows/pallas_call | solution.py:172
  71.0 0.5 collective-permute-start.18
  71.6 0.5 collective-permute-start.17
  72.0 13.5 %collective-permute-start.8 = (f32[80,128]{1,0:T(8,128)S(1)}, f32[80,128]{1,0:T(8,128)S(1)}, u32[]{:S(2)}, u32[]{:S(2)}) collective-permute-start(f32[80,128]{1,0:T(8,128)S(1)} %get-tuple-element.42), channel_id=1, source_target_pairs={{0,4},{1,5},{2,6},{3,7},{4,0},{5,1},{6,2},{7,3},{8,12},{9,13},{10,... | collective-permute-start | bytes 122888 | tf_op jit(solution)/shard_map/ppermute | solution.py:308
  85.6 2.0 %collective-permute-done.8.own_2 = f32[80,128]{1,0:T(8,128)S(1)} collective-permute-done((f32[80,128]{1,0:T(8,128)S(1)}, f32[80,128]{1,0:T(8,128)S(1)}, u32[]{:S(2)}, u32[]{:S(2)}) %collective-permute-start.8) | collective-permute-done | bytes 40992 | tf_op jit(solution)/shard_map/ppermute | solution.py:308
  87.5 3.0 %collective-permute-start.7 = (f32[80,128]{1,0:T(8,128)S(1)}, f32[80,128]{1,0:T(8,128)S(1)}, u32[]{:S(2)}, u32[]{:S(2)}) collective-permute-start(f32[80,128]{1,0:T(8,128)S(1)} %get-tuple-element.41), channel_id=1, source_target_pairs={{0,2},{1,3},{2,0},{3,1},{4,6},{5,7},{6,4},{7,5},{8,10},{9,11},{10,... | collective-permute-start | bytes 122888 | tf_op jit(solution)/shard_map/ppermute | solution.py:308
  90.6 2.0 %collective-permute-done.7.own_1 = f32[80,128]{1,0:T(8,128)S(1)} collective-permute-done((f32[80,128]{1,0:T(8,128)S(1)}, f32[80,128]{1,0:T(8,128)S(1)}, u32[]{:S(2)}, u32[]{:S(2)}) %collective-permute-start.7) | collective-permute-done | bytes 40992 | tf_op jit(solution)/shard_map/ppermute | solution.py:308
  92.6 1.9 %collective-permute-start.11 = (f32[80,128]{1,0:T(8,128)S(1)}, f32[80,128]{1,0:T(8,128)S(1)}, u32[]{:S(2)}, u32[]{:S(2)}) collective-permute-start(f32[80,128]{1,0:T(8,128)S(1)} %get-tuple-element.46), channel_id=1, source_target_pairs={{0,6},{1,7},{2,4},{3,5},{4,2},{5,3},{6,0},{7,1},{8,14},{9,15},{10,... | collective-permute-start | bytes 122888 | tf_op jit(solution)/shard_map/ppermute | solution.py:308
  94.4 4.0 %collective-permute-done.11.own_3 = f32[80,128]{1,0:T(8,128)S(1)} collective-permute-done((f32[80,128]{1,0:T(8,128)S(1)}, f32[80,128]{1,0:T(8,128)S(1)}, u32[]{:S(2)}, u32[]{:S(2)}) %collective-permute-start.11) | collective-permute-done | bytes 40992 | tf_op jit(solution)/shard_map/ppermute | solution.py:308
  98.5 0.1 collective-permute-start.12
  98.6 1.3 %collective-permute-done.12.other_ref = f32[160,128]{1,0:T(8,128)S(1)} collective-permute-done((f32[160,128]{1,0:T(8,128)S(1)}, f32[160,128]{1,0:T(8,128)S(1)}, u32[]{:S(2)}, u32[]{:S(2)}) %collective-permute-start.12) | collective-permute-done | bytes 81952 | tf_op jit(solution)/shard_map/ppermute | solution.py:308
  99.8 0.0 collective-permute-done.13.refs_4_.refs_1_
  99.8 0.0 collective-permute-done.14.refs_3_.refs_2_
  99.9 1.6 %collective-permute-start.16 = (bf16[1040,256]{1,0:T(8,128)(2,1)S(1)}, bf16[1040,256]{1,0:T(8,128)(2,1)S(1)}, u32[]{:S(2)}, u32[]{:S(2)}) collective-permute-start(bf16[1040,256]{1,0:T(8,128)(2,1)S(1)} %slice.45), channel_id=1, source_target_pairs={{0,8},{8,0},{16,24},{24,16},{1,9},{9,1},{17,25},{25,17},{2,10},{10... | collective-permute-start | bytes 1597448 | tf_op jit(solution)/shard_map/ppermute | solution.py:308
  101.5 1.5 %collective-permute-start.15 = (bf16[1040,256]{1,0:T(8,128)(2,1)S(1)}, bf16[1040,256]{1,0:T(8,128)(2,1)S(1)}, u32[]{:S(2)}, u32[]{:S(2)}) collective-permute-start(bf16[1040,256]{1,0:T(8,128)(2,1)S(1)} %slice.44), channel_id=1, source_target_pairs={{0,16},{8,24},{16,0},{24,8},{1,17},{9,25},{17,1},{25,9},{2,18},{10... | collective-permute-start | bytes 1597448 | tf_op jit(solution)/shard_map/ppermute | solution.py:308
  103.0 1.4 %gradients.2 = (f32[512,1536]{1,0:T(8,128)S(1)}, f32[768,512]{1,0:T(8,128)S(1)}) custom-call(bf16[1040,256]{1,0:T(8,128)(2,1)S(1)} %get-tuple-element.56.refs_0_, bf16[1232,256]{1,0:T(8,128)(2,1)S(1)} %collective-permute-done.6.refs_8_.refs_1_, bf16[1168,256]{1,0:T(8,128)(2,1)S(1)} %collective-permute-done.5.refs_7_.refs_2_, ...), custom_call_target="tpu_custom_call" | custom-call | flops 1000 | bytes 1000 | tf_op jit(solution)/shard_map/gradients/pallas_call | solution.py:263
  104.5 0.0 collective-permute-done.17.refs_6_
  104.5 0.0 collective-permute-done.18.refs_7_
  104.5 0.6 collective-permute-start.20
  105.1 0.6 collective-permute-start.19
  105.7 0.0 copy-done.5
  105.7 0.6 prob_gradients.1
  106.3 13.6 %collective-permute-done.19.refs_8_ = bf16[416,256]{1,0:T(8,128)(2,1)S(1)} collective-permute-done((bf16[416,256]{1,0:T(8,128)(2,1)S(1)}, bf16[416,256]{1,0:T(8,128)(2,1)S(1)}, u32[]{:S(2)}, u32[]{:S(2)}) %collective-permute-start.19) | collective-permute-done | bytes 213024 | tf_op jit(solution)/shard_map/ppermute | solution.py:308
  119.9 1.1 collective-permute-done.20.refs_9_
  121.0 0.0 collective-permute-done.16.refs_4_
  121.0 0.0 collective-permute-done.15.refs_3_
  121.0 3.6 %gradients.3 = (bf16[512,1536]{1,0:T(8,128)(2,1)}, bf16[768,512]{1,0:T(8,128)(2,1)}) custom-call(bf16[2080,256]{1,0:T(8,128)(2,1)S(1)} %get-tuple-element.48.refs_0_, bf16[2816,256]{1,0:T(8,128)(2,1)S(1)} %collective-permute-done.13.refs_4_.refs_1_, bf16[3024,256]{1,0:T(8,128)(2,1)S(1)} %collective-permute-done.14.refs_3_.refs_2_, ...), custom_call_target="tpu_custom_call" | custom-call | flops 1000 | bytes 1000 | tf_op jit(solution)/shard_map/gradients/pallas_call | solution.py:263
  (16 shorter events, 0.2 us)
Async XLA Ops:
  0.6 0.7 copy-start.4
  1.3 1.0 copy-start.6
  2.4 1.0 copy-start.7
  3.4 0.7 copy-start.8
  5.0 33.0 %collective-permute-start.3 = (bf16[80,4096]{1,0:T(8,128)(2,1)S(1)}, bf16[80,4096]{1,0:T(8,128)(2,1)S(1)}, u32[]{:S(2)}, u32[]{:S(2)}) collective-permute-start(bf16[80,4096]{1,0:T(8,128)(2,1)S(1)} %get-tuple-element.37), channel_id=1, source_target_pairs={{0,4},{1,5},{2,6},{3,7},{4,0},{5,1},{6,2},{7,3},{8,12},{9,13},{10,... | collective-permute-start | bytes 1966088 | tf_op jit(solution)/shard_map/ppermute | solution.py:308
  9.1 29.1 %collective-permute-start.1 = (bf16[80,4096]{1,0:T(8,128)(2,1)S(1)}, bf16[80,4096]{1,0:T(8,128)(2,1)S(1)}, u32[]{:S(2)}, u32[]{:S(2)}) collective-permute-start(bf16[80,4096]{1,0:T(8,128)(2,1)S(1)} %get-tuple-element.35), channel_id=1, source_target_pairs={{0,2},{1,3},{2,0},{3,1},{4,6},{5,7},{6,4},{7,5},{8,10},{9,11},{10,... | collective-permute-start | bytes 1966088 | tf_op jit(solution)/shard_map/ppermute | solution.py:308
  10.7 1.7 %collective-permute-start = (bf16[40,4096]{1,0:T(8,128)(2,1)S(1)}, bf16[40,4096]{1,0:T(8,128)(2,1)S(1)}, u32[]{:S(2)}, u32[]{:S(2)}) collective-permute-start(bf16[40,4096]{1,0:T(8,128)(2,1)S(1)} %slice.36), channel_id=1, source_target_pairs={{0,1},{1,0},{2,3},{3,2},{4,5},{5,4},{6,7},{7,6},{8,9},{9,8},{10,11... | collective-permute-start | bytes 983048 | tf_op jit(solution)/shard_map/ppermute | solution.py:308
  12.4 2.8 %copy-start = (bf16[1,2048,1536]{2,1,0:T(8,128)(2,1)S(1)}, bf16[1,2048,1536]{2,1,0:T(8,128)(2,1)}, u32[]{:S(2)}) copy-start(bf16[1,2048,1536]{2,1,0:T(8,128)(2,1)} %param.10) | copy-start | bytes 18874372
  15.2 1.9 %copy-start.2 = (bf16[1,768,2048]{2,1,0:T(8,128)(2,1)S(1)}, bf16[1,768,2048]{2,1,0:T(8,128)(2,1)}, u32[]{:S(2)}) copy-start(bf16[1,768,2048]{2,1,0:T(8,128)(2,1)} %param.11) | copy-start | bytes 9437188
  17.1 23.3 %copy-start.1 = (bf16[1,2048,1536]{2,1,0:T(8,128)(2,1)S(1)}, bf16[1,2048,1536]{2,1,0:T(8,128)(2,1)}, u32[]{:S(2)}) copy-start(bf16[1,2048,1536]{2,1,0:T(8,128)(2,1)} %param.10) | copy-start | bytes 18874372
  17.1 23.3 %copy-start.3 = (bf16[1,768,2048]{2,1,0:T(8,128)(2,1)S(1)}, bf16[1,768,2048]{2,1,0:T(8,128)(2,1)}, u32[]{:S(2)}) copy-start(bf16[1,768,2048]{2,1,0:T(8,128)(2,1)} %param.11) | copy-start | bytes 9437188
  20.7 18.2 %collective-permute-start.6 = (bf16[1232,256]{1,0:T(8,128)(2,1)S(1)}, bf16[1232,256]{1,0:T(8,128)(2,1)S(1)}, u32[]{:S(2)}, u32[]{:S(2)}) collective-permute-start(bf16[1232,256]{1,0:T(8,128)(2,1)S(1)} %get-tuple-element.40), channel_id=1, source_target_pairs={{0,8},{8,0},{16,24},{24,16},{1,9},{9,1},{17,25},{25,17},{2,10},{10... | collective-permute-start | bytes 1892360 | tf_op jit(solution)/shard_map/ppermute | solution.py:308
  22.3 16.6 %collective-permute-start.5 = (bf16[1168,256]{1,0:T(8,128)(2,1)S(1)}, bf16[1168,256]{1,0:T(8,128)(2,1)S(1)}, u32[]{:S(2)}, u32[]{:S(2)}) collective-permute-start(bf16[1168,256]{1,0:T(8,128)(2,1)S(1)} %get-tuple-element.39), channel_id=1, source_target_pairs={{0,16},{8,24},{16,0},{24,8},{1,17},{9,25},{17,1},{25,9},{2,18},{10... | collective-permute-start | bytes 1794056 | tf_op jit(solution)/shard_map/ppermute | solution.py:308
  38.3 1.7 %collective-permute-start.4 = (bf16[40,4096]{1,0:T(8,128)(2,1)S(1)}, bf16[40,4096]{1,0:T(8,128)(2,1)S(1)}, u32[]{:S(2)}, u32[]{:S(2)}) collective-permute-start(bf16[40,4096]{1,0:T(8,128)(2,1)S(1)} %slice.38), channel_id=1, source_target_pairs={{0,1},{1,0},{2,3},{3,2},{4,5},{5,4},{6,7},{7,6},{8,9},{9,8},{10,11... | collective-permute-start | bytes 983048 | tf_op jit(solution)/shard_map/ppermute | solution.py:308
  38.4 2.1 %collective-permute-start.2 = (bf16[40,4096]{1,0:T(8,128)(2,1)S(1)}, bf16[40,4096]{1,0:T(8,128)(2,1)S(1)}, u32[]{:S(2)}, u32[]{:S(2)}) collective-permute-start(bf16[40,4096]{1,0:T(8,128)(2,1)S(1)} %slice.37), channel_id=1, source_target_pairs={{0,1},{1,0},{2,3},{3,2},{4,5},{5,4},{6,7},{7,6},{8,9},{9,8},{10,11... | collective-permute-start | bytes 983048 | tf_op jit(solution)/shard_map/ppermute | solution.py:308
  44.4 55.4 %collective-permute-start.14 = (bf16[3024,256]{1,0:T(8,128)(2,1)S(1)}, bf16[3024,256]{1,0:T(8,128)(2,1)S(1)}, u32[]{:S(2)}, u32[]{:S(2)}) collective-permute-start(bf16[3024,256]{1,0:T(8,128)(2,1)S(1)} %get-tuple-element.50), channel_id=1, source_target_pairs={{0,16},{8,24},{16,0},{24,8},{1,17},{9,25},{17,1},{25,9},{2,18},{10... | collective-permute-start | bytes 4644872 | tf_op jit(solution)/shard_map/ppermute | solution.py:308
  46.1 53.8 %collective-permute-start.13 = (bf16[2816,256]{1,0:T(8,128)(2,1)S(1)}, bf16[2816,256]{1,0:T(8,128)(2,1)S(1)}, u32[]{:S(2)}, u32[]{:S(2)}) collective-permute-start(bf16[2816,256]{1,0:T(8,128)(2,1)S(1)} %get-tuple-element.49), channel_id=1, source_target_pairs={{0,8},{8,0},{16,24},{24,16},{1,9},{9,1},{17,25},{25,17},{2,10},{10... | collective-permute-start | bytes 4325384 | tf_op jit(solution)/shard_map/ppermute | solution.py:308
  47.6 18.1 %collective-permute-start.9 = (bf16[80,4096]{1,0:T(8,128)(2,1)S(1)}, bf16[80,4096]{1,0:T(8,128)(2,1)S(1)}, u32[]{:S(2)}, u32[]{:S(2)}) collective-permute-start(bf16[80,4096]{1,0:T(8,128)(2,1)S(1)} %get-tuple-element.44), channel_id=1, source_target_pairs={{0,6},{1,7},{2,4},{3,5},{4,2},{5,3},{6,0},{7,1},{8,14},{9,15},{10,... | collective-permute-start | bytes 1966088 | tf_op jit(solution)/shard_map/ppermute | solution.py:308
  65.7 1.7 %collective-permute-start.10 = (bf16[40,4096]{1,0:T(8,128)(2,1)S(1)}, bf16[40,4096]{1,0:T(8,128)(2,1)S(1)}, u32[]{:S(2)}, u32[]{:S(2)}) collective-permute-start(bf16[40,4096]{1,0:T(8,128)(2,1)S(1)} %slice.39), channel_id=1, source_target_pairs={{0,1},{1,0},{2,3},{3,2},{4,5},{5,4},{6,7},{7,6},{8,9},{9,8},{10,11... | collective-permute-start | bytes 983048 | tf_op jit(solution)/shard_map/ppermute | solution.py:308
  71.0 33.5 %collective-permute-start.18 = (bf16[1232,256]{1,0:T(8,128)(2,1)S(1)}, bf16[1232,256]{1,0:T(8,128)(2,1)S(1)}, u32[]{:S(2)}, u32[]{:S(2)}) collective-permute-start(bf16[1232,256]{1,0:T(8,128)(2,1)S(1)} %get-tuple-element.55), channel_id=1, source_target_pairs={{0,16},{8,24},{16,0},{24,8},{1,17},{9,25},{17,1},{25,9},{2,18},{10... | collective-permute-start | bytes 1892360 | tf_op jit(solution)/shard_map/ppermute | solution.py:308
  71.6 32.9 %collective-permute-start.17 = (bf16[1168,256]{1,0:T(8,128)(2,1)S(1)}, bf16[1168,256]{1,0:T(8,128)(2,1)S(1)}, u32[]{:S(2)}, u32[]{:S(2)}) collective-permute-start(bf16[1168,256]{1,0:T(8,128)(2,1)S(1)} %get-tuple-element.54), channel_id=1, source_target_pairs={{0,8},{8,0},{16,24},{24,16},{1,9},{9,1},{17,25},{25,17},{2,10},{10... | collective-permute-start | bytes 1794056 | tf_op jit(solution)/shard_map/ppermute | solution.py:308
  72.0 15.5 %collective-permute-start.8 = (f32[80,128]{1,0:T(8,128)S(1)}, f32[80,128]{1,0:T(8,128)S(1)}, u32[]{:S(2)}, u32[]{:S(2)}) collective-permute-start(f32[80,128]{1,0:T(8,128)S(1)} %get-tuple-element.42), channel_id=1, source_target_pairs={{0,4},{1,5},{2,6},{3,7},{4,0},{5,1},{6,2},{7,3},{8,12},{9,13},{10,... | collective-permute-start | bytes 122888 | tf_op jit(solution)/shard_map/ppermute | solution.py:308
  87.5 5.0 %collective-permute-start.7 = (f32[80,128]{1,0:T(8,128)S(1)}, f32[80,128]{1,0:T(8,128)S(1)}, u32[]{:S(2)}, u32[]{:S(2)}) collective-permute-start(f32[80,128]{1,0:T(8,128)S(1)} %get-tuple-element.41), channel_id=1, source_target_pairs={{0,2},{1,3},{2,0},{3,1},{4,6},{5,7},{6,4},{7,5},{8,10},{9,11},{10,... | collective-permute-start | bytes 122888 | tf_op jit(solution)/shard_map/ppermute | solution.py:308
  92.6 5.9 %collective-permute-start.11 = (f32[80,128]{1,0:T(8,128)S(1)}, f32[80,128]{1,0:T(8,128)S(1)}, u32[]{:S(2)}, u32[]{:S(2)}) collective-permute-start(f32[80,128]{1,0:T(8,128)S(1)} %get-tuple-element.46), channel_id=1, source_target_pairs={{0,6},{1,7},{2,4},{3,5},{4,2},{5,3},{6,0},{7,1},{8,14},{9,15},{10,... | collective-permute-start | bytes 122888 | tf_op jit(solution)/shard_map/ppermute | solution.py:308
  98.5 1.3 %collective-permute-start.12 = (f32[160,128]{1,0:T(8,128)S(1)}, f32[160,128]{1,0:T(8,128)S(1)}, u32[]{:S(2)}, u32[]{:S(2)}) collective-permute-start(f32[160,128]{1,0:T(8,128)S(1)} %pad_maximum_fusion), channel_id=1, source_target_pairs={{0,1},{1,0},{2,3},{3,2},{4,5},{5,4},{6,7},{7,6},{8,9},{9,8},{10,11... | collective-permute-start | bytes 245768 | tf_op jit(solution)/shard_map/ppermute | solution.py:308
  99.9 21.1 %collective-permute-start.16 = (bf16[1040,256]{1,0:T(8,128)(2,1)S(1)}, bf16[1040,256]{1,0:T(8,128)(2,1)S(1)}, u32[]{:S(2)}, u32[]{:S(2)}) collective-permute-start(bf16[1040,256]{1,0:T(8,128)(2,1)S(1)} %slice.45), channel_id=1, source_target_pairs={{0,8},{8,0},{16,24},{24,16},{1,9},{9,1},{17,25},{25,17},{2,10},{10... | collective-permute-start | bytes 1597448 | tf_op jit(solution)/shard_map/ppermute | solution.py:308
  101.5 19.5 %collective-permute-start.15 = (bf16[1040,256]{1,0:T(8,128)(2,1)S(1)}, bf16[1040,256]{1,0:T(8,128)(2,1)S(1)}, u32[]{:S(2)}, u32[]{:S(2)}) collective-permute-start(bf16[1040,256]{1,0:T(8,128)(2,1)S(1)} %slice.44), channel_id=1, source_target_pairs={{0,16},{8,24},{16,0},{24,8},{1,17},{9,25},{17,1},{25,9},{2,18},{10... | collective-permute-start | bytes 1597448 | tf_op jit(solution)/shard_map/ppermute | solution.py:308
  103.0 2.7 %copy-start.5 = (f32[128,2]{0,1:T(2,128)S(1)}, f32[128,2]{0,1:T(2,128)}, u32[]{:S(2)}) copy-start(f32[128,2]{0,1:T(2,128)} %param.8) | copy-start | bytes 3076
  104.5 16.5 %collective-permute-start.20 = (bf16[624,256]{1,0:T(8,128)(2,1)S(1)}, bf16[624,256]{1,0:T(8,128)(2,1)S(1)}, u32[]{:S(2)}, u32[]{:S(2)}) collective-permute-start(bf16[624,256]{1,0:T(8,128)(2,1)S(1)} %slice.47), channel_id=1, source_target_pairs={{0,8},{8,0},{16,24},{24,16},{1,9},{9,1},{17,25},{25,17},{2,10},{10... | collective-permute-start | bytes 958472 | tf_op jit(solution)/shard_map/ppermute | solution.py:308
  105.1 14.8 %collective-permute-start.19 = (bf16[416,256]{1,0:T(8,128)(2,1)S(1)}, bf16[416,256]{1,0:T(8,128)(2,1)S(1)}, u32[]{:S(2)}, u32[]{:S(2)}) collective-permute-start(bf16[416,256]{1,0:T(8,128)(2,1)S(1)} %slice.46), channel_id=1, source_target_pairs={{0,16},{8,24},{16,0},{24,8},{1,17},{9,25},{17,1},{25,9},{2,18},{10... | collective-permute-start | bytes 638984 | tf_op jit(solution)/shard_map/ppermute | solution.py:308

commit v5 on v4

--- a/solution.py
+++ b/solution.py
@@ -323,52 +323,51 @@
     *local, slots = dispatch_rows(ids, probs, tokens, cotangent)
     weights = (gate_up[0], down[0])
     _, _, cut_x0, cut_y0, _ = split_rows(PAIR, 48, half)
-    _, _, cut_x1, cut_y1, sizes = split_rows(2 * PAIR, PAIR, half)
-    _, _, cut_x2, cut_y2, _ = split_rows(PAIR, 32, half)
+    _, _, cut_x1, cut_y1, _ = split_rows(2 * PAIR, PAIR, half)
+    _, _, cut_x2, cut_y2, sizes = split_rows(PAIR, 32, half)
 
     def other_core(rows):
-        return exchange(rows[CAP:], "expert", 1)
+        return exchange(rows, "expert", 1)
 
     def to_plane(to_x, to_y):
         return exchange(to_x, "dp", 1), exchange(to_y, "dp", 2)
 
     rows_1 = exchange(local[1], "expert", 2)
-    rows_2 = exchange(local[2], "expert", 4)
-    own_0, to_x, to_y, inner_0 = expert_rows((local[0], other_core(local[0])), *weights, 48)
+    rows_3 = exchange(local[3], "expert", 6)
+    own_0, to_x, to_y, inner_0 = expert_rows(
+        (local[0], other_core(local[0][CAP:])), *weights, 48
+    )
     got_x0, got_y0 = to_plane(to_x, to_y)
-    rows_1 = after(rows_1, inner_0)
-    rows_3 = exchange(after(local[3], rows_2), "expert", 6)
-    rows_2 = after(rows_2, inner_0)
-    own_1, to_x, to_y, inner_1, inner_2 = expert_rows(
-        (rows_1, other_core(rows_1), rows_2, other_core(rows_2)),
+    rows_2 = exchange(after(local[2], inner_0), "expert", 4)
+    rows_1, rows_3 = after((rows_1, rows_3), inner_0)
+    own_1, to_x, to_y, inner_1, inner_3 = expert_rows(
+        (rows_1, other_core(rows_1[CAP:]), rows_3, other_core(rows_3[CAP:])), *weights, PAIR
+    )
+    got_x1, got_y1 = to_plane(to_x, to_y)
+    back_1, back_3 = after((inner_1, inner_3), got_x0, got_y0)
+    inner_1, inner_3 = exchange(back_1, "expert", 2), exchange(back_3, "expert", 6)
+    rows_2 = after(rows_2, inner_1, inner_3)
+    own_2, to_x, to_y, inner_2 = expert_rows(
+        (rows_2, other_core(rows_2[CAP:])),
         *weights,
-        PAIR,
+        32,
         (got_y0, got_x0),
         (cut_y0, cut_x0),
     )
-    got_x1, got_y1 = to_plane(to_x, to_y)
-    rows_3 = after(rows_3, inner_1)
-    own_2, to_x, to_y, inner_3 = expert_rows((rows_3, other_core(rows_3)), *weights, 32)
     got_x2, got_y2 = to_plane(to_x, to_y)
-    returned = [inner_0] + [
-        exchange(part, "expert", 2 * n + 2)
-        for n, part in enumerate((inner_1, inner_2, inner_3))
-    ]
-    other = exchange(
-        jnp.concatenate([part[CAP:] for part in returned], axis=0), "expert", 1
-    )
-    got_x1, got_y1 = after((got_x1, got_y1), inner_3, other)
-    turn_1 = (got_y1[:cut_y1], got_x1[:cut_x1])
-    low_1, top_1 = to_plane(*turn_1)
+    got_x1, got_y1 = after((got_x1, got_y1), inner_2)
+    low_1, top_1 = to_plane(got_y1[:cut_y1], got_x1[:cut_x1])
+    returned = (inner_0, inner_1, exchange(inner_2, "expert", 4), inner_3)
+    other = other_core(jnp.concatenate([part[CAP:] for part in returned], axis=0))
+    grad_probs = prob_gradients(returned, other, slots, probs)
+    got_x2, got_y2 = after((got_x2, got_y2), other)
+    low_2, top_2 = to_plane(got_y2[:cut_y2], got_x2[:cut_x2])
     sums = gradients(
         ((PAIR, 48, sizes[1], sizes[0]),),
-        (own_0, got_x0, got_y0, got_y1, got_x1),
+        (own_0, got_x0, got_y0, got_y2, got_x2),
         half,
         quarter,
     )
-    grad_probs = prob_gradients(returned, other, slots, probs)
-    got_x2, got_y2 = after((got_x2, got_y2), *sums)
-    low_2, top_2 = to_plane(got_y2[:cut_y2], got_x2[:cut_x2])
     grad_gu, grad_down = gradients(
         ((2 * PAIR, PAIR, 0, 0), (PAIR, 32, 0, 0)),
         (own_1, got_x1, got_y1, top_1, low_1, own_2, got_x2, got_y2, top_2, low_2),

time: 125 us -> 129 us (1.032)
  the two profiles are of different devices: /device:TPU:0 before, /device:TPU:20 now
where the time goes in v5:
time: 129 us
  waiting for transfers between devices  86.7 us (67%)
  Pallas kernels  17.7 us (14%)
  starting transfers between devices  15.3 us (12%)
  local copies, waits for them, and re-layouts  8.33 us (6%)
    ppermute x21, waiting for transfers between devices, exchange(): return lax.ppermute(values, axis, [(n, n ^ mask) for n in range(size)])  86.7 us
    ppermute x21, starting transfers between devices, exchange(): return lax.ppermute(values, axis, [(n, n ^ mask) for n in range(size)])  15.3 us
    pallas_call x3, Pallas kernels, expert_rows(): pl.pallas_call(functools.partial(expert_kernel, pairs, top, tuple(relays)...  11.1 us
    unnamed x18, local copies, waits for them, and re-layouts  8.12 us
    pallas_call x2, Pallas kernels, gradients(): pl.pallas_call(functools.partial(gradient_kernel, chunks, half, len(sums)...  5.03 us
  transfers between devices with their start and end apart: 21, of which 15 were waited for; matrix products, arithmetic and copies ran while one was open for 0% of the time, Pallas kernels for 10%

profile of v5, /device:TPU:20, one launch (start us, length us, event | category | flops | bytes accessed | tf_op | source)
XLA Modules:
  0.0 128.9 jit_solution(8292025622410656676)
XLA Ops:
  0.6 0.0 copy-start.4
  0.6 0.7 copy-done.4
  1.3 0.0 copy-start.6
  1.3 1.0 copy-done.6
  2.4 0.0 copy-start.7
  2.4 1.0 copy-done.7
  3.4 0.0 copy-start.8
  3.4 0.7 copy-done.8
  4.1 1.0 dispatch_rows.1
  5.0 1.6 %collective-permute-start.1 = (bf16[80,4096]{1,0:T(8,128)(2,1)S(1)}, bf16[80,4096]{1,0:T(8,128)(2,1)S(1)}, u32[]{:S(2)}, u32[]{:S(2)}) collective-permute-start(bf16[80,4096]{1,0:T(8,128)(2,1)S(1)} %get-tuple-element.37), channel_id=1, source_target_pairs={{0,2},{1,3},{2,0},{3,1},{4,6},{5,7},{6,4},{7,5},{8,10},{9,11},{10,... | collective-permute-start | bytes 1966088 | tf_op jit(solution)/shard_map/ppermute | solution.py:308
  6.7 0.0 collective-permute-start.2
  6.7 0.1 collective-permute-start
  6.8 1.6 %collective-permute-done.refs_1_ = bf16[40,4096]{1,0:T(8,128)(2,1)S(1)} collective-permute-done((bf16[40,4096]{1,0:T(8,128)(2,1)S(1)}, bf16[40,4096]{1,0:T(8,128)(2,1)S(1)}, u32[]{:S(2)}, u32[]{:S(2)}) %collective-permute-start) | collective-permute-done | bytes 327712 | tf_op jit(solution)/shard_map/ppermute | solution.py:308
  8.4 0.0 copy-start
  8.4 2.8 %copy-done = bf16[1,2048,1536]{2,1,0:T(8,128)(2,1)S(1)} copy-done((bf16[1,2048,1536]{2,1,0:T(8,128)(2,1)S(1)}, bf16[1,2048,1536]{2,1,0:T(8,128)(2,1)}, u32[]{:S(2)}) %copy-start) | copy-done | bytes 6291480
  11.2 0.0 copy-start.2
  11.2 1.9 %copy-done.2 = bf16[1,768,2048]{2,1,0:T(8,128)(2,1)S(1)} copy-done((bf16[1,768,2048]{2,1,0:T(8,128)(2,1)S(1)}, bf16[1,768,2048]{2,1,0:T(8,128)(2,1)}, u32[]{:S(2)}) %copy-start.2) | copy-done | bytes 3145752
  13.1 3.6 %expert_rows.3 = (bf16[1040,256]{1,0:T(8,128)(2,1)S(1)}, bf16[1232,256]{1,0:T(8,128)(2,1)S(1)}, bf16[1168,256]{1,0:T(8,128)(2,1)S(1)}, f32[80,128]{1,0:T(8,128)S(1)}) custom-call(bf16[80,4096]{1,0:T(8,128)(2,1)S(1)} %get-tuple-element.35.refs_0_, bf16[40,4096]{1,0:T(8,128)(2,1)S(1)} %collective-permute-done.refs_1_, bf16[2048,1536]{1,0:T(8,128)(2,1)S(1)} %bitcast.7, ...), custom_call_target="tpu_custom_call" | custom-call | flops 1000 | bytes 1000 | tf_op jit(solution)/shard_map/expert_rows/pallas_call | solution.py:172
  16.7 1.6 %collective-permute-start.5 = (bf16[1232,256]{1,0:T(8,128)(2,1)S(1)}, bf16[1232,256]{1,0:T(8,128)(2,1)S(1)}, u32[]{:S(2)}, u32[]{:S(2)}) collective-permute-start(bf16[1232,256]{1,0:T(8,128)(2,1)S(1)} %get-tuple-element.43), channel_id=1, source_target_pairs={{0,8},{8,0},{16,24},{24,16},{1,9},{9,1},{17,25},{25,17},{2,10},{10... | collective-permute-start | bytes 1892360 | tf_op jit(solution)/shard_map/ppermute | solution.py:308
  18.2 2.8 %collective-permute-start.8 = (bf16[80,4096]{1,0:T(8,128)(2,1)S(1)}, bf16[80,4096]{1,0:T(8,128)(2,1)S(1)}, u32[]{:S(2)}, u32[]{:S(2)}) collective-permute-start(bf16[80,4096]{1,0:T(8,128)(2,1)S(1)} %get-tuple-element.47), channel_id=1, source_target_pairs={{0,4},{1,5},{2,6},{3,7},{4,0},{5,1},{6,2},{7,3},{8,12},{9,13},{10,... | collective-permute-start | bytes 1966088 | tf_op jit(solution)/shard_map/ppermute | solution.py:308
  21.0 0.5 collective-permute-start.6
  21.5 1.2 collective-permute-done.1.refs_0_
  22.7 29.7 %collective-permute-done.2.refs_2_ = bf16[80,4096]{1,0:T(8,128)(2,1)S(1)} collective-permute-done((bf16[80,4096]{1,0:T(8,128)(2,1)S(1)}, bf16[80,4096]{1,0:T(8,128)(2,1)S(1)}, u32[]{:S(2)}, u32[]{:S(2)}) %collective-permute-start.2) | collective-permute-done | bytes 655392 | tf_op jit(solution)/shard_map/ppermute | solution.py:308
  52.5 0.1 collective-permute-start.4
  52.6 0.5 collective-permute-start.3
  53.1 1.1 collective-permute-done.4.refs_3_
  54.2 0.5 collective-permute-done.3.refs_1_
  54.7 0.0 copy-done.1
  54.7 0.0 copy-done.3
  54.7 3.9 %expert_rows.4 = (bf16[2080,256]{1,0:T(8,128)(2,1)S(1)}, bf16[2400,256]{1,0:T(8,128)(2,1)S(1)}, bf16[2400,256]{1,0:T(8,128)(2,1)S(1)}, f32[80,128]{1,0:T(8,128)S(1)}, f32[80,128]{1,0:T(8,128)S(1)}) custom-call(bf16[80,4096]{1,0:T(8,128)(2,1)S(1)} %collective-permute-done.1.refs_0_, bf16[40,4096]{1,0:T(8,128)(2,1)S(1)} %collective-permute-done.3.refs_1_, ...), custom_call_target="tpu_custom_call" | custom-call | flops 1000 | bytes 1000 | tf_op jit(solution)/shard_map/expert_rows/pallas_call | solution.py:172
  58.6 1.6 %collective-permute-start.13 = (bf16[2400,256]{1,0:T(8,128)(2,1)S(1)}, bf16[2400,256]{1,0:T(8,128)(2,1)S(1)}, u32[]{:S(2)}, u32[]{:S(2)}) collective-permute-start(bf16[2400,256]{1,0:T(8,128)(2,1)S(1)} %get-tuple-element.53), channel_id=1, source_target_pairs={{0,8},{8,0},{16,24},{24,16},{1,9},{9,1},{17,25},{25,17},{2,10},{10... | collective-permute-start | bytes 3686408 | tf_op jit(solution)/shard_map/ppermute | solution.py:308
  60.1 0.5 collective-permute-start.14
  60.6 0.0 collective-permute-done.6.refs_5_.refs_2_
  60.6 0.0 collective-permute-done.5.refs_6_.refs_1_
  60.6 0.0 collective-permute-start.7
  60.6 0.1 collective-permute-start.9
  60.7 3.0 %collective-permute-done.8.refs_0_ = bf16[80,4096]{1,0:T(8,128)(2,1)S(1)} collective-permute-done((bf16[80,4096]{1,0:T(8,128)(2,1)S(1)}, bf16[80,4096]{1,0:T(8,128)(2,1)S(1)}, u32[]{:S(2)}, u32[]{:S(2)}) %collective-permute-start.8) | collective-permute-done | bytes 655392 | tf_op jit(solution)/shard_map/ppermute | solution.py:308
  63.7 1.6 %collective-permute-done.7.own_1 = f32[80,128]{1,0:T(8,128)S(1)} collective-permute-done((f32[80,128]{1,0:T(8,128)S(1)}, f32[80,128]{1,0:T(8,128)S(1)}, u32[]{:S(2)}, u32[]{:S(2)}) %collective-permute-start.7) | collective-permute-done | bytes 40992 | tf_op jit(solution)/shard_map/ppermute | solution.py:308
  65.3 1.0 collective-permute-done.9.own_3
  66.4 0.1 collective-permute-start.10
  66.5 1.6 %collective-permute-done.10.refs_1_ = bf16[40,4096]{1,0:T(8,128)(2,1)S(1)} collective-permute-done((bf16[40,4096]{1,0:T(8,128)(2,1)S(1)}, bf16[40,4096]{1,0:T(8,128)(2,1)S(1)}, u32[]{:S(2)}, u32[]{:S(2)}) %collective-permute-start.10) | collective-permute-done | bytes 327712 | tf_op jit(solution)/shard_map/ppermute | solution.py:308
  68.1 3.6 %expert_rows.5 = (bf16[1040,256]{1,0:T(8,128)(2,1)S(1)}, bf16[1584,256]{1,0:T(8,128)(2,1)S(1)}, bf16[1856,256]{1,0:T(8,128)(2,1)S(1)}, f32[80,128]{1,0:T(8,128)S(1)}) custom-call(bf16[80,4096]{1,0:T(8,128)(2,1)S(1)} %collective-permute-done.8.refs_0_, bf16[40,4096]{1,0:T(8,128)(2,1)S(1)} %collective-permute-done.10.refs_1_, bf16[2048,1536]{1,0:T(8,128)(2,1)S(1)} %bitcast.11, ...), custom_call_target="tpu_custom_call" | custom-call | flops 1000 | bytes 1000 | tf_op jit(solution)/shard_map/expert_rows/pallas_call | solution.py:172
  71.7 0.1 collective-permute-start.18
  71.8 2.0 %collective-permute-start.17 = (bf16[1584,256]{1,0:T(8,128)(2,1)S(1)}, bf16[1584,256]{1,0:T(8,128)(2,1)S(1)}, u32[]{:S(2)}, u32[]{:S(2)}) collective-permute-start(bf16[1584,256]{1,0:T(8,128)(2,1)S(1)} %get-tuple-element.58), channel_id=1, source_target_pairs={{0,8},{8,0},{16,24},{24,16},{1,9},{9,1},{17,25},{25,17},{2,10},{10... | collective-permute-start | bytes 2433032 | tf_op jit(solution)/shard_map/ppermute | solution.py:308
  73.8 1.6 %collective-permute-start.11 = (f32[80,128]{1,0:T(8,128)S(1)}, f32[80,128]{1,0:T(8,128)S(1)}, u32[]{:S(2)}, u32[]{:S(2)}) collective-permute-start(f32[80,128]{1,0:T(8,128)S(1)} %get-tuple-element.50), channel_id=1, source_target_pairs={{0,4},{1,5},{2,6},{3,7},{4,0},{5,1},{6,2},{7,3},{8,12},{9,13},{10,... | collective-permute-start | bytes 122888 | tf_op jit(solution)/shard_map/ppermute | solution.py:308
  75.3 13.2 %collective-permute-done.13.refs_1_ = bf16[2400,256]{1,0:T(8,128)(2,1)S(1)} collective-permute-done((bf16[2400,256]{1,0:T(8,128)(2,1)S(1)}, bf16[2400,256]{1,0:T(8,128)(2,1)S(1)}, u32[]{:S(2)}, u32[]{:S(2)}) %collective-permute-start.13) | collective-permute-done | bytes 1228832 | tf_op jit(solution)/shard_map/ppermute | solution.py:308
  88.5 1.5 %collective-permute-done.14.refs_2_ = bf16[2400,256]{1,0:T(8,128)(2,1)S(1)} collective-permute-done((bf16[2400,256]{1,0:T(8,128)(2,1)S(1)}, bf16[2400,256]{1,0:T(8,128)(2,1)S(1)}, u32[]{:S(2)}, u32[]{:S(2)}) %collective-permute-start.14) | collective-permute-done | bytes 1228832 | tf_op jit(solution)/shard_map/ppermute | solution.py:308
  90.1 0.6 collective-permute-start.16
  90.7 0.5 collective-permute-start.15
  91.2 0.0 collective-permute-done.11.own_2
  91.3 0.1 collective-permute-start.12
  91.3 1.3 collective-permute-done.12.other_ref
  92.6 13.3 %collective-permute-done.17.refs_4_.refs_6_ = bf16[1584,256]{1,0:T(8,128)(2,1)S(1)} collective-permute-done((bf16[1584,256]{1,0:T(8,128)(2,1)S(1)}, bf16[1584,256]{1,0:T(8,128)(2,1)S(1)}, u32[]{:S(2)}, u32[]{:S(2)}) %collective-permute-start.17) | collective-permute-done | bytes 811040 | tf_op jit(solution)/shard_map/ppermute | solution.py:308
  105.9 4.5 %collective-permute-done.18.refs_3_.refs_7_ = bf16[1856,256]{1,0:T(8,128)(2,1)S(1)} collective-permute-done((bf16[1856,256]{1,0:T(8,128)(2,1)S(1)}, bf16[1856,256]{1,0:T(8,128)(2,1)S(1)}, u32[]{:S(2)}, u32[]{:S(2)}) %collective-permute-start.18) | collective-permute-done | bytes 950304 | tf_op jit(solution)/shard_map/ppermute | solution.py:308
  110.4 0.6 collective-permute-start.20
  111.0 0.6 collective-permute-start.19
  111.6 0.0 copy-done.5
  111.6 0.6 prob_gradients.1
  112.2 1.4 %gradients.2 = (f32[512,1536]{1,0:T(8,128)S(1)}, f32[768,512]{1,0:T(8,128)S(1)}) custom-call(bf16[1040,256]{1,0:T(8,128)(2,1)S(1)} %get-tuple-element.62.refs_0_, bf16[1232,256]{1,0:T(8,128)(2,1)S(1)} %collective-permute-done.5.refs_6_.refs_1_, bf16[1168,256]{1,0:T(8,128)(2,1)S(1)} %collective-permute-done.6.refs_5_.refs_2_, ...), custom_call_target="tpu_custom_call" | custom-call | flops 1000 | bytes 1000 | tf_op jit(solution)/shard_map/gradients/pallas_call | solution.py:263
  113.7 11.6 %collective-permute-done.19.refs_8_ = bf16[416,256]{1,0:T(8,128)(2,1)S(1)} collective-permute-done((bf16[416,256]{1,0:T(8,128)(2,1)S(1)}, bf16[416,256]{1,0:T(8,128)(2,1)S(1)}, u32[]{:S(2)}, u32[]{:S(2)}) %collective-permute-start.19) | collective-permute-done | bytes 213024 | tf_op jit(solution)/shard_map/ppermute | solution.py:308
  125.3 0.0 collective-permute-done.20.refs_9_
  125.3 0.0 collective-permute-done.16.refs_4_
  125.3 0.0 collective-permute-done.15.refs_3_
  125.3 3.6 %gradients.3 = (bf16[512,1536]{1,0:T(8,128)(2,1)}, bf16[768,512]{1,0:T(8,128)(2,1)}) custom-call(bf16[2080,256]{1,0:T(8,128)(2,1)S(1)} %get-tuple-element.52.refs_0_, bf16[2400,256]{1,0:T(8,128)(2,1)S(1)} %collective-permute-done.13.refs_1_, bf16[2400,256]{1,0:T(8,128)(2,1)S(1)} %collective-permute-done.14.refs_2_, ...), custom_call_target="tpu_custom_call" | custom-call | flops 1000 | bytes 1000 | tf_op jit(solution)/shard_map/gradients/pallas_call | solution.py:263
  (16 shorter events, 0.2 us)
Async XLA Ops:
  0.6 0.7 copy-start.4
  1.3 1.0 copy-start.6
  2.4 1.0 copy-start.7
  3.4 0.7 copy-start.8
  5.0 17.7 %collective-permute-start.1 = (bf16[80,4096]{1,0:T(8,128)(2,1)S(1)}, bf16[80,4096]{1,0:T(8,128)(2,1)S(1)}, u32[]{:S(2)}, u32[]{:S(2)}) collective-permute-start(bf16[80,4096]{1,0:T(8,128)(2,1)S(1)} %get-tuple-element.37), channel_id=1, source_target_pairs={{0,2},{1,3},{2,0},{3,1},{4,6},{5,7},{6,4},{7,5},{8,10},{9,11},{10,... | collective-permute-start | bytes 1966088 | tf_op jit(solution)/shard_map/ppermute | solution.py:308
  6.7 45.8 %collective-permute-start.2 = (bf16[80,4096]{1,0:T(8,128)(2,1)S(1)}, bf16[80,4096]{1,0:T(8,128)(2,1)S(1)}, u32[]{:S(2)}, u32[]{:S(2)}) collective-permute-start(bf16[80,4096]{1,0:T(8,128)(2,1)S(1)} %get-tuple-element.38), channel_id=1, source_target_pairs={{0,6},{1,7},{2,4},{3,5},{4,2},{5,3},{6,0},{7,1},{8,14},{9,15},{10,... | collective-permute-start | bytes 1966088 | tf_op jit(solution)/shard_map/ppermute | solution.py:308
  6.7 1.7 %collective-permute-start = (bf16[40,4096]{1,0:T(8,128)(2,1)S(1)}, bf16[40,4096]{1,0:T(8,128)(2,1)S(1)}, u32[]{:S(2)}, u32[]{:S(2)}) collective-permute-start(bf16[40,4096]{1,0:T(8,128)(2,1)S(1)} %slice.36), channel_id=1, source_target_pairs={{0,1},{1,0},{2,3},{3,2},{4,5},{5,4},{6,7},{7,6},{8,9},{9,8},{10,11... | collective-permute-start | bytes 983048 | tf_op jit(solution)/shard_map/ppermute | solution.py:308
  8.4 2.8 %copy-start = (bf16[1,2048,1536]{2,1,0:T(8,128)(2,1)S(1)}, bf16[1,2048,1536]{2,1,0:T(8,128)(2,1)}, u32[]{:S(2)}) copy-start(bf16[1,2048,1536]{2,1,0:T(8,128)(2,1)} %param.10) | copy-start | bytes 18874372
  11.2 1.9 %copy-start.2 = (bf16[1,768,2048]{2,1,0:T(8,128)(2,1)S(1)}, bf16[1,768,2048]{2,1,0:T(8,128)(2,1)}, u32[]{:S(2)}) copy-start(bf16[1,768,2048]{2,1,0:T(8,128)(2,1)} %param.11) | copy-start | bytes 9437188
  13.1 41.6 %copy-start.1 = (bf16[1,2048,1536]{2,1,0:T(8,128)(2,1)S(1)}, bf16[1,2048,1536]{2,1,0:T(8,128)(2,1)}, u32[]{:S(2)}) copy-start(bf16[1,2048,1536]{2,1,0:T(8,128)(2,1)} %param.10) | copy-start | bytes 18874372
  13.1 41.6 %copy-start.3 = (bf16[1,768,2048]{2,1,0:T(8,128)(2,1)S(1)}, bf16[1,768,2048]{2,1,0:T(8,128)(2,1)}, u32[]{:S(2)}) copy-start(bf16[1,768,2048]{2,1,0:T(8,128)(2,1)} %param.11) | copy-start | bytes 9437188
  16.7 44.0 %collective-permute-start.5 = (bf16[1232,256]{1,0:T(8,128)(2,1)S(1)}, bf16[1232,256]{1,0:T(8,128)(2,1)S(1)}, u32[]{:S(2)}, u32[]{:S(2)}) collective-permute-start(bf16[1232,256]{1,0:T(8,128)(2,1)S(1)} %get-tuple-element.43), channel_id=1, source_target_pairs={{0,8},{8,0},{16,24},{24,16},{1,9},{9,1},{17,25},{25,17},{2,10},{10... | collective-permute-start | bytes 1892360 | tf_op jit(solution)/shard_map/ppermute | solution.py:308
  18.2 45.5 %collective-permute-start.8 = (bf16[80,4096]{1,0:T(8,128)(2,1)S(1)}, bf16[80,4096]{1,0:T(8,128)(2,1)S(1)}, u32[]{:S(2)}, u32[]{:S(2)}) collective-permute-start(bf16[80,4096]{1,0:T(8,128)(2,1)S(1)} %get-tuple-element.47), channel_id=1, source_target_pairs={{0,4},{1,5},{2,6},{3,7},{4,0},{5,1},{6,2},{7,3},{8,12},{9,13},{10,... | collective-permute-start | bytes 1966088 | tf_op jit(solution)/shard_map/ppermute | solution.py:308
  21.0 39.6 %collective-permute-start.6 = (bf16[1168,256]{1,0:T(8,128)(2,1)S(1)}, bf16[1168,256]{1,0:T(8,128)(2,1)S(1)}, u32[]{:S(2)}, u32[]{:S(2)}) collective-permute-start(bf16[1168,256]{1,0:T(8,128)(2,1)S(1)} %get-tuple-element.44), channel_id=1, source_target_pairs={{0,16},{8,24},{16,0},{24,8},{1,17},{9,25},{17,1},{25,9},{2,18},{10... | collective-permute-start | bytes 1794056 | tf_op jit(solution)/shard_map/ppermute | solution.py:308
  52.5 1.7 %collective-permute-start.4 = (bf16[40,4096]{1,0:T(8,128)(2,1)S(1)}, bf16[40,4096]{1,0:T(8,128)(2,1)S(1)}, u32[]{:S(2)}, u32[]{:S(2)}) collective-permute-start(bf16[40,4096]{1,0:T(8,128)(2,1)S(1)} %slice.38), channel_id=1, source_target_pairs={{0,1},{1,0},{2,3},{3,2},{4,5},{5,4},{6,7},{7,6},{8,9},{9,8},{10,11... | collective-permute-start | bytes 983048 | tf_op jit(solution)/shard_map/ppermute | solution.py:308
  52.6 2.1 %collective-permute-start.3 = (bf16[40,4096]{1,0:T(8,128)(2,1)S(1)}, bf16[40,4096]{1,0:T(8,128)(2,1)S(1)}, u32[]{:S(2)}, u32[]{:S(2)}) collective-permute-start(bf16[40,4096]{1,0:T(8,128)(2,1)S(1)} %slice.37), channel_id=1, source_target_pairs={{0,1},{1,0},{2,3},{3,2},{4,5},{5,4},{6,7},{7,6},{8,9},{9,8},{10,11... | collective-permute-start | bytes 983048 | tf_op jit(solution)/shard_map/ppermute | solution.py:308
  58.6 29.9 %collective-permute-start.13 = (bf16[2400,256]{1,0:T(8,128)(2,1)S(1)}, bf16[2400,256]{1,0:T(8,128)(2,1)S(1)}, u32[]{:S(2)}, u32[]{:S(2)}) collective-permute-start(bf16[2400,256]{1,0:T(8,128)(2,1)S(1)} %get-tuple-element.53), channel_id=1, source_target_pairs={{0,8},{8,0},{16,24},{24,16},{1,9},{9,1},{17,25},{25,17},{2,10},{10... | collective-permute-start | bytes 3686408 | tf_op jit(solution)/shard_map/ppermute | solution.py:308
  60.1 29.9 %collective-permute-start.14 = (bf16[2400,256]{1,0:T(8,128)(2,1)S(1)}, bf16[2400,256]{1,0:T(8,128)(2,1)S(1)}, u32[]{:S(2)}, u32[]{:S(2)}) collective-permute-start(bf16[2400,256]{1,0:T(8,128)(2,1)S(1)} %get-tuple-element.54), channel_id=1, source_target_pairs={{0,16},{8,24},{16,0},{24,8},{1,17},{9,25},{17,1},{25,9},{2,18},{10... | collective-permute-start | bytes 3686408 | tf_op jit(solution)/shard_map/ppermute | solution.py:308
  60.6 4.7 %collective-permute-start.7 = (f32[80,128]{1,0:T(8,128)S(1)}, f32[80,128]{1,0:T(8,128)S(1)}, u32[]{:S(2)}, u32[]{:S(2)}) collective-permute-start(f32[80,128]{1,0:T(8,128)S(1)} %get-tuple-element.45), channel_id=1, source_target_pairs={{0,2},{1,3},{2,0},{3,1},{4,6},{5,7},{6,4},{7,5},{8,10},{9,11},{10,... | collective-permute-start | bytes 122888 | tf_op jit(solution)/shard_map/ppermute | solution.py:308
  60.6 5.7 %collective-permute-start.9 = (f32[80,128]{1,0:T(8,128)S(1)}, f32[80,128]{1,0:T(8,128)S(1)}, u32[]{:S(2)}, u32[]{:S(2)}) collective-permute-start(f32[80,128]{1,0:T(8,128)S(1)} %get-tuple-element.48), channel_id=1, source_target_pairs={{0,6},{1,7},{2,4},{3,5},{4,2},{5,3},{6,0},{7,1},{8,14},{9,15},{10,... | collective-permute-start | bytes 122888 | tf_op jit(solution)/shard_map/ppermute | solution.py:308
  66.4 1.7 %collective-permute-start.10 = (bf16[40,4096]{1,0:T(8,128)(2,1)S(1)}, bf16[40,4096]{1,0:T(8,128)(2,1)S(1)}, u32[]{:S(2)}, u32[]{:S(2)}) collective-permute-start(bf16[40,4096]{1,0:T(8,128)(2,1)S(1)} %slice.39), channel_id=1, source_target_pairs={{0,1},{1,0},{2,3},{3,2},{4,5},{5,4},{6,7},{7,6},{8,9},{9,8},{10,11... | collective-permute-start | bytes 983048 | tf_op jit(solution)/shard_map/ppermute | solution.py:308
  71.7 38.7 %collective-permute-start.18 = (bf16[1856,256]{1,0:T(8,128)(2,1)S(1)}, bf16[1856,256]{1,0:T(8,128)(2,1)S(1)}, u32[]{:S(2)}, u32[]{:S(2)}) collective-permute-start(bf16[1856,256]{1,0:T(8,128)(2,1)S(1)} %get-tuple-element.59), channel_id=1, source_target_pairs={{0,16},{8,24},{16,0},{24,8},{1,17},{9,25},{17,1},{25,9},{2,18},{10... | collective-permute-start | bytes 2850824 | tf_op jit(solution)/shard_map/ppermute | solution.py:308
  71.8 34.1 %collective-permute-start.17 = (bf16[1584,256]{1,0:T(8,128)(2,1)S(1)}, bf16[1584,256]{1,0:T(8,128)(2,1)S(1)}, u32[]{:S(2)}, u32[]{:S(2)}) collective-permute-start(bf16[1584,256]{1,0:T(8,128)(2,1)S(1)} %get-tuple-element.58), channel_id=1, source_target_pairs={{0,8},{8,0},{16,24},{24,16},{1,9},{9,1},{17,25},{25,17},{2,10},{10... | collective-permute-start | bytes 2433032 | tf_op jit(solution)/shard_map/ppermute | solution.py:308
  73.8 37.9 %copy-start.5 = (f32[128,2]{0,1:T(2,128)S(1)}, f32[128,2]{0,1:T(2,128)}, u32[]{:S(2)}) copy-start(f32[128,2]{0,1:T(2,128)} %param.8) | copy-start | bytes 3076
  73.8 17.5 %collective-permute-start.11 = (f32[80,128]{1,0:T(8,128)S(1)}, f32[80,128]{1,0:T(8,128)S(1)}, u32[]{:S(2)}, u32[]{:S(2)}) collective-permute-start(f32[80,128]{1,0:T(8,128)S(1)} %get-tuple-element.50), channel_id=1, source_target_pairs={{0,4},{1,5},{2,6},{3,7},{4,0},{5,1},{6,2},{7,3},{8,12},{9,13},{10,... | collective-permute-start | bytes 122888 | tf_op jit(solution)/shard_map/ppermute | solution.py:308
  90.1 35.1 %collective-permute-start.16 = (bf16[1040,256]{1,0:T(8,128)(2,1)S(1)}, bf16[1040,256]{1,0:T(8,128)(2,1)S(1)}, u32[]{:S(2)}, u32[]{:S(2)}) collective-permute-start(bf16[1040,256]{1,0:T(8,128)(2,1)S(1)} %slice.45), channel_id=1, source_target_pairs={{0,8},{8,0},{16,24},{24,16},{1,9},{9,1},{17,25},{25,17},{2,10},{10... | collective-permute-start | bytes 1597448 | tf_op jit(solution)/shard_map/ppermute | solution.py:308
  90.7 34.6 %collective-permute-start.15 = (bf16[1040,256]{1,0:T(8,128)(2,1)S(1)}, bf16[1040,256]{1,0:T(8,128)(2,1)S(1)}, u32[]{:S(2)}, u32[]{:S(2)}) collective-permute-start(bf16[1040,256]{1,0:T(8,128)(2,1)S(1)} %slice.44), channel_id=1, source_target_pairs={{0,16},{8,24},{16,0},{24,8},{1,17},{9,25},{17,1},{25,9},{2,18},{10... | collective-permute-start | bytes 1597448 | tf_op jit(solution)/shard_map/ppermute | solution.py:308
  91.3 1.3 %collective-permute-start.12 = (f32[160,128]{1,0:T(8,128)S(1)}, f32[160,128]{1,0:T(8,128)S(1)}, u32[]{:S(2)}, u32[]{:S(2)}) collective-permute-start(f32[160,128]{1,0:T(8,128)S(1)} %pad_maximum_fusion), channel_id=1, source_target_pairs={{0,1},{1,0},{2,3},{3,2},{4,5},{5,4},{6,7},{7,6},{8,9},{9,8},{10,11... | collective-permute-start | bytes 245768 | tf_op jit(solution)/shard_map/ppermute | solution.py:308
  110.4 14.8 %collective-permute-start.20 = (bf16[624,256]{1,0:T(8,128)(2,1)S(1)}, bf16[624,256]{1,0:T(8,128)(2,1)S(1)}, u32[]{:S(2)}, u32[]{:S(2)}) collective-permute-start(bf16[624,256]{1,0:T(8,128)(2,1)S(1)} %slice.47), channel_id=1, source_target_pairs={{0,8},{8,0},{16,24},{24,16},{1,9},{9,1},{17,25},{25,17},{2,10},{10... | collective-permute-start | bytes 958472 | tf_op jit(solution)/shard_map/ppermute | solution.py:308
  111.0 14.2 %collective-permute-start.19 = (bf16[416,256]{1,0:T(8,128)(2,1)S(1)}, bf16[416,256]{1,0:T(8,128)(2,1)S(1)}, u32[]{:S(2)}, u32[]{:S(2)}) collective-permute-start(bf16[416,256]{1,0:T(8,128)(2,1)S(1)} %slice.46), channel_id=1, source_target_pairs={{0,16},{8,24},{16,0},{24,8},{1,17},{9,25},{17,1},{25,9},{2,18},{10... | collective-permute-start | bytes 638984 | tf_op jit(solution)/shard_map/ppermute | solution.py:308

commit v6 on v5

--- a/solution.py
+++ b/solution.py
@@ -324,7 +324,7 @@
     weights = (gate_up[0], down[0])
     _, _, cut_x0, cut_y0, _ = split_rows(PAIR, 48, half)
     _, _, cut_x1, cut_y1, _ = split_rows(2 * PAIR, PAIR, half)
-    _, _, cut_x2, cut_y2, sizes = split_rows(PAIR, 32, half)
+    _, _, cut_x2, cut_y2, _ = split_rows(PAIR, 32, half)
 
     def other_core(rows):
         return exchange(rows, "expert", 1)
@@ -333,41 +333,36 @@
         return exchange(to_x, "dp", 1), exchange(to_y, "dp", 2)
 
     rows_1 = exchange(local[1], "expert", 2)
-    rows_3 = exchange(local[3], "expert", 6)
+    rows_2 = exchange(local[2], "expert", 4)
     own_0, to_x, to_y, inner_0 = expert_rows(
         (local[0], other_core(local[0][CAP:])), *weights, 48
     )
     got_x0, got_y0 = to_plane(to_x, to_y)
-    rows_2 = exchange(after(local[2], inner_0), "expert", 4)
-    rows_1, rows_3 = after((rows_1, rows_3), inner_0)
-    own_1, to_x, to_y, inner_1, inner_3 = expert_rows(
-        (rows_1, other_core(rows_1[CAP:]), rows_3, other_core(rows_3[CAP:])), *weights, PAIR
-    )
-    got_x1, got_y1 = to_plane(to_x, to_y)
-    back_1, back_3 = after((inner_1, inner_3), got_x0, got_y0)
-    inner_1, inner_3 = exchange(back_1, "expert", 2), exchange(back_3, "expert", 6)
-    rows_2 = after(rows_2, inner_1, inner_3)
-    own_2, to_x, to_y, inner_2 = expert_rows(
-        (rows_2, other_core(rows_2[CAP:])),
-        *weights,
-        32,
-        (got_y0, got_x0),
-        (cut_y0, cut_x0),
+    low_0, top_0 = to_plane(got_y0[:cut_y0], got_x0[:cut_x0])
+    rows_1, rows_2 = after((rows_1, rows_2), inner_0)
+    other_1, other_2 = other_core(rows_1[CAP:]), other_core(rows_2[CAP:])
+    rows_3 = exchange(after(local[3], rows_2), "expert", 6)
+    own_1, to_x, to_y, inner_1, inner_2 = expert_rows(
+        (rows_1, other_1, rows_2, other_2), *weights, PAIR
+    )
+    got_x1, got_y1 = to_plane(*after((to_x, to_y), low_0, top_0))
+    sums = gradients(
+        ((PAIR, 48, 0, 0),), (own_0, got_x0, got_y0, top_0, low_0), half, quarter
+    )
+    back_1, back_2 = after((inner_1, inner_2), *sums)
+    inner_1, inner_2 = exchange(back_1, "expert", 2), exchange(back_2, "expert", 4)
+    rows_3 = after(rows_3, inner_1, inner_2)
+    own_2, to_x, to_y, inner_3 = expert_rows(
+        (rows_3, other_core(rows_3[CAP:])), *weights, 32
     )
     got_x2, got_y2 = to_plane(to_x, to_y)
-    got_x1, got_y1 = after((got_x1, got_y1), inner_2)
+    got_x1, got_y1 = after((got_x1, got_y1), inner_3)
     low_1, top_1 = to_plane(got_y1[:cut_y1], got_x1[:cut_x1])
-    returned = (inner_0, inner_1, exchange(inner_2, "expert", 4), inner_3)
+    returned = (inner_0, inner_1, inner_2, exchange(inner_3, "expert", 6))
     other = other_core(jnp.concatenate([part[CAP:] for part in returned], axis=0))
     grad_probs = prob_gradients(returned, other, slots, probs)
     got_x2, got_y2 = after((got_x2, got_y2), other)
     low_2, top_2 = to_plane(got_y2[:cut_y2], got_x2[:cut_x2])
-    sums = gradients(
-        ((PAIR, 48, sizes[1], sizes[0]),),
-        (own_0, got_x0, got_y0, got_y2, got_x2),
-        half,
-        quarter,
-    )
     grad_gu, grad_down = gradients(
         ((2 * PAIR, PAIR, 0, 0), (PAIR, 32, 0, 0)),
         (own_1, got_x1, got_y1, top_1, low_1, own_2, got_x2, got_y2, top_2, low_2),

time: 129 us -> 119 us (0.922)
  the two profiles are of different devices: /device:TPU:20 before, /device:TPU:0 now
where the time goes in v6:
time: 119 us
  waiting for transfers between devices  63 us (53%)
  starting transfers between devices  28.8 us (24%)
  Pallas kernels  17.7 us (15%)
  local copies, waits for them, and re-layouts  8.37 us (7%)
    ppermute x23, waiting for transfers between devices, exchange(): return lax.ppermute(values, axis, [(n, n ^ mask) for n in range(size)])  63 us
    ppermute x23, starting transfers between devices, exchange(): return lax.ppermute(values, axis, [(n, n ^ mask) for n in range(size)])  28.8 us
    pallas_call x3, Pallas kernels, expert_rows(): pl.pallas_call(functools.partial(expert_kernel, pairs, top, tuple(relays)...  11.1 us
    unnamed x18, local copies, waits for them, and re-layouts  8.12 us
    pallas_call x2, Pallas kernels, gradients(): pl.pallas_call(functools.partial(gradient_kernel, chunks, half, len(sums)...  5.03 us
  transfers between devices with their start and end apart: 23, of which 11 were waited for; matrix products, arithmetic and copies ran while one was open for 0% of the time, Pallas kernels for 11%

profile of v6, /device:TPU:0, one launch (start us, length us, event | category | flops | bytes accessed | tf_op | source)
XLA Modules:
  0.0 118.7 jit_solution(16733731718507948608)
XLA Ops:
  0.6 0.0 copy-start.4
  0.6 0.7 copy-done.4
  1.3 0.0 copy-start.6
  1.3 1.0 copy-done.6
  2.4 1.0 copy-done.7
  3.4 0.7 copy-done.8
  4.1 1.0 dispatch_rows.1
  5.1 0.5 collective-permute-start
  5.6 2.7 %collective-permute-start.1 = (bf16[80,4096]{1,0:T(8,128)(2,1)S(1)}, bf16[80,4096]{1,0:T(8,128)(2,1)S(1)}, u32[]{:S(2)}, u32[]{:S(2)}) collective-permute-start(bf16[80,4096]{1,0:T(8,128)(2,1)S(1)} %get-tuple-element.39), channel_id=1, source_target_pairs={{0,2},{1,3},{2,0},{3,1},{4,6},{5,7},{6,4},{7,5},{8,10},{9,11},{10,... | collective-permute-start | bytes 1966088 | tf_op jit(solution)/shard_map/ppermute | solution.py:308
  8.2 2.6 %collective-permute-start.2 = (bf16[80,4096]{1,0:T(8,128)(2,1)S(1)}, bf16[80,4096]{1,0:T(8,128)(2,1)S(1)}, u32[]{:S(2)}, u32[]{:S(2)}) collective-permute-start(bf16[80,4096]{1,0:T(8,128)(2,1)S(1)} %get-tuple-element.40), channel_id=1, source_target_pairs={{0,4},{1,5},{2,6},{3,7},{4,0},{5,1},{6,2},{7,3},{8,12},{9,13},{10,... | collective-permute-start | bytes 1966088 | tf_op jit(solution)/shard_map/ppermute | solution.py:308
  10.8 0.0 collective-permute-done.refs_1_
  10.8 2.8 %copy-done = bf16[1,2048,1536]{2,1,0:T(8,128)(2,1)S(1)} copy-done((bf16[1,2048,1536]{2,1,0:T(8,128)(2,1)S(1)}, bf16[1,2048,1536]{2,1,0:T(8,128)(2,1)}, u32[]{:S(2)}) %copy-start) | copy-done | bytes 6291480
  13.6 1.9 %copy-done.2 = bf16[1,768,2048]{2,1,0:T(8,128)(2,1)S(1)} copy-done((bf16[1,768,2048]{2,1,0:T(8,128)(2,1)S(1)}, bf16[1,768,2048]{2,1,0:T(8,128)(2,1)}, u32[]{:S(2)}) %copy-start.2) | copy-done | bytes 3145752
  15.5 3.6 %expert_rows.3 = (bf16[1040,256]{1,0:T(8,128)(2,1)S(1)}, bf16[1232,256]{1,0:T(8,128)(2,1)S(1)}, bf16[1168,256]{1,0:T(8,128)(2,1)S(1)}, f32[80,128]{1,0:T(8,128)S(1)}) custom-call(bf16[80,4096]{1,0:T(8,128)(2,1)S(1)} %get-tuple-element.37.refs_0_, bf16[40,4096]{1,0:T(8,128)(2,1)S(1)} %collective-permute-done.refs_1_, bf16[2048,1536]{1,0:T(8,128)(2,1)S(1)} %bitcast.7, ...), custom_call_target="tpu_custom_call" | custom-call | flops 1000 | bytes 1000 | tf_op jit(solution)/shard_map/expert_rows/pallas_call | solution.py:172
  19.1 1.6 %collective-permute-start.5 = (bf16[1232,256]{1,0:T(8,128)(2,1)S(1)}, bf16[1232,256]{1,0:T(8,128)(2,1)S(1)}, u32[]{:S(2)}, u32[]{:S(2)}) collective-permute-start(bf16[1232,256]{1,0:T(8,128)(2,1)S(1)} %get-tuple-element.46), channel_id=1, source_target_pairs={{0,8},{8,0},{16,24},{24,16},{1,9},{9,1},{17,25},{25,17},{2,10},{10... | collective-permute-start | bytes 1892360 | tf_op jit(solution)/shard_map/ppermute | solution.py:308
  20.7 1.5 %collective-permute-start.6 = (bf16[1168,256]{1,0:T(8,128)(2,1)S(1)}, bf16[1168,256]{1,0:T(8,128)(2,1)S(1)}, u32[]{:S(2)}, u32[]{:S(2)}) collective-permute-start(bf16[1168,256]{1,0:T(8,128)(2,1)S(1)} %get-tuple-element.47), channel_id=1, source_target_pairs={{0,16},{8,24},{16,0},{24,8},{1,17},{9,25},{17,1},{25,9},{2,18},{10... | collective-permute-start | bytes 1794056 | tf_op jit(solution)/shard_map/ppermute | solution.py:308
  22.2 15.3 %collective-permute-done.1.refs_0_ = bf16[80,4096]{1,0:T(8,128)(2,1)S(1)} collective-permute-done((bf16[80,4096]{1,0:T(8,128)(2,1)S(1)}, bf16[80,4096]{1,0:T(8,128)(2,1)S(1)}, u32[]{:S(2)}, u32[]{:S(2)}) %collective-permute-start.1) | collective-permute-done | bytes 655392 | tf_op jit(solution)/shard_map/ppermute | solution.py:308
  37.5 2.5 %collective-permute-done.2.refs_2_ = bf16[80,4096]{1,0:T(8,128)(2,1)S(1)} collective-permute-done((bf16[80,4096]{1,0:T(8,128)(2,1)S(1)}, bf16[80,4096]{1,0:T(8,128)(2,1)S(1)}, u32[]{:S(2)}, u32[]{:S(2)}) %collective-permute-start.2) | collective-permute-done | bytes 655392 | tf_op jit(solution)/shard_map/ppermute | solution.py:308
  40.1 0.1 collective-permute-start.4
  40.2 0.5 collective-permute-start.3
  40.7 0.0 collective-permute-done.5.refs_1_
  40.7 1.6 %collective-permute-start.7 = (bf16[624,256]{1,0:T(8,128)(2,1)S(1)}, bf16[624,256]{1,0:T(8,128)(2,1)S(1)}, u32[]{:S(2)}, u32[]{:S(2)}) collective-permute-start(bf16[624,256]{1,0:T(8,128)(2,1)S(1)} %slice.56), channel_id=1, source_target_pairs={{0,16},{8,24},{16,0},{24,8},{1,17},{9,25},{17,1},{25,9},{2,18},{10... | collective-permute-start | bytes 958472 | tf_op jit(solution)/shard_map/ppermute | solution.py:308
  42.3 0.0 collective-permute-done.6.refs_2_
  42.3 1.6 %collective-permute-start.8 = (bf16[416,256]{1,0:T(8,128)(2,1)S(1)}, bf16[416,256]{1,0:T(8,128)(2,1)S(1)}, u32[]{:S(2)}, u32[]{:S(2)}) collective-permute-start(bf16[416,256]{1,0:T(8,128)(2,1)S(1)} %slice.57), channel_id=1, source_target_pairs={{0,8},{8,0},{16,24},{24,16},{1,9},{9,1},{17,25},{25,17},{2,10},{10... | collective-permute-start | bytes 638984 | tf_op jit(solution)/shard_map/ppermute | solution.py:308
  43.9 2.5 %collective-permute-start.11 = (bf16[80,4096]{1,0:T(8,128)(2,1)S(1)}, bf16[80,4096]{1,0:T(8,128)(2,1)S(1)}, u32[]{:S(2)}, u32[]{:S(2)}) collective-permute-start(bf16[80,4096]{1,0:T(8,128)(2,1)S(1)} %get-tuple-element.53), channel_id=1, source_target_pairs={{0,6},{1,7},{2,4},{3,5},{4,2},{5,3},{6,0},{7,1},{8,14},{9,15},{10,... | collective-permute-start | bytes 1966088 | tf_op jit(solution)/shard_map/ppermute | solution.py:308
  46.3 0.0 collective-permute-done.4.refs_3_
  46.3 0.0 collective-permute-done.3.refs_1_
  46.3 0.0 copy-done.1
  46.4 0.0 copy-done.3
  46.4 3.9 %expert_rows.4 = (bf16[2080,256]{1,0:T(8,128)(2,1)S(1)}, bf16[2400,256]{1,0:T(8,128)(2,1)S(1)}, bf16[2400,256]{1,0:T(8,128)(2,1)S(1)}, f32[80,128]{1,0:T(8,128)S(1)}, f32[80,128]{1,0:T(8,128)S(1)}) custom-call(bf16[80,4096]{1,0:T(8,128)(2,1)S(1)} %collective-permute-done.1.refs_0_, bf16[40,4096]{1,0:T(8,128)(2,1)S(1)} %collective-permute-done.3.refs_1_, ...), custom_call_target="tpu_custom_call" | custom-call | flops 1000 | bytes 1000 | tf_op jit(solution)/shard_map/expert_rows/pallas_call | solution.py:172
  50.3 0.0 collective-permute-done.8.refs_4_
  50.3 0.0 collective-permute-done.7.refs_3_
  50.3 1.5 %collective-permute-start.15 = (bf16[2400,256]{1,0:T(8,128)(2,1)S(1)}, bf16[2400,256]{1,0:T(8,128)(2,1)S(1)}, u32[]{:S(2)}, u32[]{:S(2)}) collective-permute-start(bf16[2400,256]{1,0:T(8,128)(2,1)S(1)} %get-tuple-element.60), channel_id=1, source_target_pairs={{0,8},{8,0},{16,24},{24,16},{1,9},{9,1},{17,25},{25,17},{2,10},{10... | collective-permute-start | bytes 3686408 | tf_op jit(solution)/shard_map/ppermute | solution.py:308
  51.8 1.5 %collective-permute-start.16 = (bf16[2400,256]{1,0:T(8,128)(2,1)S(1)}, bf16[2400,256]{1,0:T(8,128)(2,1)S(1)}, u32[]{:S(2)}, u32[]{:S(2)}) collective-permute-start(bf16[2400,256]{1,0:T(8,128)(2,1)S(1)} %get-tuple-element.61), channel_id=1, source_target_pairs={{0,16},{8,24},{16,0},{24,8},{1,17},{9,25},{17,1},{25,9},{2,18},{10... | collective-permute-start | bytes 3686408 | tf_op jit(solution)/shard_map/ppermute | solution.py:308
  53.3 1.4 %gradients.2 = (f32[512,1536]{1,0:T(8,128)S(1)}, f32[768,512]{1,0:T(8,128)S(1)}) custom-call(bf16[1040,256]{1,0:T(8,128)(2,1)S(1)} %get-tuple-element.45.refs_0_, bf16[1232,256]{1,0:T(8,128)(2,1)S(1)} %collective-permute-done.5.refs_1_, bf16[1168,256]{1,0:T(8,128)(2,1)S(1)} %collective-permute-done.6.refs_2_, ...), custom_call_target="tpu_custom_call" | custom-call | flops 1000 | bytes 1000 | tf_op jit(solution)/shard_map/gradients/pallas_call | solution.py:263
  54.8 0.5 collective-permute-start.9
  55.3 2.6 %collective-permute-start.10 = (f32[80,128]{1,0:T(8,128)S(1)}, f32[80,128]{1,0:T(8,128)S(1)}, u32[]{:S(2)}, u32[]{:S(2)}) collective-permute-start(f32[80,128]{1,0:T(8,128)S(1)} %get-tuple-element.51), channel_id=1, source_target_pairs={{0,4},{1,5},{2,6},{3,7},{4,0},{5,1},{6,2},{7,3},{8,12},{9,13},{10,... | collective-permute-start | bytes 122888 | tf_op jit(solution)/shard_map/ppermute | solution.py:308
  57.9 5.0 %collective-permute-done.11.refs_0_ = bf16[80,4096]{1,0:T(8,128)(2,1)S(1)} collective-permute-done((bf16[80,4096]{1,0:T(8,128)(2,1)S(1)}, bf16[80,4096]{1,0:T(8,128)(2,1)S(1)}, u32[]{:S(2)}, u32[]{:S(2)}) %collective-permute-start.11) | collective-permute-done | bytes 655392 | tf_op jit(solution)/shard_map/ppermute | solution.py:308
  62.8 0.0 collective-permute-done.9.own_1
  62.8 12.9 %collective-permute-done.10.own_2 = f32[80,128]{1,0:T(8,128)S(1)} collective-permute-done((f32[80,128]{1,0:T(8,128)S(1)}, f32[80,128]{1,0:T(8,128)S(1)}, u32[]{:S(2)}, u32[]{:S(2)}) %collective-permute-start.10) | collective-permute-done | bytes 40992 | tf_op jit(solution)/shard_map/ppermute | solution.py:308
  75.7 0.1 collective-permute-start.12
  75.8 1.6 %collective-permute-done.12.refs_1_ = bf16[40,4096]{1,0:T(8,128)(2,1)S(1)} collective-permute-done((bf16[40,4096]{1,0:T(8,128)(2,1)S(1)}, bf16[40,4096]{1,0:T(8,128)(2,1)S(1)}, u32[]{:S(2)}, u32[]{:S(2)}) %collective-permute-start.12) | collective-permute-done | bytes 327712 | tf_op jit(solution)/shard_map/ppermute | solution.py:308
  77.4 3.6 %expert_rows.5 = (bf16[1040,256]{1,0:T(8,128)(2,1)S(1)}, bf16[1168,256]{1,0:T(8,128)(2,1)S(1)}, bf16[1232,256]{1,0:T(8,128)(2,1)S(1)}, f32[80,128]{1,0:T(8,128)S(1)}) custom-call(bf16[80,4096]{1,0:T(8,128)(2,1)S(1)} %collective-permute-done.11.refs_0_, bf16[40,4096]{1,0:T(8,128)(2,1)S(1)} %collective-permute-done.12.refs_1_, ...), custom_call_target="tpu_custom_call" | custom-call | flops 1000 | bytes 1000 | tf_op jit(solution)/shard_map/expert_rows/pallas_call | solution.py:172
  81.0 0.6 collective-permute-start.20
  81.6 0.5 collective-permute-start.19
  82.1 1.4 %collective-permute-start.13 = (f32[80,128]{1,0:T(8,128)S(1)}, f32[80,128]{1,0:T(8,128)S(1)}, u32[]{:S(2)}, u32[]{:S(2)}) collective-permute-start(f32[80,128]{1,0:T(8,128)S(1)} %get-tuple-element.55), channel_id=1, source_target_pairs={{0,6},{1,7},{2,4},{3,5},{4,2},{5,3},{6,0},{7,1},{8,14},{9,15},{10,... | collective-permute-start | bytes 122888 | tf_op jit(solution)/shard_map/ppermute | solution.py:308
  83.5 0.0 collective-permute-done.15.refs_1_
  83.5 0.0 collective-permute-done.16.refs_2_
  83.6 1.6 %collective-permute-start.18 = (bf16[1040,256]{1,0:T(8,128)(2,1)S(1)}, bf16[1040,256]{1,0:T(8,128)(2,1)S(1)}, u32[]{:S(2)}, u32[]{:S(2)}) collective-permute-start(bf16[1040,256]{1,0:T(8,128)(2,1)S(1)} %slice.53), channel_id=1, source_target_pairs={{0,8},{8,0},{16,24},{24,16},{1,9},{9,1},{17,25},{25,17},{2,10},{10... | collective-permute-start | bytes 1597448 | tf_op jit(solution)/shard_map/ppermute | solution.py:308
  85.1 1.5 %collective-permute-start.17 = (bf16[1040,256]{1,0:T(8,128)(2,1)S(1)}, bf16[1040,256]{1,0:T(8,128)(2,1)S(1)}, u32[]{:S(2)}, u32[]{:S(2)}) collective-permute-start(bf16[1040,256]{1,0:T(8,128)(2,1)S(1)} %slice.52), channel_id=1, source_target_pairs={{0,16},{8,24},{16,0},{24,8},{1,17},{9,25},{17,1},{25,9},{2,18},{10... | collective-permute-start | bytes 1597448 | tf_op jit(solution)/shard_map/ppermute | solution.py:308
  86.6 1.3 %collective-permute-done.13.own_3 = f32[80,128]{1,0:T(8,128)S(1)} collective-permute-done((f32[80,128]{1,0:T(8,128)S(1)}, f32[80,128]{1,0:T(8,128)S(1)}, u32[]{:S(2)}, u32[]{:S(2)}) %collective-permute-start.13) | collective-permute-done | bytes 40992 | tf_op jit(solution)/shard_map/ppermute | solution.py:308
  87.9 0.1 collective-permute-start.14
  88.0 1.3 %collective-permute-done.14.other_ref = f32[160,128]{1,0:T(8,128)S(1)} collective-permute-done((f32[160,128]{1,0:T(8,128)S(1)}, f32[160,128]{1,0:T(8,128)S(1)}, u32[]{:S(2)}, u32[]{:S(2)}) %collective-permute-start.14) | collective-permute-done | bytes 81952 | tf_op jit(solution)/shard_map/ppermute | solution.py:308
  89.3 8.7 %collective-permute-done.19.refs_6_ = bf16[1168,256]{1,0:T(8,128)(2,1)S(1)} collective-permute-done((bf16[1168,256]{1,0:T(8,128)(2,1)S(1)}, bf16[1168,256]{1,0:T(8,128)(2,1)S(1)}, u32[]{:S(2)}, u32[]{:S(2)}) %collective-permute-start.19) | collective-permute-done | bytes 598048 | tf_op jit(solution)/shard_map/ppermute | solution.py:308
  98.0 0.2 collective-permute-done.20.refs_7_
  98.2 0.6 collective-permute-start.22
  98.8 1.4 %collective-permute-start.21 = (bf16[416,256]{1,0:T(8,128)(2,1)S(1)}, bf16[416,256]{1,0:T(8,128)(2,1)S(1)}, u32[]{:S(2)}, u32[]{:S(2)}) collective-permute-start(bf16[416,256]{1,0:T(8,128)(2,1)S(1)} %slice.54), channel_id=1, source_target_pairs={{0,16},{8,24},{16,0},{24,8},{1,17},{9,25},{17,1},{25,9},{2,18},{10... | collective-permute-start | bytes 638984 | tf_op jit(solution)/shard_map/ppermute | solution.py:308
  100.2 0.0 copy-done.5
  100.2 0.6 prob_gradients.1
  100.8 12.5 %collective-permute-done.21.refs_8_ = bf16[416,256]{1,0:T(8,128)(2,1)S(1)} collective-permute-done((bf16[416,256]{1,0:T(8,128)(2,1)S(1)}, bf16[416,256]{1,0:T(8,128)(2,1)S(1)}, u32[]{:S(2)}, u32[]{:S(2)}) %collective-permute-start.21) | collective-permute-done | bytes 213024 | tf_op jit(solution)/shard_map/ppermute | solution.py:308
  113.3 1.8 %collective-permute-done.22.refs_9_ = bf16[624,256]{1,0:T(8,128)(2,1)S(1)} collective-permute-done((bf16[624,256]{1,0:T(8,128)(2,1)S(1)}, bf16[624,256]{1,0:T(8,128)(2,1)S(1)}, u32[]{:S(2)}, u32[]{:S(2)}) %collective-permute-start.22) | collective-permute-done | bytes 319520 | tf_op jit(solution)/shard_map/ppermute | solution.py:308
  115.1 0.0 collective-permute-done.18.refs_4_
  115.1 0.0 collective-permute-done.17.refs_3_
  115.1 3.6 %gradients.3 = (bf16[512,1536]{1,0:T(8,128)(2,1)}, bf16[768,512]{1,0:T(8,128)(2,1)}) custom-call(bf16[2080,256]{1,0:T(8,128)(2,1)S(1)} %get-tuple-element.57.refs_0_, bf16[2400,256]{1,0:T(8,128)(2,1)S(1)} %collective-permute-done.15.refs_1_, bf16[2400,256]{1,0:T(8,128)(2,1)S(1)} %collective-permute-done.16.refs_2_, ...), custom_call_target="tpu_custom_call" | custom-call | flops 1000 | bytes 1000 | tf_op jit(solution)/shard_map/gradients/pallas_call | solution.py:263
  (22 shorter events, 0.3 us)
Async XLA Ops:
  0.6 0.7 copy-start.4
  1.3 1.0 copy-start.6
  2.4 1.0 copy-start.7
  3.4 0.7 copy-start.8
  5.1 5.8 %collective-permute-start = (bf16[40,4096]{1,0:T(8,128)(2,1)S(1)}, bf16[40,4096]{1,0:T(8,128)(2,1)S(1)}, u32[]{:S(2)}, u32[]{:S(2)}) collective-permute-start(bf16[40,4096]{1,0:T(8,128)(2,1)S(1)} %slice.42), channel_id=1, source_target_pairs={{0,1},{1,0},{2,3},{3,2},{4,5},{5,4},{6,7},{7,6},{8,9},{9,8},{10,11... | collective-permute-start | bytes 983048 | tf_op jit(solution)/shard_map/ppermute | solution.py:308
  5.6 31.9 %collective-permute-start.1 = (bf16[80,4096]{1,0:T(8,128)(2,1)S(1)}, bf16[80,4096]{1,0:T(8,128)(2,1)S(1)}, u32[]{:S(2)}, u32[]{:S(2)}) collective-permute-start(bf16[80,4096]{1,0:T(8,128)(2,1)S(1)} %get-tuple-element.39), channel_id=1, source_target_pairs={{0,2},{1,3},{2,0},{3,1},{4,6},{5,7},{6,4},{7,5},{8,10},{9,11},{10,... | collective-permute-start | bytes 1966088 | tf_op jit(solution)/shard_map/ppermute | solution.py:308
  8.2 31.8 %collective-permute-start.2 = (bf16[80,4096]{1,0:T(8,128)(2,1)S(1)}, bf16[80,4096]{1,0:T(8,128)(2,1)S(1)}, u32[]{:S(2)}, u32[]{:S(2)}) collective-permute-start(bf16[80,4096]{1,0:T(8,128)(2,1)S(1)} %get-tuple-element.40), channel_id=1, source_target_pairs={{0,4},{1,5},{2,6},{3,7},{4,0},{5,1},{6,2},{7,3},{8,12},{9,13},{10,... | collective-permute-start | bytes 1966088 | tf_op jit(solution)/shard_map/ppermute | solution.py:308
  10.8 2.8 %copy-start = (bf16[1,2048,1536]{2,1,0:T(8,128)(2,1)S(1)}, bf16[1,2048,1536]{2,1,0:T(8,128)(2,1)}, u32[]{:S(2)}) copy-start(bf16[1,2048,1536]{2,1,0:T(8,128)(2,1)} %param.10) | copy-start | bytes 18874372
  13.6 1.9 %copy-start.2 = (bf16[1,768,2048]{2,1,0:T(8,128)(2,1)S(1)}, bf16[1,768,2048]{2,1,0:T(8,128)(2,1)}, u32[]{:S(2)}) copy-start(bf16[1,768,2048]{2,1,0:T(8,128)(2,1)} %param.11) | copy-start | bytes 9437188
  15.5 30.8 %copy-start.1 = (bf16[1,2048,1536]{2,1,0:T(8,128)(2,1)S(1)}, bf16[1,2048,1536]{2,1,0:T(8,128)(2,1)}, u32[]{:S(2)}) copy-start(bf16[1,2048,1536]{2,1,0:T(8,128)(2,1)} %param.10) | copy-start | bytes 18874372
  15.5 30.8 %copy-start.3 = (bf16[1,768,2048]{2,1,0:T(8,128)(2,1)S(1)}, bf16[1,768,2048]{2,1,0:T(8,128)(2,1)}, u32[]{:S(2)}) copy-start(bf16[1,768,2048]{2,1,0:T(8,128)(2,1)} %param.11) | copy-start | bytes 9437188
  19.1 21.6 %collective-permute-start.5 = (bf16[1232,256]{1,0:T(8,128)(2,1)S(1)}, bf16[1232,256]{1,0:T(8,128)(2,1)S(1)}, u32[]{:S(2)}, u32[]{:S(2)}) collective-permute-start(bf16[1232,256]{1,0:T(8,128)(2,1)S(1)} %get-tuple-element.46), channel_id=1, source_target_pairs={{0,8},{8,0},{16,24},{24,16},{1,9},{9,1},{17,25},{25,17},{2,10},{10... | collective-permute-start | bytes 1892360 | tf_op jit(solution)/shard_map/ppermute | solution.py:308
  20.7 21.6 %collective-permute-start.6 = (bf16[1168,256]{1,0:T(8,128)(2,1)S(1)}, bf16[1168,256]{1,0:T(8,128)(2,1)S(1)}, u32[]{:S(2)}, u32[]{:S(2)}) collective-permute-start(bf16[1168,256]{1,0:T(8,128)(2,1)S(1)} %get-tuple-element.47), channel_id=1, source_target_pairs={{0,16},{8,24},{16,0},{24,8},{1,17},{9,25},{17,1},{25,9},{2,18},{10... | collective-permute-start | bytes 1794056 | tf_op jit(solution)/shard_map/ppermute | solution.py:308
  40.1 6.2 %collective-permute-start.4 = (bf16[40,4096]{1,0:T(8,128)(2,1)S(1)}, bf16[40,4096]{1,0:T(8,128)(2,1)S(1)}, u32[]{:S(2)}, u32[]{:S(2)}) collective-permute-start(bf16[40,4096]{1,0:T(8,128)(2,1)S(1)} %slice.44), channel_id=1, source_target_pairs={{0,1},{1,0},{2,3},{3,2},{4,5},{5,4},{6,7},{7,6},{8,9},{9,8},{10,11... | collective-permute-start | bytes 983048 | tf_op jit(solution)/shard_map/ppermute | solution.py:308
  40.2 6.2 %collective-permute-start.3 = (bf16[40,4096]{1,0:T(8,128)(2,1)S(1)}, bf16[40,4096]{1,0:T(8,128)(2,1)S(1)}, u32[]{:S(2)}, u32[]{:S(2)}) collective-permute-start(bf16[40,4096]{1,0:T(8,128)(2,1)S(1)} %slice.43), channel_id=1, source_target_pairs={{0,1},{1,0},{2,3},{3,2},{4,5},{5,4},{6,7},{7,6},{8,9},{9,8},{10,11... | collective-permute-start | bytes 983048 | tf_op jit(solution)/shard_map/ppermute | solution.py:308
  40.7 9.6 %collective-permute-start.7 = (bf16[624,256]{1,0:T(8,128)(2,1)S(1)}, bf16[624,256]{1,0:T(8,128)(2,1)S(1)}, u32[]{:S(2)}, u32[]{:S(2)}) collective-permute-start(bf16[624,256]{1,0:T(8,128)(2,1)S(1)} %slice.56), channel_id=1, source_target_pairs={{0,16},{8,24},{16,0},{24,8},{1,17},{9,25},{17,1},{25,9},{2,18},{10... | collective-permute-start | bytes 958472 | tf_op jit(solution)/shard_map/ppermute | solution.py:308
  42.3 8.0 %collective-permute-start.8 = (bf16[416,256]{1,0:T(8,128)(2,1)S(1)}, bf16[416,256]{1,0:T(8,128)(2,1)S(1)}, u32[]{:S(2)}, u32[]{:S(2)}) collective-permute-start(bf16[416,256]{1,0:T(8,128)(2,1)S(1)} %slice.57), channel_id=1, source_target_pairs={{0,8},{8,0},{16,24},{24,16},{1,9},{9,1},{17,25},{25,17},{2,10},{10... | collective-permute-start | bytes 638984 | tf_op jit(solution)/shard_map/ppermute | solution.py:308
  43.9 19.0 %collective-permute-start.11 = (bf16[80,4096]{1,0:T(8,128)(2,1)S(1)}, bf16[80,4096]{1,0:T(8,128)(2,1)S(1)}, u32[]{:S(2)}, u32[]{:S(2)}) collective-permute-start(bf16[80,4096]{1,0:T(8,128)(2,1)S(1)} %get-tuple-element.53), channel_id=1, source_target_pairs={{0,6},{1,7},{2,4},{3,5},{4,2},{5,3},{6,0},{7,1},{8,14},{9,15},{10,... | collective-permute-start | bytes 1966088 | tf_op jit(solution)/shard_map/ppermute | solution.py:308
  50.3 33.2 %collective-permute-start.15 = (bf16[2400,256]{1,0:T(8,128)(2,1)S(1)}, bf16[2400,256]{1,0:T(8,128)(2,1)S(1)}, u32[]{:S(2)}, u32[]{:S(2)}) collective-permute-start(bf16[2400,256]{1,0:T(8,128)(2,1)S(1)} %get-tuple-element.60), channel_id=1, source_target_pairs={{0,8},{8,0},{16,24},{24,16},{1,9},{9,1},{17,25},{25,17},{2,10},{10... | collective-permute-start | bytes 3686408 | tf_op jit(solution)/shard_map/ppermute | solution.py:308
  51.8 31.7 %collective-permute-start.16 = (bf16[2400,256]{1,0:T(8,128)(2,1)S(1)}, bf16[2400,256]{1,0:T(8,128)(2,1)S(1)}, u32[]{:S(2)}, u32[]{:S(2)}) collective-permute-start(bf16[2400,256]{1,0:T(8,128)(2,1)S(1)} %get-tuple-element.61), channel_id=1, source_target_pairs={{0,16},{8,24},{16,0},{24,8},{1,17},{9,25},{17,1},{25,9},{2,18},{10... | collective-permute-start | bytes 3686408 | tf_op jit(solution)/shard_map/ppermute | solution.py:308
  54.8 8.1 %collective-permute-start.9 = (f32[80,128]{1,0:T(8,128)S(1)}, f32[80,128]{1,0:T(8,128)S(1)}, u32[]{:S(2)}, u32[]{:S(2)}) collective-permute-start(f32[80,128]{1,0:T(8,128)S(1)} %get-tuple-element.50), channel_id=1, source_target_pairs={{0,2},{1,3},{2,0},{3,1},{4,6},{5,7},{6,4},{7,5},{8,10},{9,11},{10,... | collective-permute-start | bytes 122888 | tf_op jit(solution)/shard_map/ppermute | solution.py:308
  55.3 20.5 %collective-permute-start.10 = (f32[80,128]{1,0:T(8,128)S(1)}, f32[80,128]{1,0:T(8,128)S(1)}, u32[]{:S(2)}, u32[]{:S(2)}) collective-permute-start(f32[80,128]{1,0:T(8,128)S(1)} %get-tuple-element.51), channel_id=1, source_target_pairs={{0,4},{1,5},{2,6},{3,7},{4,0},{5,1},{6,2},{7,3},{8,12},{9,13},{10,... | collective-permute-start | bytes 122888 | tf_op jit(solution)/shard_map/ppermute | solution.py:308
  75.7 1.7 %collective-permute-start.12 = (bf16[40,4096]{1,0:T(8,128)(2,1)S(1)}, bf16[40,4096]{1,0:T(8,128)(2,1)S(1)}, u32[]{:S(2)}, u32[]{:S(2)}) collective-permute-start(bf16[40,4096]{1,0:T(8,128)(2,1)S(1)} %slice.47), channel_id=1, source_target_pairs={{0,1},{1,0},{2,3},{3,2},{4,5},{5,4},{6,7},{7,6},{8,9},{9,8},{10,11... | collective-permute-start | bytes 983048 | tf_op jit(solution)/shard_map/ppermute | solution.py:308
  81.0 17.1 %collective-permute-start.20 = (bf16[1232,256]{1,0:T(8,128)(2,1)S(1)}, bf16[1232,256]{1,0:T(8,128)(2,1)S(1)}, u32[]{:S(2)}, u32[]{:S(2)}) collective-permute-start(bf16[1232,256]{1,0:T(8,128)(2,1)S(1)} %get-tuple-element.66), channel_id=1, source_target_pairs={{0,16},{8,24},{16,0},{24,8},{1,17},{9,25},{17,1},{25,9},{2,18},{10... | collective-permute-start | bytes 1892360 | tf_op jit(solution)/shard_map/ppermute | solution.py:308
  81.6 16.4 %collective-permute-start.19 = (bf16[1168,256]{1,0:T(8,128)(2,1)S(1)}, bf16[1168,256]{1,0:T(8,128)(2,1)S(1)}, u32[]{:S(2)}, u32[]{:S(2)}) collective-permute-start(bf16[1168,256]{1,0:T(8,128)(2,1)S(1)} %get-tuple-element.65), channel_id=1, source_target_pairs={{0,8},{8,0},{16,24},{24,16},{1,9},{9,1},{17,25},{25,17},{2,10},{10... | collective-permute-start | bytes 1794056 | tf_op jit(solution)/shard_map/ppermute | solution.py:308
  82.1 18.1 %copy-start.5 = (f32[128,2]{0,1:T(2,128)S(1)}, f32[128,2]{0,1:T(2,128)}, u32[]{:S(2)}) copy-start(f32[128,2]{0,1:T(2,128)} %param.8) | copy-start | bytes 3076
  82.1 5.8 %collective-permute-start.13 = (f32[80,128]{1,0:T(8,128)S(1)}, f32[80,128]{1,0:T(8,128)S(1)}, u32[]{:S(2)}, u32[]{:S(2)}) collective-permute-start(f32[80,128]{1,0:T(8,128)S(1)} %get-tuple-element.55), channel_id=1, source_target_pairs={{0,6},{1,7},{2,4},{3,5},{4,2},{5,3},{6,0},{7,1},{8,14},{9,15},{10,... | collective-permute-start | bytes 122888 | tf_op jit(solution)/shard_map/ppermute | solution.py:308
  83.6 31.5 %collective-permute-start.18 = (bf16[1040,256]{1,0:T(8,128)(2,1)S(1)}, bf16[1040,256]{1,0:T(8,128)(2,1)S(1)}, u32[]{:S(2)}, u32[]{:S(2)}) collective-permute-start(bf16[1040,256]{1,0:T(8,128)(2,1)S(1)} %slice.53), channel_id=1, source_target_pairs={{0,8},{8,0},{16,24},{24,16},{1,9},{9,1},{17,25},{25,17},{2,10},{10... | collective-permute-start | bytes 1597448 | tf_op jit(solution)/shard_map/ppermute | solution.py:308
  85.1 30.0 %collective-permute-start.17 = (bf16[1040,256]{1,0:T(8,128)(2,1)S(1)}, bf16[1040,256]{1,0:T(8,128)(2,1)S(1)}, u32[]{:S(2)}, u32[]{:S(2)}) collective-permute-start(bf16[1040,256]{1,0:T(8,128)(2,1)S(1)} %slice.52), channel_id=1, source_target_pairs={{0,16},{8,24},{16,0},{24,8},{1,17},{9,25},{17,1},{25,9},{2,18},{10... | collective-permute-start | bytes 1597448 | tf_op jit(solution)/shard_map/ppermute | solution.py:308
  87.9 1.3 %collective-permute-start.14 = (f32[160,128]{1,0:T(8,128)S(1)}, f32[160,128]{1,0:T(8,128)S(1)}, u32[]{:S(2)}, u32[]{:S(2)}) collective-permute-start(f32[160,128]{1,0:T(8,128)S(1)} %pad_maximum_fusion), channel_id=1, source_target_pairs={{0,1},{1,0},{2,3},{3,2},{4,5},{5,4},{6,7},{7,6},{8,9},{9,8},{10,11... | collective-permute-start | bytes 245768 | tf_op jit(solution)/shard_map/ppermute | solution.py:308
  98.2 16.9 %collective-permute-start.22 = (bf16[624,256]{1,0:T(8,128)(2,1)S(1)}, bf16[624,256]{1,0:T(8,128)(2,1)S(1)}, u32[]{:S(2)}, u32[]{:S(2)}) collective-permute-start(bf16[624,256]{1,0:T(8,128)(2,1)S(1)} %slice.55), channel_id=1, source_target_pairs={{0,8},{8,0},{16,24},{24,16},{1,9},{9,1},{17,25},{25,17},{2,10},{10... | collective-permute-start | bytes 958472 | tf_op jit(solution)/shard_map/ppermute | solution.py:308
  98.8 14.5 %collective-permute-start.21 = (bf16[416,256]{1,0:T(8,128)(2,1)S(1)}, bf16[416,256]{1,0:T(8,128)(2,1)S(1)}, u32[]{:S(2)}, u32[]{:S(2)}) collective-permute-start(bf16[416,256]{1,0:T(8,128)(2,1)S(1)} %slice.54), channel_id=1, source_target_pairs={{0,16},{8,24},{16,0},{24,8},{1,17},{9,25},{17,1},{25,9},{2,18},{10... | collective-permute-start | bytes 638984 | tf_op jit(solution)/shard_map/ppermute | solution.py:308

commit v7 on v6

--- a/solution.py
+++ b/solution.py
@@ -332,15 +332,15 @@
     def to_plane(to_x, to_y):
         return exchange(to_x, "dp", 1), exchange(to_y, "dp", 2)
 
+    rows_2 = exchange(local[2], "expert", 4)
     rows_1 = exchange(local[1], "expert", 2)
-    rows_2 = exchange(local[2], "expert", 4)
     own_0, to_x, to_y, inner_0 = expert_rows(
         (local[0], other_core(local[0][CAP:])), *weights, 48
     )
     got_x0, got_y0 = to_plane(to_x, to_y)
     low_0, top_0 = to_plane(got_y0[:cut_y0], got_x0[:cut_x0])
-    rows_1, rows_2 = after((rows_1, rows_2), inner_0)
-    other_1, other_2 = other_core(rows_1[CAP:]), other_core(rows_2[CAP:])
+    rows_2, rows_1 = after((rows_2, rows_1), inner_0)
+    other_2, other_1 = other_core(rows_2[CAP:]), other_core(rows_1[CAP:])
     rows_3 = exchange(after(local[3], rows_2), "expert", 6)
     own_1, to_x, to_y, inner_1, inner_2 = expert_rows(
         (rows_1, other_1, rows_2, other_2), *weights, PAIR
@@ -363,13 +363,11 @@
     grad_probs = prob_gradients(returned, other, slots, probs)
     got_x2, got_y2 = after((got_x2, got_y2), other)
     low_2, top_2 = to_plane(got_y2[:cut_y2], got_x2[:cut_x2])
+    sums = gradients(
+        ((2 * PAIR, PAIR, 0, 0),), (own_1, got_x1, got_y1, top_1, low_1), half, quarter, sums
+    )
     grad_gu, grad_down = gradients(
-        ((2 * PAIR, PAIR, 0, 0), (PAIR, 32, 0, 0)),
-        (own_1, got_x1, got_y1, top_1, low_1, own_2, got_x2, got_y2, top_2, low_2),
-        half,
-        quarter,
-        sums,
-        True,
+        ((PAIR, 32, 0, 0),), (own_2, got_x2, got_y2, top_2, low_2), half, quarter, sums, True
     )
     return (grad_probs.T, grad_gu[None], grad_down[None])
 

time: 119 us -> 118 us (level)
  waiting for transfers between devices: 63 us -> 60.1 us
    ppermute x23, waiting for transfers between devices: 63 us -> 60.1 us  [exchange(): return lax.ppermute(values, axis, [(n, n ^ mask) for n in range(size)])]
    pallas_call x2 -> x3, Pallas kernels: 5.03 us -> 5.94 us  [gradients(): pl.pallas_call(functools.partial(gradient_kernel, chunks, half, len(sums)...]
  transfers between devices with their start and end apart: 23 -> 23, of which waited for: 11 -> 13; matrix products, arithmetic and copies ran while one was open for 0% -> 0% of each run, Pallas kernels for 11% -> 13%
where the time goes in v7:
time: 118 us; the launch traced here: 117 us
  waiting for transfers between devices  60.1 us (51%)
  starting transfers between devices  29.6 us (25%)
  Pallas kernels  18.6 us (16%)
  local copies, waits for them, and re-layouts  8.37 us (7%)
    ppermute x23, waiting for transfers between devices, exchange(): return lax.ppermute(values, axis, [(n, n ^ mask) for n in range(size)])  60.1 us
    ppermute x23, starting transfers between devices, exchange(): return lax.ppermute(values, axis, [(n, n ^ mask) for n in range(size)])  29.6 us
    pallas_call x3, Pallas kernels, expert_rows(): pl.pallas_call(functools.partial(expert_kernel, pairs, top, tuple(relays)...  11.1 us
    unnamed x18, local copies, waits for them, and re-layouts  8.12 us
    pallas_call x3, Pallas kernels, gradients(): pl.pallas_call(functools.partial(gradient_kernel, chunks, half, len(sums)...  5.94 us
  transfers between devices with their start and end apart: 23, of which 13 were waited for; matrix products, arithmetic and copies ran while one was open for 0% of the time, Pallas kernels for 13%

profile of v7, /device:TPU:0, one launch (start us, length us, event | category | flops | bytes accessed | tf_op | source)
XLA Modules:
  0.0 117.5 jit_solution(7960681565060786661)
XLA Ops:
  0.6 0.0 copy-start.4
  0.6 0.7 copy-done.4
  1.3 1.0 copy-done.6
  2.4 1.0 copy-done.7
  3.4 0.7 copy-done.8
  4.1 1.0 dispatch_rows.1
  5.1 0.5 collective-permute-start
  5.6 3.7 %collective-permute-start.1 = (bf16[80,4096]{1,0:T(8,128)(2,1)S(1)}, bf16[80,4096]{1,0:T(8,128)(2,1)S(1)}, u32[]{:S(2)}, u32[]{:S(2)}) collective-permute-start(bf16[80,4096]{1,0:T(8,128)(2,1)S(1)} %get-tuple-element.41), channel_id=1, source_target_pairs={{0,4},{1,5},{2,6},{3,7},{4,0},{5,1},{6,2},{7,3},{8,12},{9,13},{10,... | collective-permute-start | bytes 1966088 | tf_op jit(solution)/shard_map/ppermute | solution.py:308
  9.2 1.6 %collective-permute-start.2 = (bf16[80,4096]{1,0:T(8,128)(2,1)S(1)}, bf16[80,4096]{1,0:T(8,128)(2,1)S(1)}, u32[]{:S(2)}, u32[]{:S(2)}) collective-permute-start(bf16[80,4096]{1,0:T(8,128)(2,1)S(1)} %get-tuple-element.42), channel_id=1, source_target_pairs={{0,2},{1,3},{2,0},{3,1},{4,6},{5,7},{6,4},{7,5},{8,10},{9,11},{10,... | collective-permute-start | bytes 1966088 | tf_op jit(solution)/shard_map/ppermute | solution.py:308
  10.8 0.0 collective-permute-done.refs_1_
  10.8 2.8 %copy-done = bf16[1,2048,1536]{2,1,0:T(8,128)(2,1)S(1)} copy-done((bf16[1,2048,1536]{2,1,0:T(8,128)(2,1)S(1)}, bf16[1,2048,1536]{2,1,0:T(8,128)(2,1)}, u32[]{:S(2)}) %copy-start) | copy-done | bytes 6291480
  13.6 1.9 %copy-done.2 = bf16[1,768,2048]{2,1,0:T(8,128)(2,1)S(1)} copy-done((bf16[1,768,2048]{2,1,0:T(8,128)(2,1)S(1)}, bf16[1,768,2048]{2,1,0:T(8,128)(2,1)}, u32[]{:S(2)}) %copy-start.2) | copy-done | bytes 3145752
  15.5 3.6 %expert_rows.3 = (bf16[1040,256]{1,0:T(8,128)(2,1)S(1)}, bf16[1232,256]{1,0:T(8,128)(2,1)S(1)}, bf16[1168,256]{1,0:T(8,128)(2,1)S(1)}, f32[80,128]{1,0:T(8,128)S(1)}) custom-call(bf16[80,4096]{1,0:T(8,128)(2,1)S(1)} %get-tuple-element.39.refs_0_, bf16[40,4096]{1,0:T(8,128)(2,1)S(1)} %collective-permute-done.refs_1_, bf16[2048,1536]{1,0:T(8,128)(2,1)S(1)} %bitcast.7, ...), custom_call_target="tpu_custom_call" | custom-call | flops 1000 | bytes 1000 | tf_op jit(solution)/shard_map/expert_rows/pallas_call | solution.py:172
  19.1 1.6 %collective-permute-start.5 = (bf16[1232,256]{1,0:T(8,128)(2,1)S(1)}, bf16[1232,256]{1,0:T(8,128)(2,1)S(1)}, u32[]{:S(2)}, u32[]{:S(2)}) collective-permute-start(bf16[1232,256]{1,0:T(8,128)(2,1)S(1)} %get-tuple-element.48), channel_id=1, source_target_pairs={{0,8},{8,0},{16,24},{24,16},{1,9},{9,1},{17,25},{25,17},{2,10},{10... | collective-permute-start | bytes 1892360 | tf_op jit(solution)/shard_map/ppermute | solution.py:308
  20.7 1.5 %collective-permute-start.6 = (bf16[1168,256]{1,0:T(8,128)(2,1)S(1)}, bf16[1168,256]{1,0:T(8,128)(2,1)S(1)}, u32[]{:S(2)}, u32[]{:S(2)}) collective-permute-start(bf16[1168,256]{1,0:T(8,128)(2,1)S(1)} %get-tuple-element.49), channel_id=1, source_target_pairs={{0,16},{8,24},{16,0},{24,8},{1,17},{9,25},{17,1},{25,9},{2,18},{10... | collective-permute-start | bytes 1794056 | tf_op jit(solution)/shard_map/ppermute | solution.py:308
  22.2 16.5 %collective-permute-done.1.refs_2_ = bf16[80,4096]{1,0:T(8,128)(2,1)S(1)} collective-permute-done((bf16[80,4096]{1,0:T(8,128)(2,1)S(1)}, bf16[80,4096]{1,0:T(8,128)(2,1)S(1)}, u32[]{:S(2)}, u32[]{:S(2)}) %collective-permute-start.1) | collective-permute-done | bytes 655392 | tf_op jit(solution)/shard_map/ppermute | solution.py:308
  38.7 0.2 collective-permute-done.2.refs_0_
  39.0 0.1 collective-permute-start.4
  39.0 0.5 collective-permute-start.3
  39.5 0.0 collective-permute-done.5.refs_1_
  39.6 1.7 %collective-permute-start.7 = (bf16[624,256]{1,0:T(8,128)(2,1)S(1)}, bf16[624,256]{1,0:T(8,128)(2,1)S(1)}, u32[]{:S(2)}, u32[]{:S(2)}) collective-permute-start(bf16[624,256]{1,0:T(8,128)(2,1)S(1)} %slice.56), channel_id=1, source_target_pairs={{0,16},{8,24},{16,0},{24,8},{1,17},{9,25},{17,1},{25,9},{2,18},{10... | collective-permute-start | bytes 958472 | tf_op jit(solution)/shard_map/ppermute | solution.py:308
  41.2 0.0 collective-permute-done.6.refs_2_
  41.3 1.5 %collective-permute-start.8 = (bf16[416,256]{1,0:T(8,128)(2,1)S(1)}, bf16[416,256]{1,0:T(8,128)(2,1)S(1)}, u32[]{:S(2)}, u32[]{:S(2)}) collective-permute-start(bf16[416,256]{1,0:T(8,128)(2,1)S(1)} %slice.57), channel_id=1, source_target_pairs={{0,8},{8,0},{16,24},{24,16},{1,9},{9,1},{17,25},{25,17},{2,10},{10... | collective-permute-start | bytes 638984 | tf_op jit(solution)/shard_map/ppermute | solution.py:308
  42.8 3.2 %collective-permute-start.11 = (bf16[80,4096]{1,0:T(8,128)(2,1)S(1)}, bf16[80,4096]{1,0:T(8,128)(2,1)S(1)}, u32[]{:S(2)}, u32[]{:S(2)}) collective-permute-start(bf16[80,4096]{1,0:T(8,128)(2,1)S(1)} %get-tuple-element.55), channel_id=1, source_target_pairs={{0,6},{1,7},{2,4},{3,5},{4,2},{5,3},{6,0},{7,1},{8,14},{9,15},{10,... | collective-permute-start | bytes 1966088 | tf_op jit(solution)/shard_map/ppermute | solution.py:308
  46.0 0.0 collective-permute-done.4.refs_3_
  46.0 0.0 collective-permute-done.3.refs_1_
  46.0 0.0 copy-done.1
  46.0 0.0 copy-done.3
  46.0 3.9 %expert_rows.4 = (bf16[2080,256]{1,0:T(8,128)(2,1)S(1)}, bf16[2400,256]{1,0:T(8,128)(2,1)S(1)}, bf16[2400,256]{1,0:T(8,128)(2,1)S(1)}, f32[80,128]{1,0:T(8,128)S(1)}, f32[80,128]{1,0:T(8,128)S(1)}) custom-call(bf16[80,4096]{1,0:T(8,128)(2,1)S(1)} %collective-permute-done.2.refs_0_, bf16[40,4096]{1,0:T(8,128)(2,1)S(1)} %collective-permute-done.3.refs_1_, ...), custom_call_target="tpu_custom_call" | custom-call | flops 1000 | bytes 1000 | tf_op jit(solution)/shard_map/expert_rows/pallas_call | solution.py:172
  50.0 0.0 collective-permute-done.8.refs_4_
  50.0 0.0 collective-permute-done.7.refs_3_
  50.0 0.7 collective-permute-start.19
  50.7 1.5 %collective-permute-start.20 = (bf16[2400,256]{1,0:T(8,128)(2,1)S(1)}, bf16[2400,256]{1,0:T(8,128)(2,1)S(1)}, u32[]{:S(2)}, u32[]{:S(2)}) collective-permute-start(bf16[2400,256]{1,0:T(8,128)(2,1)S(1)} %get-tuple-element.68), channel_id=1, source_target_pairs={{0,16},{8,24},{16,0},{24,8},{1,17},{9,25},{17,1},{25,9},{2,18},{10... | collective-permute-start | bytes 3686408 | tf_op jit(solution)/shard_map/ppermute | solution.py:308
  52.2 1.4 %gradients.3 = (f32[512,1536]{1,0:T(8,128)S(1)}, f32[768,512]{1,0:T(8,128)S(1)}) custom-call(bf16[1040,256]{1,0:T(8,128)(2,1)S(1)} %get-tuple-element.47.refs_0_, bf16[1232,256]{1,0:T(8,128)(2,1)S(1)} %collective-permute-done.5.refs_1_, bf16[1168,256]{1,0:T(8,128)(2,1)S(1)} %collective-permute-done.6.refs_2_, ...), custom_call_target="tpu_custom_call" | custom-call | flops 1000 | bytes 1000 | tf_op jit(solution)/shard_map/gradients/pallas_call | solution.py:263
  53.7 1.5 %collective-permute-start.9 = (f32[80,128]{1,0:T(8,128)S(1)}, f32[80,128]{1,0:T(8,128)S(1)}, u32[]{:S(2)}, u32[]{:S(2)}) collective-permute-start(f32[80,128]{1,0:T(8,128)S(1)} %get-tuple-element.52), channel_id=1, source_target_pairs={{0,2},{1,3},{2,0},{3,1},{4,6},{5,7},{6,4},{7,5},{8,10},{9,11},{10,... | collective-permute-start | bytes 122888 | tf_op jit(solution)/shard_map/ppermute | solution.py:308
  55.2 2.3 %collective-permute-start.10 = (f32[80,128]{1,0:T(8,128)S(1)}, f32[80,128]{1,0:T(8,128)S(1)}, u32[]{:S(2)}, u32[]{:S(2)}) collective-permute-start(f32[80,128]{1,0:T(8,128)S(1)} %get-tuple-element.53), channel_id=1, source_target_pairs={{0,4},{1,5},{2,6},{3,7},{4,0},{5,1},{6,2},{7,3},{8,12},{9,13},{10,... | collective-permute-start | bytes 122888 | tf_op jit(solution)/shard_map/ppermute | solution.py:308
  57.5 4.3 %collective-permute-done.11.refs_0_ = bf16[80,4096]{1,0:T(8,128)(2,1)S(1)} collective-permute-done((bf16[80,4096]{1,0:T(8,128)(2,1)S(1)}, bf16[80,4096]{1,0:T(8,128)(2,1)S(1)}, u32[]{:S(2)}, u32[]{:S(2)}) %collective-permute-start.11) | collective-permute-done | bytes 655392 | tf_op jit(solution)/shard_map/ppermute | solution.py:308
  61.8 0.0 collective-permute-done.9.own_1
  61.8 13.9 %collective-permute-done.10.own_2 = f32[80,128]{1,0:T(8,128)S(1)} collective-permute-done((f32[80,128]{1,0:T(8,128)S(1)}, f32[80,128]{1,0:T(8,128)S(1)}, u32[]{:S(2)}, u32[]{:S(2)}) %collective-permute-start.10) | collective-permute-done | bytes 40992 | tf_op jit(solution)/shard_map/ppermute | solution.py:308
  75.7 0.1 collective-permute-start.12
  75.8 1.6 %collective-permute-done.12.refs_1_ = bf16[40,4096]{1,0:T(8,128)(2,1)S(1)} collective-permute-done((bf16[40,4096]{1,0:T(8,128)(2,1)S(1)}, bf16[40,4096]{1,0:T(8,128)(2,1)S(1)}, u32[]{:S(2)}, u32[]{:S(2)}) %collective-permute-start.12) | collective-permute-done | bytes 327712 | tf_op jit(solution)/shard_map/ppermute | solution.py:308
  77.4 3.6 %expert_rows.5 = (bf16[1040,256]{1,0:T(8,128)(2,1)S(1)}, bf16[1168,256]{1,0:T(8,128)(2,1)S(1)}, bf16[1232,256]{1,0:T(8,128)(2,1)S(1)}, f32[80,128]{1,0:T(8,128)S(1)}) custom-call(bf16[80,4096]{1,0:T(8,128)(2,1)S(1)} %collective-permute-done.11.refs_0_, bf16[40,4096]{1,0:T(8,128)(2,1)S(1)} %collective-permute-done.12.refs_1_, ...), custom_call_target="tpu_custom_call" | custom-call | flops 1000 | bytes 1000 | tf_op jit(solution)/shard_map/expert_rows/pallas_call | solution.py:172
  81.0 0.6 collective-permute-start.16
  81.5 0.5 collective-permute-start.15
  82.1 1.4 %collective-permute-start.13 = (f32[80,128]{1,0:T(8,128)S(1)}, f32[80,128]{1,0:T(8,128)S(1)}, u32[]{:S(2)}, u32[]{:S(2)}) collective-permute-start(f32[80,128]{1,0:T(8,128)S(1)} %get-tuple-element.57), channel_id=1, source_target_pairs={{0,6},{1,7},{2,4},{3,5},{4,2},{5,3},{6,0},{7,1},{8,14},{9,15},{10,... | collective-permute-start | bytes 122888 | tf_op jit(solution)/shard_map/ppermute | solution.py:308
  83.4 0.0 collective-permute-done.19.refs_1_
  83.4 0.0 collective-permute-done.20.refs_2_
  83.5 1.6 %collective-permute-start.22 = (bf16[1040,256]{1,0:T(8,128)(2,1)S(1)}, bf16[1040,256]{1,0:T(8,128)(2,1)S(1)}, u32[]{:S(2)}, u32[]{:S(2)}) collective-permute-start(bf16[1040,256]{1,0:T(8,128)(2,1)S(1)} %slice.55), channel_id=1, source_target_pairs={{0,8},{8,0},{16,24},{24,16},{1,9},{9,1},{17,25},{25,17},{2,10},{10... | collective-permute-start | bytes 1597448 | tf_op jit(solution)/shard_map/ppermute | solution.py:308
  85.1 1.5 %collective-permute-start.21 = (bf16[1040,256]{1,0:T(8,128)(2,1)S(1)}, bf16[1040,256]{1,0:T(8,128)(2,1)S(1)}, u32[]{:S(2)}, u32[]{:S(2)}) collective-permute-start(bf16[1040,256]{1,0:T(8,128)(2,1)S(1)} %slice.54), channel_id=1, source_target_pairs={{0,16},{8,24},{16,0},{24,8},{1,17},{9,25},{17,1},{25,9},{2,18},{10... | collective-permute-start | bytes 1597448 | tf_op jit(solution)/shard_map/ppermute | solution.py:308
  86.6 1.3 %collective-permute-done.13.own_3 = f32[80,128]{1,0:T(8,128)S(1)} collective-permute-done((f32[80,128]{1,0:T(8,128)S(1)}, f32[80,128]{1,0:T(8,128)S(1)}, u32[]{:S(2)}, u32[]{:S(2)}) %collective-permute-start.13) | collective-permute-done | bytes 40992 | tf_op jit(solution)/shard_map/ppermute | solution.py:308
  87.9 0.1 collective-permute-start.14
  87.9 1.3 %collective-permute-done.14.other_ref = f32[160,128]{1,0:T(8,128)S(1)} collective-permute-done((f32[160,128]{1,0:T(8,128)S(1)}, f32[160,128]{1,0:T(8,128)S(1)}, u32[]{:S(2)}, u32[]{:S(2)}) %collective-permute-start.14) | collective-permute-done | bytes 81952 | tf_op jit(solution)/shard_map/ppermute | solution.py:308
  89.2 8.7 %collective-permute-done.15.refs_1_ = bf16[1168,256]{1,0:T(8,128)(2,1)S(1)} collective-permute-done((bf16[1168,256]{1,0:T(8,128)(2,1)S(1)}, bf16[1168,256]{1,0:T(8,128)(2,1)S(1)}, u32[]{:S(2)}, u32[]{:S(2)}) %collective-permute-start.15) | collective-permute-done | bytes 598048 | tf_op jit(solution)/shard_map/ppermute | solution.py:308
  97.9 0.1 collective-permute-done.16.refs_2_
  98.1 0.6 collective-permute-start.18
  98.7 1.4 %collective-permute-start.17 = (bf16[416,256]{1,0:T(8,128)(2,1)S(1)}, bf16[416,256]{1,0:T(8,128)(2,1)S(1)}, u32[]{:S(2)}, u32[]{:S(2)}) collective-permute-start(bf16[416,256]{1,0:T(8,128)(2,1)S(1)} %slice.52), channel_id=1, source_target_pairs={{0,16},{8,24},{16,0},{24,8},{1,17},{9,25},{17,1},{25,9},{2,18},{10... | collective-permute-start | bytes 638984 | tf_op jit(solution)/shard_map/ppermute | solution.py:308
  100.1 0.0 copy-done.5
  100.1 0.6 prob_gradients.1
  100.8 8.6 %collective-permute-done.22.refs_4_ = bf16[1040,256]{1,0:T(8,128)(2,1)S(1)} collective-permute-done((bf16[1040,256]{1,0:T(8,128)(2,1)S(1)}, bf16[1040,256]{1,0:T(8,128)(2,1)S(1)}, u32[]{:S(2)}, u32[]{:S(2)}) %collective-permute-start.22) | collective-permute-done | bytes 532512 | tf_op jit(solution)/shard_map/ppermute | solution.py:308
  109.3 0.1 collective-permute-done.21.refs_3_
  109.5 2.0 %gradients.4 = (f32[512,1536]{1,0:T(8,128)S(1)}, f32[768,512]{1,0:T(8,128)S(1)}) custom-call(bf16[2080,256]{1,0:T(8,128)(2,1)S(1)} %get-tuple-element.64.refs_0_, bf16[2400,256]{1,0:T(8,128)(2,1)S(1)} %collective-permute-done.19.refs_1_, bf16[2400,256]{1,0:T(8,128)(2,1)S(1)} %collective-permute-done.20.refs_2_, ...), custom_call_target="tpu_custom_call" | custom-call | flops 1000 | bytes 1000 | tf_op jit(solution)/shard_map/gradients/pallas_call | solution.py:263
  111.5 1.7 %collective-permute-done.17.refs_3_ = bf16[416,256]{1,0:T(8,128)(2,1)S(1)} collective-permute-done((bf16[416,256]{1,0:T(8,128)(2,1)S(1)}, bf16[416,256]{1,0:T(8,128)(2,1)S(1)}, u32[]{:S(2)}, u32[]{:S(2)}) %collective-permute-start.17) | collective-permute-done | bytes 213024 | tf_op jit(solution)/shard_map/ppermute | solution.py:308
  113.2 1.8 %collective-permute-done.18.refs_4_ = bf16[624,256]{1,0:T(8,128)(2,1)S(1)} collective-permute-done((bf16[624,256]{1,0:T(8,128)(2,1)S(1)}, bf16[624,256]{1,0:T(8,128)(2,1)S(1)}, u32[]{:S(2)}, u32[]{:S(2)}) %collective-permute-start.18) | collective-permute-done | bytes 319520 | tf_op jit(solution)/shard_map/ppermute | solution.py:308
  115.0 2.5 %gradients.5 = (bf16[512,1536]{1,0:T(8,128)(2,1)}, bf16[768,512]{1,0:T(8,128)(2,1)}) custom-call(bf16[1040,256]{1,0:T(8,128)(2,1)S(1)} %get-tuple-element.59.refs_0_, bf16[1168,256]{1,0:T(8,128)(2,1)S(1)} %collective-permute-done.15.refs_1_, bf16[1232,256]{1,0:T(8,128)(2,1)S(1)} %collective-permute-done.16.refs_2_, ...), custom_call_target="tpu_custom_call" | custom-call | flops 1000 | bytes 1000 | tf_op jit(solution)/shard_map/gradients/pallas_call | solution.py:263
  (23 shorter events, 0.3 us)
Async XLA Ops:
  0.6 0.7 copy-start.4
  1.3 1.0 copy-start.6
  2.4 1.0 copy-start.7
  3.4 0.7 copy-start.8
  5.1 5.8 %collective-permute-start = (bf16[40,4096]{1,0:T(8,128)(2,1)S(1)}, bf16[40,4096]{1,0:T(8,128)(2,1)S(1)}, u32[]{:S(2)}, u32[]{:S(2)}) collective-permute-start(bf16[40,4096]{1,0:T(8,128)(2,1)S(1)} %slice.42), channel_id=1, source_target_pairs={{0,1},{1,0},{2,3},{3,2},{4,5},{5,4},{6,7},{7,6},{8,9},{9,8},{10,11... | collective-permute-start | bytes 983048 | tf_op jit(solution)/shard_map/ppermute | solution.py:308
  5.6 33.1 %collective-permute-start.1 = (bf16[80,4096]{1,0:T(8,128)(2,1)S(1)}, bf16[80,4096]{1,0:T(8,128)(2,1)S(1)}, u32[]{:S(2)}, u32[]{:S(2)}) collective-permute-start(bf16[80,4096]{1,0:T(8,128)(2,1)S(1)} %get-tuple-element.41), channel_id=1, source_target_pairs={{0,4},{1,5},{2,6},{3,7},{4,0},{5,1},{6,2},{7,3},{8,12},{9,13},{10,... | collective-permute-start | bytes 1966088 | tf_op jit(solution)/shard_map/ppermute | solution.py:308
  9.2 29.7 %collective-permute-start.2 = (bf16[80,4096]{1,0:T(8,128)(2,1)S(1)}, bf16[80,4096]{1,0:T(8,128)(2,1)S(1)}, u32[]{:S(2)}, u32[]{:S(2)}) collective-permute-start(bf16[80,4096]{1,0:T(8,128)(2,1)S(1)} %get-tuple-element.42), channel_id=1, source_target_pairs={{0,2},{1,3},{2,0},{3,1},{4,6},{5,7},{6,4},{7,5},{8,10},{9,11},{10,... | collective-permute-start | bytes 1966088 | tf_op jit(solution)/shard_map/ppermute | solution.py:308
  10.8 2.8 %copy-start = (bf16[1,2048,1536]{2,1,0:T(8,128)(2,1)S(1)}, bf16[1,2048,1536]{2,1,0:T(8,128)(2,1)}, u32[]{:S(2)}) copy-start(bf16[1,2048,1536]{2,1,0:T(8,128)(2,1)} %param.10) | copy-start | bytes 18874372
  13.6 1.9 %copy-start.2 = (bf16[1,768,2048]{2,1,0:T(8,128)(2,1)S(1)}, bf16[1,768,2048]{2,1,0:T(8,128)(2,1)}, u32[]{:S(2)}) copy-start(bf16[1,768,2048]{2,1,0:T(8,128)(2,1)} %param.11) | copy-start | bytes 9437188
  15.5 30.5 %copy-start.1 = (bf16[1,2048,1536]{2,1,0:T(8,128)(2,1)S(1)}, bf16[1,2048,1536]{2,1,0:T(8,128)(2,1)}, u32[]{:S(2)}) copy-start(bf16[1,2048,1536]{2,1,0:T(8,128)(2,1)} %param.10) | copy-start | bytes 18874372
  15.5 30.5 %copy-start.3 = (bf16[1,768,2048]{2,1,0:T(8,128)(2,1)S(1)}, bf16[1,768,2048]{2,1,0:T(8,128)(2,1)}, u32[]{:S(2)}) copy-start(bf16[1,768,2048]{2,1,0:T(8,128)(2,1)} %param.11) | copy-start | bytes 9437188
  19.1 20.4 %collective-permute-start.5 = (bf16[1232,256]{1,0:T(8,128)(2,1)S(1)}, bf16[1232,256]{1,0:T(8,128)(2,1)S(1)}, u32[]{:S(2)}, u32[]{:S(2)}) collective-permute-start(bf16[1232,256]{1,0:T(8,128)(2,1)S(1)} %get-tuple-element.48), channel_id=1, source_target_pairs={{0,8},{8,0},{16,24},{24,16},{1,9},{9,1},{17,25},{25,17},{2,10},{10... | collective-permute-start | bytes 1892360 | tf_op jit(solution)/shard_map/ppermute | solution.py:308
  20.7 20.6 %collective-permute-start.6 = (bf16[1168,256]{1,0:T(8,128)(2,1)S(1)}, bf16[1168,256]{1,0:T(8,128)(2,1)S(1)}, u32[]{:S(2)}, u32[]{:S(2)}) collective-permute-start(bf16[1168,256]{1,0:T(8,128)(2,1)S(1)} %get-tuple-element.49), channel_id=1, source_target_pairs={{0,16},{8,24},{16,0},{24,8},{1,17},{9,25},{17,1},{25,9},{2,18},{10... | collective-permute-start | bytes 1794056 | tf_op jit(solution)/shard_map/ppermute | solution.py:308
  39.0 7.0 %collective-permute-start.4 = (bf16[40,4096]{1,0:T(8,128)(2,1)S(1)}, bf16[40,4096]{1,0:T(8,128)(2,1)S(1)}, u32[]{:S(2)}, u32[]{:S(2)}) collective-permute-start(bf16[40,4096]{1,0:T(8,128)(2,1)S(1)} %slice.44), channel_id=1, source_target_pairs={{0,1},{1,0},{2,3},{3,2},{4,5},{5,4},{6,7},{7,6},{8,9},{9,8},{10,11... | collective-permute-start | bytes 983048 | tf_op jit(solution)/shard_map/ppermute | solution.py:308
  39.0 7.0 %collective-permute-start.3 = (bf16[40,4096]{1,0:T(8,128)(2,1)S(1)}, bf16[40,4096]{1,0:T(8,128)(2,1)S(1)}, u32[]{:S(2)}, u32[]{:S(2)}) collective-permute-start(bf16[40,4096]{1,0:T(8,128)(2,1)S(1)} %slice.43), channel_id=1, source_target_pairs={{0,1},{1,0},{2,3},{3,2},{4,5},{5,4},{6,7},{7,6},{8,9},{9,8},{10,11... | collective-permute-start | bytes 983048 | tf_op jit(solution)/shard_map/ppermute | solution.py:308
  39.6 10.4 %collective-permute-start.7 = (bf16[624,256]{1,0:T(8,128)(2,1)S(1)}, bf16[624,256]{1,0:T(8,128)(2,1)S(1)}, u32[]{:S(2)}, u32[]{:S(2)}) collective-permute-start(bf16[624,256]{1,0:T(8,128)(2,1)S(1)} %slice.56), channel_id=1, source_target_pairs={{0,16},{8,24},{16,0},{24,8},{1,17},{9,25},{17,1},{25,9},{2,18},{10... | collective-permute-start | bytes 958472 | tf_op jit(solution)/shard_map/ppermute | solution.py:308
  41.3 8.7 %collective-permute-start.8 = (bf16[416,256]{1,0:T(8,128)(2,1)S(1)}, bf16[416,256]{1,0:T(8,128)(2,1)S(1)}, u32[]{:S(2)}, u32[]{:S(2)}) collective-permute-start(bf16[416,256]{1,0:T(8,128)(2,1)S(1)} %slice.57), channel_id=1, source_target_pairs={{0,8},{8,0},{16,24},{24,16},{1,9},{9,1},{17,25},{25,17},{2,10},{10... | collective-permute-start | bytes 638984 | tf_op jit(solution)/shard_map/ppermute | solution.py:308
  42.8 19.0 %collective-permute-start.11 = (bf16[80,4096]{1,0:T(8,128)(2,1)S(1)}, bf16[80,4096]{1,0:T(8,128)(2,1)S(1)}, u32[]{:S(2)}, u32[]{:S(2)}) collective-permute-start(bf16[80,4096]{1,0:T(8,128)(2,1)S(1)} %get-tuple-element.55), channel_id=1, source_target_pairs={{0,6},{1,7},{2,4},{3,5},{4,2},{5,3},{6,0},{7,1},{8,14},{9,15},{10,... | collective-permute-start | bytes 1966088 | tf_op jit(solution)/shard_map/ppermute | solution.py:308
  50.0 33.4 %collective-permute-start.19 = (bf16[2400,256]{1,0:T(8,128)(2,1)S(1)}, bf16[2400,256]{1,0:T(8,128)(2,1)S(1)}, u32[]{:S(2)}, u32[]{:S(2)}) collective-permute-start(bf16[2400,256]{1,0:T(8,128)(2,1)S(1)} %get-tuple-element.67), channel_id=1, source_target_pairs={{0,8},{8,0},{16,24},{24,16},{1,9},{9,1},{17,25},{25,17},{2,10},{10... | collective-permute-start | bytes 3686408 | tf_op jit(solution)/shard_map/ppermute | solution.py:308
  50.7 32.7 %collective-permute-start.20 = (bf16[2400,256]{1,0:T(8,128)(2,1)S(1)}, bf16[2400,256]{1,0:T(8,128)(2,1)S(1)}, u32[]{:S(2)}, u32[]{:S(2)}) collective-permute-start(bf16[2400,256]{1,0:T(8,128)(2,1)S(1)} %get-tuple-element.68), channel_id=1, source_target_pairs={{0,16},{8,24},{16,0},{24,8},{1,17},{9,25},{17,1},{25,9},{2,18},{10... | collective-permute-start | bytes 3686408 | tf_op jit(solution)/shard_map/ppermute | solution.py:308
  53.7 8.1 %collective-permute-start.9 = (f32[80,128]{1,0:T(8,128)S(1)}, f32[80,128]{1,0:T(8,128)S(1)}, u32[]{:S(2)}, u32[]{:S(2)}) collective-permute-start(f32[80,128]{1,0:T(8,128)S(1)} %get-tuple-element.52), channel_id=1, source_target_pairs={{0,2},{1,3},{2,0},{3,1},{4,6},{5,7},{6,4},{7,5},{8,10},{9,11},{10,... | collective-permute-start | bytes 122888 | tf_op jit(solution)/shard_map/ppermute | solution.py:308
  55.2 20.4 %collective-permute-start.10 = (f32[80,128]{1,0:T(8,128)S(1)}, f32[80,128]{1,0:T(8,128)S(1)}, u32[]{:S(2)}, u32[]{:S(2)}) collective-permute-start(f32[80,128]{1,0:T(8,128)S(1)} %get-tuple-element.53), channel_id=1, source_target_pairs={{0,4},{1,5},{2,6},{3,7},{4,0},{5,1},{6,2},{7,3},{8,12},{9,13},{10,... | collective-permute-start | bytes 122888 | tf_op jit(solution)/shard_map/ppermute | solution.py:308
  75.7 1.7 %collective-permute-start.12 = (bf16[40,4096]{1,0:T(8,128)(2,1)S(1)}, bf16[40,4096]{1,0:T(8,128)(2,1)S(1)}, u32[]{:S(2)}, u32[]{:S(2)}) collective-permute-start(bf16[40,4096]{1,0:T(8,128)(2,1)S(1)} %slice.47), channel_id=1, source_target_pairs={{0,1},{1,0},{2,3},{3,2},{4,5},{5,4},{6,7},{7,6},{8,9},{9,8},{10,11... | collective-permute-start | bytes 983048 | tf_op jit(solution)/shard_map/ppermute | solution.py:308
  81.0 17.1 %collective-permute-start.16 = (bf16[1232,256]{1,0:T(8,128)(2,1)S(1)}, bf16[1232,256]{1,0:T(8,128)(2,1)S(1)}, u32[]{:S(2)}, u32[]{:S(2)}) collective-permute-start(bf16[1232,256]{1,0:T(8,128)(2,1)S(1)} %get-tuple-element.61), channel_id=1, source_target_pairs={{0,16},{8,24},{16,0},{24,8},{1,17},{9,25},{17,1},{25,9},{2,18},{10... | collective-permute-start | bytes 1892360 | tf_op jit(solution)/shard_map/ppermute | solution.py:308
  81.5 16.4 %collective-permute-start.15 = (bf16[1168,256]{1,0:T(8,128)(2,1)S(1)}, bf16[1168,256]{1,0:T(8,128)(2,1)S(1)}, u32[]{:S(2)}, u32[]{:S(2)}) collective-permute-start(bf16[1168,256]{1,0:T(8,128)(2,1)S(1)} %get-tuple-element.60), channel_id=1, source_target_pairs={{0,8},{8,0},{16,24},{24,16},{1,9},{9,1},{17,25},{25,17},{2,10},{10... | collective-permute-start | bytes 1794056 | tf_op jit(solution)/shard_map/ppermute | solution.py:308
  82.1 18.1 %copy-start.5 = (f32[128,2]{0,1:T(2,128)S(1)}, f32[128,2]{0,1:T(2,128)}, u32[]{:S(2)}) copy-start(f32[128,2]{0,1:T(2,128)} %param.8) | copy-start | bytes 3076
  82.1 5.8 %collective-permute-start.13 = (f32[80,128]{1,0:T(8,128)S(1)}, f32[80,128]{1,0:T(8,128)S(1)}, u32[]{:S(2)}, u32[]{:S(2)}) collective-permute-start(f32[80,128]{1,0:T(8,128)S(1)} %get-tuple-element.57), channel_id=1, source_target_pairs={{0,6},{1,7},{2,4},{3,5},{4,2},{5,3},{6,0},{7,1},{8,14},{9,15},{10,... | collective-permute-start | bytes 122888 | tf_op jit(solution)/shard_map/ppermute | solution.py:308
  83.5 25.8 %collective-permute-start.22 = (bf16[1040,256]{1,0:T(8,128)(2,1)S(1)}, bf16[1040,256]{1,0:T(8,128)(2,1)S(1)}, u32[]{:S(2)}, u32[]{:S(2)}) collective-permute-start(bf16[1040,256]{1,0:T(8,128)(2,1)S(1)} %slice.55), channel_id=1, source_target_pairs={{0,8},{8,0},{16,24},{24,16},{1,9},{9,1},{17,25},{25,17},{2,10},{10... | collective-permute-start | bytes 1597448 | tf_op jit(solution)/shard_map/ppermute | solution.py:308
  85.1 24.4 %collective-permute-start.21 = (bf16[1040,256]{1,0:T(8,128)(2,1)S(1)}, bf16[1040,256]{1,0:T(8,128)(2,1)S(1)}, u32[]{:S(2)}, u32[]{:S(2)}) collective-permute-start(bf16[1040,256]{1,0:T(8,128)(2,1)S(1)} %slice.54), channel_id=1, source_target_pairs={{0,16},{8,24},{16,0},{24,8},{1,17},{9,25},{17,1},{25,9},{2,18},{10... | collective-permute-start | bytes 1597448 | tf_op jit(solution)/shard_map/ppermute | solution.py:308
  87.9 1.3 %collective-permute-start.14 = (f32[160,128]{1,0:T(8,128)S(1)}, f32[160,128]{1,0:T(8,128)S(1)}, u32[]{:S(2)}, u32[]{:S(2)}) collective-permute-start(f32[160,128]{1,0:T(8,128)S(1)} %pad_maximum_fusion), channel_id=1, source_target_pairs={{0,1},{1,0},{2,3},{3,2},{4,5},{5,4},{6,7},{7,6},{8,9},{9,8},{10,11... | collective-permute-start | bytes 245768 | tf_op jit(solution)/shard_map/ppermute | solution.py:308
  98.1 17.0 %collective-permute-start.18 = (bf16[624,256]{1,0:T(8,128)(2,1)S(1)}, bf16[624,256]{1,0:T(8,128)(2,1)S(1)}, u32[]{:S(2)}, u32[]{:S(2)}) collective-permute-start(bf16[624,256]{1,0:T(8,128)(2,1)S(1)} %slice.53), channel_id=1, source_target_pairs={{0,8},{8,0},{16,24},{24,16},{1,9},{9,1},{17,25},{25,17},{2,10},{10... | collective-permute-start | bytes 958472 | tf_op jit(solution)/shard_map/ppermute | solution.py:308
  98.7 14.5 %collective-permute-start.17 = (bf16[416,256]{1,0:T(8,128)(2,1)S(1)}, bf16[416,256]{1,0:T(8,128)(2,1)S(1)}, u32[]{:S(2)}, u32[]{:S(2)}) collective-permute-start(bf16[416,256]{1,0:T(8,128)(2,1)S(1)} %slice.52), channel_id=1, source_target_pairs={{0,16},{8,24},{16,0},{24,8},{1,17},{9,25},{17,1},{25,9},{2,18},{10... | collective-permute-start | bytes 638984 | tf_op jit(solution)/shard_map/ppermute | solution.py:308

commit v8 on v7

--- a/solution.py
+++ b/solution.py
@@ -87,13 +87,19 @@
         refs[2 * pairs + 3 :],
     )
     relay_refs, rest = rest[: len(relays)], rest[len(relays) :]
-    own_ref, to_x, to_y, *inner_refs, x_rows, s_rows, s_turned, total = rest
+    *out_refs, x_rows, s_rows, s_turned, total = rest
+    direct = top is None
+    if direct:
+        plane_refs, inner_refs = out_refs[:4], out_refs[4:]
+        own_ref, to_x, to_y = plane_refs[:3]
+    else:
+        (own_ref, to_x, to_y), inner_refs = out_refs[:3], out_refs[3:]
     count = pairs * PAIR
     width = gate_ref.shape[0]
     steps = pl.num_programs(0)
     half = TILE * 3
     quarter = width // 4
-    blocks, low, from_x, from_y, sizes = split_rows(count, top, half)
+    blocks, low, from_x, from_y, sizes = split_rows(count, top or 0, half)
     step = pl.program_id(0)
     group = lax.axis_index("dp")
 
@@ -114,6 +120,10 @@
                 return rows[:, pl.ds(pl.multiple_of(at, TILE), TILE)]
 
             at = blocks + q
+            if direct:
+                for mask, ref in enumerate(plane_refs):
+                    ref[at * count : (at + 1) * count] = cut(mask)
+                continue
             own_ref[at * count : (at + 1) * count] = cut(0)
             far = cut(3)
             to_x[at * top : (at + 1) * top] = far[:top]
@@ -141,6 +151,10 @@
         def rows_at(start, count):
             return pl.ds(pl.multiple_of(start + block * count, 16), count)
 
+        if direct:
+            for ref in plane_refs:
+                ref[rows_at(0, count)] = values
+            continue
         own_ref[rows_at(0, count)] = values
         to_x[rows_at(0, top)] = values[:top]
         to_x[rows_at(from_x, low)] = values[top:]
@@ -160,10 +174,12 @@
     width, both = weight_gu.shape
     half = both // 2
     steps = half // TILE
-    blocks, _, _, _, sizes = split_rows(count, top, half)
-    sizes = [(blocks + 4) * count] + [
-        size + extra for size, extra in zip(sizes, relays or (0, 0))
-    ]
+    blocks, _, _, _, sizes = split_rows(count, top or 0, half)
+    whole_rows = (blocks + 4) * count
+    if top is None:
+        sizes = [whole_rows] * 4
+    else:
+        sizes = [whole_rows] + [size + extra for size, extra in zip(sizes, relays or (0, 0))]
     shapes = [(size, TILE) for size in sizes]
 
     def whole(shape):
@@ -195,10 +211,11 @@
 
 
 def gradient_kernel(chunks, half, adding, *refs):
-    groups, refs = (
-        [refs[5 * n : 5 * n + 5] for n in range(len(chunks))],
-        refs[5 * len(chunks) :],
-    )
+    groups = []
+    for chunk in chunks:
+        size = 4 if chunk[1] is None else 5
+        groups.append(refs[:size])
+        refs = refs[size:]
     if adding:
         (acc_gu, acc_down), refs = refs[:2], refs[2:]
     out_gu, out_down, turned, s_rows = refs
@@ -213,6 +230,9 @@
     def factor(block):
         parts = []
         for (count, top, at_top, at_low), group in zip(chunks, groups):
+            if top is None:
+                parts += [ref[block * count : (block + 1) * count] for ref in group]
+                continue
             own, got_x, got_y, *far = group
             _, low, from_x, from_y, _ = split_rows(count, top, half)
             parts += [
@@ -227,6 +247,10 @@
     def piece(q):
         parts = []
         for (count, top, at_top, at_low), group in zip(chunks, groups):
+            if top is None:
+                block = 3 * half // TILE + q
+                parts += [ref[block * count : (block + 1) * count] for ref in group]
+                continue
             own, got_x, got_y, *far = group
             blocks, low, from_x, from_y, _ = split_rows(count, top, half)
             block = blocks + q
@@ -322,7 +346,6 @@
     ids, probs = expert_ids.T, gate_probs.T
     *local, slots = dispatch_rows(ids, probs, tokens, cotangent)
     weights = (gate_up[0], down[0])
-    _, _, cut_x0, cut_y0, _ = split_rows(PAIR, 48, half)
     _, _, cut_x1, cut_y1, _ = split_rows(2 * PAIR, PAIR, half)
     _, _, cut_x2, cut_y2, _ = split_rows(PAIR, 32, half)
 
@@ -334,21 +357,18 @@
 
     rows_2 = exchange(local[2], "expert", 4)
     rows_1 = exchange(local[1], "expert", 2)
-    own_0, to_x, to_y, inner_0 = expert_rows(
-        (local[0], other_core(local[0][CAP:])), *weights, 48
-    )
-    got_x0, got_y0 = to_plane(to_x, to_y)
-    low_0, top_0 = to_plane(got_y0[:cut_y0], got_x0[:cut_x0])
+    own_0, *sent_0, inner_0 = expert_rows(
+        (local[0], other_core(local[0][CAP:])), *weights, None
+    )
+    got_0 = tuple(exchange(part, "dp", mask + 1) for mask, part in enumerate(sent_0))
     rows_2, rows_1 = after((rows_2, rows_1), inner_0)
     other_2, other_1 = other_core(rows_2[CAP:]), other_core(rows_1[CAP:])
     rows_3 = exchange(after(local[3], rows_2), "expert", 6)
     own_1, to_x, to_y, inner_1, inner_2 = expert_rows(
         (rows_1, other_1, rows_2, other_2), *weights, PAIR
     )
-    got_x1, got_y1 = to_plane(*after((to_x, to_y), low_0, top_0))
-    sums = gradients(
-        ((PAIR, 48, 0, 0),), (own_0, got_x0, got_y0, top_0, low_0), half, quarter
-    )
+    got_x1, got_y1 = to_plane(*after((to_x, to_y), *got_0))
+    sums = gradients(((PAIR, None, 0, 0),), (own_0, *got_0), half, quarter)
     back_1, back_2 = after((inner_1, inner_2), *sums)
     inner_1, inner_2 = exchange(back_1, "expert", 2), exchange(back_2, "expert", 4)
     rows_3 = after(rows_3, inner_1, inner_2)

time: 118 us -> 117 us (level)
  starting transfers between devices: 29.6 us -> 25.1 us
  waiting for transfers between devices: 60.1 us -> 63.5 us
    ppermute x23 -> x22, starting transfers between devices: 29.6 us -> 25.1 us  [exchange(): return lax.ppermute(values, axis, [(n, n ^ mask) for n in range(size)])]
    ppermute x23 -> x22, waiting for transfers between devices: 60.1 us -> 63.5 us  [exchange(): return lax.ppermute(values, axis, [(n, n ^ mask) for n in range(size)])]
  transfers between devices with their start and end apart: 23 -> 22, of which waited for: 13 -> 14; matrix products, arithmetic and copies ran while one was open for 0% -> 0% of each run, Pallas kernels for 13% -> 13%
where the time goes in v8:
time: 117 us; the launch traced here: 116 us
  waiting for transfers between devices  63.5 us (54%)
  starting transfers between devices  25.1 us (21%)
  Pallas kernels  18.6 us (16%)
  local copies, waits for them, and re-layouts  8.33 us (7%)
    ppermute x22, waiting for transfers between devices, exchange(): return lax.ppermute(values, axis, [(n, n ^ mask) for n in range(size)])  63.5 us
    ppermute x22, starting transfers between devices, exchange(): return lax.ppermute(values, axis, [(n, n ^ mask) for n in range(size)])  25.1 us
    pallas_call x3, Pallas kernels, expert_rows(): pl.pallas_call(functools.partial(expert_kernel, pairs, top, tuple(relays)...  11.1 us
    unnamed x18, local copies, waits for them, and re-layouts  8.12 us
    pallas_call x3, Pallas kernels, gradients(): pl.pallas_call(functools.partial(gradient_kernel, chunks, half, len(sums)...  5.96 us
  transfers between devices with their start and end apart: 22, of which 14 were waited for; matrix products, arithmetic and copies ran while one was open for 0% of the time, Pallas kernels for 13%

profile of v8, /device:TPU:0, one launch (start us, length us, event | category | flops | bytes accessed | tf_op | source)
XLA Modules:
  0.0 116.3 jit_solution(18434007396820795912)
XLA Ops:
  0.6 0.0 copy-start.4
  0.6 0.7 copy-done.4
  1.3 0.0 copy-start.6
  1.3 1.0 copy-done.6
  2.4 0.0 copy-start.7
  2.4 1.0 copy-done.7
  3.4 0.7 copy-done.8
  4.1 1.0 dispatch_rows.1
  5.0 4.1 %collective-permute-start.1 = (bf16[80,4096]{1,0:T(8,128)(2,1)S(1)}, bf16[80,4096]{1,0:T(8,128)(2,1)S(1)}, u32[]{:S(2)}, u32[]{:S(2)}) collective-permute-start(bf16[80,4096]{1,0:T(8,128)(2,1)S(1)} %get-tuple-element.42), channel_id=1, source_target_pairs={{0,4},{1,5},{2,6},{3,7},{4,0},{5,1},{6,2},{7,3},{8,12},{9,13},{10,... | collective-permute-start | bytes 1966088 | tf_op jit(solution)/shard_map/ppermute | solution.py:332
  9.1 1.6 %collective-permute-start.2 = (bf16[80,4096]{1,0:T(8,128)(2,1)S(1)}, bf16[80,4096]{1,0:T(8,128)(2,1)S(1)}, u32[]{:S(2)}, u32[]{:S(2)}) collective-permute-start(bf16[80,4096]{1,0:T(8,128)(2,1)S(1)} %get-tuple-element.43), channel_id=1, source_target_pairs={{0,2},{1,3},{2,0},{3,1},{4,6},{5,7},{6,4},{7,5},{8,10},{9,11},{10,... | collective-permute-start | bytes 1966088 | tf_op jit(solution)/shard_map/ppermute | solution.py:332
  10.7 0.1 collective-permute-start
  10.8 1.6 %collective-permute-done.refs_1_ = bf16[40,4096]{1,0:T(8,128)(2,1)S(1)} collective-permute-done((bf16[40,4096]{1,0:T(8,128)(2,1)S(1)}, bf16[40,4096]{1,0:T(8,128)(2,1)S(1)}, u32[]{:S(2)}, u32[]{:S(2)}) %collective-permute-start) | collective-permute-done | bytes 327712 | tf_op jit(solution)/shard_map/ppermute | solution.py:332
  12.4 2.8 %copy-done = bf16[1,2048,1536]{2,1,0:T(8,128)(2,1)S(1)} copy-done((bf16[1,2048,1536]{2,1,0:T(8,128)(2,1)S(1)}, bf16[1,2048,1536]{2,1,0:T(8,128)(2,1)}, u32[]{:S(2)}) %copy-start) | copy-done | bytes 6291480
  15.2 1.9 %copy-done.2 = bf16[1,768,2048]{2,1,0:T(8,128)(2,1)S(1)} copy-done((bf16[1,768,2048]{2,1,0:T(8,128)(2,1)S(1)}, bf16[1,768,2048]{2,1,0:T(8,128)(2,1)}, u32[]{:S(2)}) %copy-start.2) | copy-done | bytes 3145752
  17.1 3.6 %expert_rows.3 = (bf16[1040,256]{1,0:T(8,128)(2,1)S(1)}, bf16[1040,256]{1,0:T(8,128)(2,1)S(1)}, bf16[1040,256]{1,0:T(8,128)(2,1)S(1)}, bf16[1040,256]{1,0:T(8,128)(2,1)S(1)}, f32[80,128]{1,0:T(8,128)S(1)}) custom-call(bf16[80,4096]{1,0:T(8,128)(2,1)S(1)} %get-tuple-element.40.refs_0_, bf16[40,4096]{1,0:T(8,128)(2,1)S(1)} %collective-permute-done.refs_1_, ...), custom_call_target="tpu_custom_call" | custom-call | flops 1000 | bytes 1000 | tf_op jit(solution)/shard_map/expert_rows/pallas_call | solution.py:188
  20.7 1.6 %collective-permute-start.5 = (bf16[1040,256]{1,0:T(8,128)(2,1)S(1)}, bf16[1040,256]{1,0:T(8,128)(2,1)S(1)}, u32[]{:S(2)}, u32[]{:S(2)}) collective-permute-start(bf16[1040,256]{1,0:T(8,128)(2,1)S(1)} %get-tuple-element.49), channel_id=1, source_target_pairs={{0,8},{8,0},{16,24},{24,16},{1,9},{9,1},{17,25},{25,17},{2,10},{10... | collective-permute-start | bytes 1597448 | tf_op jit(solution)/shard_map/ppermute | solution.py:332
  22.3 1.5 %collective-permute-start.6 = (bf16[1040,256]{1,0:T(8,128)(2,1)S(1)}, bf16[1040,256]{1,0:T(8,128)(2,1)S(1)}, u32[]{:S(2)}, u32[]{:S(2)}) collective-permute-start(bf16[1040,256]{1,0:T(8,128)(2,1)S(1)} %get-tuple-element.50), channel_id=1, source_target_pairs={{0,16},{8,24},{16,0},{24,8},{1,17},{9,25},{17,1},{25,9},{2,18},{10... | collective-permute-start | bytes 1597448 | tf_op jit(solution)/shard_map/ppermute | solution.py:332
  23.8 0.5 collective-permute-start.7
  24.3 13.8 %collective-permute-done.1.refs_2_ = bf16[80,4096]{1,0:T(8,128)(2,1)S(1)} collective-permute-done((bf16[80,4096]{1,0:T(8,128)(2,1)S(1)}, bf16[80,4096]{1,0:T(8,128)(2,1)S(1)}, u32[]{:S(2)}, u32[]{:S(2)}) %collective-permute-start.1) | collective-permute-done | bytes 655392 | tf_op jit(solution)/shard_map/ppermute | solution.py:332
  38.0 0.2 collective-permute-done.2.refs_0_
  38.2 0.1 collective-permute-start.4
  38.4 0.6 collective-permute-start.3
  38.9 1.0 collective-permute-done.4.refs_3_
  39.9 3.2 %collective-permute-start.10 = (bf16[80,4096]{1,0:T(8,128)(2,1)S(1)}, bf16[80,4096]{1,0:T(8,128)(2,1)S(1)}, u32[]{:S(2)}, u32[]{:S(2)}) collective-permute-start(bf16[80,4096]{1,0:T(8,128)(2,1)S(1)} %get-tuple-element.57), channel_id=1, source_target_pairs={{0,6},{1,7},{2,4},{3,5},{4,2},{5,3},{6,0},{7,1},{8,14},{9,15},{10,... | collective-permute-start | bytes 1966088 | tf_op jit(solution)/shard_map/ppermute | solution.py:332
  43.2 0.0 collective-permute-done.3.refs_1_
  43.2 0.0 copy-done.1
  43.2 0.0 copy-done.3
  43.2 3.9 %expert_rows.4 = (bf16[2080,256]{1,0:T(8,128)(2,1)S(1)}, bf16[2400,256]{1,0:T(8,128)(2,1)S(1)}, bf16[2400,256]{1,0:T(8,128)(2,1)S(1)}, f32[80,128]{1,0:T(8,128)S(1)}, f32[80,128]{1,0:T(8,128)S(1)}) custom-call(bf16[80,4096]{1,0:T(8,128)(2,1)S(1)} %collective-permute-done.2.refs_0_, bf16[40,4096]{1,0:T(8,128)(2,1)S(1)} %collective-permute-done.3.refs_1_, ...), custom_call_target="tpu_custom_call" | custom-call | flops 1000 | bytes 1000 | tf_op jit(solution)/shard_map/expert_rows/pallas_call | solution.py:188
  47.1 0.0 collective-permute-done.5.refs_1_
  47.1 0.4 collective-permute-done.6.refs_2_
  47.5 0.0 collective-permute-done.7.refs_3_
  47.5 1.2 %collective-permute-start.18 = (bf16[2400,256]{1,0:T(8,128)(2,1)S(1)}, bf16[2400,256]{1,0:T(8,128)(2,1)S(1)}, u32[]{:S(2)}, u32[]{:S(2)}) collective-permute-start(bf16[2400,256]{1,0:T(8,128)(2,1)S(1)} %get-tuple-element.69), channel_id=1, source_target_pairs={{0,8},{8,0},{16,24},{24,16},{1,9},{9,1},{17,25},{25,17},{2,10},{10... | collective-permute-start | bytes 3686408 | tf_op jit(solution)/shard_map/ppermute | solution.py:332
  48.8 1.5 %collective-permute-start.19 = (bf16[2400,256]{1,0:T(8,128)(2,1)S(1)}, bf16[2400,256]{1,0:T(8,128)(2,1)S(1)}, u32[]{:S(2)}, u32[]{:S(2)}) collective-permute-start(bf16[2400,256]{1,0:T(8,128)(2,1)S(1)} %get-tuple-element.70), channel_id=1, source_target_pairs={{0,16},{8,24},{16,0},{24,8},{1,17},{9,25},{17,1},{25,9},{2,18},{10... | collective-permute-start | bytes 3686408 | tf_op jit(solution)/shard_map/ppermute | solution.py:332
  50.2 1.4 %gradients.3 = (f32[512,1536]{1,0:T(8,128)S(1)}, f32[768,512]{1,0:T(8,128)S(1)}) custom-call(bf16[1040,256]{1,0:T(8,128)(2,1)S(1)} %get-tuple-element.48.refs_0_, bf16[1040,256]{1,0:T(8,128)(2,1)S(1)} %collective-permute-done.5.refs_1_, bf16[1040,256]{1,0:T(8,128)(2,1)S(1)} %collective-permute-done.6.refs_2_, ...), custom_call_target="tpu_custom_call" | custom-call | flops 1000 | bytes 1000 | tf_op jit(solution)/shard_map/gradients/pallas_call | solution.py:287
  51.7 0.1 collective-permute-start.8
  51.8 1.2 %collective-permute-start.9 = (f32[80,128]{1,0:T(8,128)S(1)}, f32[80,128]{1,0:T(8,128)S(1)}, u32[]{:S(2)}, u32[]{:S(2)}) collective-permute-start(f32[80,128]{1,0:T(8,128)S(1)} %get-tuple-element.55), channel_id=1, source_target_pairs={{0,4},{1,5},{2,6},{3,7},{4,0},{5,1},{6,2},{7,3},{8,12},{9,13},{10,... | collective-permute-start | bytes 122888 | tf_op jit(solution)/shard_map/ppermute | solution.py:332
  52.9 6.5 %collective-permute-done.8.own_1 = f32[80,128]{1,0:T(8,128)S(1)} collective-permute-done((f32[80,128]{1,0:T(8,128)S(1)}, f32[80,128]{1,0:T(8,128)S(1)}, u32[]{:S(2)}, u32[]{:S(2)}) %collective-permute-start.8) | collective-permute-done | bytes 40992 | tf_op jit(solution)/shard_map/ppermute | solution.py:332
  59.5 13.9 %collective-permute-done.9.own_2 = f32[80,128]{1,0:T(8,128)S(1)} collective-permute-done((f32[80,128]{1,0:T(8,128)S(1)}, f32[80,128]{1,0:T(8,128)S(1)}, u32[]{:S(2)}, u32[]{:S(2)}) %collective-permute-start.9) | collective-permute-done | bytes 40992 | tf_op jit(solution)/shard_map/ppermute | solution.py:332
  73.4 0.0 collective-permute-done.10.refs_0_
  73.5 0.1 collective-permute-start.11
  73.5 1.6 %collective-permute-done.11.refs_1_ = bf16[40,4096]{1,0:T(8,128)(2,1)S(1)} collective-permute-done((bf16[40,4096]{1,0:T(8,128)(2,1)S(1)}, bf16[40,4096]{1,0:T(8,128)(2,1)S(1)}, u32[]{:S(2)}, u32[]{:S(2)}) %collective-permute-start.11) | collective-permute-done | bytes 327712 | tf_op jit(solution)/shard_map/ppermute | solution.py:332
  75.2 3.6 %expert_rows.5 = (bf16[1040,256]{1,0:T(8,128)(2,1)S(1)}, bf16[1168,256]{1,0:T(8,128)(2,1)S(1)}, bf16[1232,256]{1,0:T(8,128)(2,1)S(1)}, f32[80,128]{1,0:T(8,128)S(1)}) custom-call(bf16[80,4096]{1,0:T(8,128)(2,1)S(1)} %collective-permute-done.10.refs_0_, bf16[40,4096]{1,0:T(8,128)(2,1)S(1)} %collective-permute-done.11.refs_1_, ...), custom_call_target="tpu_custom_call" | custom-call | flops 1000 | bytes 1000 | tf_op jit(solution)/shard_map/expert_rows/pallas_call | solution.py:188
  78.7 1.6 %collective-permute-start.15 = (bf16[1232,256]{1,0:T(8,128)(2,1)S(1)}, bf16[1232,256]{1,0:T(8,128)(2,1)S(1)}, u32[]{:S(2)}, u32[]{:S(2)}) collective-permute-start(bf16[1232,256]{1,0:T(8,128)(2,1)S(1)} %get-tuple-element.63), channel_id=1, source_target_pairs={{0,16},{8,24},{16,0},{24,8},{1,17},{9,25},{17,1},{25,9},{2,18},{10... | collective-permute-start | bytes 1892360 | tf_op jit(solution)/shard_map/ppermute | solution.py:332
  80.3 1.5 %collective-permute-start.14 = (bf16[1168,256]{1,0:T(8,128)(2,1)S(1)}, bf16[1168,256]{1,0:T(8,128)(2,1)S(1)}, u32[]{:S(2)}, u32[]{:S(2)}) collective-permute-start(bf16[1168,256]{1,0:T(8,128)(2,1)S(1)} %get-tuple-element.62), channel_id=1, source_target_pairs={{0,8},{8,0},{16,24},{24,16},{1,9},{9,1},{17,25},{25,17},{2,10},{10... | collective-permute-start | bytes 1794056 | tf_op jit(solution)/shard_map/ppermute | solution.py:332
  81.8 1.4 %collective-permute-start.12 = (f32[80,128]{1,0:T(8,128)S(1)}, f32[80,128]{1,0:T(8,128)S(1)}, u32[]{:S(2)}, u32[]{:S(2)}) collective-permute-start(f32[80,128]{1,0:T(8,128)S(1)} %get-tuple-element.59), channel_id=1, source_target_pairs={{0,6},{1,7},{2,4},{3,5},{4,2},{5,3},{6,0},{7,1},{8,14},{9,15},{10,... | collective-permute-start | bytes 122888 | tf_op jit(solution)/shard_map/ppermute | solution.py:332
  83.2 0.0 collective-permute-done.18.refs_1_
  83.2 0.0 collective-permute-done.19.refs_2_
  83.3 0.6 collective-permute-start.21
  83.9 0.5 collective-permute-start.20
  84.4 3.2 %collective-permute-done.12.own_3 = f32[80,128]{1,0:T(8,128)S(1)} collective-permute-done((f32[80,128]{1,0:T(8,128)S(1)}, f32[80,128]{1,0:T(8,128)S(1)}, u32[]{:S(2)}, u32[]{:S(2)}) %collective-permute-start.12) | collective-permute-done | bytes 40992 | tf_op jit(solution)/shard_map/ppermute | solution.py:332
  87.6 0.1 collective-permute-start.13
  87.7 1.3 %collective-permute-done.13.other_ref = f32[160,128]{1,0:T(8,128)S(1)} collective-permute-done((f32[160,128]{1,0:T(8,128)S(1)}, f32[160,128]{1,0:T(8,128)S(1)}, u32[]{:S(2)}, u32[]{:S(2)}) %collective-permute-start.13) | collective-permute-done | bytes 81952 | tf_op jit(solution)/shard_map/ppermute | solution.py:332
  89.0 7.7 %collective-permute-done.14.refs_1_ = bf16[1168,256]{1,0:T(8,128)(2,1)S(1)} collective-permute-done((bf16[1168,256]{1,0:T(8,128)(2,1)S(1)}, bf16[1168,256]{1,0:T(8,128)(2,1)S(1)}, u32[]{:S(2)}, u32[]{:S(2)}) %collective-permute-start.14) | collective-permute-done | bytes 598048 | tf_op jit(solution)/shard_map/ppermute | solution.py:332
  96.7 0.0 collective-permute-done.15.refs_2_
  96.8 1.5 %collective-permute-start.17 = (bf16[624,256]{1,0:T(8,128)(2,1)S(1)}, bf16[624,256]{1,0:T(8,128)(2,1)S(1)}, u32[]{:S(2)}, u32[]{:S(2)}) collective-permute-start(bf16[624,256]{1,0:T(8,128)(2,1)S(1)} %slice.45), channel_id=1, source_target_pairs={{0,8},{8,0},{16,24},{24,16},{1,9},{9,1},{17,25},{25,17},{2,10},{10... | collective-permute-start | bytes 958472 | tf_op jit(solution)/shard_map/ppermute | solution.py:332
  98.3 0.7 collective-permute-start.16
  99.0 0.0 copy-done.5
  99.0 0.6 prob_gradients.1
  99.7 8.5 %collective-permute-done.21.refs_4_ = bf16[1040,256]{1,0:T(8,128)(2,1)S(1)} collective-permute-done((bf16[1040,256]{1,0:T(8,128)(2,1)S(1)}, bf16[1040,256]{1,0:T(8,128)(2,1)S(1)}, u32[]{:S(2)}, u32[]{:S(2)}) %collective-permute-start.21) | collective-permute-done | bytes 532512 | tf_op jit(solution)/shard_map/ppermute | solution.py:332
  108.1 0.0 collective-permute-done.20.refs_3_
  108.1 2.1 %gradients.4 = (f32[512,1536]{1,0:T(8,128)S(1)}, f32[768,512]{1,0:T(8,128)S(1)}) custom-call(bf16[2080,256]{1,0:T(8,128)(2,1)S(1)} %get-tuple-element.66.refs_0_, bf16[2400,256]{1,0:T(8,128)(2,1)S(1)} %collective-permute-done.18.refs_1_, bf16[2400,256]{1,0:T(8,128)(2,1)S(1)} %collective-permute-done.19.refs_2_, ...), custom_call_target="tpu_custom_call" | custom-call | flops 1000 | bytes 1000 | tf_op jit(solution)/shard_map/gradients/pallas_call | solution.py:287
  110.2 0.8 collective-permute-done.16.refs_3_
  111.0 2.8 %collective-permute-done.17.refs_4_ = bf16[624,256]{1,0:T(8,128)(2,1)S(1)} collective-permute-done((bf16[624,256]{1,0:T(8,128)(2,1)S(1)}, bf16[624,256]{1,0:T(8,128)(2,1)S(1)}, u32[]{:S(2)}, u32[]{:S(2)}) %collective-permute-start.17) | collective-permute-done | bytes 319520 | tf_op jit(solution)/shard_map/ppermute | solution.py:332
  113.8 2.4 %gradients.5 = (bf16[512,1536]{1,0:T(8,128)(2,1)}, bf16[768,512]{1,0:T(8,128)(2,1)}) custom-call(bf16[1040,256]{1,0:T(8,128)(2,1)S(1)} %get-tuple-element.61.refs_0_, bf16[1168,256]{1,0:T(8,128)(2,1)S(1)} %collective-permute-done.14.refs_1_, bf16[1232,256]{1,0:T(8,128)(2,1)S(1)} %collective-permute-done.15.refs_2_, ...), custom_call_target="tpu_custom_call" | custom-call | flops 1000 | bytes 1000 | tf_op jit(solution)/shard_map/gradients/pallas_call | solution.py:287
  (19 shorter events, 0.2 us)
Async XLA Ops:
  0.6 0.7 copy-start.4
  1.3 1.0 copy-start.6
  2.4 1.0 copy-start.7
  3.4 0.7 copy-start.8
  5.0 33.0 %collective-permute-start.1 = (bf16[80,4096]{1,0:T(8,128)(2,1)S(1)}, bf16[80,4096]{1,0:T(8,128)(2,1)S(1)}, u32[]{:S(2)}, u32[]{:S(2)}) collective-permute-start(bf16[80,4096]{1,0:T(8,128)(2,1)S(1)} %get-tuple-element.42), channel_id=1, source_target_pairs={{0,4},{1,5},{2,6},{3,7},{4,0},{5,1},{6,2},{7,3},{8,12},{9,13},{10,... | collective-permute-start | bytes 1966088 | tf_op jit(solution)/shard_map/ppermute | solution.py:332
  9.1 29.1 %collective-permute-start.2 = (bf16[80,4096]{1,0:T(8,128)(2,1)S(1)}, bf16[80,4096]{1,0:T(8,128)(2,1)S(1)}, u32[]{:S(2)}, u32[]{:S(2)}) collective-permute-start(bf16[80,4096]{1,0:T(8,128)(2,1)S(1)} %get-tuple-element.43), channel_id=1, source_target_pairs={{0,2},{1,3},{2,0},{3,1},{4,6},{5,7},{6,4},{7,5},{8,10},{9,11},{10,... | collective-permute-start | bytes 1966088 | tf_op jit(solution)/shard_map/ppermute | solution.py:332
  10.7 1.7 %collective-permute-start = (bf16[40,4096]{1,0:T(8,128)(2,1)S(1)}, bf16[40,4096]{1,0:T(8,128)(2,1)S(1)}, u32[]{:S(2)}, u32[]{:S(2)}) collective-permute-start(bf16[40,4096]{1,0:T(8,128)(2,1)S(1)} %slice.36), channel_id=1, source_target_pairs={{0,1},{1,0},{2,3},{3,2},{4,5},{5,4},{6,7},{7,6},{8,9},{9,8},{10,11... | collective-permute-start | bytes 983048 | tf_op jit(solution)/shard_map/ppermute | solution.py:332
  12.4 2.8 %copy-start = (bf16[1,2048,1536]{2,1,0:T(8,128)(2,1)S(1)}, bf16[1,2048,1536]{2,1,0:T(8,128)(2,1)}, u32[]{:S(2)}) copy-start(bf16[1,2048,1536]{2,1,0:T(8,128)(2,1)} %param.10) | copy-start | bytes 18874372
  15.2 1.9 %copy-start.2 = (bf16[1,768,2048]{2,1,0:T(8,128)(2,1)S(1)}, bf16[1,768,2048]{2,1,0:T(8,128)(2,1)}, u32[]{:S(2)}) copy-start(bf16[1,768,2048]{2,1,0:T(8,128)(2,1)} %param.11) | copy-start | bytes 9437188
  17.1 26.1 %copy-start.1 = (bf16[1,2048,1536]{2,1,0:T(8,128)(2,1)S(1)}, bf16[1,2048,1536]{2,1,0:T(8,128)(2,1)}, u32[]{:S(2)}) copy-start(bf16[1,2048,1536]{2,1,0:T(8,128)(2,1)} %param.10) | copy-start | bytes 18874372
  17.1 26.1 %copy-start.3 = (bf16[1,768,2048]{2,1,0:T(8,128)(2,1)S(1)}, bf16[1,768,2048]{2,1,0:T(8,128)(2,1)}, u32[]{:S(2)}) copy-start(bf16[1,768,2048]{2,1,0:T(8,128)(2,1)} %param.11) | copy-start | bytes 9437188
  20.7 26.4 %collective-permute-start.5 = (bf16[1040,256]{1,0:T(8,128)(2,1)S(1)}, bf16[1040,256]{1,0:T(8,128)(2,1)S(1)}, u32[]{:S(2)}, u32[]{:S(2)}) collective-permute-start(bf16[1040,256]{1,0:T(8,128)(2,1)S(1)} %get-tuple-element.49), channel_id=1, source_target_pairs={{0,8},{8,0},{16,24},{24,16},{1,9},{9,1},{17,25},{25,17},{2,10},{10... | collective-permute-start | bytes 1597448 | tf_op jit(solution)/shard_map/ppermute | solution.py:332
  22.3 25.3 %collective-permute-start.6 = (bf16[1040,256]{1,0:T(8,128)(2,1)S(1)}, bf16[1040,256]{1,0:T(8,128)(2,1)S(1)}, u32[]{:S(2)}, u32[]{:S(2)}) collective-permute-start(bf16[1040,256]{1,0:T(8,128)(2,1)S(1)} %get-tuple-element.50), channel_id=1, source_target_pairs={{0,16},{8,24},{16,0},{24,8},{1,17},{9,25},{17,1},{25,9},{2,18},{10... | collective-permute-start | bytes 1597448 | tf_op jit(solution)/shard_map/ppermute | solution.py:332
  23.8 23.8 %collective-permute-start.7 = (bf16[1040,256]{1,0:T(8,128)(2,1)S(1)}, bf16[1040,256]{1,0:T(8,128)(2,1)S(1)}, u32[]{:S(2)}, u32[]{:S(2)}) collective-permute-start(bf16[1040,256]{1,0:T(8,128)(2,1)S(1)} %get-tuple-element.51), channel_id=1, source_target_pairs={{0,24},{8,16},{16,8},{24,0},{1,25},{9,17},{17,9},{25,1},{2,26},{10... | collective-permute-start | bytes 1597448 | tf_op jit(solution)/shard_map/ppermute | solution.py:332
  38.2 1.7 %collective-permute-start.4 = (bf16[40,4096]{1,0:T(8,128)(2,1)S(1)}, bf16[40,4096]{1,0:T(8,128)(2,1)S(1)}, u32[]{:S(2)}, u32[]{:S(2)}) collective-permute-start(bf16[40,4096]{1,0:T(8,128)(2,1)S(1)} %slice.38), channel_id=1, source_target_pairs={{0,1},{1,0},{2,3},{3,2},{4,5},{5,4},{6,7},{7,6},{8,9},{9,8},{10,11... | collective-permute-start | bytes 983048 | tf_op jit(solution)/shard_map/ppermute | solution.py:332
  38.4 4.8 %collective-permute-start.3 = (bf16[40,4096]{1,0:T(8,128)(2,1)S(1)}, bf16[40,4096]{1,0:T(8,128)(2,1)S(1)}, u32[]{:S(2)}, u32[]{:S(2)}) collective-permute-start(bf16[40,4096]{1,0:T(8,128)(2,1)S(1)} %slice.37), channel_id=1, source_target_pairs={{0,1},{1,0},{2,3},{3,2},{4,5},{5,4},{6,7},{7,6},{8,9},{9,8},{10,11... | collective-permute-start | bytes 983048 | tf_op jit(solution)/shard_map/ppermute | solution.py:332
  39.9 33.5 %collective-permute-start.10 = (bf16[80,4096]{1,0:T(8,128)(2,1)S(1)}, bf16[80,4096]{1,0:T(8,128)(2,1)S(1)}, u32[]{:S(2)}, u32[]{:S(2)}) collective-permute-start(bf16[80,4096]{1,0:T(8,128)(2,1)S(1)} %get-tuple-element.57), channel_id=1, source_target_pairs={{0,6},{1,7},{2,4},{3,5},{4,2},{5,3},{6,0},{7,1},{8,14},{9,15},{10,... | collective-permute-start | bytes 1966088 | tf_op jit(solution)/shard_map/ppermute | solution.py:332
  47.5 35.6 %collective-permute-start.18 = (bf16[2400,256]{1,0:T(8,128)(2,1)S(1)}, bf16[2400,256]{1,0:T(8,128)(2,1)S(1)}, u32[]{:S(2)}, u32[]{:S(2)}) collective-permute-start(bf16[2400,256]{1,0:T(8,128)(2,1)S(1)} %get-tuple-element.69), channel_id=1, source_target_pairs={{0,8},{8,0},{16,24},{24,16},{1,9},{9,1},{17,25},{25,17},{2,10},{10... | collective-permute-start | bytes 3686408 | tf_op jit(solution)/shard_map/ppermute | solution.py:332
  48.8 34.4 %collective-permute-start.19 = (bf16[2400,256]{1,0:T(8,128)(2,1)S(1)}, bf16[2400,256]{1,0:T(8,128)(2,1)S(1)}, u32[]{:S(2)}, u32[]{:S(2)}) collective-permute-start(bf16[2400,256]{1,0:T(8,128)(2,1)S(1)} %get-tuple-element.70), channel_id=1, source_target_pairs={{0,16},{8,24},{16,0},{24,8},{1,17},{9,25},{17,1},{25,9},{2,18},{10... | collective-permute-start | bytes 3686408 | tf_op jit(solution)/shard_map/ppermute | solution.py:332
  51.7 7.8 %collective-permute-start.8 = (f32[80,128]{1,0:T(8,128)S(1)}, f32[80,128]{1,0:T(8,128)S(1)}, u32[]{:S(2)}, u32[]{:S(2)}) collective-permute-start(f32[80,128]{1,0:T(8,128)S(1)} %get-tuple-element.54), channel_id=1, source_target_pairs={{0,2},{1,3},{2,0},{3,1},{4,6},{5,7},{6,4},{7,5},{8,10},{9,11},{10,... | collective-permute-start | bytes 122888 | tf_op jit(solution)/shard_map/ppermute | solution.py:332
  51.8 21.7 %collective-permute-start.9 = (f32[80,128]{1,0:T(8,128)S(1)}, f32[80,128]{1,0:T(8,128)S(1)}, u32[]{:S(2)}, u32[]{:S(2)}) collective-permute-start(f32[80,128]{1,0:T(8,128)S(1)} %get-tuple-element.55), channel_id=1, source_target_pairs={{0,4},{1,5},{2,6},{3,7},{4,0},{5,1},{6,2},{7,3},{8,12},{9,13},{10,... | collective-permute-start | bytes 122888 | tf_op jit(solution)/shard_map/ppermute | solution.py:332
  73.5 1.7 %collective-permute-start.11 = (bf16[40,4096]{1,0:T(8,128)(2,1)S(1)}, bf16[40,4096]{1,0:T(8,128)(2,1)S(1)}, u32[]{:S(2)}, u32[]{:S(2)}) collective-permute-start(bf16[40,4096]{1,0:T(8,128)(2,1)S(1)} %slice.39), channel_id=1, source_target_pairs={{0,1},{1,0},{2,3},{3,2},{4,5},{5,4},{6,7},{7,6},{8,9},{9,8},{10,11... | collective-permute-start | bytes 983048 | tf_op jit(solution)/shard_map/ppermute | solution.py:332
  78.7 18.0 %collective-permute-start.15 = (bf16[1232,256]{1,0:T(8,128)(2,1)S(1)}, bf16[1232,256]{1,0:T(8,128)(2,1)S(1)}, u32[]{:S(2)}, u32[]{:S(2)}) collective-permute-start(bf16[1232,256]{1,0:T(8,128)(2,1)S(1)} %get-tuple-element.63), channel_id=1, source_target_pairs={{0,16},{8,24},{16,0},{24,8},{1,17},{9,25},{17,1},{25,9},{2,18},{10... | collective-permute-start | bytes 1892360 | tf_op jit(solution)/shard_map/ppermute | solution.py:332
  80.3 16.4 %collective-permute-start.14 = (bf16[1168,256]{1,0:T(8,128)(2,1)S(1)}, bf16[1168,256]{1,0:T(8,128)(2,1)S(1)}, u32[]{:S(2)}, u32[]{:S(2)}) collective-permute-start(bf16[1168,256]{1,0:T(8,128)(2,1)S(1)} %get-tuple-element.62), channel_id=1, source_target_pairs={{0,8},{8,0},{16,24},{24,16},{1,9},{9,1},{17,25},{25,17},{2,10},{10... | collective-permute-start | bytes 1794056 | tf_op jit(solution)/shard_map/ppermute | solution.py:332
  81.8 17.2 %copy-start.5 = (f32[128,2]{0,1:T(2,128)S(1)}, f32[128,2]{0,1:T(2,128)}, u32[]{:S(2)}) copy-start(f32[128,2]{0,1:T(2,128)} %param.8) | copy-start | bytes 3076
  81.8 5.8 %collective-permute-start.12 = (f32[80,128]{1,0:T(8,128)S(1)}, f32[80,128]{1,0:T(8,128)S(1)}, u32[]{:S(2)}, u32[]{:S(2)}) collective-permute-start(f32[80,128]{1,0:T(8,128)S(1)} %get-tuple-element.59), channel_id=1, source_target_pairs={{0,6},{1,7},{2,4},{3,5},{4,2},{5,3},{6,0},{7,1},{8,14},{9,15},{10,... | collective-permute-start | bytes 122888 | tf_op jit(solution)/shard_map/ppermute | solution.py:332
  83.3 24.9 %collective-permute-start.21 = (bf16[1040,256]{1,0:T(8,128)(2,1)S(1)}, bf16[1040,256]{1,0:T(8,128)(2,1)S(1)}, u32[]{:S(2)}, u32[]{:S(2)}) collective-permute-start(bf16[1040,256]{1,0:T(8,128)(2,1)S(1)} %slice.47), channel_id=1, source_target_pairs={{0,8},{8,0},{16,24},{24,16},{1,9},{9,1},{17,25},{25,17},{2,10},{10... | collective-permute-start | bytes 1597448 | tf_op jit(solution)/shard_map/ppermute | solution.py:332
  83.9 24.3 %collective-permute-start.20 = (bf16[1040,256]{1,0:T(8,128)(2,1)S(1)}, bf16[1040,256]{1,0:T(8,128)(2,1)S(1)}, u32[]{:S(2)}, u32[]{:S(2)}) collective-permute-start(bf16[1040,256]{1,0:T(8,128)(2,1)S(1)} %slice.46), channel_id=1, source_target_pairs={{0,16},{8,24},{16,0},{24,8},{1,17},{9,25},{17,1},{25,9},{2,18},{10... | collective-permute-start | bytes 1597448 | tf_op jit(solution)/shard_map/ppermute | solution.py:332
  87.6 1.3 %collective-permute-start.13 = (f32[160,128]{1,0:T(8,128)S(1)}, f32[160,128]{1,0:T(8,128)S(1)}, u32[]{:S(2)}, u32[]{:S(2)}) collective-permute-start(f32[160,128]{1,0:T(8,128)S(1)} %pad_maximum_fusion), channel_id=1, source_target_pairs={{0,1},{1,0},{2,3},{3,2},{4,5},{5,4},{6,7},{7,6},{8,9},{9,8},{10,11... | collective-permute-start | bytes 245768 | tf_op jit(solution)/shard_map/ppermute | solution.py:332
  96.8 17.1 %collective-permute-start.17 = (bf16[624,256]{1,0:T(8,128)(2,1)S(1)}, bf16[624,256]{1,0:T(8,128)(2,1)S(1)}, u32[]{:S(2)}, u32[]{:S(2)}) collective-permute-start(bf16[624,256]{1,0:T(8,128)(2,1)S(1)} %slice.45), channel_id=1, source_target_pairs={{0,8},{8,0},{16,24},{24,16},{1,9},{9,1},{17,25},{25,17},{2,10},{10... | collective-permute-start | bytes 958472 | tf_op jit(solution)/shard_map/ppermute | solution.py:332
  98.3 12.7 %collective-permute-start.16 = (bf16[416,256]{1,0:T(8,128)(2,1)S(1)}, bf16[416,256]{1,0:T(8,128)(2,1)S(1)}, u32[]{:S(2)}, u32[]{:S(2)}) collective-permute-start(bf16[416,256]{1,0:T(8,128)(2,1)S(1)} %slice.44), channel_id=1, source_target_pairs={{0,16},{8,24},{16,0},{24,8},{1,17},{9,25},{17,1},{25,9},{2,18},{10... | collective-permute-start | bytes 638984 | tf_op jit(solution)/shard_map/ppermute | solution.py:332

commit v9 on v8

--- a/solution.py
+++ b/solution.py
@@ -371,7 +371,7 @@
     sums = gradients(((PAIR, None, 0, 0),), (own_0, *got_0), half, quarter)
     back_1, back_2 = after((inner_1, inner_2), *sums)
     inner_1, inner_2 = exchange(back_1, "expert", 2), exchange(back_2, "expert", 4)
-    rows_3 = after(rows_3, inner_1, inner_2)
+    rows_3 = after(rows_3, *sums)
     own_2, to_x, to_y, inner_3 = expert_rows(
         (rows_3, other_core(rows_3[CAP:])), *weights, 32
     )

time: 117 us -> 112 us (0.957)
  the two profiles are of different devices: /device:TPU:0 before, /device:TPU:10 now
where the time goes in v9:
time: 112 us
  waiting for transfers between devices  65.1 us (58%)
  starting transfers between devices  19.2 us (17%)
  Pallas kernels  18.6 us (17%)
  local copies, waits for them, and re-layouts  8.33 us (7%)
    ppermute x22, waiting for transfers between devices, exchange(): return lax.ppermute(values, axis, [(n, n ^ mask) for n in range(size)])  65.1 us
    ppermute x22, starting transfers between devices, exchange(): return lax.ppermute(values, axis, [(n, n ^ mask) for n in range(size)])  19.2 us
    pallas_call x3, Pallas kernels, expert_rows(): pl.pallas_call(functools.partial(expert_kernel, pairs, top, tuple(relays)...  11.1 us
    unnamed x18, local copies, waits for them, and re-layouts  8.12 us
    pallas_call x3, Pallas kernels, gradients(): pl.pallas_call(functools.partial(gradient_kernel, chunks, half, len(sums)...  5.96 us
  transfers between devices with their start and end apart: 22, of which 15 were waited for; matrix products, arithmetic and copies ran while one was open for 0% of the time, Pallas kernels for 14%

profile of v9, /device:TPU:10, one launch (start us, length us, event | category | flops | bytes accessed | tf_op | source)
XLA Modules:
  0.0 112.1 jit_solution(7119574666898339585)
XLA Ops:
  0.6 0.0 copy-start.4
  0.6 0.7 copy-done.4
  1.3 0.0 copy-start.6
  1.3 1.0 copy-done.6
  2.4 0.0 copy-start.7
  2.4 1.0 copy-done.7
  3.4 0.7 copy-done.8
  4.1 1.0 dispatch_rows.1
  5.0 2.6 %collective-permute-start.1 = (bf16[80,4096]{1,0:T(8,128)(2,1)S(1)}, bf16[80,4096]{1,0:T(8,128)(2,1)S(1)}, u32[]{:S(2)}, u32[]{:S(2)}) collective-permute-start(bf16[80,4096]{1,0:T(8,128)(2,1)S(1)} %get-tuple-element.42), channel_id=1, source_target_pairs={{0,4},{1,5},{2,6},{3,7},{4,0},{5,1},{6,2},{7,3},{8,12},{9,13},{10,... | collective-permute-start | bytes 1966088 | tf_op jit(solution)/shard_map/ppermute | solution.py:332
  7.7 0.4 collective-permute-start.2
  8.2 0.1 collective-permute-start
  8.3 1.6 %collective-permute-done.refs_1_ = bf16[40,4096]{1,0:T(8,128)(2,1)S(1)} collective-permute-done((bf16[40,4096]{1,0:T(8,128)(2,1)S(1)}, bf16[40,4096]{1,0:T(8,128)(2,1)S(1)}, u32[]{:S(2)}, u32[]{:S(2)}) %collective-permute-start) | collective-permute-done | bytes 327712 | tf_op jit(solution)/shard_map/ppermute | solution.py:332
  9.9 2.8 %copy-done = bf16[1,2048,1536]{2,1,0:T(8,128)(2,1)S(1)} copy-done((bf16[1,2048,1536]{2,1,0:T(8,128)(2,1)S(1)}, bf16[1,2048,1536]{2,1,0:T(8,128)(2,1)}, u32[]{:S(2)}) %copy-start) | copy-done | bytes 6291480
  12.7 1.9 %copy-done.2 = bf16[1,768,2048]{2,1,0:T(8,128)(2,1)S(1)} copy-done((bf16[1,768,2048]{2,1,0:T(8,128)(2,1)S(1)}, bf16[1,768,2048]{2,1,0:T(8,128)(2,1)}, u32[]{:S(2)}) %copy-start.2) | copy-done | bytes 3145752
  14.5 3.6 %expert_rows.3 = (bf16[1040,256]{1,0:T(8,128)(2,1)S(1)}, bf16[1040,256]{1,0:T(8,128)(2,1)S(1)}, bf16[1040,256]{1,0:T(8,128)(2,1)S(1)}, bf16[1040,256]{1,0:T(8,128)(2,1)S(1)}, f32[80,128]{1,0:T(8,128)S(1)}) custom-call(bf16[80,4096]{1,0:T(8,128)(2,1)S(1)} %get-tuple-element.40.refs_0_, bf16[40,4096]{1,0:T(8,128)(2,1)S(1)} %collective-permute-done.refs_1_, ...), custom_call_target="tpu_custom_call" | custom-call | flops 1000 | bytes 1000 | tf_op jit(solution)/shard_map/expert_rows/pallas_call | solution.py:188
  18.1 0.6 collective-permute-start.5
  18.7 1.5 %collective-permute-start.6 = (bf16[1040,256]{1,0:T(8,128)(2,1)S(1)}, bf16[1040,256]{1,0:T(8,128)(2,1)S(1)}, u32[]{:S(2)}, u32[]{:S(2)}) collective-permute-start(bf16[1040,256]{1,0:T(8,128)(2,1)S(1)} %get-tuple-element.50), channel_id=1, source_target_pairs={{0,16},{8,24},{16,0},{24,8},{1,17},{9,25},{17,1},{25,9},{2,18},{10... | collective-permute-start | bytes 1597448 | tf_op jit(solution)/shard_map/ppermute | solution.py:332
  20.2 1.4 %collective-permute-start.7 = (bf16[1040,256]{1,0:T(8,128)(2,1)S(1)}, bf16[1040,256]{1,0:T(8,128)(2,1)S(1)}, u32[]{:S(2)}, u32[]{:S(2)}) collective-permute-start(bf16[1040,256]{1,0:T(8,128)(2,1)S(1)} %get-tuple-element.51), channel_id=1, source_target_pairs={{0,24},{8,16},{16,8},{24,0},{1,25},{9,17},{17,9},{25,1},{2,26},{10... | collective-permute-start | bytes 1597448 | tf_op jit(solution)/shard_map/ppermute | solution.py:332
  21.7 13.9 %collective-permute-done.1.refs_2_ = bf16[80,4096]{1,0:T(8,128)(2,1)S(1)} collective-permute-done((bf16[80,4096]{1,0:T(8,128)(2,1)S(1)}, bf16[80,4096]{1,0:T(8,128)(2,1)S(1)}, u32[]{:S(2)}, u32[]{:S(2)}) %collective-permute-start.1) | collective-permute-done | bytes 655392 | tf_op jit(solution)/shard_map/ppermute | solution.py:332
  35.6 1.1 collective-permute-done.2.refs_0_
  36.7 0.1 collective-permute-start.4
  36.8 0.6 collective-permute-start.3
  37.4 1.0 collective-permute-done.4.refs_3_
  38.4 0.5 collective-permute-start.10
  38.9 0.0 collective-permute-done.3.refs_1_
  38.9 0.0 copy-done.1
  38.9 0.0 copy-done.3
  38.9 3.9 %expert_rows.4 = (bf16[2080,256]{1,0:T(8,128)(2,1)S(1)}, bf16[2400,256]{1,0:T(8,128)(2,1)S(1)}, bf16[2400,256]{1,0:T(8,128)(2,1)S(1)}, f32[80,128]{1,0:T(8,128)S(1)}, f32[80,128]{1,0:T(8,128)S(1)}) custom-call(bf16[80,4096]{1,0:T(8,128)(2,1)S(1)} %collective-permute-done.2.refs_0_, bf16[40,4096]{1,0:T(8,128)(2,1)S(1)} %collective-permute-done.3.refs_1_, ...), custom_call_target="tpu_custom_call" | custom-call | flops 1000 | bytes 1000 | tf_op jit(solution)/shard_map/expert_rows/pallas_call | solution.py:188
  42.8 0.0 collective-permute-done.5.refs_1_
  42.8 0.3 collective-permute-done.6.refs_2_
  43.1 1.6 %collective-permute-done.7.refs_3_ = bf16[1040,256]{1,0:T(8,128)(2,1)S(1)} collective-permute-done((bf16[1040,256]{1,0:T(8,128)(2,1)S(1)}, bf16[1040,256]{1,0:T(8,128)(2,1)S(1)}, u32[]{:S(2)}, u32[]{:S(2)}) %collective-permute-start.7) | collective-permute-done | bytes 532512 | tf_op jit(solution)/shard_map/ppermute | solution.py:332
  44.7 0.8 collective-permute-start.18
  45.5 1.5 %collective-permute-start.19 = (bf16[2400,256]{1,0:T(8,128)(2,1)S(1)}, bf16[2400,256]{1,0:T(8,128)(2,1)S(1)}, u32[]{:S(2)}, u32[]{:S(2)}) collective-permute-start(bf16[2400,256]{1,0:T(8,128)(2,1)S(1)} %get-tuple-element.70), channel_id=1, source_target_pairs={{0,16},{8,24},{16,0},{24,8},{1,17},{9,25},{17,1},{25,9},{2,18},{10... | collective-permute-start | bytes 3686408 | tf_op jit(solution)/shard_map/ppermute | solution.py:332
  47.0 1.4 %gradients.3 = (f32[512,1536]{1,0:T(8,128)S(1)}, f32[768,512]{1,0:T(8,128)S(1)}) custom-call(bf16[1040,256]{1,0:T(8,128)(2,1)S(1)} %get-tuple-element.48.refs_0_, bf16[1040,256]{1,0:T(8,128)(2,1)S(1)} %collective-permute-done.5.refs_1_, bf16[1040,256]{1,0:T(8,128)(2,1)S(1)} %collective-permute-done.6.refs_2_, ...), custom_call_target="tpu_custom_call" | custom-call | flops 1000 | bytes 1000 | tf_op jit(solution)/shard_map/gradients/pallas_call | solution.py:287
  48.5 20.7 %collective-permute-done.10.refs_0_ = bf16[80,4096]{1,0:T(8,128)(2,1)S(1)} collective-permute-done((bf16[80,4096]{1,0:T(8,128)(2,1)S(1)}, bf16[80,4096]{1,0:T(8,128)(2,1)S(1)}, u32[]{:S(2)}, u32[]{:S(2)}) %collective-permute-start.10) | collective-permute-done | bytes 655392 | tf_op jit(solution)/shard_map/ppermute | solution.py:332
  69.2 0.1 collective-permute-start.11
  69.3 1.6 %collective-permute-done.11.refs_1_ = bf16[40,4096]{1,0:T(8,128)(2,1)S(1)} collective-permute-done((bf16[40,4096]{1,0:T(8,128)(2,1)S(1)}, bf16[40,4096]{1,0:T(8,128)(2,1)S(1)}, u32[]{:S(2)}, u32[]{:S(2)}) %collective-permute-start.11) | collective-permute-done | bytes 327712 | tf_op jit(solution)/shard_map/ppermute | solution.py:332
  70.9 3.6 %expert_rows.5 = (bf16[1040,256]{1,0:T(8,128)(2,1)S(1)}, bf16[1168,256]{1,0:T(8,128)(2,1)S(1)}, bf16[1232,256]{1,0:T(8,128)(2,1)S(1)}, f32[80,128]{1,0:T(8,128)S(1)}) custom-call(bf16[80,4096]{1,0:T(8,128)(2,1)S(1)} %collective-permute-done.10.refs_0_, bf16[40,4096]{1,0:T(8,128)(2,1)S(1)} %collective-permute-done.11.refs_1_, ...), custom_call_target="tpu_custom_call" | custom-call | flops 1000 | bytes 1000 | tf_op jit(solution)/shard_map/expert_rows/pallas_call | solution.py:188
  74.5 1.6 %collective-permute-start.15 = (bf16[1232,256]{1,0:T(8,128)(2,1)S(1)}, bf16[1232,256]{1,0:T(8,128)(2,1)S(1)}, u32[]{:S(2)}, u32[]{:S(2)}) collective-permute-start(bf16[1232,256]{1,0:T(8,128)(2,1)S(1)} %get-tuple-element.63), channel_id=1, source_target_pairs={{0,16},{8,24},{16,0},{24,8},{1,17},{9,25},{17,1},{25,9},{2,18},{10... | collective-permute-start | bytes 1892360 | tf_op jit(solution)/shard_map/ppermute | solution.py:332
  76.1 0.5 collective-permute-start.14
  76.6 0.0 collective-permute-start.8
  76.6 0.0 collective-permute-done.18.refs_1_
  76.6 1.9 %collective-permute-start.9 = (f32[80,128]{1,0:T(8,128)S(1)}, f32[80,128]{1,0:T(8,128)S(1)}, u32[]{:S(2)}, u32[]{:S(2)}) collective-permute-start(f32[80,128]{1,0:T(8,128)S(1)} %get-tuple-element.55), channel_id=1, source_target_pairs={{0,4},{1,5},{2,6},{3,7},{4,0},{5,1},{6,2},{7,3},{8,12},{9,13},{10,... | collective-permute-start | bytes 122888 | tf_op jit(solution)/shard_map/ppermute | solution.py:332
  78.6 0.0 collective-permute-done.19.refs_2_
  78.6 1.6 %collective-permute-start.12 = (f32[80,128]{1,0:T(8,128)S(1)}, f32[80,128]{1,0:T(8,128)S(1)}, u32[]{:S(2)}, u32[]{:S(2)}) collective-permute-start(f32[80,128]{1,0:T(8,128)S(1)} %get-tuple-element.59), channel_id=1, source_target_pairs={{0,6},{1,7},{2,4},{3,5},{4,2},{5,3},{6,0},{7,1},{8,14},{9,15},{10,... | collective-permute-start | bytes 122888 | tf_op jit(solution)/shard_map/ppermute | solution.py:332
  80.2 0.4 collective-permute-done.8.own_1
  80.6 1.5 %collective-permute-start.21 = (bf16[1040,256]{1,0:T(8,128)(2,1)S(1)}, bf16[1040,256]{1,0:T(8,128)(2,1)S(1)}, u32[]{:S(2)}, u32[]{:S(2)}) collective-permute-start(bf16[1040,256]{1,0:T(8,128)(2,1)S(1)} %slice.47), channel_id=1, source_target_pairs={{0,8},{8,0},{16,24},{24,16},{1,9},{9,1},{17,25},{25,17},{2,10},{10... | collective-permute-start | bytes 1597448 | tf_op jit(solution)/shard_map/ppermute | solution.py:332
  82.1 0.0 collective-permute-done.9.own_2
  82.1 0.5 collective-permute-start.20
  82.7 0.6 collective-permute-done.12.own_3
  83.2 0.1 collective-permute-start.13
  83.3 1.3 %collective-permute-done.13.other_ref = f32[160,128]{1,0:T(8,128)S(1)} collective-permute-done((f32[160,128]{1,0:T(8,128)S(1)}, f32[160,128]{1,0:T(8,128)S(1)}, u32[]{:S(2)}, u32[]{:S(2)}) %collective-permute-start.13) | collective-permute-done | bytes 81952 | tf_op jit(solution)/shard_map/ppermute | solution.py:332
  84.6 7.9 %collective-permute-done.14.refs_1_ = bf16[1168,256]{1,0:T(8,128)(2,1)S(1)} collective-permute-done((bf16[1168,256]{1,0:T(8,128)(2,1)S(1)}, bf16[1168,256]{1,0:T(8,128)(2,1)S(1)}, u32[]{:S(2)}, u32[]{:S(2)}) %collective-permute-start.14) | collective-permute-done | bytes 598048 | tf_op jit(solution)/shard_map/ppermute | solution.py:332
  92.5 0.0 collective-permute-done.15.refs_2_
  92.5 0.6 collective-permute-start.17
  93.1 0.7 collective-permute-start.16
  93.9 0.0 copy-done.5
  93.9 0.6 prob_gradients.1
  94.5 9.4 %collective-permute-done.21.refs_4_ = bf16[1040,256]{1,0:T(8,128)(2,1)S(1)} collective-permute-done((bf16[1040,256]{1,0:T(8,128)(2,1)S(1)}, bf16[1040,256]{1,0:T(8,128)(2,1)S(1)}, u32[]{:S(2)}, u32[]{:S(2)}) %collective-permute-start.21) | collective-permute-done | bytes 532512 | tf_op jit(solution)/shard_map/ppermute | solution.py:332
  103.9 0.0 collective-permute-done.20.refs_3_
  103.9 2.1 %gradients.4 = (f32[512,1536]{1,0:T(8,128)S(1)}, f32[768,512]{1,0:T(8,128)S(1)}) custom-call(bf16[2080,256]{1,0:T(8,128)(2,1)S(1)} %get-tuple-element.66.refs_0_, bf16[2400,256]{1,0:T(8,128)(2,1)S(1)} %collective-permute-done.18.refs_1_, bf16[2400,256]{1,0:T(8,128)(2,1)S(1)} %collective-permute-done.19.refs_2_, ...), custom_call_target="tpu_custom_call" | custom-call | flops 1000 | bytes 1000 | tf_op jit(solution)/shard_map/gradients/pallas_call | solution.py:287
  106.0 0.8 collective-permute-done.16.refs_3_
  106.8 2.8 %collective-permute-done.17.refs_4_ = bf16[624,256]{1,0:T(8,128)(2,1)S(1)} collective-permute-done((bf16[624,256]{1,0:T(8,128)(2,1)S(1)}, bf16[624,256]{1,0:T(8,128)(2,1)S(1)}, u32[]{:S(2)}, u32[]{:S(2)}) %collective-permute-start.17) | collective-permute-done | bytes 319520 | tf_op jit(solution)/shard_map/ppermute | solution.py:332
  109.6 2.4 %gradients.5 = (bf16[512,1536]{1,0:T(8,128)(2,1)}, bf16[768,512]{1,0:T(8,128)(2,1)}) custom-call(bf16[1040,256]{1,0:T(8,128)(2,1)S(1)} %get-tuple-element.61.refs_0_, bf16[1168,256]{1,0:T(8,128)(2,1)S(1)} %collective-permute-done.14.refs_1_, bf16[1232,256]{1,0:T(8,128)(2,1)S(1)} %collective-permute-done.15.refs_2_, ...), custom_call_target="tpu_custom_call" | custom-call | flops 1000 | bytes 1000 | tf_op jit(solution)/shard_map/gradients/pallas_call | solution.py:287
  (19 shorter events, 0.2 us)
Async XLA Ops:
  0.6 0.7 copy-start.4
  1.3 1.0 copy-start.6
  2.4 1.0 copy-start.7
  3.4 0.7 copy-start.8
  5.0 30.6 %collective-permute-start.1 = (bf16[80,4096]{1,0:T(8,128)(2,1)S(1)}, bf16[80,4096]{1,0:T(8,128)(2,1)S(1)}, u32[]{:S(2)}, u32[]{:S(2)}) collective-permute-start(bf16[80,4096]{1,0:T(8,128)(2,1)S(1)} %get-tuple-element.42), channel_id=1, source_target_pairs={{0,4},{1,5},{2,6},{3,7},{4,0},{5,1},{6,2},{7,3},{8,12},{9,13},{10,... | collective-permute-start | bytes 1966088 | tf_op jit(solution)/shard_map/ppermute | solution.py:332
  7.7 29.0 %collective-permute-start.2 = (bf16[80,4096]{1,0:T(8,128)(2,1)S(1)}, bf16[80,4096]{1,0:T(8,128)(2,1)S(1)}, u32[]{:S(2)}, u32[]{:S(2)}) collective-permute-start(bf16[80,4096]{1,0:T(8,128)(2,1)S(1)} %get-tuple-element.43), channel_id=1, source_target_pairs={{0,2},{1,3},{2,0},{3,1},{4,6},{5,7},{6,4},{7,5},{8,10},{9,11},{10,... | collective-permute-start | bytes 1966088 | tf_op jit(solution)/shard_map/ppermute | solution.py:332
  8.2 1.7 %collective-permute-start = (bf16[40,4096]{1,0:T(8,128)(2,1)S(1)}, bf16[40,4096]{1,0:T(8,128)(2,1)S(1)}, u32[]{:S(2)}, u32[]{:S(2)}) collective-permute-start(bf16[40,4096]{1,0:T(8,128)(2,1)S(1)} %slice.36), channel_id=1, source_target_pairs={{0,1},{1,0},{2,3},{3,2},{4,5},{5,4},{6,7},{7,6},{8,9},{9,8},{10,11... | collective-permute-start | bytes 983048 | tf_op jit(solution)/shard_map/ppermute | solution.py:332
  9.9 2.8 %copy-start = (bf16[1,2048,1536]{2,1,0:T(8,128)(2,1)S(1)}, bf16[1,2048,1536]{2,1,0:T(8,128)(2,1)}, u32[]{:S(2)}) copy-start(bf16[1,2048,1536]{2,1,0:T(8,128)(2,1)} %param.10) | copy-start | bytes 18874372
  12.7 1.9 %copy-start.2 = (bf16[1,768,2048]{2,1,0:T(8,128)(2,1)S(1)}, bf16[1,768,2048]{2,1,0:T(8,128)(2,1)}, u32[]{:S(2)}) copy-start(bf16[1,768,2048]{2,1,0:T(8,128)(2,1)} %param.11) | copy-start | bytes 9437188
  14.5 24.3 %copy-start.1 = (bf16[1,2048,1536]{2,1,0:T(8,128)(2,1)S(1)}, bf16[1,2048,1536]{2,1,0:T(8,128)(2,1)}, u32[]{:S(2)}) copy-start(bf16[1,2048,1536]{2,1,0:T(8,128)(2,1)} %param.10) | copy-start | bytes 18874372
  14.5 24.3 %copy-start.3 = (bf16[1,768,2048]{2,1,0:T(8,128)(2,1)S(1)}, bf16[1,768,2048]{2,1,0:T(8,128)(2,1)}, u32[]{:S(2)}) copy-start(bf16[1,768,2048]{2,1,0:T(8,128)(2,1)} %param.11) | copy-start | bytes 9437188
  18.1 24.7 %collective-permute-start.5 = (bf16[1040,256]{1,0:T(8,128)(2,1)S(1)}, bf16[1040,256]{1,0:T(8,128)(2,1)S(1)}, u32[]{:S(2)}, u32[]{:S(2)}) collective-permute-start(bf16[1040,256]{1,0:T(8,128)(2,1)S(1)} %get-tuple-element.49), channel_id=1, source_target_pairs={{0,8},{8,0},{16,24},{24,16},{1,9},{9,1},{17,25},{25,17},{2,10},{10... | collective-permute-start | bytes 1597448 | tf_op jit(solution)/shard_map/ppermute | solution.py:332
  18.7 24.3 %collective-permute-start.6 = (bf16[1040,256]{1,0:T(8,128)(2,1)S(1)}, bf16[1040,256]{1,0:T(8,128)(2,1)S(1)}, u32[]{:S(2)}, u32[]{:S(2)}) collective-permute-start(bf16[1040,256]{1,0:T(8,128)(2,1)S(1)} %get-tuple-element.50), channel_id=1, source_target_pairs={{0,16},{8,24},{16,0},{24,8},{1,17},{9,25},{17,1},{25,9},{2,18},{10... | collective-permute-start | bytes 1597448 | tf_op jit(solution)/shard_map/ppermute | solution.py:332
  20.2 24.5 %collective-permute-start.7 = (bf16[1040,256]{1,0:T(8,128)(2,1)S(1)}, bf16[1040,256]{1,0:T(8,128)(2,1)S(1)}, u32[]{:S(2)}, u32[]{:S(2)}) collective-permute-start(bf16[1040,256]{1,0:T(8,128)(2,1)S(1)} %get-tuple-element.51), channel_id=1, source_target_pairs={{0,24},{8,16},{16,8},{24,0},{1,25},{9,17},{17,9},{25,1},{2,26},{10... | collective-permute-start | bytes 1597448 | tf_op jit(solution)/shard_map/ppermute | solution.py:332
  36.7 1.7 %collective-permute-start.4 = (bf16[40,4096]{1,0:T(8,128)(2,1)S(1)}, bf16[40,4096]{1,0:T(8,128)(2,1)S(1)}, u32[]{:S(2)}, u32[]{:S(2)}) collective-permute-start(bf16[40,4096]{1,0:T(8,128)(2,1)S(1)} %slice.38), channel_id=1, source_target_pairs={{0,1},{1,0},{2,3},{3,2},{4,5},{5,4},{6,7},{7,6},{8,9},{9,8},{10,11... | collective-permute-start | bytes 983048 | tf_op jit(solution)/shard_map/ppermute | solution.py:332
  36.8 2.1 %collective-permute-start.3 = (bf16[40,4096]{1,0:T(8,128)(2,1)S(1)}, bf16[40,4096]{1,0:T(8,128)(2,1)S(1)}, u32[]{:S(2)}, u32[]{:S(2)}) collective-permute-start(bf16[40,4096]{1,0:T(8,128)(2,1)S(1)} %slice.37), channel_id=1, source_target_pairs={{0,1},{1,0},{2,3},{3,2},{4,5},{5,4},{6,7},{7,6},{8,9},{9,8},{10,11... | collective-permute-start | bytes 983048 | tf_op jit(solution)/shard_map/ppermute | solution.py:332
  38.4 30.8 %collective-permute-start.10 = (bf16[80,4096]{1,0:T(8,128)(2,1)S(1)}, bf16[80,4096]{1,0:T(8,128)(2,1)S(1)}, u32[]{:S(2)}, u32[]{:S(2)}) collective-permute-start(bf16[80,4096]{1,0:T(8,128)(2,1)S(1)} %get-tuple-element.57), channel_id=1, source_target_pairs={{0,6},{1,7},{2,4},{3,5},{4,2},{5,3},{6,0},{7,1},{8,14},{9,15},{10,... | collective-permute-start | bytes 1966088 | tf_op jit(solution)/shard_map/ppermute | solution.py:332
  44.7 31.9 %collective-permute-start.18 = (bf16[2400,256]{1,0:T(8,128)(2,1)S(1)}, bf16[2400,256]{1,0:T(8,128)(2,1)S(1)}, u32[]{:S(2)}, u32[]{:S(2)}) collective-permute-start(bf16[2400,256]{1,0:T(8,128)(2,1)S(1)} %get-tuple-element.69), channel_id=1, source_target_pairs={{0,8},{8,0},{16,24},{24,16},{1,9},{9,1},{17,25},{25,17},{2,10},{10... | collective-permute-start | bytes 3686408 | tf_op jit(solution)/shard_map/ppermute | solution.py:332
  45.5 33.1 %collective-permute-start.19 = (bf16[2400,256]{1,0:T(8,128)(2,1)S(1)}, bf16[2400,256]{1,0:T(8,128)(2,1)S(1)}, u32[]{:S(2)}, u32[]{:S(2)}) collective-permute-start(bf16[2400,256]{1,0:T(8,128)(2,1)S(1)} %get-tuple-element.70), channel_id=1, source_target_pairs={{0,16},{8,24},{16,0},{24,8},{1,17},{9,25},{17,1},{25,9},{2,18},{10... | collective-permute-start | bytes 3686408 | tf_op jit(solution)/shard_map/ppermute | solution.py:332
  69.2 1.7 %collective-permute-start.11 = (bf16[40,4096]{1,0:T(8,128)(2,1)S(1)}, bf16[40,4096]{1,0:T(8,128)(2,1)S(1)}, u32[]{:S(2)}, u32[]{:S(2)}) collective-permute-start(bf16[40,4096]{1,0:T(8,128)(2,1)S(1)} %slice.39), channel_id=1, source_target_pairs={{0,1},{1,0},{2,3},{3,2},{4,5},{5,4},{6,7},{7,6},{8,9},{9,8},{10,11... | collective-permute-start | bytes 983048 | tf_op jit(solution)/shard_map/ppermute | solution.py:332
  74.5 18.0 %collective-permute-start.15 = (bf16[1232,256]{1,0:T(8,128)(2,1)S(1)}, bf16[1232,256]{1,0:T(8,128)(2,1)S(1)}, u32[]{:S(2)}, u32[]{:S(2)}) collective-permute-start(bf16[1232,256]{1,0:T(8,128)(2,1)S(1)} %get-tuple-element.63), channel_id=1, source_target_pairs={{0,16},{8,24},{16,0},{24,8},{1,17},{9,25},{17,1},{25,9},{2,18},{10... | collective-permute-start | bytes 1892360 | tf_op jit(solution)/shard_map/ppermute | solution.py:332
  76.1 16.4 %collective-permute-start.14 = (bf16[1168,256]{1,0:T(8,128)(2,1)S(1)}, bf16[1168,256]{1,0:T(8,128)(2,1)S(1)}, u32[]{:S(2)}, u32[]{:S(2)}) collective-permute-start(bf16[1168,256]{1,0:T(8,128)(2,1)S(1)} %get-tuple-element.62), channel_id=1, source_target_pairs={{0,8},{8,0},{16,24},{24,16},{1,9},{9,1},{17,25},{25,17},{2,10},{10... | collective-permute-start | bytes 1794056 | tf_op jit(solution)/shard_map/ppermute | solution.py:332
  76.6 4.0 %collective-permute-start.8 = (f32[80,128]{1,0:T(8,128)S(1)}, f32[80,128]{1,0:T(8,128)S(1)}, u32[]{:S(2)}, u32[]{:S(2)}) collective-permute-start(f32[80,128]{1,0:T(8,128)S(1)} %get-tuple-element.54), channel_id=1, source_target_pairs={{0,2},{1,3},{2,0},{3,1},{4,6},{5,7},{6,4},{7,5},{8,10},{9,11},{10,... | collective-permute-start | bytes 122888 | tf_op jit(solution)/shard_map/ppermute | solution.py:332
  76.6 5.5 %collective-permute-start.9 = (f32[80,128]{1,0:T(8,128)S(1)}, f32[80,128]{1,0:T(8,128)S(1)}, u32[]{:S(2)}, u32[]{:S(2)}) collective-permute-start(f32[80,128]{1,0:T(8,128)S(1)} %get-tuple-element.55), channel_id=1, source_target_pairs={{0,4},{1,5},{2,6},{3,7},{4,0},{5,1},{6,2},{7,3},{8,12},{9,13},{10,... | collective-permute-start | bytes 122888 | tf_op jit(solution)/shard_map/ppermute | solution.py:332
  78.6 15.3 %copy-start.5 = (f32[128,2]{0,1:T(2,128)S(1)}, f32[128,2]{0,1:T(2,128)}, u32[]{:S(2)}) copy-start(f32[128,2]{0,1:T(2,128)} %param.8) | copy-start | bytes 3076
  78.6 4.7 %collective-permute-start.12 = (f32[80,128]{1,0:T(8,128)S(1)}, f32[80,128]{1,0:T(8,128)S(1)}, u32[]{:S(2)}, u32[]{:S(2)}) collective-permute-start(f32[80,128]{1,0:T(8,128)S(1)} %get-tuple-element.59), channel_id=1, source_target_pairs={{0,6},{1,7},{2,4},{3,5},{4,2},{5,3},{6,0},{7,1},{8,14},{9,15},{10,... | collective-permute-start | bytes 122888 | tf_op jit(solution)/shard_map/ppermute | solution.py:332
  80.6 23.3 %collective-permute-start.21 = (bf16[1040,256]{1,0:T(8,128)(2,1)S(1)}, bf16[1040,256]{1,0:T(8,128)(2,1)S(1)}, u32[]{:S(2)}, u32[]{:S(2)}) collective-permute-start(bf16[1040,256]{1,0:T(8,128)(2,1)S(1)} %slice.47), channel_id=1, source_target_pairs={{0,8},{8,0},{16,24},{24,16},{1,9},{9,1},{17,25},{25,17},{2,10},{10... | collective-permute-start | bytes 1597448 | tf_op jit(solution)/shard_map/ppermute | solution.py:332
  82.1 21.8 %collective-permute-start.20 = (bf16[1040,256]{1,0:T(8,128)(2,1)S(1)}, bf16[1040,256]{1,0:T(8,128)(2,1)S(1)}, u32[]{:S(2)}, u32[]{:S(2)}) collective-permute-start(bf16[1040,256]{1,0:T(8,128)(2,1)S(1)} %slice.46), channel_id=1, source_target_pairs={{0,16},{8,24},{16,0},{24,8},{1,17},{9,25},{17,1},{25,9},{2,18},{10... | collective-permute-start | bytes 1597448 | tf_op jit(solution)/shard_map/ppermute | solution.py:332
  83.2 1.3 %collective-permute-start.13 = (f32[160,128]{1,0:T(8,128)S(1)}, f32[160,128]{1,0:T(8,128)S(1)}, u32[]{:S(2)}, u32[]{:S(2)}) collective-permute-start(f32[160,128]{1,0:T(8,128)S(1)} %pad_maximum_fusion), channel_id=1, source_target_pairs={{0,1},{1,0},{2,3},{3,2},{4,5},{5,4},{6,7},{7,6},{8,9},{9,8},{10,11... | collective-permute-start | bytes 245768 | tf_op jit(solution)/shard_map/ppermute | solution.py:332
  92.5 17.1 %collective-permute-start.17 = (bf16[624,256]{1,0:T(8,128)(2,1)S(1)}, bf16[624,256]{1,0:T(8,128)(2,1)S(1)}, u32[]{:S(2)}, u32[]{:S(2)}) collective-permute-start(bf16[624,256]{1,0:T(8,128)(2,1)S(1)} %slice.45), channel_id=1, source_target_pairs={{0,8},{8,0},{16,24},{24,16},{1,9},{9,1},{17,25},{25,17},{2,10},{10... | collective-permute-start | bytes 958472 | tf_op jit(solution)/shard_map/ppermute | solution.py:332
  93.1 13.7 %collective-permute-start.16 = (bf16[416,256]{1,0:T(8,128)(2,1)S(1)}, bf16[416,256]{1,0:T(8,128)(2,1)S(1)}, u32[]{:S(2)}, u32[]{:S(2)}) collective-permute-start(bf16[416,256]{1,0:T(8,128)(2,1)S(1)} %slice.44), channel_id=1, source_target_pairs={{0,16},{8,24},{16,0},{24,8},{1,17},{9,25},{17,1},{25,9},{2,18},{10... | collective-permute-start | bytes 638984 | tf_op jit(solution)/shard_map/ppermute | solution.py:332
